TPU v7x, 128 devices: a whole 4x4x4 slice. The times are simulated.
128 devices in a mesh: ctx: 16 (over y, z_lo, core), tp: 8 (over x, z_hi).
Axes of the slice: x: 4, y: 4, z: 4 (z_hi: 2, z_lo: 2; z = z_hi * 2 + z_lo), core: 2. Of those that a mesh axis runs over, the one named last changes fastest.
Arguments:
- queries: bfloat16 [4096, 8192], P('ctx', 'tp'), may hold values from -6 to 6
- key_states: bfloat16 [4096, 1024], P('ctx', 'tp'), may hold values from -6 to 6
- value_states: bfloat16 [4096, 1024], P('ctx', 'tp'), may hold values from -6 to 6
- attn_output: bfloat16 [4096, 8192], P('ctx', 'tp'), may hold values from -3 to 3
- output_grad: bfloat16 [4096, 8192], P('ctx', 'tp'), may hold values from -16 to 16
- log_norms: float32 [64, 4096], P('tp', 'ctx')
- layer_input: bfloat16 [4096, 8192], P('ctx', 'tp'), may hold values from -6 to 6
- doc_lengths: int32 [16], replicated, may hold values from 1 to 2048, as said below
Outputs:
- query_grad: bfloat16 [4096, 8192], P('ctx', 'tp')
- key_weight_grad: float32 [8192, 1024], P('ctx', 'tp')
- value_weight_grad: float32 [8192, 1024], P('ctx', 'tp')
Inputs may be any that keep to these rules, and one draw needn't show every extreme that they name: `doc_lengths`: the 16 lengths sum to 4096; the first document is exactly 2048 tokens long.
All inputs are finite; a program needn't handle non-finite values.
Results may differ from a plain program's by a relative error of at most 0.006.
Values may be sent and summed in bfloat16 or wider, within the bound.
No kernel may reach another device: no remote copies, remote signals or barrier semaphores. Data moves between devices by JAX's collectives and lax.ppermute only.
A program may use at most 64 MiB of HBM per device.

v0:
```python
import math

import jax
import jax.numpy as jnp
from jax import lax
from jax.sharding import PartitionSpec as P

QH = 64
KVH = 8
HD = 128


def passed_along(value, axis, steps):
    count = lax.axis_size(axis)
    first, last = (max(0, -steps), min(count, count - steps))
    return lax.ppermute(value, axis, [(source, source + steps) for source in range(first, last)])


def from_behind(block, axis, distance):
    devices = range(lax.axis_size(axis))
    route = [((i - distance) % len(devices), i) for i in devices]
    return lax.ppermute(block, axis, route)


def doc_first(doc_lengths, positions):
    doc_ends = jnp.cumsum(doc_lengths)
    return jnp.max(jnp.where(doc_ends[None, :] <= positions[:, None], doc_ends[None, :], 0), axis=1)


def on_device(
    queries, key_states, value_states, attn_output, output_grad, log_norms, layer_input, doc_lengths
):
    row_count = queries.shape[0]
    local_heads = key_states.shape[1] // HD
    group_size = QH // KVH
    score_scale = 1.0 / math.sqrt(HD)
    cycle_size = lax.axis_size("ctx")
    my_index = lax.axis_index("ctx")
    query_pos = my_index * row_count + jnp.arange(row_count, dtype=jnp.int32)
    first_keys = doc_first(doc_lengths, query_pos)
    query_heads = queries.reshape(row_count, local_heads, group_size, HD)
    grad_heads = output_grad.reshape(row_count, local_heads, group_size, HD)
    out_heads = attn_output.reshape(row_count, local_heads, group_size, HD)
    row_dots = jnp.sum(grad_heads.astype(jnp.float32) * out_heads.astype(jnp.float32), axis=-1)
    row_dots = jnp.transpose(row_dots, (1, 2, 0))
    norm_heads = log_norms.reshape(local_heads, group_size, row_count)
    gathered = lax.all_gather(layer_input, "tp", axis=1, tiled=True)

    def block_terms(key_block, value_block, key_start):
        key_count = key_block.shape[0]
        key_heads = key_block.reshape(key_count, local_heads, HD)
        value_heads = value_block.reshape(key_count, local_heads, HD)
        key_pos = key_start + jnp.arange(key_count, dtype=jnp.int32)
        visible = (key_pos[None, :] <= query_pos[:, None]) & (
            key_pos[None, :] >= first_keys[:, None]
        )
        scores = (
            jnp.einsum("tkgd,skd->kgts", query_heads, key_heads, preferred_element_type=jnp.float32)
            * score_scale
        )
        probs = jnp.where(visible, jnp.exp(scores - norm_heads[..., None]), jnp.float32(0.0))
        probs_low = probs.astype(jnp.bfloat16)
        value_term = jnp.einsum(
            "kgts,tkgd->skd", probs_low, grad_heads, preferred_element_type=jnp.float32
        )
        prob_grad = jnp.einsum(
            "tkgd,skd->kgts", grad_heads, value_heads, preferred_element_type=jnp.float32
        )
        score_grad = (probs * (prob_grad - row_dots[..., None])).astype(jnp.bfloat16)
        query_term = jnp.einsum(
            "kgts,skd->tkgd", score_grad, key_heads, preferred_element_type=jnp.float32
        )
        key_term = jnp.einsum(
            "kgts,tkgd->skd", score_grad, query_heads, preferred_element_type=jnp.float32
        )
        return (
            query_term,
            key_term.reshape(key_count, local_heads * HD),
            value_term.reshape(key_count, local_heads * HD),
        )

    def guarded(key_block, value_block, key_start):
        return block_terms(key_block, value_block, key_start)

    query_empty = jnp.zeros((row_count, local_heads, group_size, HD), jnp.float32)

    def advance(step_index, carried):
        key_block, value_block, key_sums, value_sums, query_sums = carried
        anchor = (my_index - step_index) % cycle_size
        query_term, key_term, value_term = guarded(key_block, value_block, anchor * row_count)
        key_sums = key_sums + key_term
        value_sums = value_sums + value_term
        key_block, value_block = passed_along((key_block, value_block), "ctx", 1)
        key_sums, value_sums = from_behind((key_sums, value_sums), "ctx", 1)
        return (key_block, value_block, key_sums, value_sums, query_sums + query_term)

    grad_empty = jnp.zeros((row_count, local_heads * HD), jnp.float32)
    carried = lax.fori_loop(
        0, cycle_size, advance, (key_states, value_states, grad_empty, grad_empty, query_empty)
    )
    key_sums, value_sums, query_sums = (carried[2], carried[3], carried[4])
    query_grad = (
        (query_sums * score_scale)
        .reshape(row_count, local_heads * group_size * HD)
        .astype(jnp.bfloat16)
    )
    key_low = (key_sums * score_scale).astype(jnp.bfloat16)
    value_low = value_sums.astype(jnp.bfloat16)
    both_low = jnp.concatenate([key_low, value_low], axis=1)
    weights = lax.psum_scatter(
        jnp.einsum("td,tc->dc", gathered, both_low, preferred_element_type=jnp.float32),
        "ctx",
        scatter_dimension=0,
        tiled=True,
    )
    head_width = local_heads * HD
    return (query_grad, weights[:, :head_width], weights[:, head_width:])


def solution(mesh):
    placed = (
        P("ctx", "tp"),
        P("ctx", "tp"),
        P("ctx", "tp"),
        P("ctx", "tp"),
        P("ctx", "tp"),
        P("tp", "ctx"),
        P("ctx", "tp"),
        P(),
    )
    return jax.shard_map(
        on_device,
        mesh=mesh,
        in_specs=placed,
        out_specs=(P("ctx", "tp"), P("ctx", "tp"), P("ctx", "tp")),
        check_vma=False,
    )
```

profile of v0, /device:TPU:1, one launch (start us, length us, event | category | flops | bytes accessed | tf_op | source)
XLA Modules:
  0.0 402.1 jit_solution(12722647078494453463)
XLA Ops:
  14.7 270.2 %while.24 = (s32[]{:T(128)}, bf16[256,128]{1,0:T(8,128)(2,1)}, bf16[256,128]{1,0:T(8,128)(2,1)}, f32[256,128]{1,0:T(8,128)S(1)}, f32[256,128]{1,0:T(8,128)S(1)},...) while((s32[]{:T(128)}, bf16[256,128]{1,0:T(8,128)(2,1)}, ...), condition=%wide.region_4.5_spmd.clone, body=%wide.region_3.4_spmd.clone.sunk | while | flops 675545600 | bytes 16340444 | solution.py:98
  15.6 4.9 %collective-permute-start.1 = (bf16[256,128]{1,0:T(8,128)(2,1)S(1)}, bf16[256,128]{1,0:T(8,128)(2,1)}, u32[]{:S(2)}, u32[]{:S(2)}) collective-permute-start(bf16[256,128]{1,0:T(8,128)(2,1)S(1)} %copy.48), channel_id=1, source_target_pairs={{0,8},{8,16},{16,24},{24,32},{32,40},{40,48},{48,56},{56,64},{64,7... | collective-permute-start | bytes 196616 | tf_op jit(solution)/shard_map/while/body/eval_jaxpr/ppermute | solution.py:16
  34.1 4.3 %collective-permute-start.1 = (bf16[256,128]{1,0:T(8,128)(2,1)S(1)}, bf16[256,128]{1,0:T(8,128)(2,1)}, u32[]{:S(2)}, u32[]{:S(2)}) collective-permute-start(bf16[256,128]{1,0:T(8,128)(2,1)S(1)} %copy.48), channel_id=1, source_target_pairs={{0,8},{8,16},{16,24},{24,32},{32,40},{40,48},{48,56},{56,64},{64,7... | collective-permute-start | bytes 196616 | tf_op jit(solution)/shard_map/while/body/eval_jaxpr/ppermute | solution.py:16
  49.5 4.3 %collective-permute-start.1 = (bf16[256,128]{1,0:T(8,128)(2,1)S(1)}, bf16[256,128]{1,0:T(8,128)(2,1)}, u32[]{:S(2)}, u32[]{:S(2)}) collective-permute-start(bf16[256,128]{1,0:T(8,128)(2,1)S(1)} %copy.48), channel_id=1, source_target_pairs={{0,8},{8,16},{16,24},{24,32},{32,40},{40,48},{48,56},{56,64},{64,7... | collective-permute-start | bytes 196616 | tf_op jit(solution)/shard_map/while/body/eval_jaxpr/ppermute | solution.py:16
  59.7 3.3 collective-permute-start.2
  65.0 3.0 collective-permute-done.2
  67.9 4.2 %collective-permute-done.3 = f32[256,128]{1,0:T(8,128)S(1)} collective-permute-done((f32[256,128]{1,0:T(8,128)}, f32[256,128]{1,0:T(8,128)S(1)}, u32[]{:S(2)}, u32[]{:S(2)}) %collective-permute-start.3) | collective-permute-done | bytes 131104 | tf_op jit(solution)/shard_map/while/body/eval_jaxpr/ppermute | solution.py:22
  73.0 4.3 %collective-permute-start.1 = (bf16[256,128]{1,0:T(8,128)(2,1)S(1)}, bf16[256,128]{1,0:T(8,128)(2,1)}, u32[]{:S(2)}, u32[]{:S(2)}) collective-permute-start(bf16[256,128]{1,0:T(8,128)(2,1)S(1)} %copy.48), channel_id=1, source_target_pairs={{0,8},{8,16},{16,24},{24,32},{32,40},{40,48},{48,56},{56,64},{64,7... | collective-permute-start | bytes 196616 | tf_op jit(solution)/shard_map/while/body/eval_jaxpr/ppermute | solution.py:16
  88.0 4.2 %collective-permute-start.1 = (bf16[256,128]{1,0:T(8,128)(2,1)S(1)}, bf16[256,128]{1,0:T(8,128)(2,1)}, u32[]{:S(2)}, u32[]{:S(2)}) collective-permute-start(bf16[256,128]{1,0:T(8,128)(2,1)S(1)} %copy.48), channel_id=1, source_target_pairs={{0,8},{8,16},{16,24},{24,32},{32,40},{40,48},{48,56},{56,64},{64,7... | collective-permute-start | bytes 196616 | tf_op jit(solution)/shard_map/while/body/eval_jaxpr/ppermute | solution.py:16
  98.3 3.3 collective-permute-start.2
  106.1 4.3 %collective-permute-start.1 = (bf16[256,128]{1,0:T(8,128)(2,1)S(1)}, bf16[256,128]{1,0:T(8,128)(2,1)}, u32[]{:S(2)}, u32[]{:S(2)}) collective-permute-start(bf16[256,128]{1,0:T(8,128)(2,1)S(1)} %copy.48), channel_id=1, source_target_pairs={{0,8},{8,16},{16,24},{24,32},{32,40},{40,48},{48,56},{56,64},{64,7... | collective-permute-start | bytes 196616 | tf_op jit(solution)/shard_map/while/body/eval_jaxpr/ppermute | solution.py:16
  121.5 4.3 %collective-permute-start.1 = (bf16[256,128]{1,0:T(8,128)(2,1)S(1)}, bf16[256,128]{1,0:T(8,128)(2,1)}, u32[]{:S(2)}, u32[]{:S(2)}) collective-permute-start(bf16[256,128]{1,0:T(8,128)(2,1)S(1)} %copy.48), channel_id=1, source_target_pairs={{0,8},{8,16},{16,24},{24,32},{32,40},{40,48},{48,56},{56,64},{64,7... | collective-permute-start | bytes 196616 | tf_op jit(solution)/shard_map/while/body/eval_jaxpr/ppermute | solution.py:16
  131.5 2.8 collective-permute-start.2
  138.8 4.3 %collective-permute-start.1 = (bf16[256,128]{1,0:T(8,128)(2,1)S(1)}, bf16[256,128]{1,0:T(8,128)(2,1)}, u32[]{:S(2)}, u32[]{:S(2)}) collective-permute-start(bf16[256,128]{1,0:T(8,128)(2,1)S(1)} %copy.48), channel_id=1, source_target_pairs={{0,8},{8,16},{16,24},{24,32},{32,40},{40,48},{48,56},{56,64},{64,7... | collective-permute-start | bytes 196616 | tf_op jit(solution)/shard_map/while/body/eval_jaxpr/ppermute | solution.py:16
  154.2 4.3 %collective-permute-start.1 = (bf16[256,128]{1,0:T(8,128)(2,1)S(1)}, bf16[256,128]{1,0:T(8,128)(2,1)}, u32[]{:S(2)}, u32[]{:S(2)}) collective-permute-start(bf16[256,128]{1,0:T(8,128)(2,1)S(1)} %copy.48), channel_id=1, source_target_pairs={{0,8},{8,16},{16,24},{24,32},{32,40},{40,48},{48,56},{56,64},{64,7... | collective-permute-start | bytes 196616 | tf_op jit(solution)/shard_map/while/body/eval_jaxpr/ppermute | solution.py:16
  169.9 4.1 %collective-permute-start.1 = (bf16[256,128]{1,0:T(8,128)(2,1)S(1)}, bf16[256,128]{1,0:T(8,128)(2,1)}, u32[]{:S(2)}, u32[]{:S(2)}) collective-permute-start(bf16[256,128]{1,0:T(8,128)(2,1)S(1)} %copy.48), channel_id=1, source_target_pairs={{0,8},{8,16},{16,24},{24,32},{32,40},{40,48},{48,56},{56,64},{64,7... | collective-permute-start | bytes 196616 | tf_op jit(solution)/shard_map/while/body/eval_jaxpr/ppermute | solution.py:16
  186.5 4.3 %collective-permute-start.1 = (bf16[256,128]{1,0:T(8,128)(2,1)S(1)}, bf16[256,128]{1,0:T(8,128)(2,1)}, u32[]{:S(2)}, u32[]{:S(2)}) collective-permute-start(bf16[256,128]{1,0:T(8,128)(2,1)S(1)} %copy.48), channel_id=1, source_target_pairs={{0,8},{8,16},{16,24},{24,32},{32,40},{40,48},{48,56},{56,64},{64,7... | collective-permute-start | bytes 196616 | tf_op jit(solution)/shard_map/while/body/eval_jaxpr/ppermute | solution.py:16
  203.0 4.3 %collective-permute-start.1 = (bf16[256,128]{1,0:T(8,128)(2,1)S(1)}, bf16[256,128]{1,0:T(8,128)(2,1)}, u32[]{:S(2)}, u32[]{:S(2)}) collective-permute-start(bf16[256,128]{1,0:T(8,128)(2,1)S(1)} %copy.48), channel_id=1, source_target_pairs={{0,8},{8,16},{16,24},{24,32},{32,40},{40,48},{48,56},{56,64},{64,7... | collective-permute-start | bytes 196616 | tf_op jit(solution)/shard_map/while/body/eval_jaxpr/ppermute | solution.py:16
  219.6 4.3 %collective-permute-start.1 = (bf16[256,128]{1,0:T(8,128)(2,1)S(1)}, bf16[256,128]{1,0:T(8,128)(2,1)}, u32[]{:S(2)}, u32[]{:S(2)}) collective-permute-start(bf16[256,128]{1,0:T(8,128)(2,1)S(1)} %copy.48), channel_id=1, source_target_pairs={{0,8},{8,16},{16,24},{24,32},{32,40},{40,48},{48,56},{56,64},{64,7... | collective-permute-start | bytes 196616 | tf_op jit(solution)/shard_map/while/body/eval_jaxpr/ppermute | solution.py:16
  236.1 4.3 %collective-permute-start.1 = (bf16[256,128]{1,0:T(8,128)(2,1)S(1)}, bf16[256,128]{1,0:T(8,128)(2,1)}, u32[]{:S(2)}, u32[]{:S(2)}) collective-permute-start(bf16[256,128]{1,0:T(8,128)(2,1)S(1)} %copy.48), channel_id=1, source_target_pairs={{0,8},{8,16},{16,24},{24,32},{32,40},{40,48},{48,56},{56,64},{64,7... | collective-permute-start | bytes 196616 | tf_op jit(solution)/shard_map/while/body/eval_jaxpr/ppermute | solution.py:16
  252.7 4.3 %collective-permute-start.1 = (bf16[256,128]{1,0:T(8,128)(2,1)S(1)}, bf16[256,128]{1,0:T(8,128)(2,1)}, u32[]{:S(2)}, u32[]{:S(2)}) collective-permute-start(bf16[256,128]{1,0:T(8,128)(2,1)S(1)} %copy.48), channel_id=1, source_target_pairs={{0,8},{8,16},{16,24},{24,32},{32,40},{40,48},{48,56},{56,64},{64,7... | collective-permute-start | bytes 196616 | tf_op jit(solution)/shard_map/while/body/eval_jaxpr/ppermute | solution.py:16
  269.2 4.3 %collective-permute-start.1 = (bf16[256,128]{1,0:T(8,128)(2,1)S(1)}, bf16[256,128]{1,0:T(8,128)(2,1)}, u32[]{:S(2)}, u32[]{:S(2)}) collective-permute-start(bf16[256,128]{1,0:T(8,128)(2,1)S(1)} %copy.48), channel_id=1, source_target_pairs={{0,8},{8,16},{16,24},{24,32},{32,40},{40,48},{48,56},{56,64},{64,7... | collective-permute-start | bytes 196616 | tf_op jit(solution)/shard_map/while/body/eval_jaxpr/ppermute | solution.py:16
  285.0 6.7 %convolution_bitcast_fusion.3 = f32[8192,256]{0,1:T(8,128)} fusion(bf16[256,8192]{1,0:T(8,128)(2,1)} %all-gather.2.cloned.1.call-done, bf16[256,128]{1,0:T(8,128)(2,1)S(1)} %convert_element_type.63, bf16[256,128]{1,0:T(8,128)(2,1)S(1)} %multiply_convert_fusion.1), kind=kOutput, calls=%fused_computation.26 | convolution fusion | flops 1074003968 | bytes 12713984 | tf_op jit(solution)/shard_map/td,tc->dc/dot_general | solution.py:111
  293.1 99.4 %reduce-scatter.2.cloned.1.call-done = f32[512,256]{0,1:T(8,128)} async-done(((f32[8192,256]{0,1:T(8,128)}), f32[512,256]{0,1:T(8,128)}) %reduce-scatter.2.cloned.1.call-update) | async-done | bytes 524304 | tf_op jit(solution)/shard_map/reduce_scatter | solution.py:110
  (298 shorter events, 194.8 us)
Async XLA Ops:
  7.2 277.8 %all-gather.2.cloned.1.call-start = ((), (), s32[]{:S(2)}) async-start(), calls=%async_computation.1 | async-start | bytes 4718592 | tf_op jit(solution)/shard_map/all_gather | solution.py:47
  10.2 382.3 %reduce-scatter.2.cloned.1.call-start = ((), (), s32[]{:S(2)}) async-start(), calls=%async_computation.2 | async-start | bytes 8912896 | tf_op jit(solution)/shard_map/reduce_scatter | solution.py:110
  15.6 13.9 %collective-permute-start.1 = (bf16[256,128]{1,0:T(8,128)(2,1)S(1)}, bf16[256,128]{1,0:T(8,128)(2,1)}, u32[]{:S(2)}, u32[]{:S(2)}) collective-permute-start(bf16[256,128]{1,0:T(8,128)(2,1)S(1)} %copy.48), channel_id=1, source_target_pairs={{0,8},{8,16},{16,24},{24,32},{32,40},{40,48},{48,56},{56,64},{64,7... | collective-permute-start | bytes 196616 | tf_op jit(solution)/shard_map/while/body/eval_jaxpr/ppermute | solution.py:16
  34.1 13.0 %collective-permute-start.1 = (bf16[256,128]{1,0:T(8,128)(2,1)S(1)}, bf16[256,128]{1,0:T(8,128)(2,1)}, u32[]{:S(2)}, u32[]{:S(2)}) collective-permute-start(bf16[256,128]{1,0:T(8,128)(2,1)S(1)} %copy.48), channel_id=1, source_target_pairs={{0,8},{8,16},{16,24},{24,32},{32,40},{40,48},{48,56},{56,64},{64,7... | collective-permute-start | bytes 196616 | tf_op jit(solution)/shard_map/while/body/eval_jaxpr/ppermute | solution.py:16
  49.5 15.4 %collective-permute-start.1 = (bf16[256,128]{1,0:T(8,128)(2,1)S(1)}, bf16[256,128]{1,0:T(8,128)(2,1)}, u32[]{:S(2)}, u32[]{:S(2)}) collective-permute-start(bf16[256,128]{1,0:T(8,128)(2,1)S(1)} %copy.48), channel_id=1, source_target_pairs={{0,8},{8,16},{16,24},{24,32},{32,40},{40,48},{48,56},{56,64},{64,7... | collective-permute-start | bytes 196616 | tf_op jit(solution)/shard_map/while/body/eval_jaxpr/ppermute | solution.py:16
  54.6 10.3 %collective-permute-start = (bf16[256,128]{1,0:T(8,128)(2,1)S(1)}, bf16[256,128]{1,0:T(8,128)(2,1)}, u32[]{:S(2)}, u32[]{:S(2)}) collective-permute-start(bf16[256,128]{1,0:T(8,128)(2,1)S(1)} %copy.47), channel_id=1, source_target_pairs={{0,8},{8,16},{16,24},{24,32},{32,40},{40,48},{48,56},{56,64},{64,7... | collective-permute-start | bytes 196616 | tf_op jit(solution)/shard_map/while/body/eval_jaxpr/ppermute | solution.py:16
  73.0 12.8 %collective-permute-start.1 = (bf16[256,128]{1,0:T(8,128)(2,1)S(1)}, bf16[256,128]{1,0:T(8,128)(2,1)}, u32[]{:S(2)}, u32[]{:S(2)}) collective-permute-start(bf16[256,128]{1,0:T(8,128)(2,1)S(1)} %copy.48), channel_id=1, source_target_pairs={{0,8},{8,16},{16,24},{24,32},{32,40},{40,48},{48,56},{56,64},{64,7... | collective-permute-start | bytes 196616 | tf_op jit(solution)/shard_map/while/body/eval_jaxpr/ppermute | solution.py:16
  88.0 15.6 %collective-permute-start.1 = (bf16[256,128]{1,0:T(8,128)(2,1)S(1)}, bf16[256,128]{1,0:T(8,128)(2,1)}, u32[]{:S(2)}, u32[]{:S(2)}) collective-permute-start(bf16[256,128]{1,0:T(8,128)(2,1)S(1)} %copy.48), channel_id=1, source_target_pairs={{0,8},{8,16},{16,24},{24,32},{32,40},{40,48},{48,56},{56,64},{64,7... | collective-permute-start | bytes 196616 | tf_op jit(solution)/shard_map/while/body/eval_jaxpr/ppermute | solution.py:16
  93.1 10.5 %collective-permute-start = (bf16[256,128]{1,0:T(8,128)(2,1)S(1)}, bf16[256,128]{1,0:T(8,128)(2,1)}, u32[]{:S(2)}, u32[]{:S(2)}) collective-permute-start(bf16[256,128]{1,0:T(8,128)(2,1)S(1)} %copy.47), channel_id=1, source_target_pairs={{0,8},{8,16},{16,24},{24,32},{32,40},{40,48},{48,56},{56,64},{64,7... | collective-permute-start | bytes 196616 | tf_op jit(solution)/shard_map/while/body/eval_jaxpr/ppermute | solution.py:16
  106.1 12.9 %collective-permute-start.1 = (bf16[256,128]{1,0:T(8,128)(2,1)S(1)}, bf16[256,128]{1,0:T(8,128)(2,1)}, u32[]{:S(2)}, u32[]{:S(2)}) collective-permute-start(bf16[256,128]{1,0:T(8,128)(2,1)S(1)} %copy.48), channel_id=1, source_target_pairs={{0,8},{8,16},{16,24},{24,32},{32,40},{40,48},{48,56},{56,64},{64,7... | collective-permute-start | bytes 196616 | tf_op jit(solution)/shard_map/while/body/eval_jaxpr/ppermute | solution.py:16
  121.5 14.9 %collective-permute-start.1 = (bf16[256,128]{1,0:T(8,128)(2,1)S(1)}, bf16[256,128]{1,0:T(8,128)(2,1)}, u32[]{:S(2)}, u32[]{:S(2)}) collective-permute-start(bf16[256,128]{1,0:T(8,128)(2,1)S(1)} %copy.48), channel_id=1, source_target_pairs={{0,8},{8,16},{16,24},{24,32},{32,40},{40,48},{48,56},{56,64},{64,7... | collective-permute-start | bytes 196616 | tf_op jit(solution)/shard_map/while/body/eval_jaxpr/ppermute | solution.py:16
  126.6 9.7 %collective-permute-start = (bf16[256,128]{1,0:T(8,128)(2,1)S(1)}, bf16[256,128]{1,0:T(8,128)(2,1)}, u32[]{:S(2)}, u32[]{:S(2)}) collective-permute-start(bf16[256,128]{1,0:T(8,128)(2,1)S(1)} %copy.47), channel_id=1, source_target_pairs={{0,8},{8,16},{16,24},{24,32},{32,40},{40,48},{48,56},{56,64},{64,7... | collective-permute-start | bytes 196616 | tf_op jit(solution)/shard_map/while/body/eval_jaxpr/ppermute | solution.py:16
  138.8 12.9 %collective-permute-start.1 = (bf16[256,128]{1,0:T(8,128)(2,1)S(1)}, bf16[256,128]{1,0:T(8,128)(2,1)}, u32[]{:S(2)}, u32[]{:S(2)}) collective-permute-start(bf16[256,128]{1,0:T(8,128)(2,1)S(1)} %copy.48), channel_id=1, source_target_pairs={{0,8},{8,16},{16,24},{24,32},{32,40},{40,48},{48,56},{56,64},{64,7... | collective-permute-start | bytes 196616 | tf_op jit(solution)/shard_map/while/body/eval_jaxpr/ppermute | solution.py:16
  154.2 12.9 %collective-permute-start.1 = (bf16[256,128]{1,0:T(8,128)(2,1)S(1)}, bf16[256,128]{1,0:T(8,128)(2,1)}, u32[]{:S(2)}, u32[]{:S(2)}) collective-permute-start(bf16[256,128]{1,0:T(8,128)(2,1)S(1)} %copy.48), channel_id=1, source_target_pairs={{0,8},{8,16},{16,24},{24,32},{32,40},{40,48},{48,56},{56,64},{64,7... | collective-permute-start | bytes 196616 | tf_op jit(solution)/shard_map/while/body/eval_jaxpr/ppermute | solution.py:16
  169.9 14.1 %collective-permute-start.1 = (bf16[256,128]{1,0:T(8,128)(2,1)S(1)}, bf16[256,128]{1,0:T(8,128)(2,1)}, u32[]{:S(2)}, u32[]{:S(2)}) collective-permute-start(bf16[256,128]{1,0:T(8,128)(2,1)S(1)} %copy.48), channel_id=1, source_target_pairs={{0,8},{8,16},{16,24},{24,32},{32,40},{40,48},{48,56},{56,64},{64,7... | collective-permute-start | bytes 196616 | tf_op jit(solution)/shard_map/while/body/eval_jaxpr/ppermute | solution.py:16
  174.8 9.2 %collective-permute-start = (bf16[256,128]{1,0:T(8,128)(2,1)S(1)}, bf16[256,128]{1,0:T(8,128)(2,1)}, u32[]{:S(2)}, u32[]{:S(2)}) collective-permute-start(bf16[256,128]{1,0:T(8,128)(2,1)S(1)} %copy.47), channel_id=1, source_target_pairs={{0,8},{8,16},{16,24},{24,32},{32,40},{40,48},{48,56},{56,64},{64,7... | collective-permute-start | bytes 196616 | tf_op jit(solution)/shard_map/while/body/eval_jaxpr/ppermute | solution.py:16
  186.5 14.1 %collective-permute-start.1 = (bf16[256,128]{1,0:T(8,128)(2,1)S(1)}, bf16[256,128]{1,0:T(8,128)(2,1)}, u32[]{:S(2)}, u32[]{:S(2)}) collective-permute-start(bf16[256,128]{1,0:T(8,128)(2,1)S(1)} %copy.48), channel_id=1, source_target_pairs={{0,8},{8,16},{16,24},{24,32},{32,40},{40,48},{48,56},{56,64},{64,7... | collective-permute-start | bytes 196616 | tf_op jit(solution)/shard_map/while/body/eval_jaxpr/ppermute | solution.py:16
  203.0 14.1 %collective-permute-start.1 = (bf16[256,128]{1,0:T(8,128)(2,1)S(1)}, bf16[256,128]{1,0:T(8,128)(2,1)}, u32[]{:S(2)}, u32[]{:S(2)}) collective-permute-start(bf16[256,128]{1,0:T(8,128)(2,1)S(1)} %copy.48), channel_id=1, source_target_pairs={{0,8},{8,16},{16,24},{24,32},{32,40},{40,48},{48,56},{56,64},{64,7... | collective-permute-start | bytes 196616 | tf_op jit(solution)/shard_map/while/body/eval_jaxpr/ppermute | solution.py:16
  219.6 14.1 %collective-permute-start.1 = (bf16[256,128]{1,0:T(8,128)(2,1)S(1)}, bf16[256,128]{1,0:T(8,128)(2,1)}, u32[]{:S(2)}, u32[]{:S(2)}) collective-permute-start(bf16[256,128]{1,0:T(8,128)(2,1)S(1)} %copy.48), channel_id=1, source_target_pairs={{0,8},{8,16},{16,24},{24,32},{32,40},{40,48},{48,56},{56,64},{64,7... | collective-permute-start | bytes 196616 | tf_op jit(solution)/shard_map/while/body/eval_jaxpr/ppermute | solution.py:16
  224.7 9.0 %collective-permute-start = (bf16[256,128]{1,0:T(8,128)(2,1)S(1)}, bf16[256,128]{1,0:T(8,128)(2,1)}, u32[]{:S(2)}, u32[]{:S(2)}) collective-permute-start(bf16[256,128]{1,0:T(8,128)(2,1)S(1)} %copy.47), channel_id=1, source_target_pairs={{0,8},{8,16},{16,24},{24,32},{32,40},{40,48},{48,56},{56,64},{64,7... | collective-permute-start | bytes 196616 | tf_op jit(solution)/shard_map/while/body/eval_jaxpr/ppermute | solution.py:16
  236.1 14.1 %collective-permute-start.1 = (bf16[256,128]{1,0:T(8,128)(2,1)S(1)}, bf16[256,128]{1,0:T(8,128)(2,1)}, u32[]{:S(2)}, u32[]{:S(2)}) collective-permute-start(bf16[256,128]{1,0:T(8,128)(2,1)S(1)} %copy.48), channel_id=1, source_target_pairs={{0,8},{8,16},{16,24},{24,32},{32,40},{40,48},{48,56},{56,64},{64,7... | collective-permute-start | bytes 196616 | tf_op jit(solution)/shard_map/while/body/eval_jaxpr/ppermute | solution.py:16
  252.7 14.1 %collective-permute-start.1 = (bf16[256,128]{1,0:T(8,128)(2,1)S(1)}, bf16[256,128]{1,0:T(8,128)(2,1)}, u32[]{:S(2)}, u32[]{:S(2)}) collective-permute-start(bf16[256,128]{1,0:T(8,128)(2,1)S(1)} %copy.48), channel_id=1, source_target_pairs={{0,8},{8,16},{16,24},{24,32},{32,40},{40,48},{48,56},{56,64},{64,7... | collective-permute-start | bytes 196616 | tf_op jit(solution)/shard_map/while/body/eval_jaxpr/ppermute | solution.py:16
  257.8 9.0 %collective-permute-start = (bf16[256,128]{1,0:T(8,128)(2,1)S(1)}, bf16[256,128]{1,0:T(8,128)(2,1)}, u32[]{:S(2)}, u32[]{:S(2)}) collective-permute-start(bf16[256,128]{1,0:T(8,128)(2,1)S(1)} %copy.47), channel_id=1, source_target_pairs={{0,8},{8,16},{16,24},{24,32},{32,40},{40,48},{48,56},{56,64},{64,7... | collective-permute-start | bytes 196616 | tf_op jit(solution)/shard_map/while/body/eval_jaxpr/ppermute | solution.py:16
  269.2 14.1 %collective-permute-start.1 = (bf16[256,128]{1,0:T(8,128)(2,1)S(1)}, bf16[256,128]{1,0:T(8,128)(2,1)}, u32[]{:S(2)}, u32[]{:S(2)}) collective-permute-start(bf16[256,128]{1,0:T(8,128)(2,1)S(1)} %copy.48), channel_id=1, source_target_pairs={{0,8},{8,16},{16,24},{24,32},{32,40},{40,48},{48,56},{56,64},{64,7... | collective-permute-start | bytes 196616 | tf_op jit(solution)/shard_map/while/body/eval_jaxpr/ppermute | solution.py:16
  (43 other events, 210.1 us)
Sparse Core Ops, SparseCore 0:
  10.4 81.3 all-gather.1
  291.9 100.6 reduce-scatter.1
where the time goes:
time: 406 us; the launch traced here: 402 us
  waiting for transfers between devices  133 us (33%)
  starting transfers between devices  130 us (32%)
  matrix products  83 us (20%)
  local copies, waits for them, and re-layouts  37.8 us (9%)
  between operations  14.2 us (3%)
    ppermute x32, starting transfers between devices, passed_along(): lax.ppermute(value, axis, [(source, source + steps) for source in range(f...  99.7 us
    reduce_scatter x1, waiting for transfers between devices, on_device(): lax.psum_scatter(jnp.einsum('td,tc->dc', gathered, both_low, preferred_el...  99.4 us
    ppermute x32, waiting for transfers between devices, from_behind(): return lax.ppermute(block, axis, route)  33.5 us
    ppermute x32, starting transfers between devices, from_behind(): return lax.ppermute(block, axis, route)  29.9 us
    while x32, local copies, waits for them, and re-layouts  26.9 us
    dot_general x16, matrix products, block_terms(): jnp.einsum('tkgd,skd->kgts', query_heads, key_heads, preferred_element_ty...  20.4 us
    dot_general x16, matrix products, block_terms(): jnp.einsum('kgts,tkgd->skd', probs_low, grad_heads, preferred_element_typ...  17.6 us
    dot_general x16, matrix products, block_terms(): jnp.einsum('kgts,tkgd->skd', score_grad, query_heads, preferred_element_t...  17.3 us
  transfers between devices with their start and end apart: 66, of which 32 were waited for; matrix products, arithmetic and copies ran while one was open for 28% of the time, Pallas kernels for 0%

commit v1 on v0

v1 whole, which is shorter than its diff:
```python
import functools
import itertools
import math

import jax
import jax.numpy as jnp
from jax import lax
from jax.experimental import pallas as pl
from jax.experimental.pallas import tpu as pltpu
from jax.sharding import PartitionSpec as P

HD = 128
HEADS = 8
ROWS = 256
WIDTH = HEADS * HD
SCALE = 1.0 / math.sqrt(HD)
LOG2E = math.log2(math.e)
AXES = ("ctx", "tp")
STEP_HEADS = 2
VMEM = 56 * 1024 * 1024

f32 = jnp.float32
bf16 = jnp.bfloat16


def linear(x, y, z, core):
    zh, zl = divmod(z, 2)
    return ((y * 2 + zl) * 2 + core) * 8 + x * 2 + zh


def route(target):
    pairs = []
    for x, y, z, core in itertools.product(range(4), range(4), range(4), range(2)):
        to = target(x, y, z, core)
        if to is not None:
            pairs.append((linear(x, y, z, core), linear(*to)))
    return pairs


def send(value, target):
    return lax.ppermute(value, AXES, route(target))


def other_core(x, y, z, core):
    return (x, y, z, 1 - core)


def shifted(dx=0, dy=0, dz=0):
    return lambda x, y, z, core: ((x + dx) % 4, (y + dy) % 4, (z + dz) % 4, core)


def other_zl(x, y, z, core):
    return (x, y, z ^ 1, core)


def spread(x, y, z, core):
    zh, zl = divmod(z, 2)
    return ((x + y) % 4, x, zl * 2 + zh, core)


def within_half(flip, later):
    def target(x, y, z, core):
        place = (y % 2) * 2 + z % 2
        to = place ^ flip
        if (to > place) != later:
            return None
        return (x, y - y % 2 + to // 2, z - z % 2 + to % 2, core)

    return target


def nt(a, b):
    return lax.dot_general(a, b, (((1,), (1,)), ((), ())), preferred_element_type=f32)


def nn(a, b):
    return lax.dot_general(a, b, (((1,), (0,)), ((), ())), preferred_element_type=f32)


def tn(a, b):
    return lax.dot_general(a, b, (((0,), (0,)), ((), ())), preferred_element_type=f32)


def dots_kernel(do_ref, out_ref, ln_ref, aux_ref):
    for h in range(HEADS):
        cols = slice(h * HD, (h + 1) * HD)
        prod = do_ref[:, cols].astype(f32) * out_ref[:, cols].astype(f32)
        aux_ref[h : h + 1, :] = jnp.sum(prod.T, axis=0, keepdims=True)
    aux_ref[HEADS:, :] = ln_ref[...] * LOG2E


def row_aux(output_grad, attn_output, log_norms):
    return pl.pallas_call(
        dots_kernel,
        out_shape=jax.ShapeDtypeStruct((2 * HEADS, ROWS), f32),
        compiler_params=pltpu.CompilerParams(vmem_limit_bytes=VMEM),
        cost_estimate=pl.CostEstimate(flops=2 * ROWS * WIDTH, bytes_accessed=4 * ROWS * WIDTH, transcendentals=0),
    )(output_grad, attn_output, log_norms)


def attention_kernel(count, has_sum, *refs):
    (blocks, kv_ref, first_ref, aux_refs, q_refs, do_refs) = (
        refs[0], refs[1], refs[2:4], refs[4:6], refs[6:8], refs[8:10],
    )
    rest = list(refs[10:])
    sums = [rest.pop(0), rest.pop(0)] if has_sum else None
    dq_refs = [rest.pop(0), rest.pop(0)]
    dkv_ref, dk_acc, dv_acc = rest
    step = pl.program_id(0)

    @pl.when(step == 0)
    def _():
        dk_acc[...] = jnp.zeros_like(dk_acc)
        dv_acc[...] = jnp.zeros_like(dv_acc)

    keys = count * ROWS
    k = kv_ref[:, :HD]
    v = kv_ref[:, HD:]
    offset = lax.broadcasted_iota(jnp.int32, (ROWS, 1), 0)
    key_pos = [blocks[i] * ROWS + offset for i in range(count)]
    key_pos = key_pos[0] if count == 1 else jnp.concatenate(key_pos, axis=0)
    lane = lax.broadcasted_iota(jnp.int32, (1, ROWS), 1)
    for i in range(2):
        query_pos = blocks[count + i] * ROWS + lane
        visible = (key_pos <= query_pos) & (key_pos >= first_refs_row(first_ref[i]))
        for j in range(STEP_HEADS):
            cols = slice(j * HD, (j + 1) * HD)
            h = step * STEP_HEADS + j
            q = q_refs[i][:, cols]
            do = do_refs[i][:, cols]
            dots = aux_refs[i][pl.ds(h, 1), :]
            norm = aux_refs[i][pl.ds(HEADS + h, 1), :]
            p = jnp.where(visible, jnp.exp2(nt(k, q) * (SCALE * LOG2E) - norm), 0.0)
            dv_acc[...] += nn(p.astype(bf16), do)
            ds = (p * (nt(v, do) - dots)).astype(bf16)
            dk_acc[...] += nn(ds, q)
            dq = tn(ds, k)
            if has_sum:
                dq = dq + sums[i][:, cols]
            dq_refs[i][:, cols] = dq.astype(dq_refs[i].dtype)

    @pl.when(step == pl.num_programs(0) - 1)
    def _():
        dkv_ref[:, :HD] = dk_acc[...].astype(dkv_ref.dtype)
        dkv_ref[:, HD:] = dv_acc[...].astype(dkv_ref.dtype)


def first_refs_row(ref):
    return ref[0:1, :]


def attention(blocks, kv, first, aux, q, do, sums, dq_types, dkv_type):
    count = kv.shape[0] // ROWS
    whole = lambda a: pl.BlockSpec(a.shape, lambda s, b: (0,) * a.ndim)
    heads = pl.BlockSpec((ROWS, STEP_HEADS * HD), lambda s, b: (0, s))
    operands = [kv, *first, *aux, *q, *do, *(sums or ())]
    specs = [whole(kv), *map(whole, first), *map(whole, aux)] + [heads] * (len(operands) - 5)


    return pl.pallas_call(
        functools.partial(attention_kernel, count, sums is not None),
        out_shape=(
            jax.ShapeDtypeStruct((ROWS, WIDTH), dq_types[0]),
            jax.ShapeDtypeStruct((ROWS, WIDTH), dq_types[1]),
            jax.ShapeDtypeStruct((count * ROWS, 2 * HD), dkv_type),
        ),
        grid_spec=pltpu.PrefetchScalarGridSpec(
            num_scalar_prefetch=1,
            grid=(HEADS // STEP_HEADS,),
            in_specs=specs,
            out_specs=[heads, heads, pl.BlockSpec((count * ROWS, 2 * HD), lambda s, b: (0, 0))],
            scratch_shapes=[pltpu.VMEM((count * ROWS, HD), f32)] * 2,
        ),
        compiler_params=pltpu.CompilerParams(vmem_limit_bytes=VMEM),
        cost_estimate=pl.CostEstimate(
            flops=count * 4 * 5 * 2 * ROWS * ROWS * WIDTH,
            bytes_accessed=12 * ROWS * WIDTH,
            transcendentals=count * 2 * ROWS * ROWS * HEADS,
        ),
    )(blocks, *operands)


def weights_kernel(where, *refs):
    l_refs, d_refs, (out_ref, d_all) = refs[:8], refs[8:12], refs[12:]

    @pl.when(pl.program_id(0) == 0)
    def _():
        for r in range(4):
            for half in range(2):
                d_all[r * 2 + half] = d_refs[r][half * ROWS : (half + 1) * ROWS, :].T

    total = None
    for s in range(4):
        for j in range(2):
            term = nn(d_all[where[s] * 2 + where[4 + j]], l_refs[s * 2 + j][...])
            total = term if total is None else total + term
    out_ref[...] = total


def weights(where, l_blocks, d_blocks):
    tile = 256
    return pl.pallas_call(
        weights_kernel,
        out_shape=jax.ShapeDtypeStruct((2 * HD, WIDTH), f32),
        grid_spec=pltpu.PrefetchScalarGridSpec(
            num_scalar_prefetch=1,
            grid=(WIDTH // tile,),
            in_specs=[pl.BlockSpec((ROWS, tile), lambda s, w: (0, s))] * 8
            + [pl.BlockSpec((2 * ROWS, 2 * HD), lambda s, w: (0, 0))] * 4,
            out_specs=pl.BlockSpec((2 * HD, tile), lambda s, w: (0, s)),
            scratch_shapes=[pltpu.VMEM((8, 2 * HD, ROWS), bf16)],
        ),
        compiler_params=pltpu.CompilerParams(vmem_limit_bytes=VMEM),
        cost_estimate=pl.CostEstimate(
            flops=8 * 2 * ROWS * WIDTH * 2 * HD, bytes_accessed=5 << 20, transcendentals=0
        ),
    )(where, *l_blocks, *d_blocks)


def finish_kernel(mine_ref, got_ref, k_ref, v_ref):
    total = mine_ref[...] + got_ref[...]
    k_ref[...] = total[:HD, :].T
    v_ref[...] = total[HD:, :].T


def finish(mine, got):
    return pl.pallas_call(
        finish_kernel,
        out_shape=(jax.ShapeDtypeStruct((WIDTH // 2, HD), f32),) * 2,
        compiler_params=pltpu.CompilerParams(vmem_limit_bytes=VMEM),
        cost_estimate=pl.CostEstimate(flops=WIDTH * HD, bytes_accessed=6 * WIDTH * HD, transcendentals=0),
    )(mine, got)


def first_visible(doc_lengths, block):
    order = jnp.arange(doc_lengths.shape[0], dtype=jnp.int32)
    ends = jnp.sum(jnp.where(order[:, None] <= order[None, :], doc_lengths[:, None], 0), axis=0)
    positions = block * ROWS + jnp.arange(ROWS, dtype=jnp.int32)
    first = jnp.max(jnp.where(ends[None, :] <= positions[:, None], ends[None, :], 0), axis=1)
    return jnp.broadcast_to(first[None, :].astype(jnp.int32), (8, ROWS))


def on_device(queries, key_states, value_states, attn_output, output_grad, log_norms, layer_input, doc_lengths):
    me = lax.axis_index("ctx").astype(jnp.int32)
    tp = lax.axis_index("tp").astype(jnp.int32)
    core, zl, y = me % 2, (me // 2) % 2, me // 4
    x, zh = tp // 2, tp % 2
    chip = me // 2

    kv = jnp.concatenate([key_states, value_states], axis=1)
    l_own = send(layer_input, spread)
    kv_got = [send(kv, within_half(flip, True)) for flip in (1, 2, 3)]

    aux_own = row_aux(output_grad, attn_output, log_norms)
    aux_par, q_par, do_par = (send(a, other_core) for a in (aux_own, queries, output_grad))
    first = (first_visible(doc_lengths, me), first_visible(doc_lengths, me ^ 1))
    aux, q, do = (aux_own, aux_par), (queries, q_par), (output_grad, do_par)

    l_other = send(l_own, shifted(dz=2))
    l_blocks = []
    for dx in (0, 1, 2, 3):
        for block in (l_own, l_other):
            l_blocks.append(block if dx == 0 else send(block, shifted(dx=-dx)))

    mine = jnp.stack([me, me, me ^ 1])
    dq_own, dq_par, dkv_own = attention(mine, kv, first, aux, q, do, None, (f32, f32), f32)
    far = jnp.stack([me ^ 2, me ^ 4, me ^ 6, me, me ^ 1])
    dq_own, dq_par, dkv_far = attention(
        far, jnp.concatenate(kv_got, axis=0), first, aux, q, do, (dq_own, dq_par), (f32, bf16), bf16
    )

    terms = [
        send(dkv_far[i * ROWS : (i + 1) * ROWS], within_half(flip, False)) for i, flip in enumerate((1, 2, 3))
    ]
    dq_got = send(dq_par, other_core)
    query_grad = ((dq_own + dq_got.astype(f32)) * SCALE).astype(bf16)

    dkv = dkv_own + terms[0].astype(f32) + terms[1].astype(f32) + terms[2].astype(f32)
    dkv = jnp.concatenate([dkv[:, :HD] * SCALE, dkv[:, HD:]], axis=1).astype(bf16)

    pair = jnp.concatenate([dkv, send(dkv, other_zl)], axis=0)
    d_blocks = [pair if dy == 0 else send(pair, shifted(dy=-dy)) for dy in (0, 1, 2, 3)]

    where = jnp.stack([(x + s - 2 * y) % 4 for s in range(4)] + [(zh ^ j) ^ zl for j in range(2)]).astype(jnp.int32)
    partial = weights(where, l_blocks, d_blocks)
    half = WIDTH // 2
    kept = lax.dynamic_slice(partial, (0, core * half), (2 * HD, half))
    sent = lax.dynamic_slice(partial, (0, (1 - core) * half), (2 * HD, half))
    key_weight, value_weight = finish(kept, send(sent, other_core))
    return query_grad, key_weight, value_weight


def solution(mesh):
    placed = (
        P("ctx", "tp"),
        P("ctx", "tp"),
        P("ctx", "tp"),
        P("ctx", "tp"),
        P("ctx", "tp"),
        P("tp", "ctx"),
        P("ctx", "tp"),
        P(),
    )
    return jax.shard_map(
        on_device,
        mesh=mesh,
        in_specs=placed,
        out_specs=(P("ctx", "tp"), P("ctx", "tp"), P("ctx", "tp")),
        check_vma=False,
    )
```

time: 406 us -> 118 us (0.29)
  waiting for transfers between devices: 133 us -> 26 us
  starting transfers between devices: 130 us -> 45.3 us
  matrix products: 83 us -> 0 us
  Pallas kernels: 0 us -> 33 us
  local copies, waits for them, and re-layouts: 37.8 us -> 8.93 us
  between operations: 14.2 us -> 0.92 us
    reduce_scatter x1 -> x0, waiting for transfers between devices: 99.4 us -> none  [on_device(): lax.psum_scatter(jnp.einsum('td,tc->dc', gathered, both_low, preferred_el...]
    ppermute x64 -> x23, starting transfers between devices: 130 us -> 45.3 us  [send(): return lax.ppermute(value, AXES, route(target))]
    dot_general x81 -> x0, matrix products: 83 us -> none  [the longest x16 20.4 us: block_terms(): jnp.einsum('tkgd,skd->kgts', query_heads, key_heads, preferred_element_ty...]
    pallas_call x0 -> x5, Pallas kernels: none -> 33 us  [the longest x2 22.3 us: attention(): pl.pallas_call(functools.partial(attention_kernel, count, sums is not Non...]
    while x32 -> x0, local copies, waits for them, and re-layouts: 26.9 us -> none
    ppermute x64 -> x23, waiting for transfers between devices: 33.6 us -> 26 us  [send(): return lax.ppermute(value, AXES, route(target))]
    unnamed x12 -> x39, local copies, waits for them, and re-layouts: 8.78 us -> 3.11 us
  transfers between devices with their start and end apart: 66 -> 23, of which waited for: 32 -> 6; matrix products, arithmetic and copies ran while one was open for 28% -> 7% of each run, Pallas kernels for 0% -> 26%
where the time goes in v1:
time: 118 us; the launch traced here: 117 us
  starting transfers between devices  45.3 us (38%)
  Pallas kernels  33 us (28%)
  waiting for transfers between devices  26 us (22%)
  local copies, waits for them, and re-layouts  8.93 us (8%)
  other arithmetic  2.7 us (2%)
    ppermute x23, starting transfers between devices, send(): return lax.ppermute(value, AXES, route(target))  45.3 us
    ppermute x23, waiting for transfers between devices, send(): return lax.ppermute(value, AXES, route(target))  26 us
    pallas_call x2, Pallas kernels, attention(): pl.pallas_call(functools.partial(attention_kernel, count, sums is not Non...  22.3 us
    pallas_call x1, Pallas kernels, weights(): pl.pallas_call(weights_kernel, out_shape=jax.ShapeDtypeStruct((2 * HD, WI...  6.4 us
    unnamed x39, local copies, waits for them, and re-layouts  3.11 us
  transfers between devices with their start and end apart: 23, of which 6 were waited for; matrix products, arithmetic and copies ran while one was open for 7% of the time, Pallas kernels for 26%

profile of v1, /device:TPU:1, one launch (start us, length us, event | category | flops | bytes accessed | tf_op | source)
XLA Modules:
  0.0 116.9 jit_solution(17099831932876586055)
XLA Ops:
  1.6 5.4 %collective-permute-start.2 = (bf16[256,256]{1,0:T(8,128)(2,1)S(1)}, bf16[256,256]{1,0:T(8,128)(2,1)S(1)}, u32[]{:S(2)}, u32[]{:S(2)}) collective-permute-start(bf16[256,256]{1,0:T(8,128)(2,1)S(1)} %constant_dynamic-update-slice_fusion.refs_1_), channel_id=1, source_target_pairs={{0,48},{8,56},{16,32},{24,40},{1,49},{9,57},{17,33},{25,41},{64,11... | collective-permute-start | bytes 393224 | tf_op jit(solution)/shard_map/ppermute | solution.py:41
  7.0 1.3 %collective-permute-start.1 = (bf16[256,256]{1,0:T(8,128)(2,1)S(1)}, bf16[256,256]{1,0:T(8,128)(2,1)S(1)}, u32[]{:S(2)}, u32[]{:S(2)}) collective-permute-start(bf16[256,256]{1,0:T(8,128)(2,1)S(1)} %constant_dynamic-update-slice_fusion.refs_1_), channel_id=1, source_target_pairs={{0,32},{8,40},{16,48},{24,56},{1,33},{9,41},{17,49},{25,57},{64,96... | collective-permute-start | bytes 393224 | tf_op jit(solution)/shard_map/ppermute | solution.py:41
  8.3 2.2 %collective-permute-start = (bf16[256,256]{1,0:T(8,128)(2,1)S(1)}, bf16[256,256]{1,0:T(8,128)(2,1)S(1)}, u32[]{:S(2)}, u32[]{:S(2)}) collective-permute-start(bf16[256,256]{1,0:T(8,128)(2,1)S(1)} %constant_dynamic-update-slice_fusion.refs_1_), channel_id=1, source_target_pairs={{0,16},{8,24},{1,17},{9,25},{32,48},{40,56},{33,49},{41,57},{64,80... | collective-permute-start | bytes 393224 | tf_op jit(solution)/shard_map/ppermute | solution.py:41
  10.5 1.3 %collective-permute-start.4 = (bf16[256,1024]{1,0:T(8,128)(2,1)}, bf16[256,1024]{1,0:T(8,128)(2,1)S(1)}, u32[]{:S(2)}, u32[]{:S(2)}) collective-permute-start(bf16[256,1024]{1,0:T(8,128)(2,1)} %refs_6_.3), channel_id=1, source_target_pairs={{0,8},{8,0},{16,24},{24,16},{1,9},{9,1},{17,25},{25,17},{32,40},{4... | collective-permute-start | bytes 1572872 | tf_op jit(solution)/shard_map/ppermute | solution.py:41
  14.0 2.2 %shard_map.103.refs_4_ = f32[16,256]{1,0:T(8,128)} custom-call(bf16[256,1024]{1,0:T(8,128)(2,1)} %refs_8_.3, bf16[256,1024]{1,0:T(8,128)(2,1)} %out_ref.1, f32[8,256]{1,0:T(8,128)} %ln_ref.1), custom_call_target="tpu_custom_call" | custom-call | flops 524288 | bytes 1048576 | tf_op jit(solution)/shard_map/pallas_call | solution.py:93
  19.6 8.7 %shard_map.104 = (f32[256,1024]{1,0:T(8,128)}, f32[256,1024]{1,0:T(8,128)}, f32[256,256]{1,0:T(8,128)}) custom-call(s32[3]{0:T(128)} %pad_add_fusion.refs_0_, bf16[256,256]{1,0:T(8,128)(2,1)} %copy-done.13, s32[8,256]{1,0:T(8,128)} %broadcast_in_dim.57.refs_2_, s32[8,256]{1,0:T(8,128)} %broadcast_in_dim.58.refs_3_, f32[16,256]{1,0:T(8,128)} %shard_map.103.refs_4_, ...), custom_call_target="tpu_custom_call" | custom-call | flops 2684354560 | bytes 3145728 | tf_op jit(solution)/shard_map/pallas_call | solution.py:160
  28.3 13.6 %shard_map.105 = (f32[256,1024]{1,0:T(8,128)}, bf16[256,1024]{1,0:T(8,128)(2,1)}, bf16[768,256]{1,0:T(8,128)(2,1)}) custom-call(s32[5]{0:T(128)} %stack.50.refs_0_, bf16[768,256]{1,0:T(8,128)(2,1)} %pad_maximum_fusion.refs_1_, s32[8,256]{1,0:T(8,128)} %broadcast_in_dim.57.refs_2_, s32[8,256]{1,0:T(8,128)} %broadcast_in_dim.58.refs_3_, ...), custom_call_target="tpu_custom_call" | custom-call | flops 8053063680 | bytes 3145728 | tf_op jit(solution)/shard_map/pallas_call | solution.py:160
  43.0 1.3 %collective-permute-start.17 = (bf16[256,256]{1,0:T(8,128)(2,1)S(1)}, bf16[256,256]{1,0:T(8,128)(2,1)S(1)}, u32[]{:S(2)}, u32[]{:S(2)}) collective-permute-start(bf16[256,256]{1,0:T(8,128)(2,1)S(1)} %get-tuple-element.24), channel_id=1, source_target_pairs={{32,16},{40,24},{48,0},{56,8},{33,17},{41,25},{49,1},{57,9},{96,80... | collective-permute-start | bytes 393224 | tf_op jit(solution)/shard_map/ppermute | solution.py:41
  44.3 1.3 %collective-permute-start.16 = (bf16[256,256]{1,0:T(8,128)(2,1)S(1)}, bf16[256,256]{1,0:T(8,128)(2,1)S(1)}, u32[]{:S(2)}, u32[]{:S(2)}) collective-permute-start(bf16[256,256]{1,0:T(8,128)(2,1)S(1)} %get-tuple-element.25), channel_id=1, source_target_pairs={{32,0},{40,8},{48,16},{56,24},{33,1},{41,9},{49,17},{57,25},{96,64... | collective-permute-start | bytes 393224 | tf_op jit(solution)/shard_map/ppermute | solution.py:41
  46.9 4.6 %collective-permute-start.8 = (bf16[256,1024]{1,0:T(8,128)(2,1)S(1)}, bf16[256,1024]{1,0:T(8,128)(2,1)S(1)}, u32[]{:S(2)}, u32[]{:S(2)}) collective-permute-start(bf16[256,1024]{1,0:T(8,128)(2,1)S(1)} %collective-permute-done.7.refs_0_), channel_id=1, source_target_pairs={{0,1},{8,9},{16,17},{24,25},{1,0},{9,8},{17,16},{25,24},{32,33},{4... | collective-permute-start | bytes 1572872 | tf_op jit(solution)/shard_map/ppermute | solution.py:41
  51.6 2.5 %collective-permute-start.9 = (bf16[256,1024]{1,0:T(8,128)(2,1)S(1)}, bf16[256,1024]{1,0:T(8,128)(2,1)S(1)}, u32[]{:S(2)}, u32[]{:S(2)}) collective-permute-start(bf16[256,1024]{1,0:T(8,128)(2,1)S(1)} %collective-permute-done.7.refs_0_), channel_id=1, source_target_pairs={{0,6},{8,14},{16,22},{24,30},{1,7},{9,15},{17,23},{25,31},{32,38},... | collective-permute-start | bytes 1572872 | tf_op jit(solution)/shard_map/ppermute | solution.py:41
  54.0 3.1 %collective-permute-start.11 = (bf16[256,1024]{1,0:T(8,128)(2,1)S(1)}, bf16[256,1024]{1,0:T(8,128)(2,1)S(1)}, u32[]{:S(2)}, u32[]{:S(2)}) collective-permute-start(bf16[256,1024]{1,0:T(8,128)(2,1)S(1)} %collective-permute-done.7.refs_0_), channel_id=1, source_target_pairs={{0,4},{8,12},{16,20},{24,28},{1,5},{9,13},{17,21},{25,29},{32,36},... | collective-permute-start | bytes 1572872 | tf_op jit(solution)/shard_map/ppermute | solution.py:41
  57.3 2.8 %collective-permute-start.18 = (bf16[256,256]{1,0:T(8,128)(2,1)S(1)}, bf16[256,256]{1,0:T(8,128)(2,1)S(1)}, u32[]{:S(2)}, u32[]{:S(2)}) collective-permute-start(bf16[256,256]{1,0:T(8,128)(2,1)S(1)} %pad_maximum_fusion.2), channel_id=1, source_target_pairs={{0,16},{8,24},{16,0},{24,8},{1,17},{9,25},{17,1},{25,9},{32,48},{4... | collective-permute-start | bytes 393224 | tf_op jit(solution)/shard_map/ppermute | solution.py:41
  60.1 11.1 %collective-permute-done.18 = bf16[256,256]{1,0:T(8,128)(2,1)S(1)} collective-permute-done((bf16[256,256]{1,0:T(8,128)(2,1)S(1)}, bf16[256,256]{1,0:T(8,128)(2,1)S(1)}, u32[]{:S(2)}, u32[]{:S(2)}) %collective-permute-start.18) | collective-permute-done | bytes 131104 | tf_op jit(solution)/shard_map/ppermute | solution.py:41
  71.2 4.8 %collective-permute-start.19 = (bf16[512,256]{1,0:T(8,128)(2,1)S(1)}, bf16[512,256]{1,0:T(8,128)(2,1)S(1)}, u32[]{:S(2)}, u32[]{:S(2)}) collective-permute-start(bf16[512,256]{1,0:T(8,128)(2,1)S(1)} %pad_maximum_fusion.1.refs_8_), channel_id=1, source_target_pairs={{0,96},{8,104},{16,112},{24,120},{1,97},{9,105},{17,113},{25,121},... | collective-permute-start | bytes 786440 | tf_op jit(solution)/shard_map/ppermute | solution.py:41
  76.3 3.9 %collective-permute-start.14 = (bf16[256,1024]{1,0:T(8,128)(2,1)S(1)}, bf16[256,1024]{1,0:T(8,128)(2,1)}, u32[]{:S(2)}, u32[]{:S(2)}) collective-permute-start(bf16[256,1024]{1,0:T(8,128)(2,1)S(1)} %collective-permute-done.8.refs_1_), channel_id=1, source_target_pairs={{0,2},{8,10},{16,18},{24,26},{1,3},{9,11},{17,19},{25,27},{32,34},... | collective-permute-start | bytes 1572872 | tf_op jit(solution)/shard_map/ppermute | solution.py:41
  81.0 4.4 %collective-permute-start.20 = (bf16[512,256]{1,0:T(8,128)(2,1)S(1)}, bf16[512,256]{1,0:T(8,128)(2,1)S(1)}, u32[]{:S(2)}, u32[]{:S(2)}) collective-permute-start(bf16[512,256]{1,0:T(8,128)(2,1)S(1)} %pad_maximum_fusion.1.refs_8_), channel_id=1, source_target_pairs={{0,64},{8,72},{16,80},{24,88},{1,65},{9,73},{17,81},{25,89},{32,96... | collective-permute-start | bytes 786440 | tf_op jit(solution)/shard_map/ppermute | solution.py:41
  86.4 5.2 %collective-permute-done.20.refs_10_ = bf16[512,256]{1,0:T(8,128)(2,1)S(1)} collective-permute-done((bf16[512,256]{1,0:T(8,128)(2,1)S(1)}, bf16[512,256]{1,0:T(8,128)(2,1)S(1)}, u32[]{:S(2)}, u32[]{:S(2)}) %collective-permute-start.20) | collective-permute-done | bytes 262176 | tf_op jit(solution)/shard_map/ppermute | solution.py:41
  92.3 2.1 %collective-permute-start.6 = (bf16[256,1024]{1,0:T(8,128)(2,1)}, bf16[256,1024]{1,0:T(8,128)(2,1)S(1)}, u32[]{:S(2)}, u32[]{:S(2)}) collective-permute-start(bf16[256,1024]{1,0:T(8,128)(2,1)} %get-tuple-element.14), channel_id=1, source_target_pairs={{0,8},{8,0},{16,24},{24,16},{1,9},{9,1},{17,25},{25,17},{32,40},{4... | collective-permute-start | bytes 1572872 | tf_op jit(solution)/shard_map/ppermute | solution.py:41
  95.0 3.0 %collective-permute-done.21.refs_11_ = bf16[512,256]{1,0:T(8,128)(2,1)} collective-permute-done((bf16[512,256]{1,0:T(8,128)(2,1)S(1)}, bf16[512,256]{1,0:T(8,128)(2,1)}, u32[]{:S(2)}, u32[]{:S(2)}) %collective-permute-start.21) | collective-permute-done | bytes 262176 | tf_op jit(solution)/shard_map/ppermute | solution.py:41
  98.0 5.3 %collective-permute-done.14.refs_7_ = bf16[256,1024]{1,0:T(8,128)(2,1)} collective-permute-done((bf16[256,1024]{1,0:T(8,128)(2,1)S(1)}, bf16[256,1024]{1,0:T(8,128)(2,1)}, u32[]{:S(2)}, u32[]{:S(2)}) %collective-permute-start.14) | collective-permute-done | bytes 524320 | tf_op jit(solution)/shard_map/ppermute | solution.py:41
  103.3 6.4 %shard_map.106 = f32[256,1024]{1,0:T(8,128)} custom-call(s32[6]{0:T(128)} %stack.58.where, bf16[256,1024]{1,0:T(8,128)(2,1)} %copy-done.2, bf16[256,1024]{1,0:T(8,128)(2,1)} %copy-done.3, bf16[256,1024]{1,0:T(8,128)(2,1)} %copy-done.4, bf16[256,1024]{1,0:T(8,128)(2,1)} %copy-done.7, bf16[256,1024]{1,0:T(8,128)(2,1)} %copy-done.5, ...), custom_call_target="tpu_custom_call" | custom-call | flops 1073741824 | bytes 5242880 | tf_op jit(solution)/shard_map/pallas_call | solution.py:202
  109.7 2.2 %constant_dynamic-slice_fusion = (f32[256,512]{1,0:T(8,128)S(1)}, f32[256,512]{1,0:T(8,128)}) fusion(f32[256,1024]{1,0:T(8,128)} %shard_map.106, s32[]{:T(128)S(6)} %select_n.73, s32[]{:T(128)S(6)} %select_n.72), kind=kLoop, calls=%fused_computation.17 | loop fusion | bytes 2097160 | tf_op jit(solution)/shard_map/dynamic_slice | solution.py:288
  114.7 2.1 %shard_map.107 = (f32[512,128]{1,0:T(8,128)}, f32[512,128]{1,0:T(8,128)}) custom-call(f32[256,512]{1,0:T(8,128)} %get-tuple-element.22.mine_ref, f32[256,512]{1,0:T(8,128)} %copy-done.8), custom_call_target="tpu_custom_call" | custom-call | flops 131072 | bytes 786432 | tf_op jit(solution)/shard_map/pallas_call | solution.py:227
  (84 shorter events, 15.2 us)
Async XLA Ops:
  1.6 14.7 %collective-permute-start.2 = (bf16[256,256]{1,0:T(8,128)(2,1)S(1)}, bf16[256,256]{1,0:T(8,128)(2,1)S(1)}, u32[]{:S(2)}, u32[]{:S(2)}) collective-permute-start(bf16[256,256]{1,0:T(8,128)(2,1)S(1)} %constant_dynamic-update-slice_fusion.refs_1_), channel_id=1, source_target_pairs={{0,48},{8,56},{16,32},{24,40},{1,49},{9,57},{17,33},{25,41},{64,11... | collective-permute-start | bytes 393224 | tf_op jit(solution)/shard_map/ppermute | solution.py:41
  7.0 9.8 %collective-permute-start.1 = (bf16[256,256]{1,0:T(8,128)(2,1)S(1)}, bf16[256,256]{1,0:T(8,128)(2,1)S(1)}, u32[]{:S(2)}, u32[]{:S(2)}) collective-permute-start(bf16[256,256]{1,0:T(8,128)(2,1)S(1)} %constant_dynamic-update-slice_fusion.refs_1_), channel_id=1, source_target_pairs={{0,32},{8,40},{16,48},{24,56},{1,33},{9,41},{17,49},{25,57},{64,96... | collective-permute-start | bytes 393224 | tf_op jit(solution)/shard_map/ppermute | solution.py:41
  8.3 9.2 %collective-permute-start = (bf16[256,256]{1,0:T(8,128)(2,1)S(1)}, bf16[256,256]{1,0:T(8,128)(2,1)S(1)}, u32[]{:S(2)}, u32[]{:S(2)}) collective-permute-start(bf16[256,256]{1,0:T(8,128)(2,1)S(1)} %constant_dynamic-update-slice_fusion.refs_1_), channel_id=1, source_target_pairs={{0,16},{8,24},{1,17},{9,25},{32,48},{40,56},{33,49},{41,57},{64,80... | collective-permute-start | bytes 393224 | tf_op jit(solution)/shard_map/ppermute | solution.py:41
  10.5 7.8 %collective-permute-start.4 = (bf16[256,1024]{1,0:T(8,128)(2,1)}, bf16[256,1024]{1,0:T(8,128)(2,1)S(1)}, u32[]{:S(2)}, u32[]{:S(2)}) collective-permute-start(bf16[256,1024]{1,0:T(8,128)(2,1)} %refs_6_.3), channel_id=1, source_target_pairs={{0,8},{8,0},{16,24},{24,16},{1,9},{9,1},{17,25},{25,17},{32,40},{4... | collective-permute-start | bytes 1572872 | tf_op jit(solution)/shard_map/ppermute | solution.py:41
  11.8 6.5 %collective-permute-start.5 = (bf16[256,1024]{1,0:T(8,128)(2,1)}, bf16[256,1024]{1,0:T(8,128)(2,1)S(1)}, u32[]{:S(2)}, u32[]{:S(2)}) collective-permute-start(bf16[256,1024]{1,0:T(8,128)(2,1)} %refs_8_.3), channel_id=1, source_target_pairs={{0,8},{8,0},{16,24},{24,16},{1,9},{9,1},{17,25},{25,17},{32,40},{4... | collective-permute-start | bytes 1572872 | tf_op jit(solution)/shard_map/ppermute | solution.py:41
  16.3 2.0 %collective-permute-start.3 = (f32[16,256]{1,0:T(8,128)}, f32[16,256]{1,0:T(8,128)S(1)}, u32[]{:S(2)}, u32[]{:S(2)}) collective-permute-start(f32[16,256]{1,0:T(8,128)} %shard_map.103.refs_4_), channel_id=1, source_target_pairs={{0,8},{8,0},{16,24},{24,16},{1,9},{9,1},{17,25},{25,17},{32,40},{4... | collective-permute-start | bytes 49160 | tf_op jit(solution)/shard_map/ppermute | solution.py:41
  16.8 30.1 %collective-permute-start.7 = (bf16[256,1024]{1,0:T(8,128)(2,1)S(1)}, bf16[256,1024]{1,0:T(8,128)(2,1)S(1)}, u32[]{:S(2)}, u32[]{:S(2)}) collective-permute-start(bf16[256,1024]{1,0:T(8,128)(2,1)S(1)} %copy-done.14), channel_id=1, source_target_pairs={{0,0},{8,8},{16,1},{24,9},{1,16},{9,24},{17,17},{25,25},{32,2},{40... | collective-permute-start | bytes 1572872 | tf_op jit(solution)/shard_map/ppermute | solution.py:41
  43.0 11.0 %collective-permute-start.17 = (bf16[256,256]{1,0:T(8,128)(2,1)S(1)}, bf16[256,256]{1,0:T(8,128)(2,1)S(1)}, u32[]{:S(2)}, u32[]{:S(2)}) collective-permute-start(bf16[256,256]{1,0:T(8,128)(2,1)S(1)} %get-tuple-element.24), channel_id=1, source_target_pairs={{32,16},{40,24},{48,0},{56,8},{33,17},{41,25},{49,1},{57,9},{96,80... | collective-permute-start | bytes 393224 | tf_op jit(solution)/shard_map/ppermute | solution.py:41
  44.3 12.8 %collective-permute-start.16 = (bf16[256,256]{1,0:T(8,128)(2,1)S(1)}, bf16[256,256]{1,0:T(8,128)(2,1)S(1)}, u32[]{:S(2)}, u32[]{:S(2)}) collective-permute-start(bf16[256,256]{1,0:T(8,128)(2,1)S(1)} %get-tuple-element.25), channel_id=1, source_target_pairs={{32,0},{40,8},{48,16},{56,24},{33,1},{41,9},{49,17},{57,25},{96,64... | collective-permute-start | bytes 393224 | tf_op jit(solution)/shard_map/ppermute | solution.py:41
  45.6 11.5 %collective-permute-start.15 = (bf16[256,256]{1,0:T(8,128)(2,1)S(1)}, bf16[256,256]{1,0:T(8,128)(2,1)S(1)}, u32[]{:S(2)}, u32[]{:S(2)}) collective-permute-start(bf16[256,256]{1,0:T(8,128)(2,1)S(1)} %get-tuple-element.23), channel_id=1, source_target_pairs={{16,0},{24,8},{17,1},{25,9},{48,32},{56,40},{49,33},{57,41},{80,64... | collective-permute-start | bytes 393224 | tf_op jit(solution)/shard_map/ppermute | solution.py:41
  46.9 29.1 %collective-permute-start.8 = (bf16[256,1024]{1,0:T(8,128)(2,1)S(1)}, bf16[256,1024]{1,0:T(8,128)(2,1)S(1)}, u32[]{:S(2)}, u32[]{:S(2)}) collective-permute-start(bf16[256,1024]{1,0:T(8,128)(2,1)S(1)} %collective-permute-done.7.refs_0_), channel_id=1, source_target_pairs={{0,1},{8,9},{16,17},{24,25},{1,0},{9,8},{17,16},{25,24},{32,33},{4... | collective-permute-start | bytes 1572872 | tf_op jit(solution)/shard_map/ppermute | solution.py:41
  51.6 24.5 %collective-permute-start.9 = (bf16[256,1024]{1,0:T(8,128)(2,1)S(1)}, bf16[256,1024]{1,0:T(8,128)(2,1)S(1)}, u32[]{:S(2)}, u32[]{:S(2)}) collective-permute-start(bf16[256,1024]{1,0:T(8,128)(2,1)S(1)} %collective-permute-done.7.refs_0_), channel_id=1, source_target_pairs={{0,6},{8,14},{16,22},{24,30},{1,7},{9,15},{17,23},{25,31},{32,38},... | collective-permute-start | bytes 1572872 | tf_op jit(solution)/shard_map/ppermute | solution.py:41
  54.0 22.3 %collective-permute-start.11 = (bf16[256,1024]{1,0:T(8,128)(2,1)S(1)}, bf16[256,1024]{1,0:T(8,128)(2,1)S(1)}, u32[]{:S(2)}, u32[]{:S(2)}) collective-permute-start(bf16[256,1024]{1,0:T(8,128)(2,1)S(1)} %collective-permute-done.7.refs_0_), channel_id=1, source_target_pairs={{0,4},{8,12},{16,20},{24,28},{1,5},{9,13},{17,21},{25,29},{32,36},... | collective-permute-start | bytes 1572872 | tf_op jit(solution)/shard_map/ppermute | solution.py:41
  57.1 23.9 %collective-permute-start.13 = (bf16[256,1024]{1,0:T(8,128)(2,1)S(1)}, bf16[256,1024]{1,0:T(8,128)(2,1)S(1)}, u32[]{:S(2)}, u32[]{:S(2)}) collective-permute-start(bf16[256,1024]{1,0:T(8,128)(2,1)S(1)} %collective-permute-done.7.refs_0_), channel_id=1, source_target_pairs={{0,2},{8,10},{16,18},{24,26},{1,3},{9,11},{17,19},{25,27},{32,34},... | collective-permute-start | bytes 1572872 | tf_op jit(solution)/shard_map/ppermute | solution.py:41
  57.3 13.9 %collective-permute-start.18 = (bf16[256,256]{1,0:T(8,128)(2,1)S(1)}, bf16[256,256]{1,0:T(8,128)(2,1)S(1)}, u32[]{:S(2)}, u32[]{:S(2)}) collective-permute-start(bf16[256,256]{1,0:T(8,128)(2,1)S(1)} %pad_maximum_fusion.2), channel_id=1, source_target_pairs={{0,16},{8,24},{16,0},{24,8},{1,17},{9,25},{17,1},{25,9},{32,48},{4... | collective-permute-start | bytes 393224 | tf_op jit(solution)/shard_map/ppermute | solution.py:41
  71.2 32.1 %copy-start = (bf16[512,256]{1,0:T(8,128)(2,1)}, bf16[512,256]{1,0:T(8,128)(2,1)S(1)}, u32[]{:S(2)}) copy-start(bf16[512,256]{1,0:T(8,128)(2,1)S(1)} %pad_maximum_fusion.1.refs_8_) | copy-start | bytes 786436
  71.2 14.2 %collective-permute-start.19 = (bf16[512,256]{1,0:T(8,128)(2,1)S(1)}, bf16[512,256]{1,0:T(8,128)(2,1)S(1)}, u32[]{:S(2)}, u32[]{:S(2)}) collective-permute-start(bf16[512,256]{1,0:T(8,128)(2,1)S(1)} %pad_maximum_fusion.1.refs_8_), channel_id=1, source_target_pairs={{0,96},{8,104},{16,112},{24,120},{1,97},{9,105},{17,113},{25,121},... | collective-permute-start | bytes 786440 | tf_op jit(solution)/shard_map/ppermute | solution.py:41
  76.0 21.9 %collective-permute-start.10 = (bf16[256,1024]{1,0:T(8,128)(2,1)S(1)}, bf16[256,1024]{1,0:T(8,128)(2,1)S(1)}, u32[]{:S(2)}, u32[]{:S(2)}) collective-permute-start(bf16[256,1024]{1,0:T(8,128)(2,1)S(1)} %collective-permute-done.8.refs_1_), channel_id=1, source_target_pairs={{0,6},{8,14},{16,22},{24,30},{1,7},{9,15},{17,23},{25,31},{32,38},... | collective-permute-start | bytes 1572872 | tf_op jit(solution)/shard_map/ppermute | solution.py:41
  76.1 21.9 %collective-permute-start.12 = (bf16[256,1024]{1,0:T(8,128)(2,1)S(1)}, bf16[256,1024]{1,0:T(8,128)(2,1)}, u32[]{:S(2)}, u32[]{:S(2)}) collective-permute-start(bf16[256,1024]{1,0:T(8,128)(2,1)S(1)} %collective-permute-done.8.refs_1_), channel_id=1, source_target_pairs={{0,4},{8,12},{16,20},{24,28},{1,5},{9,13},{17,21},{25,29},{32,36},... | collective-permute-start | bytes 1572872 | tf_op jit(solution)/shard_map/ppermute | solution.py:41
  76.3 26.9 %collective-permute-start.14 = (bf16[256,1024]{1,0:T(8,128)(2,1)S(1)}, bf16[256,1024]{1,0:T(8,128)(2,1)}, u32[]{:S(2)}, u32[]{:S(2)}) collective-permute-start(bf16[256,1024]{1,0:T(8,128)(2,1)S(1)} %collective-permute-done.8.refs_1_), channel_id=1, source_target_pairs={{0,2},{8,10},{16,18},{24,26},{1,3},{9,11},{17,19},{25,27},{32,34},... | collective-permute-start | bytes 1572872 | tf_op jit(solution)/shard_map/ppermute | solution.py:41
  81.0 10.5 %collective-permute-start.20 = (bf16[512,256]{1,0:T(8,128)(2,1)S(1)}, bf16[512,256]{1,0:T(8,128)(2,1)S(1)}, u32[]{:S(2)}, u32[]{:S(2)}) collective-permute-start(bf16[512,256]{1,0:T(8,128)(2,1)S(1)} %pad_maximum_fusion.1.refs_8_), channel_id=1, source_target_pairs={{0,64},{8,72},{16,80},{24,88},{1,65},{9,73},{17,81},{25,89},{32,96... | collective-permute-start | bytes 786440 | tf_op jit(solution)/shard_map/ppermute | solution.py:41
  85.5 12.5 %collective-permute-start.21 = (bf16[512,256]{1,0:T(8,128)(2,1)S(1)}, bf16[512,256]{1,0:T(8,128)(2,1)}, u32[]{:S(2)}, u32[]{:S(2)}) collective-permute-start(bf16[512,256]{1,0:T(8,128)(2,1)S(1)} %pad_maximum_fusion.1.refs_8_), channel_id=1, source_target_pairs={{0,32},{8,40},{16,48},{24,56},{1,33},{9,41},{17,49},{25,57},{32,64... | collective-permute-start | bytes 786440 | tf_op jit(solution)/shard_map/ppermute | solution.py:41
  92.3 20.1 %collective-permute-start.6 = (bf16[256,1024]{1,0:T(8,128)(2,1)}, bf16[256,1024]{1,0:T(8,128)(2,1)S(1)}, u32[]{:S(2)}, u32[]{:S(2)}) collective-permute-start(bf16[256,1024]{1,0:T(8,128)(2,1)} %get-tuple-element.14), channel_id=1, source_target_pairs={{0,8},{8,0},{16,24},{24,16},{1,9},{9,1},{17,25},{25,17},{32,40},{4... | collective-permute-start | bytes 1572872 | tf_op jit(solution)/shard_map/ppermute | solution.py:41
  111.9 2.1 %collective-permute-start.22 = (f32[256,512]{1,0:T(8,128)S(1)}, f32[256,512]{1,0:T(8,128)S(1)}, u32[]{:S(2)}, u32[]{:S(2)}) collective-permute-start(f32[256,512]{1,0:T(8,128)S(1)} %get-tuple-element.21), channel_id=1, source_target_pairs={{0,8},{8,0},{16,24},{24,16},{1,9},{9,1},{17,25},{25,17},{32,40},{4... | collective-permute-start | bytes 1572872 | tf_op jit(solution)/shard_map/ppermute | solution.py:41
  (18 other events, 167.7 us)

commit v2 on v1

v2 whole, which is shorter than its diff:
```python
import functools
import itertools
import math

import jax
import jax.numpy as jnp
from jax import lax
from jax.experimental import pallas as pl
from jax.experimental.pallas import tpu as pltpu
from jax.sharding import PartitionSpec as P

HD = 128
HEADS = 8
ROWS = 256
WIDTH = HEADS * HD
SCALE = 1.0 / math.sqrt(HD)
LOG2E = math.log2(math.e)
AXES = ("ctx", "tp")
DOCS = 16
STEP_HEADS = 4

f32 = jnp.float32
bf16 = jnp.bfloat16


def linear(x, y, z, core):
    zh, zl = divmod(z, 2)
    return ((y * 2 + zl) * 2 + core) * 8 + x * 2 + zh


def route(target):
    pairs = []
    for x, y, z, core in itertools.product(range(4), range(4), range(4), range(2)):
        to = target(x, y, z, core)
        if to is not None:
            pairs.append((linear(x, y, z, core), linear(*to)))
    return pairs


def send(value, target):
    return lax.ppermute(value, AXES, route(target))


def other_core(x, y, z, core):
    return (x, y, z, 1 - core)


def shifted(dx=0, dy=0, dz=0):
    return lambda x, y, z, core: ((x + dx) % 4, (y + dy) % 4, (z + dz) % 4, core)


def other_zl(x, y, z, core):
    return (x, y, z ^ 1, core)


def spread(x, y, z, core):
    zh, zl = divmod(z, 2)
    return ((x + y) % 4, x, zl * 2 + zh, core)


def within_half(flip, later):
    def target(x, y, z, core):
        place = (y % 2) * 2 + z % 2
        to = place ^ flip
        if (to > place) != later:
            return None
        return (x, y - y % 2 + to // 2, z - z % 2 + to % 2, core)

    return target


def nt(a, b):
    return lax.dot_general(a, b, (((1,), (1,)), ((), ())), preferred_element_type=f32)


def nn(a, b):
    return lax.dot_general(a, b, (((1,), (0,)), ((), ())), preferred_element_type=f32)


def tn(a, b):
    return lax.dot_general(a, b, (((0,), (0,)), ((), ())), preferred_element_type=f32)


def call(kernel, out_shape, operands, megabytes=12, flops=0, **more):
    return pl.pallas_call(
        kernel,
        out_shape=out_shape,
        compiler_params=pltpu.CompilerParams(vmem_limit_bytes=megabytes << 20),
        cost_estimate=pl.CostEstimate(flops=flops, bytes_accessed=1 << 16, transcendentals=0),
        **more,
    )(*operands)


def struct(shape, dtype):
    return jax.ShapeDtypeStruct(shape, dtype)


def join_kernel(k_ref, v_ref, kv_ref):
    kv_ref[:, :HD] = k_ref[...]
    kv_ref[:, HD:] = v_ref[...]


def aux_kernel(lengths_ref, do_ref, out_ref, ln_ref, aux_ref):
    for h in range(HEADS):
        cols = slice(h * HD, (h + 1) * HD)
        prod = do_ref[:, cols].astype(f32) * out_ref[:, cols].astype(f32)
        aux_ref[h : h + 1, :] = jnp.sum(prod.T, axis=0, keepdims=True)
    aux_ref[HEADS : 2 * HEADS, :] = ln_ref[...] * LOG2E
    positions = lax.axis_index("ctx") * ROWS + lax.broadcasted_iota(jnp.int32, (HEADS, ROWS), 1)
    end = jnp.int32(0)
    first = jnp.zeros((HEADS, ROWS), jnp.int32)
    for i in range(DOCS):
        end = end + lengths_ref[i]
        first = jnp.where(positions >= end, end, first)
    aux_ref[2 * HEADS :, :] = first.astype(f32)


def attention_kernel(flips, has_sum, *refs):
    refs = list(refs)
    take = lambda n: [refs.pop(0) for _ in range(n)]
    kv_refs, aux_refs, q_refs, do_refs = take(len(flips)), take(2), take(2), take(2)
    sums = take(2) if has_sum else None
    dq_refs = take(2)
    dkv_ref, dk_acc, dv_acc = refs
    step = pl.program_id(0)
    me = lax.axis_index("ctx")
    k = jnp.concatenate([r[:, :HD] for r in kv_refs], axis=0)
    v = jnp.concatenate([r[:, HD:] for r in kv_refs], axis=0)
    offset = lax.broadcasted_iota(jnp.int32, (ROWS, 1), 0)
    key_pos = jnp.concatenate([(me ^ flip) * ROWS + offset for flip in flips], axis=0)
    lane = lax.broadcasted_iota(jnp.int32, (1, ROWS), 1)
    dk = dv = None
    for i in range(2):
        query_pos = (me ^ i) * ROWS + lane
        first = aux_refs[i][2 * HEADS : 2 * HEADS + 1, :].astype(jnp.int32)
        visible = (key_pos <= query_pos) & (key_pos >= first)
        for j in range(STEP_HEADS):
            cols = slice(j * HD, (j + 1) * HD)
            h = step * STEP_HEADS + j
            q = q_refs[i][:, cols]
            do = do_refs[i][:, cols]
            dots = aux_refs[i][pl.ds(h, 1), :]
            norm = aux_refs[i][pl.ds(HEADS + h, 1), :]
            p = jnp.where(visible, jnp.exp2(nt(k, q) * (SCALE * LOG2E) - norm), 0.0)
            ds = (p * (nt(v, do) - dots)).astype(bf16)
            dv_term, dk_term, dq = nn(p.astype(bf16), do), nn(ds, q), tn(ds, k)
            dv = dv_term if dv is None else dv + dv_term
            dk = dk_term if dk is None else dk + dk_term
            if has_sum:
                dq = dq + sums[i][:, cols]
            dq_refs[i][:, cols] = dq.astype(dq_refs[i].dtype)

    @pl.when(step == 0)
    def _():
        dk_acc[...] = dk
        dv_acc[...] = dv

    @pl.when(step > 0)
    def _():
        dk_acc[...] += dk
        dv_acc[...] += dv

    @pl.when(step == pl.num_programs(0) - 1)
    def _():
        dkv_ref[:, :HD] = dk_acc[...].astype(dkv_ref.dtype)
        dkv_ref[:, HD:] = dv_acc[...].astype(dkv_ref.dtype)


def attention(flips, kv, aux, q, do, sums, dq_types, dkv_type):
    keys = len(flips) * ROWS
    whole = lambda a: pl.BlockSpec(a.shape, lambda s: (0,) * a.ndim)
    heads = pl.BlockSpec((ROWS, STEP_HEADS * HD), lambda s: (0, s))
    operands = [*kv, *aux, *q, *do, *(sums or ())]
    lead = len(kv) + len(aux)
    return call(
        functools.partial(attention_kernel, flips, sums is not None),
        (
            struct((ROWS, WIDTH), dq_types[0]),
            struct((ROWS, WIDTH), dq_types[1]),
            struct((keys, 2 * HD), dkv_type),
        ),
        operands,
        megabytes=24,
        grid=(HEADS // STEP_HEADS,),
        in_specs=[*map(whole, operands[:lead])] + [heads] * (len(operands) - lead),
        out_specs=[heads, heads, pl.BlockSpec((keys, 2 * HD), lambda s: (0, 0))],
        scratch_shapes=[pltpu.VMEM((keys, HD), f32)] * 2,
    )


def add_kernel(near_ref, got_ref, sum_ref, low_ref):
    total = near_ref[...] + got_ref[...].astype(f32)
    sum_ref[...] = total
    low_ref[...] = total.astype(bf16)


def close_kernel(sum_ref, got_ref, d_ref):
    for half in range(2):
        mine = slice(half * ROWS, (half + 1) * ROWS)
        its = slice((1 - half) * ROWS, (2 - half) * ROWS)
        total = sum_ref[mine, :] + got_ref[its, :].astype(f32)
        d_ref[half * 2 * HD : half * 2 * HD + HD, :] = (total[:, :HD] * SCALE).T.astype(bf16)
        d_ref[half * 2 * HD + HD : (half + 1) * 2 * HD, :] = total[:, HD:].T.astype(bf16)


def weights_kernel(where, *refs):
    l_refs, d_refs, (sent_ref, kept_ref, d_all) = refs[:8], refs[8:12], refs[12:]
    step = pl.program_id(0)

    @pl.when(step == 0)
    def _():
        for r in range(4):
            for half in range(2):
                d_all[r * 2 + half] = d_refs[r][half * 2 * HD : (half + 1) * 2 * HD, :]

    total = None
    for s in range(4):
        for j in range(2):
            term = nn(d_all[where[s] * 2 + where[4 + j]], l_refs[s * 2 + j][...])
            total = term if total is None else total + term

    @pl.when(step < pl.num_programs(0) // 2)
    def _():
        sent_ref[...] = total

    @pl.when(step >= pl.num_programs(0) // 2)
    def _():
        kept_ref[...] = total


def weights(where, l_blocks, d_blocks):
    tile, half = 256, 2
    return pl.pallas_call(
        weights_kernel,
        out_shape=(struct((2 * HD, WIDTH // 2), f32),) * 2,
        grid_spec=pltpu.PrefetchScalarGridSpec(
            num_scalar_prefetch=1,
            grid=(2 * half,),
            in_specs=[pl.BlockSpec((ROWS, tile), lambda s, w: (0, (s + half * (1 - w[6])) % (2 * half)))] * 8
            + [pl.BlockSpec((4 * HD, ROWS), lambda s, w: (0, 0))] * 4,
            out_specs=[
                pl.BlockSpec((2 * HD, tile), lambda s, w: (0, jnp.minimum(s, half - 1))),
                pl.BlockSpec((2 * HD, tile), lambda s, w: (0, jnp.maximum(s - half, 0))),
            ],
            scratch_shapes=[pltpu.VMEM((8, 2 * HD, ROWS), bf16)],
        ),
        compiler_params=pltpu.CompilerParams(vmem_limit_bytes=12 << 20),
        cost_estimate=pl.CostEstimate(flops=1 << 30, bytes_accessed=5 << 20, transcendentals=0),
    )(where, *l_blocks, *d_blocks)


def finish_kernel(mine_ref, got_ref, k_ref, v_ref):
    total = mine_ref[...] + got_ref[...]
    k_ref[...] = total[:HD, :].T
    v_ref[...] = total[HD:, :].T


def on_device(queries, key_states, value_states, attn_output, output_grad, log_norms, layer_input, doc_lengths):
    me = lax.axis_index("ctx").astype(jnp.int32)
    tp = lax.axis_index("tp").astype(jnp.int32)
    core, zl, y = me % 2, (me // 2) % 2, me // 4
    x, zh = tp // 2, tp % 2
    where = jnp.stack([(x + s - 2 * y) % 4 for s in range(4)] + [(zh ^ j) ^ zl for j in range(2)] + [core, core])

    kv = call(join_kernel, struct((ROWS, 2 * HD), bf16), (key_states, value_states))
    kv_zl, kv_y, kv_far = (send(kv, within_half(flip, True)) for flip in (1, 2, 3))
    l_own = send(layer_input, spread)

    aux_own = call(
        aux_kernel,
        struct((3 * HEADS, ROWS), f32),
        (doc_lengths, output_grad, attn_output, log_norms),
        in_specs=[pl.BlockSpec(memory_space=pltpu.SMEM)] + [pl.BlockSpec(memory_space=pltpu.VMEM)] * 3,
    )
    q_par, do_par, aux_par = (send(a, other_core) for a in (queries, output_grad, aux_own))
    aux, q, do = (aux_own, aux_par), (queries, q_par), (output_grad, do_par)

    l_other = send(l_own, shifted(dz=2))
    l_blocks = []
    for dx in (0, 1, 2, 3):
        for block in (l_own, l_other):
            l_blocks.append(block if dx == 0 else send(block, shifted(dx=-dx)))

    dq_own, dq_par, dkv_far = attention((4, 6), (kv_y, kv_far), aux, q, do, None, (f32, f32), bf16)
    got_far = send(dkv_far, within_half(2, False))
    dq_own, dq_par, dkv_near = attention((0, 2), (kv, kv_zl), aux, q, do, (dq_own, dq_par), (f32, bf16), f32)
    dq_got = send(dq_par, other_core)
    query_grad = ((dq_own + dq_got.astype(f32)) * SCALE).astype(bf16)

    pair = (2 * ROWS, 2 * HD)
    dkv, dkv_low = call(add_kernel, (struct(pair, f32), struct(pair, bf16)), (dkv_near, got_far))
    d_own = call(close_kernel, struct((4 * HD, ROWS), bf16), (dkv, send(dkv_low, other_zl)))
    d_blocks = [d_own if dy == 0 else send(d_own, shifted(dy=-dy)) for dy in (0, 1, 2, 3)]

    sent, kept = weights(where, l_blocks, d_blocks)
    key_weight, value_weight = call(
        finish_kernel, (struct((WIDTH // 2, HD), f32),) * 2, (kept, send(sent, other_core))
    )
    return query_grad, key_weight, value_weight


def solution(mesh):
    placed = (
        P("ctx", "tp"),
        P("ctx", "tp"),
        P("ctx", "tp"),
        P("ctx", "tp"),
        P("ctx", "tp"),
        P("tp", "ctx"),
        P("ctx", "tp"),
        P(),
    )
    return jax.shard_map(
        on_device,
        mesh=mesh,
        in_specs=placed,
        out_specs=(P("ctx", "tp"), P("ctx", "tp"), P("ctx", "tp")),
        check_vma=False,
    )
```

time: 118 us -> 101 us (0.86)
  Pallas kernels: 33 us -> 22 us
  waiting for transfers between devices: 26 us -> 19.4 us
  starting transfers between devices: 45.3 us -> 47 us
    pallas_call x5 -> x8, Pallas kernels: 33 us -> 22 us  [the longest x7 17.1 us: call(): pl.pallas_call(kernel, out_shape=out_shape, compiler_params=pltpu.Compile...]
    ppermute x23 -> x21, waiting for transfers between devices: 26 us -> 19.4 us  [send(): return lax.ppermute(value, AXES, route(target))]
    unnamed x39 -> x28, local copies, waits for them, and re-layouts: 3.11 us -> 8.92 us
    dynamic_slice x1 -> x0, local copies, waits for them, and re-layouts: 2.16 us -> none  [on_device(): sent = lax.dynamic_slice(partial, (0, (1 - core) * half), (2 * HD, half))]
    ppermute x23 -> x21, starting transfers between devices: 45.3 us -> 47 us  [send(): return lax.ppermute(value, AXES, route(target))]
    broadcast_in_dim x2 -> x0, local copies, waits for them, and re-layouts: 1.26 us -> none  [first_visible(): return jnp.broadcast_to(first[None, :].astype(jnp.int32), (8, ROWS))]
  transfers between devices with their start and end apart: 23 -> 21, of which waited for: 6 -> 5; matrix products, arithmetic and copies ran while one was open for 7% -> 2% of each run, Pallas kernels for 26% -> 21%
where the time goes in v2:
time: 101 us; the launch traced here: 100 us
  starting transfers between devices  47 us (47%)
  Pallas kernels  22 us (22%)
  waiting for transfers between devices  19.4 us (19%)
  local copies, waits for them, and re-layouts  9.01 us (9%)
  other arithmetic  1.99 us (2%)
    ppermute x21, starting transfers between devices, send(): return lax.ppermute(value, AXES, route(target))  47 us
    ppermute x21, waiting for transfers between devices, send(): return lax.ppermute(value, AXES, route(target))  19.4 us
    pallas_call x7, Pallas kernels, call(): pl.pallas_call(kernel, out_shape=out_shape, compiler_params=pltpu.Compile...  17.1 us
    unnamed x28, local copies, waits for them, and re-layouts  8.92 us
    pallas_call x1, Pallas kernels, weights(): pl.pallas_call(weights_kernel, out_shape=(struct((2 * HD, WIDTH // 2), f3...  4.91 us
  transfers between devices with their start and end apart: 21, of which 5 were waited for; matrix products, arithmetic and copies ran while one was open for 2% of the time, Pallas kernels for 21%

profile of v2, /device:TPU:1, one launch (start us, length us, event | category | flops | bytes accessed | tf_op | source)
XLA Modules:
  0.0 100.2 jit_solution(15366896327250746014)
XLA Ops:
  0.6 1.5 %collective-permute-start.2 = (bf16[256,1024]{1,0:T(8,128)(2,1)}, bf16[256,1024]{1,0:T(8,128)(2,1)S(1)}, u32[]{:S(2)}, u32[]{:S(2)}) collective-permute-start(bf16[256,1024]{1,0:T(8,128)(2,1)} %refs_4_.3), channel_id=1, source_target_pairs={{0,8},{8,0},{16,24},{24,16},{1,9},{9,1},{17,25},{25,17},{32,40},{4... | collective-permute-start | bytes 1572872 | tf_op jit(solution)/shard_map/ppermute | solution.py:41
  2.2 1.7 %collective-permute-start.7 = (bf16[256,1024]{1,0:T(8,128)(2,1)}, bf16[256,1024]{1,0:T(8,128)(2,1)S(1)}, u32[]{:S(2)}, u32[]{:S(2)}) collective-permute-start(bf16[256,1024]{1,0:T(8,128)(2,1)} %param.14), channel_id=1, source_target_pairs={{0,0},{8,8},{16,1},{24,9},{1,16},{9,24},{17,17},{25,25},{32,2},{40... | collective-permute-start | bytes 1572872 | tf_op jit(solution)/shard_map/ppermute | solution.py:41
  5.6 4.6 %collective-permute-start.4 = (bf16[256,256]{1,0:T(8,128)(2,1)S(1)}, bf16[256,256]{1,0:T(8,128)(2,1)S(1)}, u32[]{:S(2)}, u32[]{:S(2)}) collective-permute-start(bf16[256,256]{1,0:T(8,128)(2,1)S(1)} %shard_map.103.refs_0_), channel_id=1, source_target_pairs={{0,32},{8,40},{16,48},{24,56},{1,33},{9,41},{17,49},{25,57},{64,96... | collective-permute-start | bytes 393224 | tf_op jit(solution)/shard_map/ppermute | solution.py:41
  13.2 1.1 %collective-permute-start.1 = (f32[24,256]{1,0:T(8,128)S(1)}, f32[24,256]{1,0:T(8,128)S(1)}, u32[]{:S(2)}, u32[]{:S(2)}) collective-permute-start(f32[24,256]{1,0:T(8,128)S(1)} %shard_map.104.refs_2_), channel_id=1, source_target_pairs={{0,8},{8,0},{16,24},{24,16},{1,9},{9,1},{17,25},{25,17},{32,40},{4... | collective-permute-start | bytes 73736 | tf_op jit(solution)/shard_map/ppermute | solution.py:41
  15.2 3.7 %collective-permute-start.5 = (bf16[256,256]{1,0:T(8,128)(2,1)S(1)}, bf16[256,256]{1,0:T(8,128)(2,1)S(1)}, u32[]{:S(2)}, u32[]{:S(2)}) collective-permute-start(bf16[256,256]{1,0:T(8,128)(2,1)S(1)} %shard_map.103.refs_0_), channel_id=1, source_target_pairs={{0,48},{8,56},{16,32},{24,40},{1,49},{9,57},{17,33},{25,41},{64,11... | collective-permute-start | bytes 393224 | tf_op jit(solution)/shard_map/ppermute | solution.py:41
  18.9 2.5 %collective-permute-start = (bf16[256,256]{1,0:T(8,128)(2,1)S(1)}, bf16[256,256]{1,0:T(8,128)(2,1)S(1)}, u32[]{:S(2)}, u32[]{:S(2)}) collective-permute-start(bf16[256,256]{1,0:T(8,128)(2,1)S(1)} %shard_map.103.refs_0_), channel_id=1, source_target_pairs={{0,16},{8,24},{1,17},{9,25},{32,48},{40,56},{33,49},{41,57},{64,80... | collective-permute-start | bytes 393224 | tf_op jit(solution)/shard_map/ppermute | solution.py:41
  21.4 7.2 %shard_map.105 = (f32[256,1024]{1,0:T(8,128)S(1)}, f32[256,1024]{1,0:T(8,128)S(1)}, bf16[512,256]{1,0:T(8,128)(2,1)S(1)}) custom-call(bf16[256,256]{1,0:T(8,128)(2,1)S(1)} %collective-permute-done.4.refs_0_, bf16[256,256]{1,0:T(8,128)(2,1)S(1)} %collective-permute-done.5.refs_1_, f32[24,256]{1,0:T(8,128)S(1)} %shard_map.104.refs_2_, ...), custom_call_target="tpu_custom_call" | custom-call | bytes 65536 | tf_op jit(solution)/shard_map/pallas_call | solution.py:85
  28.6 1.3 %collective-permute-start.15 = (bf16[512,256]{1,0:T(8,128)(2,1)S(1)}, bf16[512,256]{1,0:T(8,128)(2,1)S(1)}, u32[]{:S(2)}, u32[]{:S(2)}) collective-permute-start(bf16[512,256]{1,0:T(8,128)(2,1)S(1)} %get-tuple-element.20), channel_id=1, source_target_pairs={{32,0},{40,8},{48,16},{56,24},{33,1},{41,9},{49,17},{57,25},{96,64... | collective-permute-start | bytes 786440 | tf_op jit(solution)/shard_map/ppermute | solution.py:41
  29.9 2.0 %collective-permute-start.8 = (bf16[256,1024]{1,0:T(8,128)(2,1)S(1)}, bf16[256,1024]{1,0:T(8,128)(2,1)S(1)}, u32[]{:S(2)}, u32[]{:S(2)}) collective-permute-start(bf16[256,1024]{1,0:T(8,128)(2,1)S(1)} %collective-permute-done.7.refs_0_), channel_id=1, source_target_pairs={{0,1},{8,9},{16,17},{24,25},{1,0},{9,8},{17,16},{25,24},{32,33},{4... | collective-permute-start | bytes 1572872 | tf_op jit(solution)/shard_map/ppermute | solution.py:41
  32.0 3.3 %collective-permute-start.9 = (bf16[256,1024]{1,0:T(8,128)(2,1)S(1)}, bf16[256,1024]{1,0:T(8,128)(2,1)S(1)}, u32[]{:S(2)}, u32[]{:S(2)}) collective-permute-start(bf16[256,1024]{1,0:T(8,128)(2,1)S(1)} %collective-permute-done.7.refs_0_), channel_id=1, source_target_pairs={{0,6},{8,14},{16,22},{24,30},{1,7},{9,15},{17,23},{25,31},{32,38},... | collective-permute-start | bytes 1572872 | tf_op jit(solution)/shard_map/ppermute | solution.py:41
  35.3 4.0 %collective-permute-start.11 = (bf16[256,1024]{1,0:T(8,128)(2,1)S(1)}, bf16[256,1024]{1,0:T(8,128)(2,1)S(1)}, u32[]{:S(2)}, u32[]{:S(2)}) collective-permute-start(bf16[256,1024]{1,0:T(8,128)(2,1)S(1)} %collective-permute-done.7.refs_0_), channel_id=1, source_target_pairs={{0,4},{8,12},{16,20},{24,28},{1,5},{9,13},{17,21},{25,29},{32,36},... | collective-permute-start | bytes 1572872 | tf_op jit(solution)/shard_map/ppermute | solution.py:41
  40.1 7.9 %shard_map.106 = (f32[256,1024]{1,0:T(8,128)S(1)}, bf16[256,1024]{1,0:T(8,128)(2,1)}, f32[512,256]{1,0:T(8,128)S(1)}) custom-call(bf16[256,256]{1,0:T(8,128)(2,1)S(1)} %shard_map.103.refs_0_, bf16[256,256]{1,0:T(8,128)(2,1)S(1)} %collective-permute-done.refs_1_, f32[24,256]{1,0:T(8,128)S(1)} %shard_map.104.refs_2_, ...), custom_call_target="tpu_custom_call" | custom-call | bytes 65536 | tf_op jit(solution)/shard_map/pallas_call | solution.py:85
  48.4 5.2 %collective-permute-done.16.got_ref = bf16[512,256]{1,0:T(8,128)(2,1)S(1)} collective-permute-done((bf16[512,256]{1,0:T(8,128)(2,1)S(1)}, bf16[512,256]{1,0:T(8,128)(2,1)S(1)}, u32[]{:S(2)}, u32[]{:S(2)}) %collective-permute-start.16) | collective-permute-done | bytes 262176 | tf_op jit(solution)/shard_map/ppermute | solution.py:41
  53.8 6.2 %collective-permute-start.17 = (bf16[512,256]{1,0:T(8,128)(2,1)S(1)}, bf16[512,256]{1,0:T(8,128)(2,1)S(1)}, u32[]{:S(2)}, u32[]{:S(2)}) collective-permute-start(bf16[512,256]{1,0:T(8,128)(2,1)S(1)} %shard_map.108.refs_8_), channel_id=1, source_target_pairs={{0,96},{8,104},{16,112},{24,120},{1,97},{9,105},{17,113},{25,121},... | collective-permute-start | bytes 786440 | tf_op jit(solution)/shard_map/ppermute | solution.py:41
  60.0 2.4 %collective-permute-start.10 = (bf16[256,1024]{1,0:T(8,128)(2,1)S(1)}, bf16[256,1024]{1,0:T(8,128)(2,1)}, u32[]{:S(2)}, u32[]{:S(2)}) collective-permute-start(bf16[256,1024]{1,0:T(8,128)(2,1)S(1)} %collective-permute-done.8.refs_1_), channel_id=1, source_target_pairs={{0,6},{8,14},{16,22},{24,30},{1,7},{9,15},{17,23},{25,31},{32,38},... | collective-permute-start | bytes 1572872 | tf_op jit(solution)/shard_map/ppermute | solution.py:41
  63.9 5.7 %collective-permute-start.18 = (bf16[512,256]{1,0:T(8,128)(2,1)S(1)}, bf16[512,256]{1,0:T(8,128)(2,1)S(1)}, u32[]{:S(2)}, u32[]{:S(2)}) collective-permute-start(bf16[512,256]{1,0:T(8,128)(2,1)S(1)} %shard_map.108.refs_8_), channel_id=1, source_target_pairs={{0,64},{8,72},{16,80},{24,88},{1,65},{9,73},{17,81},{25,89},{32,96... | collective-permute-start | bytes 786440 | tf_op jit(solution)/shard_map/ppermute | solution.py:41
  70.3 1.8 %collective-permute-start.19 = (bf16[512,256]{1,0:T(8,128)(2,1)S(1)}, bf16[512,256]{1,0:T(8,128)(2,1)}, u32[]{:S(2)}, u32[]{:S(2)}) collective-permute-start(bf16[512,256]{1,0:T(8,128)(2,1)S(1)} %shard_map.108.refs_8_), channel_id=1, source_target_pairs={{0,32},{8,40},{16,48},{24,56},{1,33},{9,41},{17,49},{25,57},{32,64... | collective-permute-start | bytes 786440 | tf_op jit(solution)/shard_map/ppermute | solution.py:41
  72.1 3.4 %collective-permute-done.18.refs_10_ = bf16[512,256]{1,0:T(8,128)(2,1)S(1)} collective-permute-done((bf16[512,256]{1,0:T(8,128)(2,1)S(1)}, bf16[512,256]{1,0:T(8,128)(2,1)S(1)}, u32[]{:S(2)}, u32[]{:S(2)}) %collective-permute-start.18) | collective-permute-done | bytes 262176 | tf_op jit(solution)/shard_map/ppermute | solution.py:41
  76.2 2.5 %collective-permute-start.6 = (bf16[256,1024]{1,0:T(8,128)(2,1)}, bf16[256,1024]{1,0:T(8,128)(2,1)}, u32[]{:S(2)}, u32[]{:S(2)}) collective-permute-start(bf16[256,1024]{1,0:T(8,128)(2,1)} %get-tuple-element.18), channel_id=1, source_target_pairs={{0,8},{8,0},{16,24},{24,16},{1,9},{9,1},{17,25},{25,17},{32,40},{4... | collective-permute-start | bytes 1572872 | tf_op jit(solution)/shard_map/ppermute | solution.py:41
  78.7 3.3 %collective-permute-done.19.refs_11_ = bf16[512,256]{1,0:T(8,128)(2,1)} collective-permute-done((bf16[512,256]{1,0:T(8,128)(2,1)S(1)}, bf16[512,256]{1,0:T(8,128)(2,1)}, u32[]{:S(2)}, u32[]{:S(2)}) %collective-permute-start.19) | collective-permute-done | bytes 262176 | tf_op jit(solution)/shard_map/ppermute | solution.py:41
  82.0 6.6 %collective-permute-done.14.refs_7_ = bf16[256,1024]{1,0:T(8,128)(2,1)} collective-permute-done((bf16[256,1024]{1,0:T(8,128)(2,1)S(1)}, bf16[256,1024]{1,0:T(8,128)(2,1)}, u32[]{:S(2)}, u32[]{:S(2)}) %collective-permute-start.14) | collective-permute-done | bytes 524320 | tf_op jit(solution)/shard_map/ppermute | solution.py:41
  88.7 1.0 %copy-done.5 = bf16[256,1024]{1,0:T(8,128)(2,1)S(1)} copy-done((bf16[256,1024]{1,0:T(8,128)(2,1)S(1)}, bf16[256,1024]{1,0:T(8,128)(2,1)}, u32[]{:S(2)}) %copy-start.5) | copy-done | bytes 524312
  91.6 4.9 %shard_map.109 = (f32[256,512]{1,0:T(8,128)S(1)}, f32[256,512]{1,0:T(8,128)S(1)}) custom-call(s32[8]{0:T(128)S(1)} %stack.32.where, bf16[256,1024]{1,0:T(8,128)(2,1)S(1)} %collective-permute-done.7.refs_0_, bf16[256,1024]{1,0:T(8,128)(2,1)S(1)} %collective-permute-done.8.refs_1_, bf16[256,1024]{1,0:T(8,128)(2,1)S(1)} %collective-permute-done.9.refs_2_, ...), custom_call_target="tpu_custom_call" | custom-call | flops 1073741824 | bytes 5242880 | tf_op jit(solution)/shard_map/pallas_call | solution.py:233
  97.3 2.0 %multiply_convert_fusion = bf16[256,1024]{1,0:T(8,128)(2,1)} fusion(f32[256,1024]{1,0:T(8,128)S(1)} %get-tuple-element.17, bf16[256,1024]{1,0:T(8,128)(2,1)} %collective-permute-done.6), kind=kLoop, calls=%fused_computation | loop fusion | flops 1048576 | bytes 2097152 | tf_op jit(solution)/shard_map/convert_element_type | solution.py:288
  (56 shorter events, 13.7 us)
Async XLA Ops:
  0.6 20.8 %collective-permute-start.2 = (bf16[256,1024]{1,0:T(8,128)(2,1)}, bf16[256,1024]{1,0:T(8,128)(2,1)S(1)}, u32[]{:S(2)}, u32[]{:S(2)}) collective-permute-start(bf16[256,1024]{1,0:T(8,128)(2,1)} %refs_4_.3), channel_id=1, source_target_pairs={{0,8},{8,0},{16,24},{24,16},{1,9},{9,1},{17,25},{25,17},{32,40},{4... | collective-permute-start | bytes 1572872 | tf_op jit(solution)/shard_map/ppermute | solution.py:41
  2.1 19.3 %collective-permute-start.3 = (bf16[256,1024]{1,0:T(8,128)(2,1)}, bf16[256,1024]{1,0:T(8,128)(2,1)S(1)}, u32[]{:S(2)}, u32[]{:S(2)}) collective-permute-start(bf16[256,1024]{1,0:T(8,128)(2,1)} %refs_6_.3), channel_id=1, source_target_pairs={{0,8},{8,0},{16,24},{24,16},{1,9},{9,1},{17,25},{25,17},{32,40},{4... | collective-permute-start | bytes 1572872 | tf_op jit(solution)/shard_map/ppermute | solution.py:41
  2.2 27.7 %collective-permute-start.7 = (bf16[256,1024]{1,0:T(8,128)(2,1)}, bf16[256,1024]{1,0:T(8,128)(2,1)S(1)}, u32[]{:S(2)}, u32[]{:S(2)}) collective-permute-start(bf16[256,1024]{1,0:T(8,128)(2,1)} %param.14), channel_id=1, source_target_pairs={{0,0},{8,8},{16,1},{24,9},{1,16},{9,24},{17,17},{25,25},{32,2},{40... | collective-permute-start | bytes 1572872 | tf_op jit(solution)/shard_map/ppermute | solution.py:41
  5.6 4.7 %copy-start.13 = (s32[16]{0:T(128)S(1)}, s32[16]{0:T(128)}, u32[]{:S(2)}) copy-start(s32[16]{0:T(128)} %lengths_ref.1) | copy-start | bytes 196
  5.6 13.2 %collective-permute-start.4 = (bf16[256,256]{1,0:T(8,128)(2,1)S(1)}, bf16[256,256]{1,0:T(8,128)(2,1)S(1)}, u32[]{:S(2)}, u32[]{:S(2)}) collective-permute-start(bf16[256,256]{1,0:T(8,128)(2,1)S(1)} %shard_map.103.refs_0_), channel_id=1, source_target_pairs={{0,32},{8,40},{16,48},{24,56},{1,33},{9,41},{17,49},{25,57},{64,96... | collective-permute-start | bytes 393224 | tf_op jit(solution)/shard_map/ppermute | solution.py:41
  12.3 9.1 %copy-start.1 = (bf16[256,1024]{1,0:T(8,128)(2,1)S(1)}, bf16[256,1024]{1,0:T(8,128)(2,1)}, u32[]{:S(2)}) copy-start(bf16[256,1024]{1,0:T(8,128)(2,1)} %refs_6_.3) | copy-start | bytes 1572868
  12.3 9.1 %copy-start.2 = (bf16[256,1024]{1,0:T(8,128)(2,1)S(1)}, bf16[256,1024]{1,0:T(8,128)(2,1)}, u32[]{:S(2)}) copy-start(bf16[256,1024]{1,0:T(8,128)(2,1)} %refs_4_.3) | copy-start | bytes 1572868
  13.2 1.9 %collective-permute-start.1 = (f32[24,256]{1,0:T(8,128)S(1)}, f32[24,256]{1,0:T(8,128)S(1)}, u32[]{:S(2)}, u32[]{:S(2)}) collective-permute-start(f32[24,256]{1,0:T(8,128)S(1)} %shard_map.104.refs_2_), channel_id=1, source_target_pairs={{0,8},{8,0},{16,24},{24,16},{1,9},{9,1},{17,25},{25,17},{32,40},{4... | collective-permute-start | bytes 73736 | tf_op jit(solution)/shard_map/ppermute | solution.py:41
  15.2 6.2 %collective-permute-start.5 = (bf16[256,256]{1,0:T(8,128)(2,1)S(1)}, bf16[256,256]{1,0:T(8,128)(2,1)S(1)}, u32[]{:S(2)}, u32[]{:S(2)}) collective-permute-start(bf16[256,256]{1,0:T(8,128)(2,1)S(1)} %shard_map.103.refs_0_), channel_id=1, source_target_pairs={{0,48},{8,56},{16,32},{24,40},{1,49},{9,57},{17,33},{25,41},{64,11... | collective-permute-start | bytes 393224 | tf_op jit(solution)/shard_map/ppermute | solution.py:41
  18.9 20.4 %collective-permute-start = (bf16[256,256]{1,0:T(8,128)(2,1)S(1)}, bf16[256,256]{1,0:T(8,128)(2,1)S(1)}, u32[]{:S(2)}, u32[]{:S(2)}) collective-permute-start(bf16[256,256]{1,0:T(8,128)(2,1)S(1)} %shard_map.103.refs_0_), channel_id=1, source_target_pairs={{0,16},{8,24},{1,17},{9,25},{32,48},{40,56},{33,49},{41,57},{64,80... | collective-permute-start | bytes 393224 | tf_op jit(solution)/shard_map/ppermute | solution.py:41
  28.6 19.4 %collective-permute-start.15 = (bf16[512,256]{1,0:T(8,128)(2,1)S(1)}, bf16[512,256]{1,0:T(8,128)(2,1)S(1)}, u32[]{:S(2)}, u32[]{:S(2)}) collective-permute-start(bf16[512,256]{1,0:T(8,128)(2,1)S(1)} %get-tuple-element.20), channel_id=1, source_target_pairs={{32,0},{40,8},{48,16},{56,24},{33,1},{41,9},{49,17},{57,25},{96,64... | collective-permute-start | bytes 786440 | tf_op jit(solution)/shard_map/ppermute | solution.py:41
  29.9 30.1 %collective-permute-start.8 = (bf16[256,1024]{1,0:T(8,128)(2,1)S(1)}, bf16[256,1024]{1,0:T(8,128)(2,1)S(1)}, u32[]{:S(2)}, u32[]{:S(2)}) collective-permute-start(bf16[256,1024]{1,0:T(8,128)(2,1)S(1)} %collective-permute-done.7.refs_0_), channel_id=1, source_target_pairs={{0,1},{8,9},{16,17},{24,25},{1,0},{9,8},{17,16},{25,24},{32,33},{4... | collective-permute-start | bytes 1572872 | tf_op jit(solution)/shard_map/ppermute | solution.py:41
  32.0 30.4 %collective-permute-start.9 = (bf16[256,1024]{1,0:T(8,128)(2,1)S(1)}, bf16[256,1024]{1,0:T(8,128)(2,1)S(1)}, u32[]{:S(2)}, u32[]{:S(2)}) collective-permute-start(bf16[256,1024]{1,0:T(8,128)(2,1)S(1)} %collective-permute-done.7.refs_0_), channel_id=1, source_target_pairs={{0,6},{8,14},{16,22},{24,30},{1,7},{9,15},{17,23},{25,31},{32,38},... | collective-permute-start | bytes 1572872 | tf_op jit(solution)/shard_map/ppermute | solution.py:41
  35.3 27.1 %collective-permute-start.11 = (bf16[256,1024]{1,0:T(8,128)(2,1)S(1)}, bf16[256,1024]{1,0:T(8,128)(2,1)S(1)}, u32[]{:S(2)}, u32[]{:S(2)}) collective-permute-start(bf16[256,1024]{1,0:T(8,128)(2,1)S(1)} %collective-permute-done.7.refs_0_), channel_id=1, source_target_pairs={{0,4},{8,12},{16,20},{24,28},{1,5},{9,13},{17,21},{25,29},{32,36},... | collective-permute-start | bytes 1572872 | tf_op jit(solution)/shard_map/ppermute | solution.py:41
  39.2 23.8 %collective-permute-start.13 = (bf16[256,1024]{1,0:T(8,128)(2,1)S(1)}, bf16[256,1024]{1,0:T(8,128)(2,1)S(1)}, u32[]{:S(2)}, u32[]{:S(2)}) collective-permute-start(bf16[256,1024]{1,0:T(8,128)(2,1)S(1)} %collective-permute-done.7.refs_0_), channel_id=1, source_target_pairs={{0,2},{8,10},{16,18},{24,26},{1,3},{9,11},{17,19},{25,27},{32,34},... | collective-permute-start | bytes 1572872 | tf_op jit(solution)/shard_map/ppermute | solution.py:41
  48.1 5.6 %collective-permute-start.16 = (bf16[512,256]{1,0:T(8,128)(2,1)S(1)}, bf16[512,256]{1,0:T(8,128)(2,1)S(1)}, u32[]{:S(2)}, u32[]{:S(2)}) collective-permute-start(bf16[512,256]{1,0:T(8,128)(2,1)S(1)} %get-tuple-element.22), channel_id=1, source_target_pairs={{0,16},{8,24},{16,0},{24,8},{1,17},{9,25},{17,1},{25,9},{32,48},{4... | collective-permute-start | bytes 786440 | tf_op jit(solution)/shard_map/ppermute | solution.py:41
  53.8 15.8 %collective-permute-start.17 = (bf16[512,256]{1,0:T(8,128)(2,1)S(1)}, bf16[512,256]{1,0:T(8,128)(2,1)S(1)}, u32[]{:S(2)}, u32[]{:S(2)}) collective-permute-start(bf16[512,256]{1,0:T(8,128)(2,1)S(1)} %shard_map.108.refs_8_), channel_id=1, source_target_pairs={{0,96},{8,104},{16,112},{24,120},{1,97},{9,105},{17,113},{25,121},... | collective-permute-start | bytes 786440 | tf_op jit(solution)/shard_map/ppermute | solution.py:41
  60.0 22.0 %collective-permute-start.10 = (bf16[256,1024]{1,0:T(8,128)(2,1)S(1)}, bf16[256,1024]{1,0:T(8,128)(2,1)}, u32[]{:S(2)}, u32[]{:S(2)}) collective-permute-start(bf16[256,1024]{1,0:T(8,128)(2,1)S(1)} %collective-permute-done.8.refs_1_), channel_id=1, source_target_pairs={{0,6},{8,14},{16,22},{24,30},{1,7},{9,15},{17,23},{25,31},{32,38},... | collective-permute-start | bytes 1572872 | tf_op jit(solution)/shard_map/ppermute | solution.py:41
  62.4 19.6 %collective-permute-start.12 = (bf16[256,1024]{1,0:T(8,128)(2,1)S(1)}, bf16[256,1024]{1,0:T(8,128)(2,1)}, u32[]{:S(2)}, u32[]{:S(2)}) collective-permute-start(bf16[256,1024]{1,0:T(8,128)(2,1)S(1)} %collective-permute-done.8.refs_1_), channel_id=1, source_target_pairs={{0,4},{8,12},{16,20},{24,28},{1,5},{9,13},{17,21},{25,29},{32,36},... | collective-permute-start | bytes 1572872 | tf_op jit(solution)/shard_map/ppermute | solution.py:41
  62.4 26.2 %collective-permute-start.14 = (bf16[256,1024]{1,0:T(8,128)(2,1)S(1)}, bf16[256,1024]{1,0:T(8,128)(2,1)}, u32[]{:S(2)}, u32[]{:S(2)}) collective-permute-start(bf16[256,1024]{1,0:T(8,128)(2,1)S(1)} %collective-permute-done.8.refs_1_), channel_id=1, source_target_pairs={{0,2},{8,10},{16,18},{24,26},{1,3},{9,11},{17,19},{25,27},{32,34},... | collective-permute-start | bytes 1572872 | tf_op jit(solution)/shard_map/ppermute | solution.py:41
  63.9 11.6 %collective-permute-start.18 = (bf16[512,256]{1,0:T(8,128)(2,1)S(1)}, bf16[512,256]{1,0:T(8,128)(2,1)S(1)}, u32[]{:S(2)}, u32[]{:S(2)}) collective-permute-start(bf16[512,256]{1,0:T(8,128)(2,1)S(1)} %shard_map.108.refs_8_), channel_id=1, source_target_pairs={{0,64},{8,72},{16,80},{24,88},{1,65},{9,73},{17,81},{25,89},{32,96... | collective-permute-start | bytes 786440 | tf_op jit(solution)/shard_map/ppermute | solution.py:41
  70.3 11.7 %collective-permute-start.19 = (bf16[512,256]{1,0:T(8,128)(2,1)S(1)}, bf16[512,256]{1,0:T(8,128)(2,1)}, u32[]{:S(2)}, u32[]{:S(2)}) collective-permute-start(bf16[512,256]{1,0:T(8,128)(2,1)S(1)} %shard_map.108.refs_8_), channel_id=1, source_target_pairs={{0,32},{8,40},{16,48},{24,56},{1,33},{9,41},{17,49},{25,57},{32,64... | collective-permute-start | bytes 786440 | tf_op jit(solution)/shard_map/ppermute | solution.py:41
  76.2 21.1 %collective-permute-start.6 = (bf16[256,1024]{1,0:T(8,128)(2,1)}, bf16[256,1024]{1,0:T(8,128)(2,1)}, u32[]{:S(2)}, u32[]{:S(2)}) collective-permute-start(bf16[256,1024]{1,0:T(8,128)(2,1)} %get-tuple-element.18), channel_id=1, source_target_pairs={{0,8},{8,0},{16,24},{24,16},{1,9},{9,1},{17,25},{25,17},{32,40},{4... | collective-permute-start | bytes 1572872 | tf_op jit(solution)/shard_map/ppermute | solution.py:41
  96.5 2.8 %collective-permute-start.20 = (f32[256,512]{1,0:T(8,128)S(1)}, f32[256,512]{1,0:T(8,128)S(1)}, u32[]{:S(2)}, u32[]{:S(2)}) collective-permute-start(f32[256,512]{1,0:T(8,128)S(1)} %get-tuple-element.24), channel_id=1, source_target_pairs={{0,8},{8,0},{16,24},{24,16},{1,9},{9,1},{17,25},{25,17},{32,40},{4... | collective-permute-start | bytes 1572872 | tf_op jit(solution)/shard_map/ppermute | solution.py:41
  (11 other events, 13.6 us)

commit v3 on v2

v3 whole, which is shorter than its diff:
```python
import functools
import itertools
import math

import jax
import jax.numpy as jnp
from jax import lax
from jax.experimental import pallas as pl
from jax.experimental.pallas import tpu as pltpu
from jax.sharding import PartitionSpec as P

HD = 128
HEADS = 8
ROWS = 256
WIDTH = HEADS * HD
SCALE = 1.0 / math.sqrt(HD)
LOG2E = math.log2(math.e)
AXES = ("ctx", "tp")
DOCS = 16
STEP_HEADS = 4

f32 = jnp.float32
bf16 = jnp.bfloat16


def linear(x, y, z, core):
    zh, zl = divmod(z, 2)
    return ((y * 2 + zl) * 2 + core) * 8 + x * 2 + zh


def route(target):
    pairs = []
    for x, y, z, core in itertools.product(range(4), range(4), range(4), range(2)):
        to = target(x, y, z, core)
        if to is not None:
            pairs.append((linear(x, y, z, core), linear(*to)))
    return pairs


def send(value, target):
    return lax.ppermute(value, AXES, route(target))


def other_core(x, y, z, core):
    return (x, y, z, 1 - core)


def shifted(dx=0, dy=0, dz=0):
    return lambda x, y, z, core: ((x + dx) % 4, (y + dy) % 4, (z + dz) % 4, core)


def other_zl(x, y, z, core):
    return (x, y, z ^ 1, core)


def spread(x, y, z, core):
    zh, zl = divmod(z, 2)
    return ((x + y) % 4, x, zl * 2 + zh, core)


def within_half(flip, later):
    def target(x, y, z, core):
        place = (y % 2) * 2 + z % 2
        to = place ^ flip
        if (to > place) != later:
            return None
        return (x, y - y % 2 + to // 2, z - z % 2 + to % 2, core)

    return target


def nt(a, b):
    return lax.dot_general(a, b, (((1,), (1,)), ((), ())), preferred_element_type=f32)


def nn(a, b):
    return lax.dot_general(a, b, (((1,), (0,)), ((), ())), preferred_element_type=f32)


def tn(a, b):
    return lax.dot_general(a, b, (((0,), (0,)), ((), ())), preferred_element_type=f32)


def together(*arrays):
    return lax.optimization_barrier(arrays)


def call(kernel, out_shape, operands, megabytes=12, micros=0.01, **more):
    return pl.pallas_call(
        kernel,
        out_shape=out_shape,
        compiler_params=pltpu.CompilerParams(vmem_limit_bytes=megabytes << 20),
        cost_estimate=pl.CostEstimate(flops=int(micros * 1.15e9), bytes_accessed=1 << 16, transcendentals=0),
        **more,
    )(*operands)


def struct(shape, dtype):
    return jax.ShapeDtypeStruct(shape, dtype)


def prepare_kernel(lengths_ref, k_any, v_any, do_any, out_any, ln_any, kv_ref, aux_ref, do_ref, out_ref, sems):
    copies = [
        pltpu.make_async_copy(src, dst, sems.at[i])
        for i, (src, dst) in enumerate(
            (
                (k_any, kv_ref.at[:, :HD]),
                (v_any, kv_ref.at[:, HD:]),
                (ln_any, aux_ref.at[HEADS : 2 * HEADS, :]),
                (do_any, do_ref),
                (out_any, out_ref),
            )
        )
    ]
    for copy in copies:
        copy.start()
    positions = lax.axis_index("ctx") * ROWS + lax.broadcasted_iota(jnp.int32, (HEADS, ROWS), 1)
    end = jnp.int32(0)
    first = jnp.zeros((HEADS, ROWS), jnp.int32)
    for i in range(DOCS):
        end = end + lengths_ref[i]
        first = jnp.where(positions >= end, end, first)
    aux_ref[2 * HEADS :, :] = first.astype(f32)
    for copy in copies:
        copy.wait()
    aux_ref[HEADS : 2 * HEADS, :] = aux_ref[HEADS : 2 * HEADS, :] * LOG2E
    for h in range(HEADS):
        cols = slice(h * HD, (h + 1) * HD)
        prod = do_ref[:, cols].astype(f32) * out_ref[:, cols].astype(f32)
        aux_ref[h : h + 1, :] = jnp.sum(prod.T, axis=0, keepdims=True)


def prepare(doc_lengths, k, v, do, out, ln):
    return call(
        prepare_kernel,
        (struct((ROWS, 2 * HD), bf16), struct((3 * HEADS, ROWS), f32)),
        (doc_lengths, k, v, do, out, ln),
        in_specs=[pl.BlockSpec(memory_space=pltpu.SMEM)] + [pl.BlockSpec(memory_space=pltpu.HBM)] * 5,
        megabytes=60,
        micros=0.3,
        scratch_shapes=[pltpu.VMEM((ROWS, WIDTH), bf16)] * 2 + [pltpu.SemaphoreType.DMA((5,))],
    )


def attention_kernel(flips, has_sum, *refs):
    refs = list(refs)
    take = lambda n: [refs.pop(0) for _ in range(n)]
    kv_refs, aux_refs, q_refs, do_refs = take(len(flips)), take(2), take(2), take(2)
    sums = take(2) if has_sum else None
    dq_refs = take(2)
    dkv_ref, dk_acc, dv_acc = refs
    me = lax.axis_index("ctx")
    dk_acc[...] = jnp.zeros_like(dk_acc)
    dv_acc[...] = jnp.zeros_like(dv_acc)

    @pl.loop(0, HEADS // STEP_HEADS)
    def _(step):
        k = jnp.concatenate([r[:, :HD] for r in kv_refs], axis=0)
        v = jnp.concatenate([r[:, HD:] for r in kv_refs], axis=0)
        offset = lax.broadcasted_iota(jnp.int32, (ROWS, 1), 0)
        key_pos = jnp.concatenate([(me ^ flip) * ROWS + offset for flip in flips], axis=0)
        lane = lax.broadcasted_iota(jnp.int32, (1, ROWS), 1)
        dk = dv = None
        for i in range(2):
            query_pos = (me ^ i) * ROWS + lane
            first = aux_refs[i][2 * HEADS : 2 * HEADS + 1, :].astype(jnp.int32)
            visible = (key_pos <= query_pos) & (key_pos >= first)
            for j in range(STEP_HEADS):
                h = step * STEP_HEADS + j
                cols = pl.ds(pl.multiple_of(h * HD, HD), HD)
                q = q_refs[i][:, cols]
                do = do_refs[i][:, cols]
                dots = aux_refs[i][pl.ds(h, 1), :]
                norm = aux_refs[i][pl.ds(HEADS + h, 1), :]
                p = jnp.where(visible, jnp.exp2(nt(k, q) * (SCALE * LOG2E) - norm), 0.0)
                ds = (p * (nt(v, do) - dots)).astype(bf16)
                dv_term, dk_term, dq = nn(p.astype(bf16), do), nn(ds, q), tn(ds, k)
                dv = dv_term if dv is None else dv + dv_term
                dk = dk_term if dk is None else dk + dk_term
                if has_sum:
                    dq = dq + sums[i][:, cols]
                dq_refs[i][:, cols] = dq.astype(dq_refs[i].dtype)
        dk_acc[...] += dk
        dv_acc[...] += dv

    dkv_ref[:, :HD] = dk_acc[...].astype(dkv_ref.dtype)
    dkv_ref[:, HD:] = dv_acc[...].astype(dkv_ref.dtype)


def attention(flips, kv, aux, q, do, sums, dq_types, dkv_type, micros):
    keys = len(flips) * ROWS
    return call(
        functools.partial(attention_kernel, flips, sums is not None),
        (
            struct((ROWS, WIDTH), dq_types[0]),
            struct((ROWS, WIDTH), dq_types[1]),
            struct((keys, 2 * HD), dkv_type),
        ),
        [*kv, *aux, *q, *do, *(sums or ())],
        megabytes=24,
        micros=micros,
        scratch_shapes=[pltpu.VMEM((keys, HD), f32)] * 2,
    )


def add_kernel(own_ref, zl_ref, got_ref, sum_ref, low_ref):
    for half, near_ref in enumerate((own_ref, zl_ref)):
        rows = slice(half * ROWS, (half + 1) * ROWS)
        total = near_ref[...] + got_ref[rows, :].astype(f32)
        sum_ref[rows, :] = total
        low_ref[rows, :] = total.astype(bf16)


def close_kernel(sum_ref, got_ref, d_ref):
    for half in range(2):
        mine = slice(half * ROWS, (half + 1) * ROWS)
        its = slice((1 - half) * ROWS, (2 - half) * ROWS)
        total = sum_ref[mine, :] + got_ref[its, :].astype(f32)
        d_ref[half * 2 * HD : half * 2 * HD + HD, :] = (total[:, :HD] * SCALE).T.astype(bf16)
        d_ref[half * 2 * HD + HD : (half + 1) * 2 * HD, :] = total[:, HD:].T.astype(bf16)


def weights_kernel(*refs):
    l_refs, d_refs, (sent_ref, kept_ref, d_all) = refs[:8], refs[8:12], refs[12:]
    me, tp = lax.axis_index("ctx"), lax.axis_index("tp")
    core, zl, y = me % 2, (me // 2) % 2, me // 4
    x, zh = tp // 2, tp % 2
    for r in range(4):
        for half in range(2):
            d_all[r * 2 + half] = d_refs[r][half * 2 * HD : (half + 1) * 2 * HD, :]
    half_width = WIDTH // 2
    for out_ref, whose in ((sent_ref, 1 - core), (kept_ref, core)):
        for t in range(2):
            tile = half_width // 2
            cols = pl.ds(pl.multiple_of(whose * half_width + t * tile, tile), tile)
            total = None
            for s in range(4):
                for j in range(2):
                    slot = ((x + s + 2 * y) % 4) * 2 + ((zh ^ j) ^ zl)
                    term = nn(d_all[slot], l_refs[s * 2 + j][:, cols])
                    total = term if total is None else total + term
            out_ref[:, t * tile : (t + 1) * tile] = total


def weights(l_blocks, d_blocks):
    return call(
        weights_kernel,
        (struct((2 * HD, WIDTH // 2), f32),) * 2,
        (*l_blocks, *d_blocks),
        scratch_shapes=[pltpu.VMEM((8, 2 * HD, ROWS), bf16)],
    )


def finish_kernel(mine_ref, got_ref, k_ref, v_ref):
    total = mine_ref[...] + got_ref[...]
    k_ref[...] = total[:HD, :].T
    v_ref[...] = total[HD:, :].T


def on_device(queries, key_states, value_states, attn_output, output_grad, log_norms, layer_input, doc_lengths):
    q_par, do_par = (send(a, other_core) for a in (queries, output_grad))
    l_own = send(layer_input, spread)
    kv, aux_own = prepare(doc_lengths, key_states, value_states, output_grad, attn_output, log_norms)
    kv, aux_own, q_par, do_par = together(kv, aux_own, q_par, do_par)
    aux_par = send(aux_own, other_core)
    aux, q, do = (aux_own, aux_par), (queries, q_par), (output_grad, do_par)

    kv_far, kv_y, kv_zl = (send(kv, within_half(flip, True)) for flip in (3, 2, 1))

    behind, ahead, across = shifted(dx=-1), shifted(dx=1), shifted(dz=2)
    *dqs, dkv_own = attention((0,), (kv,), aux, q, do, None, (f32, f32), f32, 0.3)
    l_own, dkv_own, kv_y, kv_far, *dqs = together(l_own, dkv_own, kv_y, kv_far, *dqs)
    own_1, own_3, other_0 = send(l_own, behind), send(l_own, ahead), send(l_own, across)

    *dqs, dkv_far = attention((4, 6), (kv_y, kv_far), aux, q, do, dqs, (f32, f32), bf16, 0.3)
    got_far = send(dkv_far, within_half(2, False))
    dq_own, dq_par, dkv_zl = attention((2,), (kv_zl,), aux, q, do, dqs, (f32, bf16), f32, 1.5)
    dq_own, dq_par, dkv_zl, got_far, own_1, own_3, other_0 = together(
        dq_own, dq_par, dkv_zl, got_far, own_1, own_3, other_0
    )
    own_2, other_3 = send(own_1, behind), send(other_0, ahead)

    dq_got = send(dq_par, other_core)
    query_grad = ((dq_own + dq_got.astype(f32)) * SCALE).astype(bf16)

    pair = (2 * ROWS, 2 * HD)
    dkv, dkv_low = call(add_kernel, (struct(pair, f32), struct(pair, bf16)), (dkv_own, dkv_zl, got_far))
    got_zl = send(dkv_low, other_zl)
    got_zl, query_grad = together(got_zl, query_grad)
    d_own = call(close_kernel, struct((4 * HD, ROWS), bf16), (dkv, got_zl))
    own_2, other_3, other_0, _ = together(own_2, other_3, other_0, d_own)
    other_1, other_2 = send(other_0, behind), send(own_2, across)
    d_blocks = (d_own, *(send(d_own, shifted(dy=-dy)) for dy in (1, 2, 3)))

    l_blocks = (l_own, other_0, own_1, other_1, own_2, other_2, own_3, other_3)
    sent, kept = weights(l_blocks, d_blocks)
    key_weight, value_weight = call(
        finish_kernel, (struct((WIDTH // 2, HD), f32),) * 2, (kept, send(sent, other_core))
    )
    return query_grad, key_weight, value_weight


def solution(mesh):
    placed = (
        P("ctx", "tp"),
        P("ctx", "tp"),
        P("ctx", "tp"),
        P("ctx", "tp"),
        P("ctx", "tp"),
        P("tp", "ctx"),
        P("ctx", "tp"),
        P(),
    )
    return jax.shard_map(
        on_device,
        mesh=mesh,
        in_specs=placed,
        out_specs=(P("ctx", "tp"), P("ctx", "tp"), P("ctx", "tp")),
        check_vma=False,
    )
```

time: 101 us -> 91.6 us (0.907)
  starting transfers between devices: 47 us -> 33.6 us
  waiting for transfers between devices: 19.4 us -> 31.5 us
  local copies, waits for them, and re-layouts: 9.01 us -> 1.66 us
  other arithmetic: 1.99 us -> 0.95 us
    ppermute x21, starting transfers between devices: 47 us -> 33.6 us  [send(): return lax.ppermute(value, AXES, route(target))]
    ppermute x21, waiting for transfers between devices: 19.4 us -> 31.5 us  [send(): return lax.ppermute(value, AXES, route(target))]
    unnamed x28 -> x12, local copies, waits for them, and re-layouts: 8.92 us -> 1.66 us
    pallas_call x7 -> x8, Pallas kernels: 17.1 us -> 22.7 us  [call(): pl.pallas_call(kernel, out_shape=out_shape, compiler_params=pltpu.Compile...]
    pallas_call x1 -> x0, Pallas kernels: 4.91 us -> none  [weights(): pl.pallas_call(weights_kernel, out_shape=(struct((2 * HD, WIDTH // 2), f3...]
    convert_element_type x1, other arithmetic: 1.99 us -> 0.95 us  [on_device(): query_grad = ((dq_own + dq_got.astype(f32)) * SCALE).astype(bf16)]
  transfers between devices with their start and end apart: 21 -> 21, of which waited for: 5 -> 9; matrix products, arithmetic and copies ran while one was open for 2% -> 1% of each run, Pallas kernels for 21% -> 22%
where the time goes in v3:
time: 91.6 us; the launch traced here: 91.3 us
  starting transfers between devices  33.6 us (37%)
  waiting for transfers between devices  31.5 us (34%)
  Pallas kernels  22.7 us (25%)
  local copies, waits for them, and re-layouts  1.66 us (2%)
  other arithmetic  0.95 us (1%)
    ppermute x21, starting transfers between devices, send(): return lax.ppermute(value, AXES, route(target))  33.6 us
    ppermute x21, waiting for transfers between devices, send(): return lax.ppermute(value, AXES, route(target))  31.5 us
    pallas_call x8, Pallas kernels, call(): pl.pallas_call(kernel, out_shape=out_shape, compiler_params=pltpu.Compile...  22.7 us
  transfers between devices with their start and end apart: 21, of which 9 were waited for; matrix products, arithmetic and copies ran while one was open for 1% of the time, Pallas kernels for 22%

profile of v3, /device:TPU:1, one launch (start us, length us, event | category | flops | bytes accessed | tf_op | source)
XLA Modules:
  0.0 91.3 jit_solution(2796714761179010302)
XLA Ops:
  0.7 1.5 %collective-permute-start.1 = (bf16[256,1024]{1,0:T(8,128)(2,1)}, bf16[256,1024]{1,0:T(8,128)(2,1)S(1)}, u32[]{:S(2)}, u32[]{:S(2)}) collective-permute-start(bf16[256,1024]{1,0:T(8,128)(2,1)} %refs_3_.3), channel_id=1, source_target_pairs={{0,8},{8,0},{16,24},{24,16},{1,9},{9,1},{17,25},{25,17},{32,40},{4... | collective-permute-start | bytes 1572872 | tf_op jit(solution)/shard_map/ppermute | solution.py:41
  2.2 1.7 %collective-permute-start = (bf16[256,1024]{1,0:T(8,128)(2,1)}, bf16[256,1024]{1,0:T(8,128)(2,1)S(1)}, u32[]{:S(2)}, u32[]{:S(2)}) collective-permute-start(bf16[256,1024]{1,0:T(8,128)(2,1)} %param.14), channel_id=1, source_target_pairs={{0,0},{8,8},{16,1},{24,9},{1,16},{9,24},{17,17},{25,25},{32,2},{40... | collective-permute-start | bytes 1572872 | tf_op jit(solution)/shard_map/ppermute | solution.py:41
  3.9 3.0 %shard_map.103 = (bf16[256,256]{1,0:T(8,128)(2,1)}, f32[24,256]{1,0:T(8,128)}) custom-call(s32[16]{0:T(128)} %lengths_ref.1, bf16[256,128]{1,0:T(8,128)(2,1)} %k_any.1, bf16[256,128]{1,0:T(8,128)(2,1)} %v_any.1, bf16[256,1024]{1,0:T(8,128)(2,1)} %refs_5_.3, bf16[256,1024]{1,0:T(8,128)(2,1)} %out_any.1, f32[8,256]{1,0:T(8,128)} %ln_any.1), custom_call_target="tpu_custom_call" | custom-call | flops 345000000 | bytes 65536 | tf_op jit(solution)/shard_map/pallas_call | solution.py:89
  6.9 4.6 %collective-permute-start.4 = (bf16[256,256]{1,0:T(8,128)(2,1)}, bf16[256,256]{1,0:T(8,128)(2,1)S(1)}, u32[]{:S(2)}, u32[]{:S(2)}) collective-permute-start(bf16[256,256]{1,0:T(8,128)(2,1)} %get-tuple-element.44.refs_0_), channel_id=1, source_target_pairs={{0,32},{8,40},{16,48},{24,56},{1,33},{9,41},{17,49},{25,57},{64,96... | collective-permute-start | bytes 393224 | tf_op jit(solution)/shard_map/ppermute | solution.py:41
  11.5 4.0 %collective-permute-start.5 = (bf16[256,256]{1,0:T(8,128)(2,1)}, bf16[256,256]{1,0:T(8,128)(2,1)S(1)}, u32[]{:S(2)}, u32[]{:S(2)}) collective-permute-start(bf16[256,256]{1,0:T(8,128)(2,1)} %get-tuple-element.44.refs_0_), channel_id=1, source_target_pairs={{0,48},{8,56},{16,32},{24,40},{1,49},{9,57},{17,33},{25,41},{64,11... | collective-permute-start | bytes 393224 | tf_op jit(solution)/shard_map/ppermute | solution.py:41
  19.3 5.3 %shard_map.104 = (f32[256,1024]{1,0:T(8,128)S(1)}, f32[256,1024]{1,0:T(8,128)S(1)}, f32[256,256]{1,0:T(8,128)S(1)}) custom-call(bf16[256,256]{1,0:T(8,128)(2,1)S(1)} %copy-done.2, f32[24,256]{1,0:T(8,128)S(1)} %copy-done.4, f32[24,256]{1,0:T(8,128)S(1)} %collective-permute-done.3.refs_2_.refs_3_, bf16[256,1024]{1,0:T(8,128)(2,1)S(1)} %copy-done.1, ...), custom_call_target="tpu_custom_call" | custom-call | flops 345000000 | bytes 65536 | tf_op jit(solution)/shard_map/pallas_call | solution.py:89
  24.7 3.4 %collective-permute-start.8 = (bf16[256,1024]{1,0:T(8,128)(2,1)S(1)}, bf16[256,1024]{1,0:T(8,128)(2,1)S(1)}, u32[]{:S(2)}, u32[]{:S(2)}) collective-permute-start(bf16[256,1024]{1,0:T(8,128)(2,1)S(1)} %collective-permute-done.refs_0_), channel_id=1, source_target_pairs={{0,6},{8,14},{16,22},{24,30},{1,7},{9,15},{17,23},{25,31},{32,38},... | collective-permute-start | bytes 1572872 | tf_op jit(solution)/shard_map/ppermute | solution.py:41
  28.1 1.9 %collective-permute-start.10 = (bf16[256,1024]{1,0:T(8,128)(2,1)S(1)}, bf16[256,1024]{1,0:T(8,128)(2,1)S(1)}, u32[]{:S(2)}, u32[]{:S(2)}) collective-permute-start(bf16[256,1024]{1,0:T(8,128)(2,1)S(1)} %collective-permute-done.refs_0_), channel_id=1, source_target_pairs={{0,1},{8,9},{16,17},{24,25},{1,0},{9,8},{17,16},{25,24},{32,33},{4... | collective-permute-start | bytes 1572872 | tf_op jit(solution)/shard_map/ppermute | solution.py:41
  30.0 1.6 %collective-permute-start.6 = (bf16[256,256]{1,0:T(8,128)(2,1)S(1)}, bf16[256,256]{1,0:T(8,128)(2,1)S(1)}, u32[]{:S(2)}, u32[]{:S(2)}) collective-permute-start(bf16[256,256]{1,0:T(8,128)(2,1)S(1)} %copy-done.3), channel_id=1, source_target_pairs={{0,16},{8,24},{1,17},{9,25},{32,48},{40,56},{33,49},{41,57},{64,80... | collective-permute-start | bytes 393224 | tf_op jit(solution)/shard_map/ppermute | solution.py:41
  31.6 6.8 %shard_map.105 = (f32[256,1024]{1,0:T(8,128)S(1)}, f32[256,1024]{1,0:T(8,128)S(1)}, bf16[512,256]{1,0:T(8,128)(2,1)S(1)}) custom-call(bf16[256,256]{1,0:T(8,128)(2,1)S(1)} %collective-permute-done.4.refs_0_, bf16[256,256]{1,0:T(8,128)(2,1)S(1)} %collective-permute-done.5.refs_1_, f32[24,256]{1,0:T(8,128)S(1)} %copy-done.5, ...), custom_call_target="tpu_custom_call" | custom-call | flops 345000000 | bytes 65536 | tf_op jit(solution)/shard_map/pallas_call | solution.py:89
  39.7 3.8 %collective-permute-done.6.refs_0_ = bf16[256,256]{1,0:T(8,128)(2,1)S(1)} collective-permute-done((bf16[256,256]{1,0:T(8,128)(2,1)S(1)}, bf16[256,256]{1,0:T(8,128)(2,1)S(1)}, u32[]{:S(2)}, u32[]{:S(2)}) %collective-permute-start.6) | collective-permute-done | bytes 131104 | tf_op jit(solution)/shard_map/ppermute | solution.py:41
  43.5 5.2 %shard_map.106 = (f32[256,1024]{1,0:T(8,128)S(1)}, bf16[256,1024]{1,0:T(8,128)(2,1)S(1)}, f32[256,256]{1,0:T(8,128)S(1)}) custom-call(bf16[256,256]{1,0:T(8,128)(2,1)S(1)} %collective-permute-done.6.refs_0_, f32[24,256]{1,0:T(8,128)S(1)} %copy-done.5, f32[24,256]{1,0:T(8,128)S(1)} %collective-permute-done.3.refs_2_.refs_3_, bf16[256,1024]{1,0:T(8,128)(2,1)S(1)} %copy-done.1, ...), custom_call_target="tpu_custom_call" | custom-call | flops 1724999936 | bytes 65536 | tf_op jit(solution)/shard_map/pallas_call | solution.py:89
  48.7 1.6 %collective-permute-start.12 = (bf16[256,1024]{1,0:T(8,128)(2,1)S(1)}, bf16[256,1024]{1,0:T(8,128)(2,1)S(1)}, u32[]{:S(2)}, u32[]{:S(2)}) collective-permute-start(bf16[256,1024]{1,0:T(8,128)(2,1)S(1)} %get-tuple-element.67), channel_id=1, source_target_pairs={{0,8},{8,0},{16,24},{24,16},{1,9},{9,1},{17,25},{25,17},{32,40},{4... | collective-permute-start | bytes 1572872 | tf_op jit(solution)/shard_map/ppermute | solution.py:41
  50.3 2.7 %collective-permute-start.13 = (bf16[256,1024]{1,0:T(8,128)(2,1)S(1)}, bf16[256,1024]{1,0:T(8,128)(2,1)S(1)}, u32[]{:S(2)}, u32[]{:S(2)}) collective-permute-start(bf16[256,1024]{1,0:T(8,128)(2,1)S(1)} %collective-permute-done.8.refs_2_), channel_id=1, source_target_pairs={{0,6},{8,14},{16,22},{24,30},{1,7},{9,15},{17,23},{25,31},{32,38},... | collective-permute-start | bytes 1572872 | tf_op jit(solution)/shard_map/ppermute | solution.py:41
  53.1 2.3 %collective-permute-start.11 = (bf16[512,256]{1,0:T(8,128)(2,1)S(1)}, bf16[512,256]{1,0:T(8,128)(2,1)S(1)}, u32[]{:S(2)}, u32[]{:S(2)}) collective-permute-start(bf16[512,256]{1,0:T(8,128)(2,1)S(1)} %get-tuple-element.65), channel_id=1, source_target_pairs={{0,16},{8,24},{16,0},{24,8},{1,17},{9,25},{17,1},{25,9},{32,48},{4... | collective-permute-start | bytes 786440 | tf_op jit(solution)/shard_map/ppermute | solution.py:41
  56.3 5.4 %collective-permute-done.11.got_ref = bf16[512,256]{1,0:T(8,128)(2,1)S(1)} collective-permute-done((bf16[512,256]{1,0:T(8,128)(2,1)S(1)}, bf16[512,256]{1,0:T(8,128)(2,1)S(1)}, u32[]{:S(2)}, u32[]{:S(2)}) %collective-permute-start.11) | collective-permute-done | bytes 262176 | tf_op jit(solution)/shard_map/ppermute | solution.py:41
  61.9 2.4 %collective-permute-done.13.refs_4_ = bf16[256,1024]{1,0:T(8,128)(2,1)S(1)} collective-permute-done((bf16[256,1024]{1,0:T(8,128)(2,1)S(1)}, bf16[256,1024]{1,0:T(8,128)(2,1)S(1)}, u32[]{:S(2)}, u32[]{:S(2)}) %collective-permute-start.13) | collective-permute-done | bytes 524320 | tf_op jit(solution)/shard_map/ppermute | solution.py:41
  64.3 3.1 %collective-permute-done.14.refs_7_ = bf16[256,1024]{1,0:T(8,128)(2,1)S(1)} collective-permute-done((bf16[256,1024]{1,0:T(8,128)(2,1)S(1)}, bf16[256,1024]{1,0:T(8,128)(2,1)S(1)}, u32[]{:S(2)}, u32[]{:S(2)}) %collective-permute-start.14) | collective-permute-done | bytes 524320 | tf_op jit(solution)/shard_map/ppermute | solution.py:41
  68.7 3.1 %collective-permute-start.17 = (bf16[512,256]{1,0:T(8,128)(2,1)S(1)}, bf16[512,256]{1,0:T(8,128)(2,1)S(1)}, u32[]{:S(2)}, u32[]{:S(2)}) collective-permute-start(bf16[512,256]{1,0:T(8,128)(2,1)S(1)} %shard_map.108.refs_8_), channel_id=1, source_target_pairs={{0,96},{8,104},{16,112},{24,120},{1,97},{9,105},{17,113},{25,121},... | collective-permute-start | bytes 786440 | tf_op jit(solution)/shard_map/ppermute | solution.py:41
  72.4 4.9 %collective-permute-done.17.refs_9_ = bf16[512,256]{1,0:T(8,128)(2,1)S(1)} collective-permute-done((bf16[512,256]{1,0:T(8,128)(2,1)S(1)}, bf16[512,256]{1,0:T(8,128)(2,1)S(1)}, u32[]{:S(2)}, u32[]{:S(2)}) %collective-permute-start.17) | collective-permute-done | bytes 262176 | tf_op jit(solution)/shard_map/ppermute | solution.py:41
  77.3 2.0 %collective-permute-done.18.refs_10_ = bf16[512,256]{1,0:T(8,128)(2,1)S(1)} collective-permute-done((bf16[512,256]{1,0:T(8,128)(2,1)S(1)}, bf16[512,256]{1,0:T(8,128)(2,1)S(1)}, u32[]{:S(2)}, u32[]{:S(2)}) %collective-permute-start.18) | collective-permute-done | bytes 262176 | tf_op jit(solution)/shard_map/ppermute | solution.py:41
  79.2 7.3 %collective-permute-done.19.refs_11_ = bf16[512,256]{1,0:T(8,128)(2,1)S(1)} collective-permute-done((bf16[512,256]{1,0:T(8,128)(2,1)S(1)}, bf16[512,256]{1,0:T(8,128)(2,1)S(1)}, u32[]{:S(2)}, u32[]{:S(2)}) %collective-permute-start.19) | collective-permute-done | bytes 262176 | tf_op jit(solution)/shard_map/ppermute | solution.py:41
  86.5 1.3 %shard_map.109 = (f32[256,512]{1,0:T(8,128)S(1)}, f32[256,512]{1,0:T(8,128)S(1)}) custom-call(bf16[256,1024]{1,0:T(8,128)(2,1)S(1)} %collective-permute-done.refs_0_, bf16[256,1024]{1,0:T(8,128)(2,1)S(1)} %collective-permute-done.10.refs_1_, bf16[256,1024]{1,0:T(8,128)(2,1)S(1)} %collective-permute-done.8.refs_2_, ...), custom_call_target="tpu_custom_call" | custom-call | flops 11500000 | bytes 65536 | tf_op jit(solution)/shard_map/pallas_call | solution.py:89
  88.8 1.5 %collective-permute-done.20.got_ref = f32[256,512]{1,0:T(8,128)S(1)} collective-permute-done((f32[256,512]{1,0:T(8,128)S(1)}, f32[256,512]{1,0:T(8,128)S(1)}, u32[]{:S(2)}, u32[]{:S(2)}) %collective-permute-start.20) | collective-permute-done | bytes 524320 | tf_op jit(solution)/shard_map/ppermute | solution.py:41
  (39 shorter events, 10.1 us)
Async XLA Ops:
  0.6 17.0 %copy-start.1 = (bf16[256,1024]{1,0:T(8,128)(2,1)S(1)}, bf16[256,1024]{1,0:T(8,128)(2,1)}, u32[]{:S(2)}) copy-start(bf16[256,1024]{1,0:T(8,128)(2,1)} %refs_3_.3) | copy-start | bytes 1572868
  0.6 17.0 %copy-start = (bf16[256,1024]{1,0:T(8,128)(2,1)S(1)}, bf16[256,1024]{1,0:T(8,128)(2,1)}, u32[]{:S(2)}) copy-start(bf16[256,1024]{1,0:T(8,128)(2,1)} %refs_5_.3) | copy-start | bytes 1572868
  0.7 6.3 %collective-permute-start.1 = (bf16[256,1024]{1,0:T(8,128)(2,1)}, bf16[256,1024]{1,0:T(8,128)(2,1)S(1)}, u32[]{:S(2)}, u32[]{:S(2)}) collective-permute-start(bf16[256,1024]{1,0:T(8,128)(2,1)} %refs_3_.3), channel_id=1, source_target_pairs={{0,8},{8,0},{16,24},{24,16},{1,9},{9,1},{17,25},{25,17},{32,40},{4... | collective-permute-start | bytes 1572872 | tf_op jit(solution)/shard_map/ppermute | solution.py:41
  2.2 4.8 %collective-permute-start.2 = (bf16[256,1024]{1,0:T(8,128)(2,1)}, bf16[256,1024]{1,0:T(8,128)(2,1)S(1)}, u32[]{:S(2)}, u32[]{:S(2)}) collective-permute-start(bf16[256,1024]{1,0:T(8,128)(2,1)} %refs_5_.3), channel_id=1, source_target_pairs={{0,8},{8,0},{16,24},{24,16},{1,9},{9,1},{17,25},{25,17},{32,40},{4... | collective-permute-start | bytes 1572872 | tf_op jit(solution)/shard_map/ppermute | solution.py:41
  2.2 22.4 %collective-permute-start = (bf16[256,1024]{1,0:T(8,128)(2,1)}, bf16[256,1024]{1,0:T(8,128)(2,1)S(1)}, u32[]{:S(2)}, u32[]{:S(2)}) collective-permute-start(bf16[256,1024]{1,0:T(8,128)(2,1)} %param.14), channel_id=1, source_target_pairs={{0,0},{8,8},{16,1},{24,9},{1,16},{9,24},{17,17},{25,25},{32,2},{40... | collective-permute-start | bytes 1572872 | tf_op jit(solution)/shard_map/ppermute | solution.py:41
  6.9 17.7 %collective-permute-start.4 = (bf16[256,256]{1,0:T(8,128)(2,1)}, bf16[256,256]{1,0:T(8,128)(2,1)S(1)}, u32[]{:S(2)}, u32[]{:S(2)}) collective-permute-start(bf16[256,256]{1,0:T(8,128)(2,1)} %get-tuple-element.44.refs_0_), channel_id=1, source_target_pairs={{0,32},{8,40},{16,48},{24,56},{1,33},{9,41},{17,49},{25,57},{64,96... | collective-permute-start | bytes 393224 | tf_op jit(solution)/shard_map/ppermute | solution.py:41
  11.5 13.1 %collective-permute-start.5 = (bf16[256,256]{1,0:T(8,128)(2,1)}, bf16[256,256]{1,0:T(8,128)(2,1)S(1)}, u32[]{:S(2)}, u32[]{:S(2)}) collective-permute-start(bf16[256,256]{1,0:T(8,128)(2,1)} %get-tuple-element.44.refs_0_), channel_id=1, source_target_pairs={{0,48},{8,56},{16,32},{24,40},{1,49},{9,57},{17,33},{25,41},{64,11... | collective-permute-start | bytes 393224 | tf_op jit(solution)/shard_map/ppermute | solution.py:41
  15.6 2.1 %collective-permute-start.3 = (f32[24,256]{1,0:T(8,128)}, f32[24,256]{1,0:T(8,128)S(1)}, u32[]{:S(2)}, u32[]{:S(2)}) collective-permute-start(f32[24,256]{1,0:T(8,128)} %get-tuple-element.45.refs_1_.refs_2_), channel_id=1, source_target_pairs={{0,8},{8,0},{16,24},{24,16},{1,9},{9,1},{17,25},{25,17},{32,40},{4... | collective-permute-start | bytes 73736 | tf_op jit(solution)/shard_map/ppermute | solution.py:41
  19.3 12.3 %copy-start.5 = (f32[24,256]{1,0:T(8,128)S(1)}, f32[24,256]{1,0:T(8,128)}, u32[]{:S(2)}) copy-start(f32[24,256]{1,0:T(8,128)} %get-tuple-element.45.refs_1_.refs_2_) | copy-start | bytes 73732
  24.7 24.0 %collective-permute-start.8 = (bf16[256,1024]{1,0:T(8,128)(2,1)S(1)}, bf16[256,1024]{1,0:T(8,128)(2,1)S(1)}, u32[]{:S(2)}, u32[]{:S(2)}) collective-permute-start(bf16[256,1024]{1,0:T(8,128)(2,1)S(1)} %collective-permute-done.refs_0_), channel_id=1, source_target_pairs={{0,6},{8,14},{16,22},{24,30},{1,7},{9,15},{17,23},{25,31},{32,38},... | collective-permute-start | bytes 1572872 | tf_op jit(solution)/shard_map/ppermute | solution.py:41
  28.0 20.7 %collective-permute-start.9 = (bf16[256,1024]{1,0:T(8,128)(2,1)S(1)}, bf16[256,1024]{1,0:T(8,128)(2,1)S(1)}, u32[]{:S(2)}, u32[]{:S(2)}) collective-permute-start(bf16[256,1024]{1,0:T(8,128)(2,1)S(1)} %collective-permute-done.refs_0_), channel_id=1, source_target_pairs={{0,2},{8,10},{16,18},{24,26},{1,3},{9,11},{17,19},{25,27},{32,34},... | collective-permute-start | bytes 1572872 | tf_op jit(solution)/shard_map/ppermute | solution.py:41
  28.1 20.7 %collective-permute-start.10 = (bf16[256,1024]{1,0:T(8,128)(2,1)S(1)}, bf16[256,1024]{1,0:T(8,128)(2,1)S(1)}, u32[]{:S(2)}, u32[]{:S(2)}) collective-permute-start(bf16[256,1024]{1,0:T(8,128)(2,1)S(1)} %collective-permute-done.refs_0_), channel_id=1, source_target_pairs={{0,1},{8,9},{16,17},{24,25},{1,0},{9,8},{17,16},{25,24},{32,33},{4... | collective-permute-start | bytes 1572872 | tf_op jit(solution)/shard_map/ppermute | solution.py:41
  30.0 13.5 %collective-permute-start.6 = (bf16[256,256]{1,0:T(8,128)(2,1)S(1)}, bf16[256,256]{1,0:T(8,128)(2,1)S(1)}, u32[]{:S(2)}, u32[]{:S(2)}) collective-permute-start(bf16[256,256]{1,0:T(8,128)(2,1)S(1)} %copy-done.3), channel_id=1, source_target_pairs={{0,16},{8,24},{1,17},{9,25},{32,48},{40,56},{33,49},{41,57},{64,80... | collective-permute-start | bytes 393224 | tf_op jit(solution)/shard_map/ppermute | solution.py:41
  38.4 10.3 %collective-permute-start.7 = (bf16[512,256]{1,0:T(8,128)(2,1)S(1)}, bf16[512,256]{1,0:T(8,128)(2,1)S(1)}, u32[]{:S(2)}, u32[]{:S(2)}) collective-permute-start(bf16[512,256]{1,0:T(8,128)(2,1)S(1)} %get-tuple-element.61), channel_id=1, source_target_pairs={{32,0},{40,8},{48,16},{56,24},{33,1},{41,9},{49,17},{57,25},{96,64... | collective-permute-start | bytes 786440 | tf_op jit(solution)/shard_map/ppermute | solution.py:41
  48.7 6.6 %collective-permute-start.12 = (bf16[256,1024]{1,0:T(8,128)(2,1)S(1)}, bf16[256,1024]{1,0:T(8,128)(2,1)S(1)}, u32[]{:S(2)}, u32[]{:S(2)}) collective-permute-start(bf16[256,1024]{1,0:T(8,128)(2,1)S(1)} %get-tuple-element.67), channel_id=1, source_target_pairs={{0,8},{8,0},{16,24},{24,16},{1,9},{9,1},{17,25},{25,17},{32,40},{4... | collective-permute-start | bytes 1572872 | tf_op jit(solution)/shard_map/ppermute | solution.py:41
  50.3 14.0 %collective-permute-start.13 = (bf16[256,1024]{1,0:T(8,128)(2,1)S(1)}, bf16[256,1024]{1,0:T(8,128)(2,1)S(1)}, u32[]{:S(2)}, u32[]{:S(2)}) collective-permute-start(bf16[256,1024]{1,0:T(8,128)(2,1)S(1)} %collective-permute-done.8.refs_2_), channel_id=1, source_target_pairs={{0,6},{8,14},{16,22},{24,30},{1,7},{9,15},{17,23},{25,31},{32,38},... | collective-permute-start | bytes 1572872 | tf_op jit(solution)/shard_map/ppermute | solution.py:41
  53.0 14.4 %collective-permute-start.14 = (bf16[256,1024]{1,0:T(8,128)(2,1)S(1)}, bf16[256,1024]{1,0:T(8,128)(2,1)S(1)}, u32[]{:S(2)}, u32[]{:S(2)}) collective-permute-start(bf16[256,1024]{1,0:T(8,128)(2,1)S(1)} %collective-permute-done.10.refs_1_), channel_id=1, source_target_pairs={{0,2},{8,10},{16,18},{24,26},{1,3},{9,11},{17,19},{25,27},{32,34},... | collective-permute-start | bytes 1572872 | tf_op jit(solution)/shard_map/ppermute | solution.py:41
  53.1 8.7 %collective-permute-start.11 = (bf16[512,256]{1,0:T(8,128)(2,1)S(1)}, bf16[512,256]{1,0:T(8,128)(2,1)S(1)}, u32[]{:S(2)}, u32[]{:S(2)}) collective-permute-start(bf16[512,256]{1,0:T(8,128)(2,1)S(1)} %get-tuple-element.65), channel_id=1, source_target_pairs={{0,16},{8,24},{16,0},{24,8},{1,17},{9,25},{17,1},{25,9},{32,48},{4... | collective-permute-start | bytes 786440 | tf_op jit(solution)/shard_map/ppermute | solution.py:41
  67.4 19.1 %collective-permute-start.15 = (bf16[256,1024]{1,0:T(8,128)(2,1)S(1)}, bf16[256,1024]{1,0:T(8,128)(2,1)S(1)}, u32[]{:S(2)}, u32[]{:S(2)}) collective-permute-start(bf16[256,1024]{1,0:T(8,128)(2,1)S(1)} %collective-permute-done.10.refs_1_), channel_id=1, source_target_pairs={{0,6},{8,14},{16,22},{24,30},{1,7},{9,15},{17,23},{25,31},{32,38},... | collective-permute-start | bytes 1572872 | tf_op jit(solution)/shard_map/ppermute | solution.py:41
  67.7 18.8 %collective-permute-start.16 = (bf16[256,1024]{1,0:T(8,128)(2,1)S(1)}, bf16[256,1024]{1,0:T(8,128)(2,1)S(1)}, u32[]{:S(2)}, u32[]{:S(2)}) collective-permute-start(bf16[256,1024]{1,0:T(8,128)(2,1)S(1)} %collective-permute-done.13.refs_4_), channel_id=1, source_target_pairs={{0,1},{8,9},{16,17},{24,25},{1,0},{9,8},{17,16},{25,24},{32,33},{4... | collective-permute-start | bytes 1572872 | tf_op jit(solution)/shard_map/ppermute | solution.py:41
  68.7 8.5 %collective-permute-start.17 = (bf16[512,256]{1,0:T(8,128)(2,1)S(1)}, bf16[512,256]{1,0:T(8,128)(2,1)S(1)}, u32[]{:S(2)}, u32[]{:S(2)}) collective-permute-start(bf16[512,256]{1,0:T(8,128)(2,1)S(1)} %shard_map.108.refs_8_), channel_id=1, source_target_pairs={{0,96},{8,104},{16,112},{24,120},{1,97},{9,105},{17,113},{25,121},... | collective-permute-start | bytes 786440 | tf_op jit(solution)/shard_map/ppermute | solution.py:41
  71.8 7.4 %collective-permute-start.18 = (bf16[512,256]{1,0:T(8,128)(2,1)S(1)}, bf16[512,256]{1,0:T(8,128)(2,1)S(1)}, u32[]{:S(2)}, u32[]{:S(2)}) collective-permute-start(bf16[512,256]{1,0:T(8,128)(2,1)S(1)} %shard_map.108.refs_8_), channel_id=1, source_target_pairs={{0,64},{8,72},{16,80},{24,88},{1,65},{9,73},{17,81},{25,89},{32,96... | collective-permute-start | bytes 786440 | tf_op jit(solution)/shard_map/ppermute | solution.py:41
  71.8 14.7 %collective-permute-start.19 = (bf16[512,256]{1,0:T(8,128)(2,1)S(1)}, bf16[512,256]{1,0:T(8,128)(2,1)S(1)}, u32[]{:S(2)}, u32[]{:S(2)}) collective-permute-start(bf16[512,256]{1,0:T(8,128)(2,1)S(1)} %shard_map.108.refs_8_), channel_id=1, source_target_pairs={{0,32},{8,40},{16,48},{24,56},{1,33},{9,41},{17,49},{25,57},{32,64... | collective-permute-start | bytes 786440 | tf_op jit(solution)/shard_map/ppermute | solution.py:41
  87.9 2.5 %collective-permute-start.20 = (f32[256,512]{1,0:T(8,128)S(1)}, f32[256,512]{1,0:T(8,128)S(1)}, u32[]{:S(2)}, u32[]{:S(2)}) collective-permute-start(f32[256,512]{1,0:T(8,128)S(1)} %get-tuple-element.78), channel_id=1, source_target_pairs={{0,8},{8,0},{16,24},{24,16},{1,9},{9,1},{17,25},{25,17},{32,40},{4... | collective-permute-start | bytes 1572872 | tf_op jit(solution)/shard_map/ppermute | solution.py:41
  (3 other events, 12.3 us)

commit v4 on v3

--- a/solution.py
+++ b/solution.py
@@ -97,6 +97,20 @@
 
 def struct(shape, dtype):
     return jax.ShapeDtypeStruct(shape, dtype)
+
+
+def arrived_kernel(*refs):
+    refs[-1][...] = jnp.zeros_like(refs[-1])
+
+
+def arrived(arrays, micros):
+    return call(
+        arrived_kernel,
+        struct((8, 128), f32),
+        arrays,
+        micros=micros,
+        in_specs=[pl.BlockSpec(memory_space=pl.ANY)] * len(arrays),
+    )
 
 
 def prepare_kernel(lengths_ref, k_any, v_any, do_any, out_any, ln_any, kv_ref, aux_ref, do_ref, out_ref, sems):
@@ -136,7 +150,7 @@
         (struct((ROWS, 2 * HD), bf16), struct((3 * HEADS, ROWS), f32)),
         (doc_lengths, k, v, do, out, ln),
         in_specs=[pl.BlockSpec(memory_space=pltpu.SMEM)] + [pl.BlockSpec(memory_space=pltpu.HBM)] * 5,
-        megabytes=60,
+        megabytes=56,
         micros=0.3,
         scratch_shapes=[pltpu.VMEM((ROWS, WIDTH), bf16)] * 2 + [pltpu.SemaphoreType.DMA((5,))],
     )
@@ -216,18 +230,18 @@
         mine = slice(half * ROWS, (half + 1) * ROWS)
         its = slice((1 - half) * ROWS, (2 - half) * ROWS)
         total = sum_ref[mine, :] + got_ref[its, :].astype(f32)
-        d_ref[half * 2 * HD : half * 2 * HD + HD, :] = (total[:, :HD] * SCALE).T.astype(bf16)
-        d_ref[half * 2 * HD + HD : (half + 1) * 2 * HD, :] = total[:, HD:].T.astype(bf16)
+        k_grad = (total[:, :HD] * SCALE).T.astype(bf16)
+        v_grad = total[:, HD:].T.astype(bf16)
+        for copy in range(4):
+            d_ref[copy, half * 2 * HD : half * 2 * HD + HD, :] = k_grad
+            d_ref[copy, half * 2 * HD + HD : (half + 1) * 2 * HD, :] = v_grad
 
 
 def weights_kernel(*refs):
-    l_refs, d_refs, (sent_ref, kept_ref, d_all) = refs[:8], refs[8:12], refs[12:]
+    l_refs, (d_ref, _, sent_ref, kept_ref) = refs[:8], refs[8:]
     me, tp = lax.axis_index("ctx"), lax.axis_index("tp")
     core, zl, y = me % 2, (me // 2) % 2, me // 4
     x, zh = tp // 2, tp % 2
-    for r in range(4):
-        for half in range(2):
-            d_all[r * 2 + half] = d_refs[r][half * 2 * HD : (half + 1) * 2 * HD, :]
     half_width = WIDTH // 2
     for out_ref, whose in ((sent_ref, 1 - core), (kept_ref, core)):
         for t in range(2):
@@ -236,18 +250,17 @@
             total = None
             for s in range(4):
                 for j in range(2):
-                    slot = ((x + s + 2 * y) % 4) * 2 + ((zh ^ j) ^ zl)
-                    term = nn(d_all[slot], l_refs[s * 2 + j][:, cols])
+                    rows = pl.ds(pl.multiple_of(((zh ^ j) ^ zl) * 2 * HD, 2 * HD), 2 * HD)
+                    term = nn(d_ref[(x + s + 3 * y) % 4, rows, :], l_refs[s * 2 + j][:, cols])
                     total = term if total is None else total + term
             out_ref[:, t * tile : (t + 1) * tile] = total
 
 
-def weights(l_blocks, d_blocks):
+def weights(l_blocks, d_blocks, ready):
     return call(
         weights_kernel,
         (struct((2 * HD, WIDTH // 2), f32),) * 2,
-        (*l_blocks, *d_blocks),
-        scratch_shapes=[pltpu.VMEM((8, 2 * HD, ROWS), bf16)],
+        (*l_blocks, d_blocks, ready),
     )
 
 
@@ -269,31 +282,32 @@
 
     behind, ahead, across = shifted(dx=-1), shifted(dx=1), shifted(dz=2)
     *dqs, dkv_own = attention((0,), (kv,), aux, q, do, None, (f32, f32), f32, 0.3)
-    l_own, dkv_own, kv_y, kv_far, *dqs = together(l_own, dkv_own, kv_y, kv_far, *dqs)
-    own_1, own_3, other_0 = send(l_own, behind), send(l_own, ahead), send(l_own, across)
+    l_own, dkv_own, kv_y, kv_far, kv_zl, *dqs = together(l_own, dkv_own, kv_y, kv_far, kv_zl, *dqs)
+    own_1, own_3, other_0 = (send(l_own, t) for t in (behind, ahead, across))
 
     *dqs, dkv_far = attention((4, 6), (kv_y, kv_far), aux, q, do, dqs, (f32, f32), bf16, 0.3)
     got_far = send(dkv_far, within_half(2, False))
     dq_own, dq_par, dkv_zl = attention((2,), (kv_zl,), aux, q, do, dqs, (f32, bf16), f32, 1.5)
-    dq_own, dq_par, dkv_zl, got_far, own_1, own_3, other_0 = together(
-        dq_own, dq_par, dkv_zl, got_far, own_1, own_3, other_0
-    )
-    own_2, other_3 = send(own_1, behind), send(other_0, ahead)
-
+    dq_own, dq_par, dkv_zl, got_far, l_own, own_1, own_3, other_0 = together(
+        dq_own, dq_par, dkv_zl, got_far, l_own, own_1, own_3, other_0
+    )
     dq_got = send(dq_par, other_core)
     query_grad = ((dq_own + dq_got.astype(f32)) * SCALE).astype(bf16)
 
     pair = (2 * ROWS, 2 * HD)
     dkv, dkv_low = call(add_kernel, (struct(pair, f32), struct(pair, bf16)), (dkv_own, dkv_zl, got_far))
     got_zl = send(dkv_low, other_zl)
-    got_zl, query_grad = together(got_zl, query_grad)
-    d_own = call(close_kernel, struct((4 * HD, ROWS), bf16), (dkv, got_zl))
-    own_2, other_3, other_0, _ = together(own_2, other_3, other_0, d_own)
-    other_1, other_2 = send(other_0, behind), send(own_2, across)
-    d_blocks = (d_own, *(send(d_own, shifted(dy=-dy)) for dy in (1, 2, 3)))
-
+    other_0, own_1, _ = together(other_0, own_1, dkv_low)
+    other_3, own_2, other_1 = send(other_0, ahead), send(own_1, behind), send(other_0, behind)
+    got_zl, query_grad, other_3 = together(got_zl, query_grad, other_3)
+    d_copies = call(close_kernel, struct((4, 4 * HD, ROWS), bf16), (dkv, got_zl))
+    columns = [[y * 4 + rest for y in range(4)] for rest in range(4)]
+    d_blocks = lax.all_to_all(d_copies, "ctx", 0, 0, axis_index_groups=columns)
+
+    other_2 = send(other_3, ahead)
+    ready = arrived((own_2, other_1, other_2), 8)
     l_blocks = (l_own, other_0, own_1, other_1, own_2, other_2, own_3, other_3)
-    sent, kept = weights(l_blocks, d_blocks)
+    sent, kept = weights(l_blocks, d_blocks, ready)
     key_weight, value_weight = call(
         finish_kernel, (struct((WIDTH // 2, HD), f32),) * 2, (kept, send(sent, other_core))
     )

time: 91.6 us -> 91.4 us (level)
  waiting for transfers between devices: 31.5 us -> 28.9 us
  Pallas kernels: 22.7 us -> 25.2 us
    ppermute x21 -> x18, waiting for transfers between devices: 31.5 us -> 24.2 us  [send(): return lax.ppermute(value, AXES, route(target))]
    all_to_all x0 -> x1, waiting for transfers between devices: none -> 4.7 us  [on_device(): d_blocks = lax.all_to_all(d_copies, 'ctx', 0, 0, axis_index_groups=columns)]
    ppermute x21 -> x18, starting transfers between devices: 33.6 us -> 30 us  [send(): return lax.ppermute(value, AXES, route(target))]
    all_to_all x0 -> x1, starting transfers between devices: none -> 3.51 us  [on_device(): d_blocks = lax.all_to_all(d_copies, 'ctx', 0, 0, axis_index_groups=columns)]
    pallas_call x8 -> x9, Pallas kernels: 22.7 us -> 25.2 us  [call(): pl.pallas_call(kernel, out_shape=out_shape, compiler_params=pltpu.Compile...]
  transfers between devices with their start and end apart: 21 -> 19, of which waited for: 9 -> 8; matrix products, arithmetic and copies ran while one was open for 1% -> 1% of each run, Pallas kernels for 22% -> 24%
where the time goes in v4:
time: 91.4 us; the launch traced here: 91 us
  starting transfers between devices  33.5 us (37%)
  waiting for transfers between devices  28.9 us (32%)
  Pallas kernels  25.2 us (28%)
  local copies, waits for them, and re-layouts  1.66 us (2%)
  other arithmetic  0.95 us (1%)
    ppermute x18, starting transfers between devices, send(): return lax.ppermute(value, AXES, route(target))  30 us
    pallas_call x9, Pallas kernels, call(): pl.pallas_call(kernel, out_shape=out_shape, compiler_params=pltpu.Compile...  25.2 us
    ppermute x18, waiting for transfers between devices, send(): return lax.ppermute(value, AXES, route(target))  24.2 us
    all_to_all x1, waiting for transfers between devices, on_device(): d_blocks = lax.all_to_all(d_copies, 'ctx', 0, 0, axis_index_groups=columns)  4.7 us
    all_to_all x1, starting transfers between devices, on_device(): d_blocks = lax.all_to_all(d_copies, 'ctx', 0, 0, axis_index_groups=columns)  3.51 us
  transfers between devices with their start and end apart: 19, of which 8 were waited for; matrix products, arithmetic and copies ran while one was open for 1% of the time, Pallas kernels for 24%

profile of v4, /device:TPU:1, one launch (start us, length us, event | category | flops | bytes accessed | tf_op | source)
XLA Modules:
  0.0 91.0 jit_solution(13580408997298379608)
XLA Ops:
  0.7 1.5 %collective-permute-start.1 = (bf16[256,1024]{1,0:T(8,128)(2,1)}, bf16[256,1024]{1,0:T(8,128)(2,1)S(1)}, u32[]{:S(2)}, u32[]{:S(2)}) collective-permute-start(bf16[256,1024]{1,0:T(8,128)(2,1)} %refs_3_.3), channel_id=1, source_target_pairs={{0,8},{8,0},{16,24},{24,16},{1,9},{9,1},{17,25},{25,17},{32,40},{4... | collective-permute-start | bytes 1572872 | tf_op jit(solution)/shard_map/ppermute | solution.py:41
  2.2 1.7 %collective-permute-start = (bf16[256,1024]{1,0:T(8,128)(2,1)}, bf16[256,1024]{1,0:T(8,128)(2,1)S(1)}, u32[]{:S(2)}, u32[]{:S(2)}) collective-permute-start(bf16[256,1024]{1,0:T(8,128)(2,1)} %param.14), channel_id=1, source_target_pairs={{0,0},{8,8},{16,1},{24,9},{1,16},{9,24},{17,17},{25,25},{32,2},{40... | collective-permute-start | bytes 1572872 | tf_op jit(solution)/shard_map/ppermute | solution.py:41
  3.9 3.0 %shard_map.103 = (bf16[256,256]{1,0:T(8,128)(2,1)}, f32[24,256]{1,0:T(8,128)}) custom-call(s32[16]{0:T(128)} %lengths_ref.1, bf16[256,128]{1,0:T(8,128)(2,1)} %k_any.1, bf16[256,128]{1,0:T(8,128)(2,1)} %v_any.1, bf16[256,1024]{1,0:T(8,128)(2,1)} %refs_5_.3, bf16[256,1024]{1,0:T(8,128)(2,1)} %out_any.1, f32[8,256]{1,0:T(8,128)} %ln_any.1), custom_call_target="tpu_custom_call" | custom-call | flops 345000000 | bytes 65536 | tf_op jit(solution)/shard_map/pallas_call | solution.py:89
  6.9 4.6 %collective-permute-start.4 = (bf16[256,256]{1,0:T(8,128)(2,1)}, bf16[256,256]{1,0:T(8,128)(2,1)S(1)}, u32[]{:S(2)}, u32[]{:S(2)}) collective-permute-start(bf16[256,256]{1,0:T(8,128)(2,1)} %get-tuple-element.46.refs_0_), channel_id=1, source_target_pairs={{0,32},{8,40},{16,48},{24,56},{1,33},{9,41},{17,49},{25,57},{64,96... | collective-permute-start | bytes 393224 | tf_op jit(solution)/shard_map/ppermute | solution.py:41
  11.5 4.0 %collective-permute-start.5 = (bf16[256,256]{1,0:T(8,128)(2,1)}, bf16[256,256]{1,0:T(8,128)(2,1)S(1)}, u32[]{:S(2)}, u32[]{:S(2)}) collective-permute-start(bf16[256,256]{1,0:T(8,128)(2,1)} %get-tuple-element.46.refs_0_), channel_id=1, source_target_pairs={{0,48},{8,56},{16,32},{24,40},{1,49},{9,57},{17,33},{25,41},{64,11... | collective-permute-start | bytes 393224 | tf_op jit(solution)/shard_map/ppermute | solution.py:41
  15.6 2.2 %collective-permute-start.6 = (bf16[256,256]{1,0:T(8,128)(2,1)}, bf16[256,256]{1,0:T(8,128)(2,1)S(1)}, u32[]{:S(2)}, u32[]{:S(2)}) collective-permute-start(bf16[256,256]{1,0:T(8,128)(2,1)} %get-tuple-element.46.refs_0_), channel_id=1, source_target_pairs={{0,16},{8,24},{1,17},{9,25},{32,48},{40,56},{33,49},{41,57},{64,80... | collective-permute-start | bytes 393224 | tf_op jit(solution)/shard_map/ppermute | solution.py:41
  17.8 1.3 %collective-permute-start.3 = (f32[24,256]{1,0:T(8,128)}, f32[24,256]{1,0:T(8,128)S(1)}, u32[]{:S(2)}, u32[]{:S(2)}) collective-permute-start(f32[24,256]{1,0:T(8,128)} %get-tuple-element.47.refs_1_.refs_2_), channel_id=1, source_target_pairs={{0,8},{8,0},{16,24},{24,16},{1,9},{9,1},{17,25},{25,17},{32,40},{4... | collective-permute-start | bytes 73736 | tf_op jit(solution)/shard_map/ppermute | solution.py:41
  21.8 5.3 %shard_map.104 = (f32[256,1024]{1,0:T(8,128)S(1)}, f32[256,1024]{1,0:T(8,128)S(1)}, f32[256,256]{1,0:T(8,128)S(1)}) custom-call(bf16[256,256]{1,0:T(8,128)(2,1)S(1)} %copy-done.2, f32[24,256]{1,0:T(8,128)S(1)} %copy-done.3, f32[24,256]{1,0:T(8,128)S(1)} %collective-permute-done.3.refs_2_.refs_3_, bf16[256,1024]{1,0:T(8,128)(2,1)S(1)} %copy-done.1, ...), custom_call_target="tpu_custom_call" | custom-call | flops 345000000 | bytes 65536 | tf_op jit(solution)/shard_map/pallas_call | solution.py:89
  27.2 3.4 %collective-permute-start.8 = (bf16[256,1024]{1,0:T(8,128)(2,1)S(1)}, bf16[256,1024]{1,0:T(8,128)(2,1)S(1)}, u32[]{:S(2)}, u32[]{:S(2)}) collective-permute-start(bf16[256,1024]{1,0:T(8,128)(2,1)S(1)} %collective-permute-done.refs_0_), channel_id=1, source_target_pairs={{0,6},{8,14},{16,22},{24,30},{1,7},{9,15},{17,23},{25,31},{32,38},... | collective-permute-start | bytes 1572872 | tf_op jit(solution)/shard_map/ppermute | solution.py:41
  30.6 2.0 %collective-permute-start.10 = (bf16[256,1024]{1,0:T(8,128)(2,1)S(1)}, bf16[256,1024]{1,0:T(8,128)(2,1)S(1)}, u32[]{:S(2)}, u32[]{:S(2)}) collective-permute-start(bf16[256,1024]{1,0:T(8,128)(2,1)S(1)} %collective-permute-done.refs_0_), channel_id=1, source_target_pairs={{0,1},{8,9},{16,17},{24,25},{1,0},{9,8},{17,16},{25,24},{32,33},{4... | collective-permute-start | bytes 1572872 | tf_op jit(solution)/shard_map/ppermute | solution.py:41
  32.5 6.8 %shard_map.105 = (f32[256,1024]{1,0:T(8,128)S(1)}, f32[256,1024]{1,0:T(8,128)S(1)}, bf16[512,256]{1,0:T(8,128)(2,1)S(1)}) custom-call(bf16[256,256]{1,0:T(8,128)(2,1)S(1)} %collective-permute-done.4.refs_0_, bf16[256,256]{1,0:T(8,128)(2,1)S(1)} %collective-permute-done.5.refs_1_, f32[24,256]{1,0:T(8,128)S(1)} %copy-done.3, ...), custom_call_target="tpu_custom_call" | custom-call | flops 345000000 | bytes 65536 | tf_op jit(solution)/shard_map/pallas_call | solution.py:89
  40.6 5.2 %shard_map.106 = (f32[256,1024]{1,0:T(8,128)S(1)}, bf16[256,1024]{1,0:T(8,128)(2,1)S(1)}, f32[256,256]{1,0:T(8,128)S(1)}) custom-call(bf16[256,256]{1,0:T(8,128)(2,1)S(1)} %collective-permute-done.6.refs_0_, f32[24,256]{1,0:T(8,128)S(1)} %copy-done.4, f32[24,256]{1,0:T(8,128)S(1)} %collective-permute-done.3.refs_2_.refs_3_, bf16[256,1024]{1,0:T(8,128)(2,1)S(1)} %copy-done.1, ...), custom_call_target="tpu_custom_call" | custom-call | flops 1724999936 | bytes 65536 | tf_op jit(solution)/shard_map/pallas_call | solution.py:89
  45.8 2.3 %collective-permute-done.7.got_ref = bf16[512,256]{1,0:T(8,128)(2,1)S(1)} collective-permute-done((bf16[512,256]{1,0:T(8,128)(2,1)S(1)}, bf16[512,256]{1,0:T(8,128)(2,1)S(1)}, u32[]{:S(2)}, u32[]{:S(2)}) %collective-permute-start.7) | collective-permute-done | bytes 262176 | tf_op jit(solution)/shard_map/ppermute | solution.py:41
  48.1 1.9 %collective-permute-start.12 = (bf16[256,1024]{1,0:T(8,128)(2,1)S(1)}, bf16[256,1024]{1,0:T(8,128)(2,1)S(1)}, u32[]{:S(2)}, u32[]{:S(2)}) collective-permute-start(bf16[256,1024]{1,0:T(8,128)(2,1)S(1)} %get-tuple-element.70), channel_id=1, source_target_pairs={{0,8},{8,0},{16,24},{24,16},{1,9},{9,1},{17,25},{25,17},{32,40},{4... | collective-permute-start | bytes 1572872 | tf_op jit(solution)/shard_map/ppermute | solution.py:41
  50.2 2.9 %collective-permute-start.14 = (bf16[256,1024]{1,0:T(8,128)(2,1)S(1)}, bf16[256,1024]{1,0:T(8,128)(2,1)}, u32[]{:S(2)}, u32[]{:S(2)}) collective-permute-start(bf16[256,1024]{1,0:T(8,128)(2,1)S(1)} %collective-permute-done.10.refs_1_), channel_id=1, source_target_pairs={{0,6},{8,14},{16,22},{24,30},{1,7},{9,15},{17,23},{25,31},{32,38},... | collective-permute-start | bytes 1572872 | tf_op jit(solution)/shard_map/ppermute | solution.py:41
  55.2 2.8 %collective-permute-done.11.got_ref = bf16[512,256]{1,0:T(8,128)(2,1)S(1)} collective-permute-done((bf16[512,256]{1,0:T(8,128)(2,1)S(1)}, bf16[512,256]{1,0:T(8,128)(2,1)S(1)}, u32[]{:S(2)}, u32[]{:S(2)}) %collective-permute-start.11) | collective-permute-done | bytes 262176 | tf_op jit(solution)/shard_map/ppermute | solution.py:41
  58.0 7.0 %collective-permute-done.13.refs_7_ = bf16[256,1024]{1,0:T(8,128)(2,1)} collective-permute-done((bf16[256,1024]{1,0:T(8,128)(2,1)S(1)}, bf16[256,1024]{1,0:T(8,128)(2,1)}, u32[]{:S(2)}, u32[]{:S(2)}) %collective-permute-start.13) | collective-permute-done | bytes 524320 | tf_op jit(solution)/shard_map/ppermute | solution.py:41
  66.1 3.5 %all-to-all-start = ((bf16[4,512,256]{2,1,0:T(8,128)(2,1)}), bf16[4,512,256]{2,1,0:T(8,128)(2,1)S(1)}, u32[]{:S(2)}, u32[]{:S(2)}) async-start(bf16[4,512,256]{2,1,0:T(8,128)(2,1)} %shard_map.108), calls=%async_computation | async-start | bytes 2097152 | tf_op jit(solution)/shard_map/all_to_all | solution.py:305
  69.6 6.1 %collective-permute-done.15.refs_0_.refs_4_ = bf16[256,1024]{1,0:T(8,128)(2,1)} collective-permute-done((bf16[256,1024]{1,0:T(8,128)(2,1)S(1)}, bf16[256,1024]{1,0:T(8,128)(2,1)}, u32[]{:S(2)}, u32[]{:S(2)}) %collective-permute-start.15) | collective-permute-done | bytes 524320 | tf_op jit(solution)/shard_map/ppermute | solution.py:41
  75.7 3.4 %collective-permute-done.16.refs_2_.refs_5_ = bf16[256,1024]{1,0:T(8,128)(2,1)} collective-permute-done((bf16[256,1024]{1,0:T(8,128)(2,1)}, bf16[256,1024]{1,0:T(8,128)(2,1)}, u32[]{:S(2)}, u32[]{:S(2)}) %collective-permute-start.16) | collective-permute-done | bytes 524320 | tf_op jit(solution)/shard_map/ppermute | solution.py:41
  79.2 4.7 %all-to-all-done.refs_8_ = bf16[4,512,256]{2,1,0:T(8,128)(2,1)S(1)} async-done(((bf16[4,512,256]{2,1,0:T(8,128)(2,1)}), bf16[4,512,256]{2,1,0:T(8,128)(2,1)S(1)}, u32[]{:S(2)}, u32[]{:S(2)}) %all-to-all-start) | async-done | bytes 1048608 | tf_op jit(solution)/shard_map/all_to_all | solution.py:305
  83.9 2.8 %shard_map.110 = (f32[256,512]{1,0:T(8,128)S(1)}, f32[256,512]{1,0:T(8,128)S(1)}) custom-call(bf16[256,1024]{1,0:T(8,128)(2,1)S(1)} %collective-permute-done.refs_0_, bf16[256,1024]{1,0:T(8,128)(2,1)S(1)} %collective-permute-done.10.refs_1_, bf16[256,1024]{1,0:T(8,128)(2,1)S(1)} %collective-permute-done.8.refs_2_, ...), custom_call_target="tpu_custom_call" | custom-call | flops 11500000 | bytes 65536 | tf_op jit(solution)/shard_map/pallas_call | solution.py:89
  86.7 1.8 %collective-permute-start.17 = (f32[256,512]{1,0:T(8,128)S(1)}, f32[256,512]{1,0:T(8,128)S(1)}, u32[]{:S(2)}, u32[]{:S(2)}) collective-permute-start(f32[256,512]{1,0:T(8,128)S(1)} %get-tuple-element.82), channel_id=1, source_target_pairs={{0,8},{8,0},{16,24},{24,16},{1,9},{9,1},{17,25},{25,17},{32,40},{4... | collective-permute-start | bytes 1572872 | tf_op jit(solution)/shard_map/ppermute | solution.py:41
  88.5 1.5 %collective-permute-done.17.got_ref = f32[256,512]{1,0:T(8,128)S(1)} collective-permute-done((f32[256,512]{1,0:T(8,128)S(1)}, f32[256,512]{1,0:T(8,128)S(1)}, u32[]{:S(2)}, u32[]{:S(2)}) %collective-permute-start.17) | collective-permute-done | bytes 524320 | tf_op jit(solution)/shard_map/ppermute | solution.py:41
  (34 shorter events, 8.5 us)
Async XLA Ops:
  0.6 19.5 %copy-start.1 = (bf16[256,1024]{1,0:T(8,128)(2,1)S(1)}, bf16[256,1024]{1,0:T(8,128)(2,1)}, u32[]{:S(2)}) copy-start(bf16[256,1024]{1,0:T(8,128)(2,1)} %refs_3_.3) | copy-start | bytes 1572868
  0.6 19.5 %copy-start = (bf16[256,1024]{1,0:T(8,128)(2,1)S(1)}, bf16[256,1024]{1,0:T(8,128)(2,1)}, u32[]{:S(2)}) copy-start(bf16[256,1024]{1,0:T(8,128)(2,1)} %refs_5_.3) | copy-start | bytes 1572868
  0.7 6.3 %collective-permute-start.1 = (bf16[256,1024]{1,0:T(8,128)(2,1)}, bf16[256,1024]{1,0:T(8,128)(2,1)S(1)}, u32[]{:S(2)}, u32[]{:S(2)}) collective-permute-start(bf16[256,1024]{1,0:T(8,128)(2,1)} %refs_3_.3), channel_id=1, source_target_pairs={{0,8},{8,0},{16,24},{24,16},{1,9},{9,1},{17,25},{25,17},{32,40},{4... | collective-permute-start | bytes 1572872 | tf_op jit(solution)/shard_map/ppermute | solution.py:41
  2.2 4.8 %collective-permute-start.2 = (bf16[256,1024]{1,0:T(8,128)(2,1)}, bf16[256,1024]{1,0:T(8,128)(2,1)S(1)}, u32[]{:S(2)}, u32[]{:S(2)}) collective-permute-start(bf16[256,1024]{1,0:T(8,128)(2,1)} %refs_5_.3), channel_id=1, source_target_pairs={{0,8},{8,0},{16,24},{24,16},{1,9},{9,1},{17,25},{25,17},{32,40},{4... | collective-permute-start | bytes 1572872 | tf_op jit(solution)/shard_map/ppermute | solution.py:41
  2.2 24.9 %collective-permute-start = (bf16[256,1024]{1,0:T(8,128)(2,1)}, bf16[256,1024]{1,0:T(8,128)(2,1)S(1)}, u32[]{:S(2)}, u32[]{:S(2)}) collective-permute-start(bf16[256,1024]{1,0:T(8,128)(2,1)} %param.14), channel_id=1, source_target_pairs={{0,0},{8,8},{16,1},{24,9},{1,16},{9,24},{17,17},{25,25},{32,2},{40... | collective-permute-start | bytes 1572872 | tf_op jit(solution)/shard_map/ppermute | solution.py:41
  6.9 20.2 %collective-permute-start.4 = (bf16[256,256]{1,0:T(8,128)(2,1)}, bf16[256,256]{1,0:T(8,128)(2,1)S(1)}, u32[]{:S(2)}, u32[]{:S(2)}) collective-permute-start(bf16[256,256]{1,0:T(8,128)(2,1)} %get-tuple-element.46.refs_0_), channel_id=1, source_target_pairs={{0,32},{8,40},{16,48},{24,56},{1,33},{9,41},{17,49},{25,57},{64,96... | collective-permute-start | bytes 393224 | tf_op jit(solution)/shard_map/ppermute | solution.py:41
  11.5 15.6 %collective-permute-start.5 = (bf16[256,256]{1,0:T(8,128)(2,1)}, bf16[256,256]{1,0:T(8,128)(2,1)S(1)}, u32[]{:S(2)}, u32[]{:S(2)}) collective-permute-start(bf16[256,256]{1,0:T(8,128)(2,1)} %get-tuple-element.46.refs_0_), channel_id=1, source_target_pairs={{0,48},{8,56},{16,32},{24,40},{1,49},{9,57},{17,33},{25,41},{64,11... | collective-permute-start | bytes 393224 | tf_op jit(solution)/shard_map/ppermute | solution.py:41
  15.6 11.6 %collective-permute-start.6 = (bf16[256,256]{1,0:T(8,128)(2,1)}, bf16[256,256]{1,0:T(8,128)(2,1)S(1)}, u32[]{:S(2)}, u32[]{:S(2)}) collective-permute-start(bf16[256,256]{1,0:T(8,128)(2,1)} %get-tuple-element.46.refs_0_), channel_id=1, source_target_pairs={{0,16},{8,24},{1,17},{9,25},{32,48},{40,56},{33,49},{41,57},{64,80... | collective-permute-start | bytes 393224 | tf_op jit(solution)/shard_map/ppermute | solution.py:41
  17.8 2.4 %collective-permute-start.3 = (f32[24,256]{1,0:T(8,128)}, f32[24,256]{1,0:T(8,128)S(1)}, u32[]{:S(2)}, u32[]{:S(2)}) collective-permute-start(f32[24,256]{1,0:T(8,128)} %get-tuple-element.47.refs_1_.refs_2_), channel_id=1, source_target_pairs={{0,8},{8,0},{16,24},{24,16},{1,9},{9,1},{17,25},{25,17},{32,40},{4... | collective-permute-start | bytes 73736 | tf_op jit(solution)/shard_map/ppermute | solution.py:41
  20.2 0.9 copy-start.2
  21.1 0.7 copy-start.3
  27.2 13.4 %copy-start.4 = (f32[24,256]{1,0:T(8,128)S(1)}, f32[24,256]{1,0:T(8,128)}, u32[]{:S(2)}) copy-start(f32[24,256]{1,0:T(8,128)} %get-tuple-element.47.refs_1_.refs_2_) | copy-start | bytes 73732
  27.2 20.9 %collective-permute-start.8 = (bf16[256,1024]{1,0:T(8,128)(2,1)S(1)}, bf16[256,1024]{1,0:T(8,128)(2,1)S(1)}, u32[]{:S(2)}, u32[]{:S(2)}) collective-permute-start(bf16[256,1024]{1,0:T(8,128)(2,1)S(1)} %collective-permute-done.refs_0_), channel_id=1, source_target_pairs={{0,6},{8,14},{16,22},{24,30},{1,7},{9,15},{17,23},{25,31},{32,38},... | collective-permute-start | bytes 1572872 | tf_op jit(solution)/shard_map/ppermute | solution.py:41
  30.5 17.5 %collective-permute-start.9 = (bf16[256,1024]{1,0:T(8,128)(2,1)S(1)}, bf16[256,1024]{1,0:T(8,128)(2,1)S(1)}, u32[]{:S(2)}, u32[]{:S(2)}) collective-permute-start(bf16[256,1024]{1,0:T(8,128)(2,1)S(1)} %collective-permute-done.refs_0_), channel_id=1, source_target_pairs={{0,2},{8,10},{16,18},{24,26},{1,3},{9,11},{17,19},{25,27},{32,34},... | collective-permute-start | bytes 1572872 | tf_op jit(solution)/shard_map/ppermute | solution.py:41
  30.6 17.5 %collective-permute-start.10 = (bf16[256,1024]{1,0:T(8,128)(2,1)S(1)}, bf16[256,1024]{1,0:T(8,128)(2,1)S(1)}, u32[]{:S(2)}, u32[]{:S(2)}) collective-permute-start(bf16[256,1024]{1,0:T(8,128)(2,1)S(1)} %collective-permute-done.refs_0_), channel_id=1, source_target_pairs={{0,1},{8,9},{16,17},{24,25},{1,0},{9,8},{17,16},{25,24},{32,33},{4... | collective-permute-start | bytes 1572872 | tf_op jit(solution)/shard_map/ppermute | solution.py:41
  39.3 8.8 %collective-permute-start.7 = (bf16[512,256]{1,0:T(8,128)(2,1)S(1)}, bf16[512,256]{1,0:T(8,128)(2,1)S(1)}, u32[]{:S(2)}, u32[]{:S(2)}) collective-permute-start(bf16[512,256]{1,0:T(8,128)(2,1)S(1)} %get-tuple-element.64), channel_id=1, source_target_pairs={{32,0},{40,8},{48,16},{56,24},{33,1},{41,9},{49,17},{57,25},{96,64... | collective-permute-start | bytes 786440 | tf_op jit(solution)/shard_map/ppermute | solution.py:41
  48.1 6.2 %collective-permute-start.12 = (bf16[256,1024]{1,0:T(8,128)(2,1)S(1)}, bf16[256,1024]{1,0:T(8,128)(2,1)S(1)}, u32[]{:S(2)}, u32[]{:S(2)}) collective-permute-start(bf16[256,1024]{1,0:T(8,128)(2,1)S(1)} %get-tuple-element.70), channel_id=1, source_target_pairs={{0,8},{8,0},{16,24},{24,16},{1,9},{9,1},{17,25},{25,17},{32,40},{4... | collective-permute-start | bytes 1572872 | tf_op jit(solution)/shard_map/ppermute | solution.py:41
  50.0 14.9 %collective-permute-start.13 = (bf16[256,1024]{1,0:T(8,128)(2,1)S(1)}, bf16[256,1024]{1,0:T(8,128)(2,1)}, u32[]{:S(2)}, u32[]{:S(2)}) collective-permute-start(bf16[256,1024]{1,0:T(8,128)(2,1)S(1)} %collective-permute-done.10.refs_1_), channel_id=1, source_target_pairs={{0,2},{8,10},{16,18},{24,26},{1,3},{9,11},{17,19},{25,27},{32,34},... | collective-permute-start | bytes 1572872 | tf_op jit(solution)/shard_map/ppermute | solution.py:41
  50.1 7.9 %collective-permute-start.11 = (bf16[512,256]{1,0:T(8,128)(2,1)S(1)}, bf16[512,256]{1,0:T(8,128)(2,1)S(1)}, u32[]{:S(2)}, u32[]{:S(2)}) collective-permute-start(bf16[512,256]{1,0:T(8,128)(2,1)S(1)} %get-tuple-element.68), channel_id=1, source_target_pairs={{0,16},{8,24},{16,0},{24,8},{1,17},{9,25},{17,1},{25,9},{32,48},{4... | collective-permute-start | bytes 786440 | tf_op jit(solution)/shard_map/ppermute | solution.py:41
  50.2 19.4 %collective-permute-start.14 = (bf16[256,1024]{1,0:T(8,128)(2,1)S(1)}, bf16[256,1024]{1,0:T(8,128)(2,1)}, u32[]{:S(2)}, u32[]{:S(2)}) collective-permute-start(bf16[256,1024]{1,0:T(8,128)(2,1)S(1)} %collective-permute-done.10.refs_1_), channel_id=1, source_target_pairs={{0,6},{8,14},{16,22},{24,30},{1,7},{9,15},{17,23},{25,31},{32,38},... | collective-permute-start | bytes 1572872 | tf_op jit(solution)/shard_map/ppermute | solution.py:41
  53.1 22.6 %collective-permute-start.15 = (bf16[256,1024]{1,0:T(8,128)(2,1)S(1)}, bf16[256,1024]{1,0:T(8,128)(2,1)}, u32[]{:S(2)}, u32[]{:S(2)}) collective-permute-start(bf16[256,1024]{1,0:T(8,128)(2,1)S(1)} %collective-permute-done.8.refs_2_), channel_id=1, source_target_pairs={{0,6},{8,14},{16,22},{24,30},{1,7},{9,15},{17,23},{25,31},{32,38},... | collective-permute-start | bytes 1572872 | tf_op jit(solution)/shard_map/ppermute | solution.py:41
  65.0 14.2 %collective-permute-start.16 = (bf16[256,1024]{1,0:T(8,128)(2,1)}, bf16[256,1024]{1,0:T(8,128)(2,1)}, u32[]{:S(2)}, u32[]{:S(2)}) collective-permute-start(bf16[256,1024]{1,0:T(8,128)(2,1)} %collective-permute-done.13.refs_7_), channel_id=1, source_target_pairs={{0,2},{8,10},{16,18},{24,26},{1,3},{9,11},{17,19},{25,27},{32,34},... | collective-permute-start | bytes 1572872 | tf_op jit(solution)/shard_map/ppermute | solution.py:41
  66.1 17.8 %all-to-all-start = ((bf16[4,512,256]{2,1,0:T(8,128)(2,1)}), bf16[4,512,256]{2,1,0:T(8,128)(2,1)S(1)}, u32[]{:S(2)}, u32[]{:S(2)}) async-start(bf16[4,512,256]{2,1,0:T(8,128)(2,1)} %shard_map.108), calls=%async_computation | async-start | bytes 2097152 | tf_op jit(solution)/shard_map/all_to_all | solution.py:305
  86.7 3.4 %collective-permute-start.17 = (f32[256,512]{1,0:T(8,128)S(1)}, f32[256,512]{1,0:T(8,128)S(1)}, u32[]{:S(2)}, u32[]{:S(2)}) collective-permute-start(f32[256,512]{1,0:T(8,128)S(1)} %get-tuple-element.82), channel_id=1, source_target_pairs={{0,8},{8,0},{16,24},{24,16},{1,9},{9,1},{17,25},{25,17},{32,40},{4... | collective-permute-start | bytes 1572872 | tf_op jit(solution)/shard_map/ppermute | solution.py:41

commit v5 on v4

--- a/solution.py
+++ b/solution.py
@@ -211,7 +211,7 @@
             struct((keys, 2 * HD), dkv_type),
         ),
         [*kv, *aux, *q, *do, *(sums or ())],
-        megabytes=24,
+        megabytes=14,
         micros=micros,
         scratch_shapes=[pltpu.VMEM((keys, HD), f32)] * 2,
     )
@@ -237,30 +237,39 @@
             d_ref[copy, half * 2 * HD + HD : (half + 1) * 2 * HD, :] = v_grad
 
 
-def weights_kernel(*refs):
-    l_refs, (d_ref, _, sent_ref, kept_ref) = refs[:8], refs[8:]
+def weights_kernel(own_half, *refs):
+    l_refs, (d_ref, _, out_ref, held, sems) = refs[:8], refs[8:]
     me, tp = lax.axis_index("ctx"), lax.axis_index("tp")
     core, zl, y = me % 2, (me // 2) % 2, me // 4
     x, zh = tp // 2, tp % 2
     half_width = WIDTH // 2
-    for out_ref, whose in ((sent_ref, 1 - core), (kept_ref, core)):
-        for t in range(2):
-            tile = half_width // 2
-            cols = pl.ds(pl.multiple_of(whose * half_width + t * tile, tile), tile)
-            total = None
-            for s in range(4):
-                for j in range(2):
-                    rows = pl.ds(pl.multiple_of(((zh ^ j) ^ zl) * 2 * HD, 2 * HD), 2 * HD)
-                    term = nn(d_ref[(x + s + 3 * y) % 4, rows, :], l_refs[s * 2 + j][:, cols])
-                    total = term if total is None else total + term
-            out_ref[:, t * tile : (t + 1) * tile] = total
-
-
-def weights(l_blocks, d_blocks, ready):
+    whose = core if own_half else 1 - core
+    cols = pl.ds(pl.multiple_of(whose * half_width, half_width), half_width)
+    copies = [pltpu.make_async_copy(ref.at[:, cols], held.at[i], sems.at[i]) for i, ref in enumerate(l_refs)]
+    for copy in copies:
+        copy.start()
+    for s in range(4):
+        for j in range(2):
+            i = s * 2 + j
+            rows = pl.ds(pl.multiple_of(((zh ^ j) ^ zl) * 2 * HD, 2 * HD), 2 * HD)
+            copies[i].wait()
+            term = nn(d_ref[(x + s + 3 * y) % 4, rows, :], held[i])
+            if i == 0:
+                out_ref[...] = term
+            else:
+                out_ref[...] += term
+
+
+def weights(own_half, l_blocks, d_blocks, ready):
+    vmem = pl.BlockSpec(memory_space=pltpu.VMEM)
     return call(
-        weights_kernel,
-        (struct((2 * HD, WIDTH // 2), f32),) * 2,
+        functools.partial(weights_kernel, own_half),
+        struct((2 * HD, WIDTH // 2), f32),
         (*l_blocks, d_blocks, ready),
+        megabytes=57,
+        micros=2,
+        in_specs=[pl.BlockSpec(memory_space=pl.ANY)] * 8 + [vmem] * 2,
+        scratch_shapes=[pltpu.VMEM((8, ROWS, WIDTH // 2), bf16), pltpu.SemaphoreType.DMA((8,))],
     )
 
 
@@ -276,6 +285,7 @@
     kv, aux_own = prepare(doc_lengths, key_states, value_states, output_grad, attn_output, log_norms)
     kv, aux_own, q_par, do_par = together(kv, aux_own, q_par, do_par)
     aux_par = send(aux_own, other_core)
+    kv, aux_par = together(kv, aux_par)
     aux, q, do = (aux_own, aux_par), (queries, q_par), (output_grad, do_par)
 
     kv_far, kv_y, kv_zl = (send(kv, within_half(flip, True)) for flip in (3, 2, 1))
@@ -291,25 +301,26 @@
     dq_own, dq_par, dkv_zl, got_far, l_own, own_1, own_3, other_0 = together(
         dq_own, dq_par, dkv_zl, got_far, l_own, own_1, own_3, other_0
     )
-    dq_got = send(dq_par, other_core)
-    query_grad = ((dq_own + dq_got.astype(f32)) * SCALE).astype(bf16)
-
     pair = (2 * ROWS, 2 * HD)
     dkv, dkv_low = call(add_kernel, (struct(pair, f32), struct(pair, bf16)), (dkv_own, dkv_zl, got_far))
     got_zl = send(dkv_low, other_zl)
     other_0, own_1, _ = together(other_0, own_1, dkv_low)
     other_3, own_2, other_1 = send(other_0, ahead), send(own_1, behind), send(other_0, behind)
-    got_zl, query_grad, other_3 = together(got_zl, query_grad, other_3)
     d_copies = call(close_kernel, struct((4, 4 * HD, ROWS), bf16), (dkv, got_zl))
     columns = [[y * 4 + rest for y in range(4)] for rest in range(4)]
     d_blocks = lax.all_to_all(d_copies, "ctx", 0, 0, axis_index_groups=columns)
 
+    other_3, dq_par, _ = together(other_3, dq_par, d_copies)
     other_2 = send(other_3, ahead)
-    ready = arrived((own_2, other_1, other_2), 8)
+    dq_got = send(dq_par, other_core)
+    query_grad = ((dq_own + dq_got.astype(f32)) * SCALE).astype(bf16)
+    ready = arrived((own_2, other_1), 4)
     l_blocks = (l_own, other_0, own_1, other_1, own_2, other_2, own_3, other_3)
-    sent, kept = weights(l_blocks, d_blocks, ready)
+    sent = weights(False, l_blocks, d_blocks, ready)
+    got = send(sent, other_core)
+    kept = weights(True, l_blocks, d_blocks, ready)
     key_weight, value_weight = call(
-        finish_kernel, (struct((WIDTH // 2, HD), f32),) * 2, (kept, send(sent, other_core))
+        finish_kernel, (struct((WIDTH // 2, HD), f32),) * 2, (kept, got)
     )
     return query_grad, key_weight, value_weight
 

time: 91.4 us -> 86.4 us (0.945)
  waiting for transfers between devices: 28.9 us -> 13.1 us
  Pallas kernels: 25.2 us -> 30.5 us
  starting transfers between devices: 33.5 us -> 37.3 us
  local copies, waits for them, and re-layouts: 1.66 us -> 3.16 us
    ppermute x18, waiting for transfers between devices: 24.2 us -> 13.1 us  [send(): return lax.ppermute(value, AXES, route(target))]
    pallas_call x9 -> x10, Pallas kernels: 25.2 us -> 30.5 us  [call(): pl.pallas_call(kernel, out_shape=out_shape, compiler_params=pltpu.Compile...]
    all_to_all x1, waiting for transfers between devices: 4.7 us -> 0.01 us  [on_device(): d_blocks = lax.all_to_all(d_copies, 'ctx', 0, 0, axis_index_groups=columns)]
    ppermute x18, starting transfers between devices: 30 us -> 33.1 us  [send(): return lax.ppermute(value, AXES, route(target))]
    unnamed x10 -> x20, local copies, waits for them, and re-layouts: 1.66 us -> 3.16 us
  transfers between devices with their start and end apart: 19 -> 19, of which waited for: 8 -> 5; matrix products, arithmetic and copies ran while one was open for 1% -> 1% of each run, Pallas kernels for 24% -> 34%
where the time goes in v5:
time: 86.4 us; the launch traced here: 85.9 us
  starting transfers between devices  37.3 us (43%)
  Pallas kernels  30.5 us (35%)
  waiting for transfers between devices  13.1 us (15%)
  local copies, waits for them, and re-layouts  3.16 us (4%)
  other arithmetic  0.95 us (1%)
  between operations  0.89 us (1%)
    ppermute x18, starting transfers between devices, send(): return lax.ppermute(value, AXES, route(target))  33.1 us
    pallas_call x10, Pallas kernels, call(): pl.pallas_call(kernel, out_shape=out_shape, compiler_params=pltpu.Compile...  30.5 us
    ppermute x18, waiting for transfers between devices, send(): return lax.ppermute(value, AXES, route(target))  13.1 us
    all_to_all x1, starting transfers between devices, on_device(): d_blocks = lax.all_to_all(d_copies, 'ctx', 0, 0, axis_index_groups=columns)  4.23 us
    unnamed x20, local copies, waits for them, and re-layouts  3.16 us
  transfers between devices with their start and end apart: 19, of which 5 were waited for; matrix products, arithmetic and copies ran while one was open for 1% of the time, Pallas kernels for 34%

profile of v5, /device:TPU:1, one launch (start us, length us, event | category | flops | bytes accessed | tf_op | source)
XLA Modules:
  0.0 85.9 jit_solution(14240726825104344586)
XLA Ops:
  0.7 1.5 %collective-permute-start.1 = (bf16[256,1024]{1,0:T(8,128)(2,1)}, bf16[256,1024]{1,0:T(8,128)(2,1)S(1)}, u32[]{:S(2)}, u32[]{:S(2)}) collective-permute-start(bf16[256,1024]{1,0:T(8,128)(2,1)} %refs_3_.3), channel_id=1, source_target_pairs={{0,8},{8,0},{16,24},{24,16},{1,9},{9,1},{17,25},{25,17},{32,40},{4... | collective-permute-start | bytes 1572872 | tf_op jit(solution)/shard_map/ppermute | solution.py:41
  2.2 1.7 %collective-permute-start = (bf16[256,1024]{1,0:T(8,128)(2,1)}, bf16[256,1024]{1,0:T(8,128)(2,1)S(1)}, u32[]{:S(2)}, u32[]{:S(2)}) collective-permute-start(bf16[256,1024]{1,0:T(8,128)(2,1)} %param.14), channel_id=1, source_target_pairs={{0,0},{8,8},{16,1},{24,9},{1,16},{9,24},{17,17},{25,25},{32,2},{40... | collective-permute-start | bytes 1572872 | tf_op jit(solution)/shard_map/ppermute | solution.py:41
  3.9 3.0 %shard_map.103 = (bf16[256,256]{1,0:T(8,128)(2,1)}, f32[24,256]{1,0:T(8,128)}) custom-call(s32[16]{0:T(128)} %lengths_ref.1, bf16[256,128]{1,0:T(8,128)(2,1)} %k_any.1, bf16[256,128]{1,0:T(8,128)(2,1)} %v_any.1, bf16[256,1024]{1,0:T(8,128)(2,1)} %refs_5_.3, bf16[256,1024]{1,0:T(8,128)(2,1)} %out_any.1, f32[8,256]{1,0:T(8,128)} %ln_any.1), custom_call_target="tpu_custom_call" | custom-call | flops 345000000 | bytes 65536 | tf_op jit(solution)/shard_map/pallas_call | solution.py:89
  8.5 4.9 %collective-permute-start.4 = (bf16[256,256]{1,0:T(8,128)(2,1)}, bf16[256,256]{1,0:T(8,128)(2,1)S(1)}, u32[]{:S(2)}, u32[]{:S(2)}) collective-permute-start(bf16[256,256]{1,0:T(8,128)(2,1)} %get-tuple-element.47.refs_0_), channel_id=1, source_target_pairs={{0,32},{8,40},{16,48},{24,56},{1,33},{9,41},{17,49},{25,57},{64,96... | collective-permute-start | bytes 393224 | tf_op jit(solution)/shard_map/ppermute | solution.py:41
  13.4 4.0 %collective-permute-start.5 = (bf16[256,256]{1,0:T(8,128)(2,1)}, bf16[256,256]{1,0:T(8,128)(2,1)S(1)}, u32[]{:S(2)}, u32[]{:S(2)}) collective-permute-start(bf16[256,256]{1,0:T(8,128)(2,1)} %get-tuple-element.47.refs_0_), channel_id=1, source_target_pairs={{0,48},{8,56},{16,32},{24,40},{1,49},{9,57},{17,33},{25,41},{64,11... | collective-permute-start | bytes 393224 | tf_op jit(solution)/shard_map/ppermute | solution.py:41
  17.4 2.2 %collective-permute-start.6 = (bf16[256,256]{1,0:T(8,128)(2,1)}, bf16[256,256]{1,0:T(8,128)(2,1)S(1)}, u32[]{:S(2)}, u32[]{:S(2)}) collective-permute-start(bf16[256,256]{1,0:T(8,128)(2,1)} %get-tuple-element.47.refs_0_), channel_id=1, source_target_pairs={{0,16},{8,24},{1,17},{9,25},{32,48},{40,56},{33,49},{41,57},{64,80... | collective-permute-start | bytes 393224 | tf_op jit(solution)/shard_map/ppermute | solution.py:41
  21.3 5.3 %shard_map.104 = (f32[256,1024]{1,0:T(8,128)S(1)}, f32[256,1024]{1,0:T(8,128)S(1)}, f32[256,256]{1,0:T(8,128)S(1)}) custom-call(bf16[256,256]{1,0:T(8,128)(2,1)S(1)} %copy-done.3, f32[24,256]{1,0:T(8,128)S(1)} %copy-done.4, f32[24,256]{1,0:T(8,128)S(1)} %collective-permute-done.3.refs_2_.refs_3_, bf16[256,1024]{1,0:T(8,128)(2,1)S(1)} %copy-done.1, ...), custom_call_target="tpu_custom_call" | custom-call | flops 345000000 | bytes 65536 | tf_op jit(solution)/shard_map/pallas_call | solution.py:89
  26.6 3.4 %collective-permute-start.8 = (bf16[256,1024]{1,0:T(8,128)(2,1)S(1)}, bf16[256,1024]{1,0:T(8,128)(2,1)}, u32[]{:S(2)}, u32[]{:S(2)}) collective-permute-start(bf16[256,1024]{1,0:T(8,128)(2,1)S(1)} %collective-permute-done.refs_0_), channel_id=1, source_target_pairs={{0,6},{8,14},{16,22},{24,30},{1,7},{9,15},{17,23},{25,31},{32,38},... | collective-permute-start | bytes 1572872 | tf_op jit(solution)/shard_map/ppermute | solution.py:41
  30.0 2.0 %collective-permute-start.10 = (bf16[256,1024]{1,0:T(8,128)(2,1)S(1)}, bf16[256,1024]{1,0:T(8,128)(2,1)}, u32[]{:S(2)}, u32[]{:S(2)}) collective-permute-start(bf16[256,1024]{1,0:T(8,128)(2,1)S(1)} %collective-permute-done.refs_0_), channel_id=1, source_target_pairs={{0,1},{8,9},{16,17},{24,25},{1,0},{9,8},{17,16},{25,24},{32,33},{4... | collective-permute-start | bytes 1572872 | tf_op jit(solution)/shard_map/ppermute | solution.py:41
  32.0 6.7 %shard_map.105 = (f32[256,1024]{1,0:T(8,128)S(1)}, f32[256,1024]{1,0:T(8,128)S(1)}, bf16[512,256]{1,0:T(8,128)(2,1)S(1)}) custom-call(bf16[256,256]{1,0:T(8,128)(2,1)S(1)} %collective-permute-done.4.refs_0_, bf16[256,256]{1,0:T(8,128)(2,1)S(1)} %collective-permute-done.5.refs_1_, f32[24,256]{1,0:T(8,128)S(1)} %copy-done.4, ...), custom_call_target="tpu_custom_call" | custom-call | flops 345000000 | bytes 65536 | tf_op jit(solution)/shard_map/pallas_call | solution.py:89
  38.7 1.3 %collective-permute-start.7 = (bf16[512,256]{1,0:T(8,128)(2,1)S(1)}, bf16[512,256]{1,0:T(8,128)(2,1)S(1)}, u32[]{:S(2)}, u32[]{:S(2)}) collective-permute-start(bf16[512,256]{1,0:T(8,128)(2,1)S(1)} %get-tuple-element.64), channel_id=1, source_target_pairs={{32,0},{40,8},{48,16},{56,24},{33,1},{41,9},{49,17},{57,25},{96,64... | collective-permute-start | bytes 786440 | tf_op jit(solution)/shard_map/ppermute | solution.py:41
  40.0 5.2 %shard_map.106 = (f32[256,1024]{1,0:T(8,128)S(1)}, bf16[256,1024]{1,0:T(8,128)(2,1)S(1)}, f32[256,256]{1,0:T(8,128)S(1)}) custom-call(bf16[256,256]{1,0:T(8,128)(2,1)S(1)} %collective-permute-done.6.refs_0_, f32[24,256]{1,0:T(8,128)S(1)} %copy-done.4, f32[24,256]{1,0:T(8,128)S(1)} %collective-permute-done.3.refs_2_.refs_3_, bf16[256,1024]{1,0:T(8,128)(2,1)S(1)} %copy-done.1, ...), custom_call_target="tpu_custom_call" | custom-call | flops 1724999936 | bytes 65536 | tf_op jit(solution)/shard_map/pallas_call | solution.py:89
  45.3 1.7 %collective-permute-done.7.got_ref = bf16[512,256]{1,0:T(8,128)(2,1)S(1)} collective-permute-done((bf16[512,256]{1,0:T(8,128)(2,1)S(1)}, bf16[512,256]{1,0:T(8,128)(2,1)S(1)}, u32[]{:S(2)}, u32[]{:S(2)}) %collective-permute-start.7) | collective-permute-done | bytes 262176 | tf_op jit(solution)/shard_map/ppermute | solution.py:41
  47.2 2.7 %collective-permute-start.14 = (bf16[256,1024]{1,0:T(8,128)(2,1)}, bf16[256,1024]{1,0:T(8,128)(2,1)S(1)}, u32[]{:S(2)}, u32[]{:S(2)}) collective-permute-start(bf16[256,1024]{1,0:T(8,128)(2,1)} %collective-permute-done.10.refs_1_), channel_id=1, source_target_pairs={{0,6},{8,14},{16,22},{24,30},{1,7},{9,15},{17,23},{25,31},{32,38},... | collective-permute-start | bytes 1572872 | tf_op jit(solution)/shard_map/ppermute | solution.py:41
  49.9 1.2 %collective-permute-start.15 = (bf16[256,1024]{1,0:T(8,128)(2,1)}, bf16[256,1024]{1,0:T(8,128)(2,1)S(1)}, u32[]{:S(2)}, u32[]{:S(2)}) collective-permute-start(bf16[256,1024]{1,0:T(8,128)(2,1)} %collective-permute-done.8.refs_2_), channel_id=1, source_target_pairs={{0,6},{8,14},{16,22},{24,30},{1,7},{9,15},{17,23},{25,31},{32,38},... | collective-permute-start | bytes 1572872 | tf_op jit(solution)/shard_map/ppermute | solution.py:41
  51.1 1.3 %collective-permute-done.12.got_ref = bf16[512,256]{1,0:T(8,128)(2,1)S(1)} collective-permute-done((bf16[512,256]{1,0:T(8,128)(2,1)S(1)}, bf16[512,256]{1,0:T(8,128)(2,1)S(1)}, u32[]{:S(2)}, u32[]{:S(2)}) %collective-permute-start.12) | collective-permute-done | bytes 262176 | tf_op jit(solution)/shard_map/ppermute | solution.py:41
  52.4 1.1 %shard_map.108 = bf16[4,512,256]{2,1,0:T(8,128)(2,1)} custom-call(f32[512,256]{1,0:T(8,128)S(1)} %get-tuple-element.75.sum_ref, bf16[512,256]{1,0:T(8,128)(2,1)S(1)} %collective-permute-done.12.got_ref), custom_call_target="tpu_custom_call" | custom-call | flops 11500000 | bytes 65536 | tf_op jit(solution)/shard_map/pallas_call | solution.py:89
  53.5 4.2 %all-to-all-start = ((bf16[4,512,256]{2,1,0:T(8,128)(2,1)}), bf16[4,512,256]{2,1,0:T(8,128)(2,1)}, u32[]{:S(2)}, u32[]{:S(2)}) async-start(bf16[4,512,256]{2,1,0:T(8,128)(2,1)} %shard_map.108), calls=%async_computation | async-start | bytes 2097152 | tf_op jit(solution)/shard_map/all_to_all | solution.py:311
  57.7 2.1 %collective-permute-done.11.refs_7_ = bf16[256,1024]{1,0:T(8,128)(2,1)} collective-permute-done((bf16[256,1024]{1,0:T(8,128)(2,1)}, bf16[256,1024]{1,0:T(8,128)(2,1)}, u32[]{:S(2)}, u32[]{:S(2)}) %collective-permute-start.11) | collective-permute-done | bytes 524320 | tf_op jit(solution)/shard_map/ppermute | solution.py:41
  59.8 3.3 %collective-permute-start.13 = (bf16[256,1024]{1,0:T(8,128)(2,1)S(1)}, bf16[256,1024]{1,0:T(8,128)(2,1)S(1)}, u32[]{:S(2)}, u32[]{:S(2)}) collective-permute-start(bf16[256,1024]{1,0:T(8,128)(2,1)S(1)} %get-tuple-element.76), channel_id=1, source_target_pairs={{0,8},{8,0},{16,24},{24,16},{1,9},{9,1},{17,25},{25,17},{32,40},{4... | collective-permute-start | bytes 1572872 | tf_op jit(solution)/shard_map/ppermute | solution.py:41
  63.1 6.9 %collective-permute-done.15.refs_0_.refs_4_ = bf16[256,1024]{1,0:T(8,128)(2,1)S(1)} collective-permute-done((bf16[256,1024]{1,0:T(8,128)(2,1)}, bf16[256,1024]{1,0:T(8,128)(2,1)S(1)}, u32[]{:S(2)}, u32[]{:S(2)}) %collective-permute-start.15) | collective-permute-done | bytes 524320 | tf_op jit(solution)/shard_map/ppermute | solution.py:41
  71.5 4.1 %shard_map.111 = f32[256,512]{1,0:T(8,128)} custom-call(bf16[256,1024]{1,0:T(8,128)(2,1)} %copy-done.8, bf16[256,1024]{1,0:T(8,128)(2,1)} %collective-permute-done.10.refs_1_, bf16[256,1024]{1,0:T(8,128)(2,1)} %collective-permute-done.8.refs_2_, bf16[256,1024]{1,0:T(8,128)(2,1)} %copy-done.5, bf16[256,1024]{1,0:T(8,128)(2,1)} %copy-done.6, ...), custom_call_target="tpu_custom_call" | custom-call | flops 2300000000 | bytes 65536 | tf_op jit(solution)/shard_map/pallas_call | solution.py:89
  75.5 4.3 %collective-permute-start.17 = (f32[256,512]{1,0:T(8,128)}, f32[256,512]{1,0:T(8,128)S(1)}, u32[]{:S(2)}, u32[]{:S(2)}) collective-permute-start(f32[256,512]{1,0:T(8,128)} %shard_map.111), channel_id=1, source_target_pairs={{0,8},{8,0},{16,24},{24,16},{1,9},{9,1},{17,25},{25,17},{32,40},{4... | collective-permute-start | bytes 1572872 | tf_op jit(solution)/shard_map/ppermute | solution.py:41
  79.8 4.1 %shard_map.110.mine_ref = f32[256,512]{1,0:T(8,128)} custom-call(bf16[256,1024]{1,0:T(8,128)(2,1)} %copy-done.8, bf16[256,1024]{1,0:T(8,128)(2,1)} %collective-permute-done.10.refs_1_, bf16[256,1024]{1,0:T(8,128)(2,1)} %collective-permute-done.8.refs_2_, bf16[256,1024]{1,0:T(8,128)(2,1)} %copy-done.5, bf16[256,1024]{1,0:T(8,128)(2,1)} %copy-done.6, ...), custom_call_target="tpu_custom_call" | custom-call | flops 2300000000 | bytes 65536 | tf_op jit(solution)/shard_map/pallas_call | solution.py:89
  (45 shorter events, 7.0 us)
Async XLA Ops:
  0.6 19.0 %copy-start.1 = (bf16[256,1024]{1,0:T(8,128)(2,1)S(1)}, bf16[256,1024]{1,0:T(8,128)(2,1)}, u32[]{:S(2)}) copy-start(bf16[256,1024]{1,0:T(8,128)(2,1)} %refs_3_.3) | copy-start | bytes 1572868
  0.6 19.0 %copy-start = (bf16[256,1024]{1,0:T(8,128)(2,1)S(1)}, bf16[256,1024]{1,0:T(8,128)(2,1)}, u32[]{:S(2)}) copy-start(bf16[256,1024]{1,0:T(8,128)(2,1)} %refs_5_.3) | copy-start | bytes 1572868
  0.7 6.3 %collective-permute-start.1 = (bf16[256,1024]{1,0:T(8,128)(2,1)}, bf16[256,1024]{1,0:T(8,128)(2,1)S(1)}, u32[]{:S(2)}, u32[]{:S(2)}) collective-permute-start(bf16[256,1024]{1,0:T(8,128)(2,1)} %refs_3_.3), channel_id=1, source_target_pairs={{0,8},{8,0},{16,24},{24,16},{1,9},{9,1},{17,25},{25,17},{32,40},{4... | collective-permute-start | bytes 1572872 | tf_op jit(solution)/shard_map/ppermute | solution.py:41
  2.2 4.8 %collective-permute-start.2 = (bf16[256,1024]{1,0:T(8,128)(2,1)}, bf16[256,1024]{1,0:T(8,128)(2,1)S(1)}, u32[]{:S(2)}, u32[]{:S(2)}) collective-permute-start(bf16[256,1024]{1,0:T(8,128)(2,1)} %refs_5_.3), channel_id=1, source_target_pairs={{0,8},{8,0},{16,24},{24,16},{1,9},{9,1},{17,25},{25,17},{32,40},{4... | collective-permute-start | bytes 1572872 | tf_op jit(solution)/shard_map/ppermute | solution.py:41
  2.2 24.3 %collective-permute-start = (bf16[256,1024]{1,0:T(8,128)(2,1)}, bf16[256,1024]{1,0:T(8,128)(2,1)S(1)}, u32[]{:S(2)}, u32[]{:S(2)}) collective-permute-start(bf16[256,1024]{1,0:T(8,128)(2,1)} %param.14), channel_id=1, source_target_pairs={{0,0},{8,8},{16,1},{24,9},{1,16},{9,24},{17,17},{25,25},{32,2},{40... | collective-permute-start | bytes 1572872 | tf_op jit(solution)/shard_map/ppermute | solution.py:41
  6.9 1.6 %collective-permute-start.3 = (f32[24,256]{1,0:T(8,128)}, f32[24,256]{1,0:T(8,128)S(1)}, u32[]{:S(2)}, u32[]{:S(2)}) collective-permute-start(f32[24,256]{1,0:T(8,128)} %get-tuple-element.46.refs_1_.refs_2_), channel_id=1, source_target_pairs={{0,8},{8,0},{16,24},{24,16},{1,9},{9,1},{17,25},{25,17},{32,40},{4... | collective-permute-start | bytes 73736 | tf_op jit(solution)/shard_map/ppermute | solution.py:41
  8.5 18.1 %collective-permute-start.4 = (bf16[256,256]{1,0:T(8,128)(2,1)}, bf16[256,256]{1,0:T(8,128)(2,1)S(1)}, u32[]{:S(2)}, u32[]{:S(2)}) collective-permute-start(bf16[256,256]{1,0:T(8,128)(2,1)} %get-tuple-element.47.refs_0_), channel_id=1, source_target_pairs={{0,32},{8,40},{16,48},{24,56},{1,33},{9,41},{17,49},{25,57},{64,96... | collective-permute-start | bytes 393224 | tf_op jit(solution)/shard_map/ppermute | solution.py:41
  13.4 13.2 %collective-permute-start.5 = (bf16[256,256]{1,0:T(8,128)(2,1)}, bf16[256,256]{1,0:T(8,128)(2,1)S(1)}, u32[]{:S(2)}, u32[]{:S(2)}) collective-permute-start(bf16[256,256]{1,0:T(8,128)(2,1)} %get-tuple-element.47.refs_0_), channel_id=1, source_target_pairs={{0,48},{8,56},{16,32},{24,40},{1,49},{9,57},{17,33},{25,41},{64,11... | collective-permute-start | bytes 393224 | tf_op jit(solution)/shard_map/ppermute | solution.py:41
  17.4 9.3 %collective-permute-start.6 = (bf16[256,256]{1,0:T(8,128)(2,1)}, bf16[256,256]{1,0:T(8,128)(2,1)S(1)}, u32[]{:S(2)}, u32[]{:S(2)}) collective-permute-start(bf16[256,256]{1,0:T(8,128)(2,1)} %get-tuple-element.47.refs_0_), channel_id=1, source_target_pairs={{0,16},{8,24},{1,17},{9,25},{32,48},{40,56},{33,49},{41,57},{64,80... | collective-permute-start | bytes 393224 | tf_op jit(solution)/shard_map/ppermute | solution.py:41
  26.6 12.1 %copy-start.8 = (bf16[256,1024]{1,0:T(8,128)(2,1)}, bf16[256,1024]{1,0:T(8,128)(2,1)S(1)}, u32[]{:S(2)}) copy-start(bf16[256,1024]{1,0:T(8,128)(2,1)S(1)} %collective-permute-done.refs_0_) | copy-start | bytes 1572868
  26.6 20.3 %collective-permute-start.8 = (bf16[256,1024]{1,0:T(8,128)(2,1)S(1)}, bf16[256,1024]{1,0:T(8,128)(2,1)}, u32[]{:S(2)}, u32[]{:S(2)}) collective-permute-start(bf16[256,1024]{1,0:T(8,128)(2,1)S(1)} %collective-permute-done.refs_0_), channel_id=1, source_target_pairs={{0,6},{8,14},{16,22},{24,30},{1,7},{9,15},{17,23},{25,31},{32,38},... | collective-permute-start | bytes 1572872 | tf_op jit(solution)/shard_map/ppermute | solution.py:41
  30.0 17.0 %collective-permute-start.9 = (bf16[256,1024]{1,0:T(8,128)(2,1)S(1)}, bf16[256,1024]{1,0:T(8,128)(2,1)S(1)}, u32[]{:S(2)}, u32[]{:S(2)}) collective-permute-start(bf16[256,1024]{1,0:T(8,128)(2,1)S(1)} %collective-permute-done.refs_0_), channel_id=1, source_target_pairs={{0,2},{8,10},{16,18},{24,26},{1,3},{9,11},{17,19},{25,27},{32,34},... | collective-permute-start | bytes 1572872 | tf_op jit(solution)/shard_map/ppermute | solution.py:41
  30.0 17.0 %collective-permute-start.10 = (bf16[256,1024]{1,0:T(8,128)(2,1)S(1)}, bf16[256,1024]{1,0:T(8,128)(2,1)}, u32[]{:S(2)}, u32[]{:S(2)}) collective-permute-start(bf16[256,1024]{1,0:T(8,128)(2,1)S(1)} %collective-permute-done.refs_0_), channel_id=1, source_target_pairs={{0,1},{8,9},{16,17},{24,25},{1,0},{9,8},{17,16},{25,24},{32,33},{4... | collective-permute-start | bytes 1572872 | tf_op jit(solution)/shard_map/ppermute | solution.py:41
  38.7 8.2 %collective-permute-start.7 = (bf16[512,256]{1,0:T(8,128)(2,1)S(1)}, bf16[512,256]{1,0:T(8,128)(2,1)S(1)}, u32[]{:S(2)}, u32[]{:S(2)}) collective-permute-start(bf16[512,256]{1,0:T(8,128)(2,1)S(1)} %get-tuple-element.64), channel_id=1, source_target_pairs={{32,0},{40,8},{48,16},{56,24},{33,1},{41,9},{49,17},{57,25},{96,64... | collective-permute-start | bytes 786440 | tf_op jit(solution)/shard_map/ppermute | solution.py:41
  47.0 5.4 %copy-start.9 = (bf16[256,1024]{1,0:T(8,128)(2,1)}, bf16[256,1024]{1,0:T(8,128)(2,1)S(1)}, u32[]{:S(2)}) copy-start(bf16[256,1024]{1,0:T(8,128)(2,1)S(1)} %collective-permute-done.9.refs_6_) | copy-start | bytes 1572868
  47.1 5.3 %collective-permute-start.12 = (bf16[512,256]{1,0:T(8,128)(2,1)S(1)}, bf16[512,256]{1,0:T(8,128)(2,1)S(1)}, u32[]{:S(2)}, u32[]{:S(2)}) collective-permute-start(bf16[512,256]{1,0:T(8,128)(2,1)S(1)} %get-tuple-element.72), channel_id=1, source_target_pairs={{0,16},{8,24},{16,0},{24,8},{1,17},{9,25},{17,1},{25,9},{32,48},{4... | collective-permute-start | bytes 786440 | tf_op jit(solution)/shard_map/ppermute | solution.py:41
  47.2 12.6 %collective-permute-start.11 = (bf16[256,1024]{1,0:T(8,128)(2,1)}, bf16[256,1024]{1,0:T(8,128)(2,1)}, u32[]{:S(2)}, u32[]{:S(2)}) collective-permute-start(bf16[256,1024]{1,0:T(8,128)(2,1)} %collective-permute-done.10.refs_1_), channel_id=1, source_target_pairs={{0,2},{8,10},{16,18},{24,26},{1,3},{9,11},{17,19},{25,27},{32,34},... | collective-permute-start | bytes 1572872 | tf_op jit(solution)/shard_map/ppermute | solution.py:41
  47.2 15.9 %collective-permute-start.14 = (bf16[256,1024]{1,0:T(8,128)(2,1)}, bf16[256,1024]{1,0:T(8,128)(2,1)S(1)}, u32[]{:S(2)}, u32[]{:S(2)}) collective-permute-start(bf16[256,1024]{1,0:T(8,128)(2,1)} %collective-permute-done.10.refs_1_), channel_id=1, source_target_pairs={{0,6},{8,14},{16,22},{24,30},{1,7},{9,15},{17,23},{25,31},{32,38},... | collective-permute-start | bytes 1572872 | tf_op jit(solution)/shard_map/ppermute | solution.py:41
  49.9 20.1 %collective-permute-start.15 = (bf16[256,1024]{1,0:T(8,128)(2,1)}, bf16[256,1024]{1,0:T(8,128)(2,1)S(1)}, u32[]{:S(2)}, u32[]{:S(2)}) collective-permute-start(bf16[256,1024]{1,0:T(8,128)(2,1)} %collective-permute-done.8.refs_2_), channel_id=1, source_target_pairs={{0,6},{8,14},{16,22},{24,30},{1,7},{9,15},{17,23},{25,31},{32,38},... | collective-permute-start | bytes 1572872 | tf_op jit(solution)/shard_map/ppermute | solution.py:41
  53.5 18.0 %all-to-all-start = ((bf16[4,512,256]{2,1,0:T(8,128)(2,1)}), bf16[4,512,256]{2,1,0:T(8,128)(2,1)}, u32[]{:S(2)}, u32[]{:S(2)}) async-start(bf16[4,512,256]{2,1,0:T(8,128)(2,1)} %shard_map.108), calls=%async_computation | async-start | bytes 2097152 | tf_op jit(solution)/shard_map/all_to_all | solution.py:311
  59.8 11.7 %collective-permute-start.16 = (bf16[256,1024]{1,0:T(8,128)(2,1)}, bf16[256,1024]{1,0:T(8,128)(2,1)}, u32[]{:S(2)}, u32[]{:S(2)}) collective-permute-start(bf16[256,1024]{1,0:T(8,128)(2,1)} %collective-permute-done.11.refs_7_), channel_id=1, source_target_pairs={{0,2},{8,10},{16,18},{24,26},{1,3},{9,11},{17,19},{25,27},{32,34},... | collective-permute-start | bytes 1572872 | tf_op jit(solution)/shard_map/ppermute | solution.py:41
  59.8 24.1 %collective-permute-start.13 = (bf16[256,1024]{1,0:T(8,128)(2,1)S(1)}, bf16[256,1024]{1,0:T(8,128)(2,1)S(1)}, u32[]{:S(2)}, u32[]{:S(2)}) collective-permute-start(bf16[256,1024]{1,0:T(8,128)(2,1)S(1)} %get-tuple-element.76), channel_id=1, source_target_pairs={{0,8},{8,0},{16,24},{24,16},{1,9},{9,1},{17,25},{25,17},{32,40},{4... | collective-permute-start | bytes 1572872 | tf_op jit(solution)/shard_map/ppermute | solution.py:41
  63.1 6.9 %copy-start.5 = (bf16[256,1024]{1,0:T(8,128)(2,1)}, bf16[256,1024]{1,0:T(8,128)(2,1)S(1)}, u32[]{:S(2)}) copy-start(bf16[256,1024]{1,0:T(8,128)(2,1)S(1)} %collective-permute-done.14.refs_1_.refs_3_) | copy-start | bytes 1572868
  75.5 9.3 %collective-permute-start.17 = (f32[256,512]{1,0:T(8,128)}, f32[256,512]{1,0:T(8,128)S(1)}, u32[]{:S(2)}, u32[]{:S(2)}) collective-permute-start(f32[256,512]{1,0:T(8,128)} %shard_map.111), channel_id=1, source_target_pairs={{0,8},{8,0},{16,24},{24,16},{1,9},{9,1},{17,25},{25,17},{32,40},{4... | collective-permute-start | bytes 1572872 | tf_op jit(solution)/shard_map/ppermute | solution.py:41
  (5 other events, 4.1 us)

commit v6 on v4

--- a/solution.py
+++ b/solution.py
@@ -211,7 +211,7 @@
             struct((keys, 2 * HD), dkv_type),
         ),
         [*kv, *aux, *q, *do, *(sums or ())],
-        megabytes=24,
+        megabytes=14,
         micros=micros,
         scratch_shapes=[pltpu.VMEM((keys, HD), f32)] * 2,
     )
@@ -232,16 +232,17 @@
         total = sum_ref[mine, :] + got_ref[its, :].astype(f32)
         k_grad = (total[:, :HD] * SCALE).T.astype(bf16)
         v_grad = total[:, HD:].T.astype(bf16)
-        for copy in range(4):
-            d_ref[copy, half * 2 * HD : half * 2 * HD + HD, :] = k_grad
-            d_ref[copy, half * 2 * HD + HD : (half + 1) * 2 * HD, :] = v_grad
+        d_ref[half * 2 * HD : half * 2 * HD + HD, :] = k_grad
+        d_ref[half * 2 * HD + HD : (half + 1) * 2 * HD, :] = v_grad
 
 
 def weights_kernel(*refs):
-    l_refs, (d_ref, _, sent_ref, kept_ref) = refs[:8], refs[8:]
+    l_refs, d_refs, (_, sent_ref, kept_ref, d_all) = refs[:8], refs[8:12], refs[12:]
     me, tp = lax.axis_index("ctx"), lax.axis_index("tp")
     core, zl, y = me % 2, (me // 2) % 2, me // 4
     x, zh = tp // 2, tp % 2
+    for r in range(4):
+        d_all[r] = d_refs[r][...]
     half_width = WIDTH // 2
     for out_ref, whose in ((sent_ref, 1 - core), (kept_ref, core)):
         for t in range(2):
@@ -251,7 +252,7 @@
             for s in range(4):
                 for j in range(2):
                     rows = pl.ds(pl.multiple_of(((zh ^ j) ^ zl) * 2 * HD, 2 * HD), 2 * HD)
-                    term = nn(d_ref[(x + s + 3 * y) % 4, rows, :], l_refs[s * 2 + j][:, cols])
+                    term = nn(d_all[(x + s + 2 * y) % 4, rows, :], l_refs[s * 2 + j][:, cols])
                     total = term if total is None else total + term
             out_ref[:, t * tile : (t + 1) * tile] = total
 
@@ -260,7 +261,8 @@
     return call(
         weights_kernel,
         (struct((2 * HD, WIDTH // 2), f32),) * 2,
-        (*l_blocks, d_blocks, ready),
+        (*l_blocks, *d_blocks, ready),
+        scratch_shapes=[pltpu.VMEM((4, 4 * HD, ROWS), bf16)],
     )
 
 
@@ -276,6 +278,7 @@
     kv, aux_own = prepare(doc_lengths, key_states, value_states, output_grad, attn_output, log_norms)
     kv, aux_own, q_par, do_par = together(kv, aux_own, q_par, do_par)
     aux_par = send(aux_own, other_core)
+    kv, aux_par = together(kv, aux_par)
     aux, q, do = (aux_own, aux_par), (queries, q_par), (output_grad, do_par)
 
     kv_far, kv_y, kv_zl = (send(kv, within_half(flip, True)) for flip in (3, 2, 1))
@@ -291,25 +294,26 @@
     dq_own, dq_par, dkv_zl, got_far, l_own, own_1, own_3, other_0 = together(
         dq_own, dq_par, dkv_zl, got_far, l_own, own_1, own_3, other_0
     )
-    dq_got = send(dq_par, other_core)
-    query_grad = ((dq_own + dq_got.astype(f32)) * SCALE).astype(bf16)
-
     pair = (2 * ROWS, 2 * HD)
     dkv, dkv_low = call(add_kernel, (struct(pair, f32), struct(pair, bf16)), (dkv_own, dkv_zl, got_far))
     got_zl = send(dkv_low, other_zl)
-    other_0, own_1, _ = together(other_0, own_1, dkv_low)
-    other_3, own_2, other_1 = send(other_0, ahead), send(own_1, behind), send(other_0, behind)
-    got_zl, query_grad, other_3 = together(got_zl, query_grad, other_3)
-    d_copies = call(close_kernel, struct((4, 4 * HD, ROWS), bf16), (dkv, got_zl))
-    columns = [[y * 4 + rest for y in range(4)] for rest in range(4)]
-    d_blocks = lax.all_to_all(d_copies, "ctx", 0, 0, axis_index_groups=columns)
-
-    other_2 = send(other_3, ahead)
-    ready = arrived((own_2, other_1, other_2), 8)
+    other_0, dq_par, _ = together(other_0, dq_par, dkv_low)
+    other_3, other_1 = send(other_0, ahead), send(other_0, behind)
+    dq_got = send(dq_par, other_core)
+    query_grad = ((dq_own + dq_got.astype(f32)) * SCALE).astype(bf16)
+    got_zl, query_grad = together(got_zl, query_grad)
+    d_own = call(close_kernel, struct((4 * HD, ROWS), bf16), (dkv, got_zl))
+    d_2, d_1, d_3 = (send(d_own, shifted(dy=-dy)) for dy in (2, 1, 3))
+    ready = arrived((d_1, d_2, d_3), 8)
+
+    other_3, other_1, own_1, _ = together(other_3, other_1, own_1, d_own)
+    own_2, other_2 = send(own_1, behind), send(other_3, ahead)
     l_blocks = (l_own, other_0, own_1, other_1, own_2, other_2, own_3, other_3)
+    d_blocks = (d_own, d_1, d_2, d_3)
     sent, kept = weights(l_blocks, d_blocks, ready)
+    got = send(sent, other_core)
     key_weight, value_weight = call(
-        finish_kernel, (struct((WIDTH // 2, HD), f32),) * 2, (kept, send(sent, other_core))
+        finish_kernel, (struct((WIDTH // 2, HD), f32),) * 2, (kept, got)
     )
     return query_grad, key_weight, value_weight
 

time: 91.4 us -> 86.2 us (0.943)
  waiting for transfers between devices: 28.9 us -> 25.1 us
  Pallas kernels: 25.2 us -> 22.7 us
  starting transfers between devices: 33.5 us -> 34.5 us
    all_to_all x1 -> x0, waiting for transfers between devices: 4.7 us -> none  [on_device(): d_blocks = lax.all_to_all(d_copies, 'ctx', 0, 0, axis_index_groups=columns)]
    ppermute x18 -> x21, starting transfers between devices: 30 us -> 34.5 us  [send(): return lax.ppermute(value, AXES, route(target))]
    all_to_all x1 -> x0, starting transfers between devices: 3.51 us -> none  [on_device(): d_blocks = lax.all_to_all(d_copies, 'ctx', 0, 0, axis_index_groups=columns)]
    pallas_call x9, Pallas kernels: 25.2 us -> 22.7 us  [call(): pl.pallas_call(kernel, out_shape=out_shape, compiler_params=pltpu.Compile...]
    ppermute x18 -> x21, waiting for transfers between devices: 24.2 us -> 25.1 us  [send(): return lax.ppermute(value, AXES, route(target))]
  transfers between devices with their start and end apart: 19 -> 21, of which waited for: 8 -> 8; matrix products, arithmetic and copies ran while one was open for 1% -> 1% of each run, Pallas kernels for 24% -> 24%
where the time goes in v6:
time: 86.2 us; the launch traced here: 85.9 us
  starting transfers between devices  34.5 us (40%)
  waiting for transfers between devices  25.1 us (29%)
  Pallas kernels  22.7 us (26%)
  local copies, waits for them, and re-layouts  1.67 us (2%)
  other arithmetic  0.97 us (1%)
    ppermute x21, starting transfers between devices, send(): return lax.ppermute(value, AXES, route(target))  34.5 us
    ppermute x21, waiting for transfers between devices, send(): return lax.ppermute(value, AXES, route(target))  25.1 us
    pallas_call x9, Pallas kernels, call(): pl.pallas_call(kernel, out_shape=out_shape, compiler_params=pltpu.Compile...  22.7 us
  transfers between devices with their start and end apart: 21, of which 8 were waited for; matrix products, arithmetic and copies ran while one was open for 1% of the time, Pallas kernels for 24%

profile of v6, /device:TPU:1, one launch (start us, length us, event | category | flops | bytes accessed | tf_op | source)
XLA Modules:
  0.0 85.9 jit_solution(11420027997034165357)
XLA Ops:
  0.7 1.5 %collective-permute-start.1 = (bf16[256,1024]{1,0:T(8,128)(2,1)}, bf16[256,1024]{1,0:T(8,128)(2,1)S(1)}, u32[]{:S(2)}, u32[]{:S(2)}) collective-permute-start(bf16[256,1024]{1,0:T(8,128)(2,1)} %refs_3_.3), channel_id=1, source_target_pairs={{0,8},{8,0},{16,24},{24,16},{1,9},{9,1},{17,25},{25,17},{32,40},{4... | collective-permute-start | bytes 1572872 | tf_op jit(solution)/shard_map/ppermute | solution.py:41
  2.2 1.7 %collective-permute-start = (bf16[256,1024]{1,0:T(8,128)(2,1)}, bf16[256,1024]{1,0:T(8,128)(2,1)S(1)}, u32[]{:S(2)}, u32[]{:S(2)}) collective-permute-start(bf16[256,1024]{1,0:T(8,128)(2,1)} %param.14), channel_id=1, source_target_pairs={{0,0},{8,8},{16,1},{24,9},{1,16},{9,24},{17,17},{25,25},{32,2},{40... | collective-permute-start | bytes 1572872 | tf_op jit(solution)/shard_map/ppermute | solution.py:41
  3.9 3.0 %shard_map.103 = (bf16[256,256]{1,0:T(8,128)(2,1)}, f32[24,256]{1,0:T(8,128)}) custom-call(s32[16]{0:T(128)} %lengths_ref.1, bf16[256,128]{1,0:T(8,128)(2,1)} %k_any.1, bf16[256,128]{1,0:T(8,128)(2,1)} %v_any.1, bf16[256,1024]{1,0:T(8,128)(2,1)} %refs_5_.3, bf16[256,1024]{1,0:T(8,128)(2,1)} %out_any.1, f32[8,256]{1,0:T(8,128)} %ln_any.1), custom_call_target="tpu_custom_call" | custom-call | flops 345000000 | bytes 65536 | tf_op jit(solution)/shard_map/pallas_call | solution.py:89
  8.5 4.9 %collective-permute-start.4 = (bf16[256,256]{1,0:T(8,128)(2,1)}, bf16[256,256]{1,0:T(8,128)(2,1)S(1)}, u32[]{:S(2)}, u32[]{:S(2)}) collective-permute-start(bf16[256,256]{1,0:T(8,128)(2,1)} %get-tuple-element.52.refs_0_), channel_id=1, source_target_pairs={{0,32},{8,40},{16,48},{24,56},{1,33},{9,41},{17,49},{25,57},{64,96... | collective-permute-start | bytes 393224 | tf_op jit(solution)/shard_map/ppermute | solution.py:41
  13.4 4.0 %collective-permute-start.5 = (bf16[256,256]{1,0:T(8,128)(2,1)}, bf16[256,256]{1,0:T(8,128)(2,1)S(1)}, u32[]{:S(2)}, u32[]{:S(2)}) collective-permute-start(bf16[256,256]{1,0:T(8,128)(2,1)} %get-tuple-element.52.refs_0_), channel_id=1, source_target_pairs={{0,48},{8,56},{16,32},{24,40},{1,49},{9,57},{17,33},{25,41},{64,11... | collective-permute-start | bytes 393224 | tf_op jit(solution)/shard_map/ppermute | solution.py:41
  17.4 2.2 %collective-permute-start.6 = (bf16[256,256]{1,0:T(8,128)(2,1)}, bf16[256,256]{1,0:T(8,128)(2,1)S(1)}, u32[]{:S(2)}, u32[]{:S(2)}) collective-permute-start(bf16[256,256]{1,0:T(8,128)(2,1)} %get-tuple-element.52.refs_0_), channel_id=1, source_target_pairs={{0,16},{8,24},{1,17},{9,25},{32,48},{40,56},{33,49},{41,57},{64,80... | collective-permute-start | bytes 393224 | tf_op jit(solution)/shard_map/ppermute | solution.py:41
  21.3 5.3 %shard_map.104 = (f32[256,1024]{1,0:T(8,128)S(1)}, f32[256,1024]{1,0:T(8,128)S(1)}, f32[256,256]{1,0:T(8,128)S(1)}) custom-call(bf16[256,256]{1,0:T(8,128)(2,1)S(1)} %copy-done.2, f32[24,256]{1,0:T(8,128)S(1)} %copy-done.3, f32[24,256]{1,0:T(8,128)S(1)} %collective-permute-done.3.refs_2_.refs_3_, bf16[256,1024]{1,0:T(8,128)(2,1)S(1)} %copy-done.1, ...), custom_call_target="tpu_custom_call" | custom-call | flops 345000000 | bytes 65536 | tf_op jit(solution)/shard_map/pallas_call | solution.py:89
  26.6 3.4 %collective-permute-start.8 = (bf16[256,1024]{1,0:T(8,128)(2,1)S(1)}, bf16[256,1024]{1,0:T(8,128)(2,1)S(1)}, u32[]{:S(2)}, u32[]{:S(2)}) collective-permute-start(bf16[256,1024]{1,0:T(8,128)(2,1)S(1)} %collective-permute-done.refs_0_), channel_id=1, source_target_pairs={{0,6},{8,14},{16,22},{24,30},{1,7},{9,15},{17,23},{25,31},{32,38},... | collective-permute-start | bytes 1572872 | tf_op jit(solution)/shard_map/ppermute | solution.py:41
  30.0 2.0 %collective-permute-start.10 = (bf16[256,1024]{1,0:T(8,128)(2,1)S(1)}, bf16[256,1024]{1,0:T(8,128)(2,1)S(1)}, u32[]{:S(2)}, u32[]{:S(2)}) collective-permute-start(bf16[256,1024]{1,0:T(8,128)(2,1)S(1)} %collective-permute-done.refs_0_), channel_id=1, source_target_pairs={{0,1},{8,9},{16,17},{24,25},{1,0},{9,8},{17,16},{25,24},{32,33},{4... | collective-permute-start | bytes 1572872 | tf_op jit(solution)/shard_map/ppermute | solution.py:41
  32.0 6.8 %shard_map.105 = (f32[256,1024]{1,0:T(8,128)S(1)}, f32[256,1024]{1,0:T(8,128)S(1)}, bf16[512,256]{1,0:T(8,128)(2,1)S(1)}) custom-call(bf16[256,256]{1,0:T(8,128)(2,1)S(1)} %collective-permute-done.4.refs_0_, bf16[256,256]{1,0:T(8,128)(2,1)S(1)} %collective-permute-done.5.refs_1_, f32[24,256]{1,0:T(8,128)S(1)} %copy-done.3, ...), custom_call_target="tpu_custom_call" | custom-call | flops 345000000 | bytes 65536 | tf_op jit(solution)/shard_map/pallas_call | solution.py:89
  40.0 5.2 %shard_map.106 = (f32[256,1024]{1,0:T(8,128)S(1)}, bf16[256,1024]{1,0:T(8,128)(2,1)S(1)}, f32[256,256]{1,0:T(8,128)S(1)}) custom-call(bf16[256,256]{1,0:T(8,128)(2,1)S(1)} %collective-permute-done.6.refs_0_, f32[24,256]{1,0:T(8,128)S(1)} %copy-done.3, f32[24,256]{1,0:T(8,128)S(1)} %collective-permute-done.3.refs_2_.refs_3_, bf16[256,1024]{1,0:T(8,128)(2,1)S(1)} %copy-done.1, ...), custom_call_target="tpu_custom_call" | custom-call | flops 1724999936 | bytes 65536 | tf_op jit(solution)/shard_map/pallas_call | solution.py:89
  45.3 1.7 %collective-permute-done.7.got_ref = bf16[512,256]{1,0:T(8,128)(2,1)S(1)} collective-permute-done((bf16[512,256]{1,0:T(8,128)(2,1)S(1)}, bf16[512,256]{1,0:T(8,128)(2,1)S(1)}, u32[]{:S(2)}, u32[]{:S(2)}) %collective-permute-start.7) | collective-permute-done | bytes 262176 | tf_op jit(solution)/shard_map/ppermute | solution.py:41
  47.0 2.5 %collective-permute-start.12 = (bf16[256,1024]{1,0:T(8,128)(2,1)S(1)}, bf16[256,1024]{1,0:T(8,128)(2,1)S(1)}, u32[]{:S(2)}, u32[]{:S(2)}) collective-permute-start(bf16[256,1024]{1,0:T(8,128)(2,1)S(1)} %get-tuple-element.78), channel_id=1, source_target_pairs={{0,8},{8,0},{16,24},{24,16},{1,9},{9,1},{17,25},{25,17},{32,40},{4... | collective-permute-start | bytes 1572872 | tf_op jit(solution)/shard_map/ppermute | solution.py:41
  49.5 2.7 %collective-permute-start.14 = (bf16[256,1024]{1,0:T(8,128)(2,1)S(1)}, bf16[256,1024]{1,0:T(8,128)(2,1)S(1)}, u32[]{:S(2)}, u32[]{:S(2)}) collective-permute-start(bf16[256,1024]{1,0:T(8,128)(2,1)S(1)} %collective-permute-done.10.refs_1_), channel_id=1, source_target_pairs={{0,6},{8,14},{16,22},{24,30},{1,7},{9,15},{17,23},{25,31},{32,38},... | collective-permute-start | bytes 1572872 | tf_op jit(solution)/shard_map/ppermute | solution.py:41
  53.2 4.2 %collective-permute-done.11.got_ref = bf16[512,256]{1,0:T(8,128)(2,1)S(1)} collective-permute-done((bf16[512,256]{1,0:T(8,128)(2,1)S(1)}, bf16[512,256]{1,0:T(8,128)(2,1)S(1)}, u32[]{:S(2)}, u32[]{:S(2)}) %collective-permute-start.11) | collective-permute-done | bytes 262176 | tf_op jit(solution)/shard_map/ppermute | solution.py:41
  58.3 1.4 %collective-permute-start.18 = (bf16[512,256]{1,0:T(8,128)(2,1)S(1)}, bf16[512,256]{1,0:T(8,128)(2,1)S(1)}, u32[]{:S(2)}, u32[]{:S(2)}) collective-permute-start(bf16[512,256]{1,0:T(8,128)(2,1)S(1)} %shard_map.108.refs_8_), channel_id=1, source_target_pairs={{0,64},{8,72},{16,80},{24,88},{1,65},{9,73},{17,81},{25,89},{32,96... | collective-permute-start | bytes 786440 | tf_op jit(solution)/shard_map/ppermute | solution.py:41
  60.5 3.6 %collective-permute-done.13.refs_7_ = bf16[256,1024]{1,0:T(8,128)(2,1)S(1)} collective-permute-done((bf16[256,1024]{1,0:T(8,128)(2,1)S(1)}, bf16[256,1024]{1,0:T(8,128)(2,1)S(1)}, u32[]{:S(2)}, u32[]{:S(2)}) %collective-permute-start.13) | collective-permute-done | bytes 524320 | tf_op jit(solution)/shard_map/ppermute | solution.py:41
  64.1 2.4 %collective-permute-start.15 = (bf16[256,1024]{1,0:T(8,128)(2,1)S(1)}, bf16[256,1024]{1,0:T(8,128)(2,1)S(1)}, u32[]{:S(2)}, u32[]{:S(2)}) collective-permute-start(bf16[256,1024]{1,0:T(8,128)(2,1)S(1)} %collective-permute-done.8.refs_2_), channel_id=1, source_target_pairs={{0,6},{8,14},{16,22},{24,30},{1,7},{9,15},{17,23},{25,31},{32,38},... | collective-permute-start | bytes 1572872 | tf_op jit(solution)/shard_map/ppermute | solution.py:41
  66.5 7.2 %collective-permute-done.19.refs_2_.refs_11_ = bf16[512,256]{1,0:T(8,128)(2,1)S(1)} collective-permute-done((bf16[512,256]{1,0:T(8,128)(2,1)S(1)}, bf16[512,256]{1,0:T(8,128)(2,1)S(1)}, u32[]{:S(2)}, u32[]{:S(2)}) %collective-permute-start.19) | collective-permute-done | bytes 262176 | tf_op jit(solution)/shard_map/ppermute | solution.py:41
  73.6 2.9 %collective-permute-done.15.refs_4_ = bf16[256,1024]{1,0:T(8,128)(2,1)S(1)} collective-permute-done((bf16[256,1024]{1,0:T(8,128)(2,1)S(1)}, bf16[256,1024]{1,0:T(8,128)(2,1)S(1)}, u32[]{:S(2)}, u32[]{:S(2)}) %collective-permute-start.15) | collective-permute-done | bytes 524320 | tf_op jit(solution)/shard_map/ppermute | solution.py:41
  76.5 3.0 %collective-permute-done.16.refs_5_ = bf16[256,1024]{1,0:T(8,128)(2,1)S(1)} collective-permute-done((bf16[256,1024]{1,0:T(8,128)(2,1)S(1)}, bf16[256,1024]{1,0:T(8,128)(2,1)S(1)}, u32[]{:S(2)}, u32[]{:S(2)}) %collective-permute-start.16) | collective-permute-done | bytes 524320 | tf_op jit(solution)/shard_map/ppermute | solution.py:41
  79.5 1.3 %shard_map.110 = (f32[256,512]{1,0:T(8,128)S(1)}, f32[256,512]{1,0:T(8,128)S(1)}) custom-call(bf16[256,1024]{1,0:T(8,128)(2,1)S(1)} %collective-permute-done.refs_0_, bf16[256,1024]{1,0:T(8,128)(2,1)S(1)} %collective-permute-done.10.refs_1_, bf16[256,1024]{1,0:T(8,128)(2,1)S(1)} %collective-permute-done.8.refs_2_, ...), custom_call_target="tpu_custom_call" | custom-call | flops 11500000 | bytes 65536 | tf_op jit(solution)/shard_map/pallas_call | solution.py:89
  80.8 2.6 %collective-permute-start.20 = (f32[256,512]{1,0:T(8,128)S(1)}, f32[256,512]{1,0:T(8,128)S(1)}, u32[]{:S(2)}, u32[]{:S(2)}) collective-permute-start(f32[256,512]{1,0:T(8,128)S(1)} %get-tuple-element.90), channel_id=1, source_target_pairs={{0,8},{8,0},{16,24},{24,16},{1,9},{9,1},{17,25},{25,17},{32,40},{4... | collective-permute-start | bytes 1572872 | tf_op jit(solution)/shard_map/ppermute | solution.py:41
  83.4 1.5 %collective-permute-done.20.got_ref = f32[256,512]{1,0:T(8,128)S(1)} collective-permute-done((f32[256,512]{1,0:T(8,128)S(1)}, f32[256,512]{1,0:T(8,128)S(1)}, u32[]{:S(2)}, u32[]{:S(2)}) %collective-permute-start.20) | collective-permute-done | bytes 524320 | tf_op jit(solution)/shard_map/ppermute | solution.py:41
  (36 shorter events, 8.3 us)
Async XLA Ops:
  0.6 19.0 %copy-start.1 = (bf16[256,1024]{1,0:T(8,128)(2,1)S(1)}, bf16[256,1024]{1,0:T(8,128)(2,1)}, u32[]{:S(2)}) copy-start(bf16[256,1024]{1,0:T(8,128)(2,1)} %refs_3_.3) | copy-start | bytes 1572868
  0.6 19.0 %copy-start = (bf16[256,1024]{1,0:T(8,128)(2,1)S(1)}, bf16[256,1024]{1,0:T(8,128)(2,1)}, u32[]{:S(2)}) copy-start(bf16[256,1024]{1,0:T(8,128)(2,1)} %refs_5_.3) | copy-start | bytes 1572868
  0.7 6.3 %collective-permute-start.1 = (bf16[256,1024]{1,0:T(8,128)(2,1)}, bf16[256,1024]{1,0:T(8,128)(2,1)S(1)}, u32[]{:S(2)}, u32[]{:S(2)}) collective-permute-start(bf16[256,1024]{1,0:T(8,128)(2,1)} %refs_3_.3), channel_id=1, source_target_pairs={{0,8},{8,0},{16,24},{24,16},{1,9},{9,1},{17,25},{25,17},{32,40},{4... | collective-permute-start | bytes 1572872 | tf_op jit(solution)/shard_map/ppermute | solution.py:41
  2.2 4.8 %collective-permute-start.2 = (bf16[256,1024]{1,0:T(8,128)(2,1)}, bf16[256,1024]{1,0:T(8,128)(2,1)S(1)}, u32[]{:S(2)}, u32[]{:S(2)}) collective-permute-start(bf16[256,1024]{1,0:T(8,128)(2,1)} %refs_5_.3), channel_id=1, source_target_pairs={{0,8},{8,0},{16,24},{24,16},{1,9},{9,1},{17,25},{25,17},{32,40},{4... | collective-permute-start | bytes 1572872 | tf_op jit(solution)/shard_map/ppermute | solution.py:41
  2.2 24.3 %collective-permute-start = (bf16[256,1024]{1,0:T(8,128)(2,1)}, bf16[256,1024]{1,0:T(8,128)(2,1)S(1)}, u32[]{:S(2)}, u32[]{:S(2)}) collective-permute-start(bf16[256,1024]{1,0:T(8,128)(2,1)} %param.14), channel_id=1, source_target_pairs={{0,0},{8,8},{16,1},{24,9},{1,16},{9,24},{17,17},{25,25},{32,2},{40... | collective-permute-start | bytes 1572872 | tf_op jit(solution)/shard_map/ppermute | solution.py:41
  6.9 1.6 %collective-permute-start.3 = (f32[24,256]{1,0:T(8,128)}, f32[24,256]{1,0:T(8,128)S(1)}, u32[]{:S(2)}, u32[]{:S(2)}) collective-permute-start(f32[24,256]{1,0:T(8,128)} %get-tuple-element.51.refs_1_.refs_2_), channel_id=1, source_target_pairs={{0,8},{8,0},{16,24},{24,16},{1,9},{9,1},{17,25},{25,17},{32,40},{4... | collective-permute-start | bytes 73736 | tf_op jit(solution)/shard_map/ppermute | solution.py:41
  8.5 18.1 %collective-permute-start.4 = (bf16[256,256]{1,0:T(8,128)(2,1)}, bf16[256,256]{1,0:T(8,128)(2,1)S(1)}, u32[]{:S(2)}, u32[]{:S(2)}) collective-permute-start(bf16[256,256]{1,0:T(8,128)(2,1)} %get-tuple-element.52.refs_0_), channel_id=1, source_target_pairs={{0,32},{8,40},{16,48},{24,56},{1,33},{9,41},{17,49},{25,57},{64,96... | collective-permute-start | bytes 393224 | tf_op jit(solution)/shard_map/ppermute | solution.py:41
  13.4 13.2 %collective-permute-start.5 = (bf16[256,256]{1,0:T(8,128)(2,1)}, bf16[256,256]{1,0:T(8,128)(2,1)S(1)}, u32[]{:S(2)}, u32[]{:S(2)}) collective-permute-start(bf16[256,256]{1,0:T(8,128)(2,1)} %get-tuple-element.52.refs_0_), channel_id=1, source_target_pairs={{0,48},{8,56},{16,32},{24,40},{1,49},{9,57},{17,33},{25,41},{64,11... | collective-permute-start | bytes 393224 | tf_op jit(solution)/shard_map/ppermute | solution.py:41
  17.4 9.2 %collective-permute-start.6 = (bf16[256,256]{1,0:T(8,128)(2,1)}, bf16[256,256]{1,0:T(8,128)(2,1)S(1)}, u32[]{:S(2)}, u32[]{:S(2)}) collective-permute-start(bf16[256,256]{1,0:T(8,128)(2,1)} %get-tuple-element.52.refs_0_), channel_id=1, source_target_pairs={{0,16},{8,24},{1,17},{9,25},{32,48},{40,56},{33,49},{41,57},{64,80... | collective-permute-start | bytes 393224 | tf_op jit(solution)/shard_map/ppermute | solution.py:41
  19.6 0.9 %copy-start.2 = (bf16[256,256]{1,0:T(8,128)(2,1)S(1)}, bf16[256,256]{1,0:T(8,128)(2,1)}, u32[]{:S(2)}) copy-start(bf16[256,256]{1,0:T(8,128)(2,1)} %get-tuple-element.52.refs_0_) | copy-start | bytes 393220
  26.6 20.3 %collective-permute-start.8 = (bf16[256,1024]{1,0:T(8,128)(2,1)S(1)}, bf16[256,1024]{1,0:T(8,128)(2,1)S(1)}, u32[]{:S(2)}, u32[]{:S(2)}) collective-permute-start(bf16[256,1024]{1,0:T(8,128)(2,1)S(1)} %collective-permute-done.refs_0_), channel_id=1, source_target_pairs={{0,6},{8,14},{16,22},{24,30},{1,7},{9,15},{17,23},{25,31},{32,38},... | collective-permute-start | bytes 1572872 | tf_op jit(solution)/shard_map/ppermute | solution.py:41
  30.0 17.0 %collective-permute-start.9 = (bf16[256,1024]{1,0:T(8,128)(2,1)S(1)}, bf16[256,1024]{1,0:T(8,128)(2,1)S(1)}, u32[]{:S(2)}, u32[]{:S(2)}) collective-permute-start(bf16[256,1024]{1,0:T(8,128)(2,1)S(1)} %collective-permute-done.refs_0_), channel_id=1, source_target_pairs={{0,2},{8,10},{16,18},{24,26},{1,3},{9,11},{17,19},{25,27},{32,34},... | collective-permute-start | bytes 1572872 | tf_op jit(solution)/shard_map/ppermute | solution.py:41
  30.0 17.0 %collective-permute-start.10 = (bf16[256,1024]{1,0:T(8,128)(2,1)S(1)}, bf16[256,1024]{1,0:T(8,128)(2,1)S(1)}, u32[]{:S(2)}, u32[]{:S(2)}) collective-permute-start(bf16[256,1024]{1,0:T(8,128)(2,1)S(1)} %collective-permute-done.refs_0_), channel_id=1, source_target_pairs={{0,1},{8,9},{16,17},{24,25},{1,0},{9,8},{17,16},{25,24},{32,33},{4... | collective-permute-start | bytes 1572872 | tf_op jit(solution)/shard_map/ppermute | solution.py:41
  38.7 8.2 %collective-permute-start.7 = (bf16[512,256]{1,0:T(8,128)(2,1)S(1)}, bf16[512,256]{1,0:T(8,128)(2,1)S(1)}, u32[]{:S(2)}, u32[]{:S(2)}) collective-permute-start(bf16[512,256]{1,0:T(8,128)(2,1)S(1)} %get-tuple-element.70), channel_id=1, source_target_pairs={{32,0},{40,8},{48,16},{56,24},{33,1},{41,9},{49,17},{57,25},{96,64... | collective-permute-start | bytes 786440 | tf_op jit(solution)/shard_map/ppermute | solution.py:41
  47.0 5.2 %collective-permute-start.12 = (bf16[256,1024]{1,0:T(8,128)(2,1)S(1)}, bf16[256,1024]{1,0:T(8,128)(2,1)S(1)}, u32[]{:S(2)}, u32[]{:S(2)}) collective-permute-start(bf16[256,1024]{1,0:T(8,128)(2,1)S(1)} %get-tuple-element.78), channel_id=1, source_target_pairs={{0,8},{8,0},{16,24},{24,16},{1,9},{9,1},{17,25},{25,17},{32,40},{4... | collective-permute-start | bytes 1572872 | tf_op jit(solution)/shard_map/ppermute | solution.py:41
  49.5 7.9 %collective-permute-start.11 = (bf16[512,256]{1,0:T(8,128)(2,1)S(1)}, bf16[512,256]{1,0:T(8,128)(2,1)S(1)}, u32[]{:S(2)}, u32[]{:S(2)}) collective-permute-start(bf16[512,256]{1,0:T(8,128)(2,1)S(1)} %get-tuple-element.74), channel_id=1, source_target_pairs={{0,16},{8,24},{16,0},{24,8},{1,17},{9,25},{17,1},{25,9},{32,48},{4... | collective-permute-start | bytes 786440 | tf_op jit(solution)/shard_map/ppermute | solution.py:41
  49.5 14.6 %collective-permute-start.13 = (bf16[256,1024]{1,0:T(8,128)(2,1)S(1)}, bf16[256,1024]{1,0:T(8,128)(2,1)S(1)}, u32[]{:S(2)}, u32[]{:S(2)}) collective-permute-start(bf16[256,1024]{1,0:T(8,128)(2,1)S(1)} %collective-permute-done.10.refs_1_), channel_id=1, source_target_pairs={{0,2},{8,10},{16,18},{24,26},{1,3},{9,11},{17,19},{25,27},{32,34},... | collective-permute-start | bytes 1572872 | tf_op jit(solution)/shard_map/ppermute | solution.py:41
  49.5 14.6 %collective-permute-start.14 = (bf16[256,1024]{1,0:T(8,128)(2,1)S(1)}, bf16[256,1024]{1,0:T(8,128)(2,1)S(1)}, u32[]{:S(2)}, u32[]{:S(2)}) collective-permute-start(bf16[256,1024]{1,0:T(8,128)(2,1)S(1)} %collective-permute-done.10.refs_1_), channel_id=1, source_target_pairs={{0,6},{8,14},{16,22},{24,30},{1,7},{9,15},{17,23},{25,31},{32,38},... | collective-permute-start | bytes 1572872 | tf_op jit(solution)/shard_map/ppermute | solution.py:41
  57.5 8.9 %collective-permute-start.17 = (bf16[512,256]{1,0:T(8,128)(2,1)S(1)}, bf16[512,256]{1,0:T(8,128)(2,1)S(1)}, u32[]{:S(2)}, u32[]{:S(2)}) collective-permute-start(bf16[512,256]{1,0:T(8,128)(2,1)S(1)} %shard_map.108.refs_8_), channel_id=1, source_target_pairs={{0,96},{8,104},{16,112},{24,120},{1,97},{9,105},{17,113},{25,121},... | collective-permute-start | bytes 786440 | tf_op jit(solution)/shard_map/ppermute | solution.py:41
  58.3 8.2 %collective-permute-start.18 = (bf16[512,256]{1,0:T(8,128)(2,1)S(1)}, bf16[512,256]{1,0:T(8,128)(2,1)S(1)}, u32[]{:S(2)}, u32[]{:S(2)}) collective-permute-start(bf16[512,256]{1,0:T(8,128)(2,1)S(1)} %shard_map.108.refs_8_), channel_id=1, source_target_pairs={{0,64},{8,72},{16,80},{24,88},{1,65},{9,73},{17,81},{25,89},{32,96... | collective-permute-start | bytes 786440 | tf_op jit(solution)/shard_map/ppermute | solution.py:41
  59.7 13.9 %collective-permute-start.19 = (bf16[512,256]{1,0:T(8,128)(2,1)S(1)}, bf16[512,256]{1,0:T(8,128)(2,1)S(1)}, u32[]{:S(2)}, u32[]{:S(2)}) collective-permute-start(bf16[512,256]{1,0:T(8,128)(2,1)S(1)} %shard_map.108.refs_8_), channel_id=1, source_target_pairs={{0,32},{8,40},{16,48},{24,56},{1,33},{9,41},{17,49},{25,57},{32,64... | collective-permute-start | bytes 786440 | tf_op jit(solution)/shard_map/ppermute | solution.py:41
  64.1 12.4 %collective-permute-start.15 = (bf16[256,1024]{1,0:T(8,128)(2,1)S(1)}, bf16[256,1024]{1,0:T(8,128)(2,1)S(1)}, u32[]{:S(2)}, u32[]{:S(2)}) collective-permute-start(bf16[256,1024]{1,0:T(8,128)(2,1)S(1)} %collective-permute-done.8.refs_2_), channel_id=1, source_target_pairs={{0,6},{8,14},{16,22},{24,30},{1,7},{9,15},{17,23},{25,31},{32,38},... | collective-permute-start | bytes 1572872 | tf_op jit(solution)/shard_map/ppermute | solution.py:41
  66.4 13.1 %collective-permute-start.16 = (bf16[256,1024]{1,0:T(8,128)(2,1)S(1)}, bf16[256,1024]{1,0:T(8,128)(2,1)S(1)}, u32[]{:S(2)}, u32[]{:S(2)}) collective-permute-start(bf16[256,1024]{1,0:T(8,128)(2,1)S(1)} %collective-permute-done.13.refs_7_), channel_id=1, source_target_pairs={{0,2},{8,10},{16,18},{24,26},{1,3},{9,11},{17,19},{25,27},{32,34},... | collective-permute-start | bytes 1572872 | tf_op jit(solution)/shard_map/ppermute | solution.py:41
  80.8 4.1 %collective-permute-start.20 = (f32[256,512]{1,0:T(8,128)S(1)}, f32[256,512]{1,0:T(8,128)S(1)}, u32[]{:S(2)}, u32[]{:S(2)}) collective-permute-start(f32[256,512]{1,0:T(8,128)S(1)} %get-tuple-element.90), channel_id=1, source_target_pairs={{0,8},{8,0},{16,24},{24,16},{1,9},{9,1},{17,25},{25,17},{32,40},{4... | collective-permute-start | bytes 1572872 | tf_op jit(solution)/shard_map/ppermute | solution.py:41
  (1 other events, 0.7 us)

commit v7 on v6

--- a/solution.py
+++ b/solution.py
@@ -17,7 +17,8 @@
 LOG2E = math.log2(math.e)
 AXES = ("ctx", "tp")
 DOCS = 16
-STEP_HEADS = 4
+STEP_HEADS = 8
+GROUP = 16
 
 f32 = jnp.float32
 bf16 = jnp.bfloat16
@@ -174,7 +175,7 @@
         offset = lax.broadcasted_iota(jnp.int32, (ROWS, 1), 0)
         key_pos = jnp.concatenate([(me ^ flip) * ROWS + offset for flip in flips], axis=0)
         lane = lax.broadcasted_iota(jnp.int32, (1, ROWS), 1)
-        dk = dv = None
+        tiles = []
         for i in range(2):
             query_pos = (me ^ i) * ROWS + lane
             first = aux_refs[i][2 * HEADS : 2 * HEADS + 1, :].astype(jnp.int32)
@@ -182,13 +183,22 @@
             for j in range(STEP_HEADS):
                 h = step * STEP_HEADS + j
                 cols = pl.ds(pl.multiple_of(h * HD, HD), HD)
-                q = q_refs[i][:, cols]
-                do = do_refs[i][:, cols]
                 dots = aux_refs[i][pl.ds(h, 1), :]
                 norm = aux_refs[i][pl.ds(HEADS + h, 1), :]
-                p = jnp.where(visible, jnp.exp2(nt(k, q) * (SCALE * LOG2E) - norm), 0.0)
-                ds = (p * (nt(v, do) - dots)).astype(bf16)
-                dv_term, dk_term, dq = nn(p.astype(bf16), do), nn(ds, q), tn(ds, k)
+                tiles.append((i, cols, visible, dots, norm))
+        dk = dv = None
+        for start in range(0, len(tiles), GROUP):
+            group = tiles[start : start + GROUP]
+            products = []
+            for i, cols, *_ in group:
+                q, do = q_refs[i][:, cols], do_refs[i][:, cols]
+                products.append((q, do, nt(k, q), nt(v, do)))
+            low = []
+            for (_, _, visible, dots, norm), (_, _, score, prob_grad) in zip(group, products):
+                p = jnp.where(visible, jnp.exp2(score * (SCALE * LOG2E) - norm), 0.0)
+                low.append((p.astype(bf16), (p * (prob_grad - dots)).astype(bf16)))
+            for (i, cols, *_), (q, do, *_), (p, ds) in zip(group, products, low):
+                dv_term, dk_term, dq = nn(p, do), nn(ds, q), tn(ds, k)
                 dv = dv_term if dv is None else dv + dv_term
                 dk = dk_term if dk is None else dk + dk_term
                 if has_sum:
@@ -211,7 +221,7 @@
             struct((keys, 2 * HD), dkv_type),
         ),
         [*kv, *aux, *q, *do, *(sums or ())],
-        megabytes=14,
+        megabytes=24,
         micros=micros,
         scratch_shapes=[pltpu.VMEM((keys, HD), f32)] * 2,
     )

time: 86.2 us -> 83.6 us (0.970)
  Pallas kernels: 22.7 us -> 17.3 us
  starting transfers between devices: 34.5 us -> 37.1 us
    pallas_call x9, Pallas kernels: 22.7 us -> 17.3 us  [call(): pl.pallas_call(kernel, out_shape=out_shape, compiler_params=pltpu.Compile...]
    ppermute x21, starting transfers between devices: 34.5 us -> 37.1 us  [send(): return lax.ppermute(value, AXES, route(target))]
  transfers between devices with their start and end apart: 21 -> 21, of which waited for: 8 -> 9; matrix products, arithmetic and copies ran while one was open for 1% -> 1% of each run, Pallas kernels for 24% -> 18%
where the time goes in v7:
time: 83.6 us; the launch traced here: 82.6 us
  starting transfers between devices  37.1 us (44%)
  waiting for transfers between devices  24.7 us (30%)
  Pallas kernels  17.3 us (21%)
  local copies, waits for them, and re-layouts  1.67 us (2%)
  other arithmetic  0.95 us (1%)
    ppermute x21, starting transfers between devices, send(): return lax.ppermute(value, AXES, route(target))  37.1 us
    ppermute x21, waiting for transfers between devices, send(): return lax.ppermute(value, AXES, route(target))  24.7 us
    pallas_call x9, Pallas kernels, call(): pl.pallas_call(kernel, out_shape=out_shape, compiler_params=pltpu.Compile...  17.3 us
    unnamed x10, local copies, waits for them, and re-layouts  1.67 us
  transfers between devices with their start and end apart: 21, of which 9 were waited for; matrix products, arithmetic and copies ran while one was open for 1% of the time, Pallas kernels for 18%

profile of v7, /device:TPU:1, one launch (start us, length us, event | category | flops | bytes accessed | tf_op | source)
XLA Modules:
  0.0 82.6 jit_solution(1560499827149636379)
XLA Ops:
  0.7 1.5 %collective-permute-start.1 = (bf16[256,1024]{1,0:T(8,128)(2,1)}, bf16[256,1024]{1,0:T(8,128)(2,1)S(1)}, u32[]{:S(2)}, u32[]{:S(2)}) collective-permute-start(bf16[256,1024]{1,0:T(8,128)(2,1)} %refs_3_.3), channel_id=1, source_target_pairs={{0,8},{8,0},{16,24},{24,16},{1,9},{9,1},{17,25},{25,17},{32,40},{4... | collective-permute-start | bytes 1572872 | tf_op jit(solution)/shard_map/ppermute | solution.py:42
  2.2 1.7 %collective-permute-start = (bf16[256,1024]{1,0:T(8,128)(2,1)}, bf16[256,1024]{1,0:T(8,128)(2,1)S(1)}, u32[]{:S(2)}, u32[]{:S(2)}) collective-permute-start(bf16[256,1024]{1,0:T(8,128)(2,1)} %param.14), channel_id=1, source_target_pairs={{0,0},{8,8},{16,1},{24,9},{1,16},{9,24},{17,17},{25,25},{32,2},{40... | collective-permute-start | bytes 1572872 | tf_op jit(solution)/shard_map/ppermute | solution.py:42
  3.9 3.0 %shard_map.103 = (bf16[256,256]{1,0:T(8,128)(2,1)}, f32[24,256]{1,0:T(8,128)}) custom-call(s32[16]{0:T(128)} %lengths_ref.1, bf16[256,128]{1,0:T(8,128)(2,1)} %k_any.1, bf16[256,128]{1,0:T(8,128)(2,1)} %v_any.1, bf16[256,1024]{1,0:T(8,128)(2,1)} %refs_5_.3, bf16[256,1024]{1,0:T(8,128)(2,1)} %out_any.1, f32[8,256]{1,0:T(8,128)} %ln_any.1), custom_call_target="tpu_custom_call" | custom-call | flops 345000000 | bytes 65536 | tf_op jit(solution)/shard_map/pallas_call | solution.py:90
  8.5 4.9 %collective-permute-start.4 = (bf16[256,256]{1,0:T(8,128)(2,1)}, bf16[256,256]{1,0:T(8,128)(2,1)S(1)}, u32[]{:S(2)}, u32[]{:S(2)}) collective-permute-start(bf16[256,256]{1,0:T(8,128)(2,1)} %get-tuple-element.52.refs_0_), channel_id=1, source_target_pairs={{0,32},{8,40},{16,48},{24,56},{1,33},{9,41},{17,49},{25,57},{64,96... | collective-permute-start | bytes 393224 | tf_op jit(solution)/shard_map/ppermute | solution.py:42
  13.4 4.0 %collective-permute-start.5 = (bf16[256,256]{1,0:T(8,128)(2,1)}, bf16[256,256]{1,0:T(8,128)(2,1)S(1)}, u32[]{:S(2)}, u32[]{:S(2)}) collective-permute-start(bf16[256,256]{1,0:T(8,128)(2,1)} %get-tuple-element.52.refs_0_), channel_id=1, source_target_pairs={{0,48},{8,56},{16,32},{24,40},{1,49},{9,57},{17,33},{25,41},{64,11... | collective-permute-start | bytes 393224 | tf_op jit(solution)/shard_map/ppermute | solution.py:42
  17.4 2.2 %collective-permute-start.6 = (bf16[256,256]{1,0:T(8,128)(2,1)}, bf16[256,256]{1,0:T(8,128)(2,1)S(1)}, u32[]{:S(2)}, u32[]{:S(2)}) collective-permute-start(bf16[256,256]{1,0:T(8,128)(2,1)} %get-tuple-element.52.refs_0_), channel_id=1, source_target_pairs={{0,16},{8,24},{1,17},{9,25},{32,48},{40,56},{33,49},{41,57},{64,80... | collective-permute-start | bytes 393224 | tf_op jit(solution)/shard_map/ppermute | solution.py:42
  21.3 3.0 %shard_map.104 = (f32[256,1024]{1,0:T(8,128)S(1)}, f32[256,1024]{1,0:T(8,128)S(1)}, f32[256,256]{1,0:T(8,128)S(1)}) custom-call(bf16[256,256]{1,0:T(8,128)(2,1)S(1)} %copy-done.2, f32[24,256]{1,0:T(8,128)S(1)} %copy-done.3, f32[24,256]{1,0:T(8,128)S(1)} %collective-permute-done.3.refs_2_.refs_3_, bf16[256,1024]{1,0:T(8,128)(2,1)S(1)} %copy-done.1, ...), custom_call_target="tpu_custom_call" | custom-call | flops 345000000 | bytes 65536 | tf_op jit(solution)/shard_map/pallas_call | solution.py:90
  24.3 3.4 %collective-permute-start.8 = (bf16[256,1024]{1,0:T(8,128)(2,1)S(1)}, bf16[256,1024]{1,0:T(8,128)(2,1)S(1)}, u32[]{:S(2)}, u32[]{:S(2)}) collective-permute-start(bf16[256,1024]{1,0:T(8,128)(2,1)S(1)} %collective-permute-done.refs_0_), channel_id=1, source_target_pairs={{0,6},{8,14},{16,22},{24,30},{1,7},{9,15},{17,23},{25,31},{32,38},... | collective-permute-start | bytes 1572872 | tf_op jit(solution)/shard_map/ppermute | solution.py:42
  27.7 1.9 %collective-permute-start.10 = (bf16[256,1024]{1,0:T(8,128)(2,1)S(1)}, bf16[256,1024]{1,0:T(8,128)(2,1)S(1)}, u32[]{:S(2)}, u32[]{:S(2)}) collective-permute-start(bf16[256,1024]{1,0:T(8,128)(2,1)S(1)} %collective-permute-done.refs_0_), channel_id=1, source_target_pairs={{0,1},{8,9},{16,17},{24,25},{1,0},{9,8},{17,16},{25,24},{32,33},{4... | collective-permute-start | bytes 1572872 | tf_op jit(solution)/shard_map/ppermute | solution.py:42
  29.7 5.8 %shard_map.105 = (f32[256,1024]{1,0:T(8,128)S(1)}, f32[256,1024]{1,0:T(8,128)S(1)}, bf16[512,256]{1,0:T(8,128)(2,1)S(1)}) custom-call(bf16[256,256]{1,0:T(8,128)(2,1)S(1)} %collective-permute-done.4.refs_0_, bf16[256,256]{1,0:T(8,128)(2,1)S(1)} %collective-permute-done.5.refs_1_, f32[24,256]{1,0:T(8,128)S(1)} %copy-done.4, ...), custom_call_target="tpu_custom_call" | custom-call | flops 345000000 | bytes 65536 | tf_op jit(solution)/shard_map/pallas_call | solution.py:90
  35.5 1.5 %collective-permute-start.7 = (bf16[512,256]{1,0:T(8,128)(2,1)S(1)}, bf16[512,256]{1,0:T(8,128)(2,1)S(1)}, u32[]{:S(2)}, u32[]{:S(2)}) collective-permute-start(bf16[512,256]{1,0:T(8,128)(2,1)S(1)} %get-tuple-element.70), channel_id=1, source_target_pairs={{32,0},{40,8},{48,16},{56,24},{33,1},{41,9},{49,17},{57,25},{96,64... | collective-permute-start | bytes 786440 | tf_op jit(solution)/shard_map/ppermute | solution.py:42
  37.0 3.0 %shard_map.106 = (f32[256,1024]{1,0:T(8,128)S(1)}, bf16[256,1024]{1,0:T(8,128)(2,1)S(1)}, f32[256,256]{1,0:T(8,128)S(1)}) custom-call(bf16[256,256]{1,0:T(8,128)(2,1)S(1)} %collective-permute-done.6.refs_0_, f32[24,256]{1,0:T(8,128)S(1)} %copy-done.4, f32[24,256]{1,0:T(8,128)S(1)} %collective-permute-done.3.refs_2_.refs_3_, bf16[256,1024]{1,0:T(8,128)(2,1)S(1)} %copy-done.1, ...), custom_call_target="tpu_custom_call" | custom-call | flops 1724999936 | bytes 65536 | tf_op jit(solution)/shard_map/pallas_call | solution.py:90
  40.0 3.7 %collective-permute-done.7.got_ref = bf16[512,256]{1,0:T(8,128)(2,1)S(1)} collective-permute-done((bf16[512,256]{1,0:T(8,128)(2,1)S(1)}, bf16[512,256]{1,0:T(8,128)(2,1)S(1)}, u32[]{:S(2)}, u32[]{:S(2)}) %collective-permute-start.7) | collective-permute-done | bytes 262176 | tf_op jit(solution)/shard_map/ppermute | solution.py:42
  43.8 2.5 %collective-permute-start.12 = (bf16[256,1024]{1,0:T(8,128)(2,1)S(1)}, bf16[256,1024]{1,0:T(8,128)(2,1)S(1)}, u32[]{:S(2)}, u32[]{:S(2)}) collective-permute-start(bf16[256,1024]{1,0:T(8,128)(2,1)S(1)} %get-tuple-element.78), channel_id=1, source_target_pairs={{0,8},{8,0},{16,24},{24,16},{1,9},{9,1},{17,25},{25,17},{32,40},{4... | collective-permute-start | bytes 1572872 | tf_op jit(solution)/shard_map/ppermute | solution.py:42
  46.3 1.4 %collective-permute-start.13 = (bf16[256,1024]{1,0:T(8,128)(2,1)S(1)}, bf16[256,1024]{1,0:T(8,128)(2,1)S(1)}, u32[]{:S(2)}, u32[]{:S(2)}) collective-permute-start(bf16[256,1024]{1,0:T(8,128)(2,1)S(1)} %collective-permute-done.10.refs_1_), channel_id=1, source_target_pairs={{0,2},{8,10},{16,18},{24,26},{1,3},{9,11},{17,19},{25,27},{32,34},... | collective-permute-start | bytes 1572872 | tf_op jit(solution)/shard_map/ppermute | solution.py:42
  49.9 4.2 %collective-permute-done.11.got_ref = bf16[512,256]{1,0:T(8,128)(2,1)S(1)} collective-permute-done((bf16[512,256]{1,0:T(8,128)(2,1)S(1)}, bf16[512,256]{1,0:T(8,128)(2,1)S(1)}, u32[]{:S(2)}, u32[]{:S(2)}) %collective-permute-start.11) | collective-permute-done | bytes 262176 | tf_op jit(solution)/shard_map/ppermute | solution.py:42
  54.3 2.7 %collective-permute-start.17 = (bf16[512,256]{1,0:T(8,128)(2,1)S(1)}, bf16[512,256]{1,0:T(8,128)(2,1)S(1)}, u32[]{:S(2)}, u32[]{:S(2)}) collective-permute-start(bf16[512,256]{1,0:T(8,128)(2,1)S(1)} %shard_map.108.refs_8_), channel_id=1, source_target_pairs={{0,96},{8,104},{16,112},{24,120},{1,97},{9,105},{17,113},{25,121},... | collective-permute-start | bytes 786440 | tf_op jit(solution)/shard_map/ppermute | solution.py:42
  57.0 1.8 %collective-permute-start.18 = (bf16[512,256]{1,0:T(8,128)(2,1)S(1)}, bf16[512,256]{1,0:T(8,128)(2,1)S(1)}, u32[]{:S(2)}, u32[]{:S(2)}) collective-permute-start(bf16[512,256]{1,0:T(8,128)(2,1)S(1)} %shard_map.108.refs_8_), channel_id=1, source_target_pairs={{0,64},{8,72},{16,80},{24,88},{1,65},{9,73},{17,81},{25,89},{32,96... | collective-permute-start | bytes 786440 | tf_op jit(solution)/shard_map/ppermute | solution.py:42
  60.8 2.4 %collective-permute-start.15 = (bf16[256,1024]{1,0:T(8,128)(2,1)S(1)}, bf16[256,1024]{1,0:T(8,128)(2,1)S(1)}, u32[]{:S(2)}, u32[]{:S(2)}) collective-permute-start(bf16[256,1024]{1,0:T(8,128)(2,1)S(1)} %collective-permute-done.8.refs_2_), channel_id=1, source_target_pairs={{0,6},{8,14},{16,22},{24,30},{1,7},{9,15},{17,23},{25,31},{32,38},... | collective-permute-start | bytes 1572872 | tf_op jit(solution)/shard_map/ppermute | solution.py:42
  63.1 2.1 %collective-permute-done.18.refs_1_.refs_10_ = bf16[512,256]{1,0:T(8,128)(2,1)S(1)} collective-permute-done((bf16[512,256]{1,0:T(8,128)(2,1)S(1)}, bf16[512,256]{1,0:T(8,128)(2,1)S(1)}, u32[]{:S(2)}, u32[]{:S(2)}) %collective-permute-start.18) | collective-permute-done | bytes 262176 | tf_op jit(solution)/shard_map/ppermute | solution.py:42
  65.2 7.2 %collective-permute-done.19.refs_2_.refs_11_ = bf16[512,256]{1,0:T(8,128)(2,1)S(1)} collective-permute-done((bf16[512,256]{1,0:T(8,128)(2,1)S(1)}, bf16[512,256]{1,0:T(8,128)(2,1)S(1)}, u32[]{:S(2)}, u32[]{:S(2)}) %collective-permute-start.19) | collective-permute-done | bytes 262176 | tf_op jit(solution)/shard_map/ppermute | solution.py:42
  73.0 3.1 %collective-permute-done.16.refs_5_ = bf16[256,1024]{1,0:T(8,128)(2,1)S(1)} collective-permute-done((bf16[256,1024]{1,0:T(8,128)(2,1)S(1)}, bf16[256,1024]{1,0:T(8,128)(2,1)S(1)}, u32[]{:S(2)}, u32[]{:S(2)}) %collective-permute-start.16) | collective-permute-done | bytes 524320 | tf_op jit(solution)/shard_map/ppermute | solution.py:42
  77.4 2.7 %collective-permute-start.20 = (f32[256,512]{1,0:T(8,128)S(1)}, f32[256,512]{1,0:T(8,128)S(1)}, u32[]{:S(2)}, u32[]{:S(2)}) collective-permute-start(f32[256,512]{1,0:T(8,128)S(1)} %get-tuple-element.90), channel_id=1, source_target_pairs={{0,8},{8,0},{16,24},{24,16},{1,9},{9,1},{17,25},{25,17},{32,40},{4... | collective-permute-start | bytes 1572872 | tf_op jit(solution)/shard_map/ppermute | solution.py:42
  80.1 1.5 %collective-permute-done.20.got_ref = f32[256,512]{1,0:T(8,128)S(1)} collective-permute-done((f32[256,512]{1,0:T(8,128)S(1)}, f32[256,512]{1,0:T(8,128)S(1)}, u32[]{:S(2)}, u32[]{:S(2)}) %collective-permute-start.20) | collective-permute-done | bytes 524320 | tf_op jit(solution)/shard_map/ppermute | solution.py:42
  (38 shorter events, 10.6 us)
Async XLA Ops:
  0.6 19.0 %copy-start.1 = (bf16[256,1024]{1,0:T(8,128)(2,1)S(1)}, bf16[256,1024]{1,0:T(8,128)(2,1)}, u32[]{:S(2)}) copy-start(bf16[256,1024]{1,0:T(8,128)(2,1)} %refs_3_.3) | copy-start | bytes 1572868
  0.6 19.0 %copy-start = (bf16[256,1024]{1,0:T(8,128)(2,1)S(1)}, bf16[256,1024]{1,0:T(8,128)(2,1)}, u32[]{:S(2)}) copy-start(bf16[256,1024]{1,0:T(8,128)(2,1)} %refs_5_.3) | copy-start | bytes 1572868
  0.7 6.3 %collective-permute-start.1 = (bf16[256,1024]{1,0:T(8,128)(2,1)}, bf16[256,1024]{1,0:T(8,128)(2,1)S(1)}, u32[]{:S(2)}, u32[]{:S(2)}) collective-permute-start(bf16[256,1024]{1,0:T(8,128)(2,1)} %refs_3_.3), channel_id=1, source_target_pairs={{0,8},{8,0},{16,24},{24,16},{1,9},{9,1},{17,25},{25,17},{32,40},{4... | collective-permute-start | bytes 1572872 | tf_op jit(solution)/shard_map/ppermute | solution.py:42
  2.2 4.8 %collective-permute-start.2 = (bf16[256,1024]{1,0:T(8,128)(2,1)}, bf16[256,1024]{1,0:T(8,128)(2,1)S(1)}, u32[]{:S(2)}, u32[]{:S(2)}) collective-permute-start(bf16[256,1024]{1,0:T(8,128)(2,1)} %refs_5_.3), channel_id=1, source_target_pairs={{0,8},{8,0},{16,24},{24,16},{1,9},{9,1},{17,25},{25,17},{32,40},{4... | collective-permute-start | bytes 1572872 | tf_op jit(solution)/shard_map/ppermute | solution.py:42
  2.2 22.1 %collective-permute-start = (bf16[256,1024]{1,0:T(8,128)(2,1)}, bf16[256,1024]{1,0:T(8,128)(2,1)S(1)}, u32[]{:S(2)}, u32[]{:S(2)}) collective-permute-start(bf16[256,1024]{1,0:T(8,128)(2,1)} %param.14), channel_id=1, source_target_pairs={{0,0},{8,8},{16,1},{24,9},{1,16},{9,24},{17,17},{25,25},{32,2},{40... | collective-permute-start | bytes 1572872 | tf_op jit(solution)/shard_map/ppermute | solution.py:42
  6.9 1.6 %collective-permute-start.3 = (f32[24,256]{1,0:T(8,128)}, f32[24,256]{1,0:T(8,128)S(1)}, u32[]{:S(2)}, u32[]{:S(2)}) collective-permute-start(f32[24,256]{1,0:T(8,128)} %get-tuple-element.51.refs_1_.refs_2_), channel_id=1, source_target_pairs={{0,8},{8,0},{16,24},{24,16},{1,9},{9,1},{17,25},{25,17},{32,40},{4... | collective-permute-start | bytes 73736 | tf_op jit(solution)/shard_map/ppermute | solution.py:42
  8.5 15.8 %collective-permute-start.4 = (bf16[256,256]{1,0:T(8,128)(2,1)}, bf16[256,256]{1,0:T(8,128)(2,1)S(1)}, u32[]{:S(2)}, u32[]{:S(2)}) collective-permute-start(bf16[256,256]{1,0:T(8,128)(2,1)} %get-tuple-element.52.refs_0_), channel_id=1, source_target_pairs={{0,32},{8,40},{16,48},{24,56},{1,33},{9,41},{17,49},{25,57},{64,96... | collective-permute-start | bytes 393224 | tf_op jit(solution)/shard_map/ppermute | solution.py:42
  13.4 10.9 %collective-permute-start.5 = (bf16[256,256]{1,0:T(8,128)(2,1)}, bf16[256,256]{1,0:T(8,128)(2,1)S(1)}, u32[]{:S(2)}, u32[]{:S(2)}) collective-permute-start(bf16[256,256]{1,0:T(8,128)(2,1)} %get-tuple-element.52.refs_0_), channel_id=1, source_target_pairs={{0,48},{8,56},{16,32},{24,40},{1,49},{9,57},{17,33},{25,41},{64,11... | collective-permute-start | bytes 393224 | tf_op jit(solution)/shard_map/ppermute | solution.py:42
  17.4 6.9 %collective-permute-start.6 = (bf16[256,256]{1,0:T(8,128)(2,1)}, bf16[256,256]{1,0:T(8,128)(2,1)S(1)}, u32[]{:S(2)}, u32[]{:S(2)}) collective-permute-start(bf16[256,256]{1,0:T(8,128)(2,1)} %get-tuple-element.52.refs_0_), channel_id=1, source_target_pairs={{0,16},{8,24},{1,17},{9,25},{32,48},{40,56},{33,49},{41,57},{64,80... | collective-permute-start | bytes 393224 | tf_op jit(solution)/shard_map/ppermute | solution.py:42
  21.3 8.4 %copy-start.4 = (f32[24,256]{1,0:T(8,128)S(1)}, f32[24,256]{1,0:T(8,128)}, u32[]{:S(2)}) copy-start(f32[24,256]{1,0:T(8,128)} %get-tuple-element.51.refs_1_.refs_2_) | copy-start | bytes 73732
  24.3 19.4 %collective-permute-start.8 = (bf16[256,1024]{1,0:T(8,128)(2,1)S(1)}, bf16[256,1024]{1,0:T(8,128)(2,1)S(1)}, u32[]{:S(2)}, u32[]{:S(2)}) collective-permute-start(bf16[256,1024]{1,0:T(8,128)(2,1)S(1)} %collective-permute-done.refs_0_), channel_id=1, source_target_pairs={{0,6},{8,14},{16,22},{24,30},{1,7},{9,15},{17,23},{25,31},{32,38},... | collective-permute-start | bytes 1572872 | tf_op jit(solution)/shard_map/ppermute | solution.py:42
  27.7 16.0 %collective-permute-start.9 = (bf16[256,1024]{1,0:T(8,128)(2,1)S(1)}, bf16[256,1024]{1,0:T(8,128)(2,1)S(1)}, u32[]{:S(2)}, u32[]{:S(2)}) collective-permute-start(bf16[256,1024]{1,0:T(8,128)(2,1)S(1)} %collective-permute-done.refs_0_), channel_id=1, source_target_pairs={{0,2},{8,10},{16,18},{24,26},{1,3},{9,11},{17,19},{25,27},{32,34},... | collective-permute-start | bytes 1572872 | tf_op jit(solution)/shard_map/ppermute | solution.py:42
  27.7 16.0 %collective-permute-start.10 = (bf16[256,1024]{1,0:T(8,128)(2,1)S(1)}, bf16[256,1024]{1,0:T(8,128)(2,1)S(1)}, u32[]{:S(2)}, u32[]{:S(2)}) collective-permute-start(bf16[256,1024]{1,0:T(8,128)(2,1)S(1)} %collective-permute-done.refs_0_), channel_id=1, source_target_pairs={{0,1},{8,9},{16,17},{24,25},{1,0},{9,8},{17,16},{25,24},{32,33},{4... | collective-permute-start | bytes 1572872 | tf_op jit(solution)/shard_map/ppermute | solution.py:42
  35.5 8.2 %collective-permute-start.7 = (bf16[512,256]{1,0:T(8,128)(2,1)S(1)}, bf16[512,256]{1,0:T(8,128)(2,1)S(1)}, u32[]{:S(2)}, u32[]{:S(2)}) collective-permute-start(bf16[512,256]{1,0:T(8,128)(2,1)S(1)} %get-tuple-element.70), channel_id=1, source_target_pairs={{32,0},{40,8},{48,16},{56,24},{33,1},{41,9},{49,17},{57,25},{96,64... | collective-permute-start | bytes 786440 | tf_op jit(solution)/shard_map/ppermute | solution.py:42
  43.8 5.2 %collective-permute-start.12 = (bf16[256,1024]{1,0:T(8,128)(2,1)S(1)}, bf16[256,1024]{1,0:T(8,128)(2,1)S(1)}, u32[]{:S(2)}, u32[]{:S(2)}) collective-permute-start(bf16[256,1024]{1,0:T(8,128)(2,1)S(1)} %get-tuple-element.78), channel_id=1, source_target_pairs={{0,8},{8,0},{16,24},{24,16},{1,9},{9,1},{17,25},{25,17},{32,40},{4... | collective-permute-start | bytes 1572872 | tf_op jit(solution)/shard_map/ppermute | solution.py:42
  46.3 7.9 %collective-permute-start.11 = (bf16[512,256]{1,0:T(8,128)(2,1)S(1)}, bf16[512,256]{1,0:T(8,128)(2,1)S(1)}, u32[]{:S(2)}, u32[]{:S(2)}) collective-permute-start(bf16[512,256]{1,0:T(8,128)(2,1)S(1)} %get-tuple-element.74), channel_id=1, source_target_pairs={{0,16},{8,24},{16,0},{24,8},{1,17},{9,25},{17,1},{25,9},{32,48},{4... | collective-permute-start | bytes 786440 | tf_op jit(solution)/shard_map/ppermute | solution.py:42
  46.3 14.5 %collective-permute-start.13 = (bf16[256,1024]{1,0:T(8,128)(2,1)S(1)}, bf16[256,1024]{1,0:T(8,128)(2,1)S(1)}, u32[]{:S(2)}, u32[]{:S(2)}) collective-permute-start(bf16[256,1024]{1,0:T(8,128)(2,1)S(1)} %collective-permute-done.10.refs_1_), channel_id=1, source_target_pairs={{0,2},{8,10},{16,18},{24,26},{1,3},{9,11},{17,19},{25,27},{32,34},... | collective-permute-start | bytes 1572872 | tf_op jit(solution)/shard_map/ppermute | solution.py:42
  47.7 13.1 %collective-permute-start.14 = (bf16[256,1024]{1,0:T(8,128)(2,1)S(1)}, bf16[256,1024]{1,0:T(8,128)(2,1)S(1)}, u32[]{:S(2)}, u32[]{:S(2)}) collective-permute-start(bf16[256,1024]{1,0:T(8,128)(2,1)S(1)} %collective-permute-done.10.refs_1_), channel_id=1, source_target_pairs={{0,6},{8,14},{16,22},{24,30},{1,7},{9,15},{17,23},{25,31},{32,38},... | collective-permute-start | bytes 1572872 | tf_op jit(solution)/shard_map/ppermute | solution.py:42
  54.3 8.8 %collective-permute-start.17 = (bf16[512,256]{1,0:T(8,128)(2,1)S(1)}, bf16[512,256]{1,0:T(8,128)(2,1)S(1)}, u32[]{:S(2)}, u32[]{:S(2)}) collective-permute-start(bf16[512,256]{1,0:T(8,128)(2,1)S(1)} %shard_map.108.refs_8_), channel_id=1, source_target_pairs={{0,96},{8,104},{16,112},{24,120},{1,97},{9,105},{17,113},{25,121},... | collective-permute-start | bytes 786440 | tf_op jit(solution)/shard_map/ppermute | solution.py:42
  57.0 8.2 %collective-permute-start.18 = (bf16[512,256]{1,0:T(8,128)(2,1)S(1)}, bf16[512,256]{1,0:T(8,128)(2,1)S(1)}, u32[]{:S(2)}, u32[]{:S(2)}) collective-permute-start(bf16[512,256]{1,0:T(8,128)(2,1)S(1)} %shard_map.108.refs_8_), channel_id=1, source_target_pairs={{0,64},{8,72},{16,80},{24,88},{1,65},{9,73},{17,81},{25,89},{32,96... | collective-permute-start | bytes 786440 | tf_op jit(solution)/shard_map/ppermute | solution.py:42
  58.8 13.6 %collective-permute-start.19 = (bf16[512,256]{1,0:T(8,128)(2,1)S(1)}, bf16[512,256]{1,0:T(8,128)(2,1)S(1)}, u32[]{:S(2)}, u32[]{:S(2)}) collective-permute-start(bf16[512,256]{1,0:T(8,128)(2,1)S(1)} %shard_map.108.refs_8_), channel_id=1, source_target_pairs={{0,32},{8,40},{16,48},{24,56},{1,33},{9,41},{17,49},{25,57},{32,64... | collective-permute-start | bytes 786440 | tf_op jit(solution)/shard_map/ppermute | solution.py:42
  60.8 12.2 %collective-permute-start.15 = (bf16[256,1024]{1,0:T(8,128)(2,1)S(1)}, bf16[256,1024]{1,0:T(8,128)(2,1)S(1)}, u32[]{:S(2)}, u32[]{:S(2)}) collective-permute-start(bf16[256,1024]{1,0:T(8,128)(2,1)S(1)} %collective-permute-done.8.refs_2_), channel_id=1, source_target_pairs={{0,6},{8,14},{16,22},{24,30},{1,7},{9,15},{17,23},{25,31},{32,38},... | collective-permute-start | bytes 1572872 | tf_op jit(solution)/shard_map/ppermute | solution.py:42
  63.1 12.9 %collective-permute-start.16 = (bf16[256,1024]{1,0:T(8,128)(2,1)S(1)}, bf16[256,1024]{1,0:T(8,128)(2,1)S(1)}, u32[]{:S(2)}, u32[]{:S(2)}) collective-permute-start(bf16[256,1024]{1,0:T(8,128)(2,1)S(1)} %collective-permute-done.13.refs_7_), channel_id=1, source_target_pairs={{0,2},{8,10},{16,18},{24,26},{1,3},{9,11},{17,19},{25,27},{32,34},... | collective-permute-start | bytes 1572872 | tf_op jit(solution)/shard_map/ppermute | solution.py:42
  77.4 4.2 %collective-permute-start.20 = (f32[256,512]{1,0:T(8,128)S(1)}, f32[256,512]{1,0:T(8,128)S(1)}, u32[]{:S(2)}, u32[]{:S(2)}) collective-permute-start(f32[256,512]{1,0:T(8,128)S(1)} %get-tuple-element.90), channel_id=1, source_target_pairs={{0,8},{8,0},{16,24},{24,16},{1,9},{9,1},{17,25},{25,17},{32,40},{4... | collective-permute-start | bytes 1572872 | tf_op jit(solution)/shard_map/ppermute | solution.py:42
  (2 other events, 1.7 us)

commit v8 on v7

--- a/solution.py
+++ b/solution.py
@@ -296,18 +296,19 @@
     behind, ahead, across = shifted(dx=-1), shifted(dx=1), shifted(dz=2)
     *dqs, dkv_own = attention((0,), (kv,), aux, q, do, None, (f32, f32), f32, 0.3)
     l_own, dkv_own, kv_y, kv_far, kv_zl, *dqs = together(l_own, dkv_own, kv_y, kv_far, kv_zl, *dqs)
-    own_1, own_3, other_0 = (send(l_own, t) for t in (behind, ahead, across))
+    other_0, own_1, own_3 = (send(l_own, t) for t in (across, behind, ahead))
 
     *dqs, dkv_far = attention((4, 6), (kv_y, kv_far), aux, q, do, dqs, (f32, f32), bf16, 0.3)
     got_far = send(dkv_far, within_half(2, False))
     dq_own, dq_par, dkv_zl = attention((2,), (kv_zl,), aux, q, do, dqs, (f32, bf16), f32, 1.5)
-    dq_own, dq_par, dkv_zl, got_far, l_own, own_1, own_3, other_0 = together(
-        dq_own, dq_par, dkv_zl, got_far, l_own, own_1, own_3, other_0
-    )
+    other_0, own_1, own_3, l_own, got_far, dkv_zl, dq_own, dq_par = together(
+        other_0, own_1, own_3, l_own, got_far, dkv_zl, dq_own, dq_par
+    )
+
     pair = (2 * ROWS, 2 * HD)
     dkv, dkv_low = call(add_kernel, (struct(pair, f32), struct(pair, bf16)), (dkv_own, dkv_zl, got_far))
     got_zl = send(dkv_low, other_zl)
-    other_0, dq_par, _ = together(other_0, dq_par, dkv_low)
+    dq_par, _ = together(dq_par, dkv_low)
     other_3, other_1 = send(other_0, ahead), send(other_0, behind)
     dq_got = send(dq_par, other_core)
     query_grad = ((dq_own + dq_got.astype(f32)) * SCALE).astype(bf16)

time: 83.6 us -> 83.6 us (level)
  no operation moved by 1% of the time
where the time goes in v8:
time: 83.6 us; the launch traced here: 82.6 us
  starting transfers between devices  37.1 us (44%)
  waiting for transfers between devices  24.7 us (30%)
  Pallas kernels  17.3 us (21%)
  local copies, waits for them, and re-layouts  1.67 us (2%)
  other arithmetic  0.95 us (1%)
    ppermute x21, starting transfers between devices, send(): return lax.ppermute(value, AXES, route(target))  37.1 us
    ppermute x21, waiting for transfers between devices, send(): return lax.ppermute(value, AXES, route(target))  24.7 us
    pallas_call x9, Pallas kernels, call(): pl.pallas_call(kernel, out_shape=out_shape, compiler_params=pltpu.Compile...  17.3 us
    unnamed x10, local copies, waits for them, and re-layouts  1.67 us
  transfers between devices with their start and end apart: 21, of which 9 were waited for; matrix products, arithmetic and copies ran while one was open for 1% of the time, Pallas kernels for 18%

profile of v8, /device:TPU:1, one launch (start us, length us, event | category | flops | bytes accessed | tf_op | source)
XLA Modules:
  0.0 82.6 jit_solution(13990761796717113462)
XLA Ops:
  0.7 1.5 %collective-permute-start.1 = (bf16[256,1024]{1,0:T(8,128)(2,1)}, bf16[256,1024]{1,0:T(8,128)(2,1)S(1)}, u32[]{:S(2)}, u32[]{:S(2)}) collective-permute-start(bf16[256,1024]{1,0:T(8,128)(2,1)} %refs_3_.3), channel_id=1, source_target_pairs={{0,8},{8,0},{16,24},{24,16},{1,9},{9,1},{17,25},{25,17},{32,40},{4... | collective-permute-start | bytes 1572872 | tf_op jit(solution)/shard_map/ppermute | solution.py:42
  2.2 1.7 %collective-permute-start = (bf16[256,1024]{1,0:T(8,128)(2,1)}, bf16[256,1024]{1,0:T(8,128)(2,1)S(1)}, u32[]{:S(2)}, u32[]{:S(2)}) collective-permute-start(bf16[256,1024]{1,0:T(8,128)(2,1)} %param.14), channel_id=1, source_target_pairs={{0,0},{8,8},{16,1},{24,9},{1,16},{9,24},{17,17},{25,25},{32,2},{40... | collective-permute-start | bytes 1572872 | tf_op jit(solution)/shard_map/ppermute | solution.py:42
  3.9 3.0 %shard_map.103 = (bf16[256,256]{1,0:T(8,128)(2,1)}, f32[24,256]{1,0:T(8,128)}) custom-call(s32[16]{0:T(128)} %lengths_ref.1, bf16[256,128]{1,0:T(8,128)(2,1)} %k_any.1, bf16[256,128]{1,0:T(8,128)(2,1)} %v_any.1, bf16[256,1024]{1,0:T(8,128)(2,1)} %refs_5_.3, bf16[256,1024]{1,0:T(8,128)(2,1)} %out_any.1, f32[8,256]{1,0:T(8,128)} %ln_any.1), custom_call_target="tpu_custom_call" | custom-call | flops 345000000 | bytes 65536 | tf_op jit(solution)/shard_map/pallas_call | solution.py:90
  8.5 4.9 %collective-permute-start.4 = (bf16[256,256]{1,0:T(8,128)(2,1)}, bf16[256,256]{1,0:T(8,128)(2,1)S(1)}, u32[]{:S(2)}, u32[]{:S(2)}) collective-permute-start(bf16[256,256]{1,0:T(8,128)(2,1)} %get-tuple-element.51.refs_0_), channel_id=1, source_target_pairs={{0,32},{8,40},{16,48},{24,56},{1,33},{9,41},{17,49},{25,57},{64,96... | collective-permute-start | bytes 393224 | tf_op jit(solution)/shard_map/ppermute | solution.py:42
  13.4 4.0 %collective-permute-start.5 = (bf16[256,256]{1,0:T(8,128)(2,1)}, bf16[256,256]{1,0:T(8,128)(2,1)S(1)}, u32[]{:S(2)}, u32[]{:S(2)}) collective-permute-start(bf16[256,256]{1,0:T(8,128)(2,1)} %get-tuple-element.51.refs_0_), channel_id=1, source_target_pairs={{0,48},{8,56},{16,32},{24,40},{1,49},{9,57},{17,33},{25,41},{64,11... | collective-permute-start | bytes 393224 | tf_op jit(solution)/shard_map/ppermute | solution.py:42
  17.4 2.2 %collective-permute-start.6 = (bf16[256,256]{1,0:T(8,128)(2,1)}, bf16[256,256]{1,0:T(8,128)(2,1)S(1)}, u32[]{:S(2)}, u32[]{:S(2)}) collective-permute-start(bf16[256,256]{1,0:T(8,128)(2,1)} %get-tuple-element.51.refs_0_), channel_id=1, source_target_pairs={{0,16},{8,24},{1,17},{9,25},{32,48},{40,56},{33,49},{41,57},{64,80... | collective-permute-start | bytes 393224 | tf_op jit(solution)/shard_map/ppermute | solution.py:42
  21.3 3.0 %shard_map.104 = (f32[256,1024]{1,0:T(8,128)S(1)}, f32[256,1024]{1,0:T(8,128)S(1)}, f32[256,256]{1,0:T(8,128)S(1)}) custom-call(bf16[256,256]{1,0:T(8,128)(2,1)S(1)} %copy-done.2, f32[24,256]{1,0:T(8,128)S(1)} %copy-done.3, f32[24,256]{1,0:T(8,128)S(1)} %collective-permute-done.3.refs_2_.refs_3_, bf16[256,1024]{1,0:T(8,128)(2,1)S(1)} %copy-done.1, ...), custom_call_target="tpu_custom_call" | custom-call | flops 345000000 | bytes 65536 | tf_op jit(solution)/shard_map/pallas_call | solution.py:90
  24.3 2.0 %collective-permute-start.7 = (bf16[256,1024]{1,0:T(8,128)(2,1)S(1)}, bf16[256,1024]{1,0:T(8,128)(2,1)S(1)}, u32[]{:S(2)}, u32[]{:S(2)}) collective-permute-start(bf16[256,1024]{1,0:T(8,128)(2,1)S(1)} %collective-permute-done.refs_0_), channel_id=1, source_target_pairs={{0,1},{8,9},{16,17},{24,25},{1,0},{9,8},{17,16},{25,24},{32,33},{4... | collective-permute-start | bytes 1572872 | tf_op jit(solution)/shard_map/ppermute | solution.py:42
  26.4 3.3 %collective-permute-start.8 = (bf16[256,1024]{1,0:T(8,128)(2,1)S(1)}, bf16[256,1024]{1,0:T(8,128)(2,1)S(1)}, u32[]{:S(2)}, u32[]{:S(2)}) collective-permute-start(bf16[256,1024]{1,0:T(8,128)(2,1)S(1)} %collective-permute-done.refs_0_), channel_id=1, source_target_pairs={{0,6},{8,14},{16,22},{24,30},{1,7},{9,15},{17,23},{25,31},{32,38},... | collective-permute-start | bytes 1572872 | tf_op jit(solution)/shard_map/ppermute | solution.py:42
  29.7 5.8 %shard_map.105 = (f32[256,1024]{1,0:T(8,128)S(1)}, f32[256,1024]{1,0:T(8,128)S(1)}, bf16[512,256]{1,0:T(8,128)(2,1)S(1)}) custom-call(bf16[256,256]{1,0:T(8,128)(2,1)S(1)} %collective-permute-done.4.refs_0_, bf16[256,256]{1,0:T(8,128)(2,1)S(1)} %collective-permute-done.5.refs_1_, f32[24,256]{1,0:T(8,128)S(1)} %copy-done.4, ...), custom_call_target="tpu_custom_call" | custom-call | flops 345000000 | bytes 65536 | tf_op jit(solution)/shard_map/pallas_call | solution.py:90
  35.5 1.5 %collective-permute-start.10 = (bf16[512,256]{1,0:T(8,128)(2,1)S(1)}, bf16[512,256]{1,0:T(8,128)(2,1)S(1)}, u32[]{:S(2)}, u32[]{:S(2)}) collective-permute-start(bf16[512,256]{1,0:T(8,128)(2,1)S(1)} %get-tuple-element.64), channel_id=1, source_target_pairs={{32,0},{40,8},{48,16},{56,24},{33,1},{41,9},{49,17},{57,25},{96,64... | collective-permute-start | bytes 786440 | tf_op jit(solution)/shard_map/ppermute | solution.py:42
  37.0 3.0 %shard_map.106 = (f32[256,1024]{1,0:T(8,128)S(1)}, bf16[256,1024]{1,0:T(8,128)(2,1)S(1)}, f32[256,256]{1,0:T(8,128)S(1)}) custom-call(bf16[256,256]{1,0:T(8,128)(2,1)S(1)} %collective-permute-done.6.refs_0_, f32[24,256]{1,0:T(8,128)S(1)} %copy-done.4, f32[24,256]{1,0:T(8,128)S(1)} %collective-permute-done.3.refs_2_.refs_3_, bf16[256,1024]{1,0:T(8,128)(2,1)S(1)} %copy-done.1, ...), custom_call_target="tpu_custom_call" | custom-call | flops 1724999936 | bytes 65536 | tf_op jit(solution)/shard_map/pallas_call | solution.py:90
  40.0 3.7 %collective-permute-done.10.got_ref = bf16[512,256]{1,0:T(8,128)(2,1)S(1)} collective-permute-done((bf16[512,256]{1,0:T(8,128)(2,1)S(1)}, bf16[512,256]{1,0:T(8,128)(2,1)S(1)}, u32[]{:S(2)}, u32[]{:S(2)}) %collective-permute-start.10) | collective-permute-done | bytes 262176 | tf_op jit(solution)/shard_map/ppermute | solution.py:42
  43.8 2.5 %collective-permute-start.12 = (bf16[256,1024]{1,0:T(8,128)(2,1)S(1)}, bf16[256,1024]{1,0:T(8,128)(2,1)S(1)}, u32[]{:S(2)}, u32[]{:S(2)}) collective-permute-start(bf16[256,1024]{1,0:T(8,128)(2,1)S(1)} %get-tuple-element.76), channel_id=1, source_target_pairs={{0,8},{8,0},{16,24},{24,16},{1,9},{9,1},{17,25},{25,17},{32,40},{4... | collective-permute-start | bytes 1572872 | tf_op jit(solution)/shard_map/ppermute | solution.py:42
  46.3 1.4 %collective-permute-start.13 = (bf16[256,1024]{1,0:T(8,128)(2,1)S(1)}, bf16[256,1024]{1,0:T(8,128)(2,1)S(1)}, u32[]{:S(2)}, u32[]{:S(2)}) collective-permute-start(bf16[256,1024]{1,0:T(8,128)(2,1)S(1)} %collective-permute-done.7.refs_1_), channel_id=1, source_target_pairs={{0,2},{8,10},{16,18},{24,26},{1,3},{9,11},{17,19},{25,27},{32,34},... | collective-permute-start | bytes 1572872 | tf_op jit(solution)/shard_map/ppermute | solution.py:42
  49.9 4.2 %collective-permute-done.11.got_ref = bf16[512,256]{1,0:T(8,128)(2,1)S(1)} collective-permute-done((bf16[512,256]{1,0:T(8,128)(2,1)S(1)}, bf16[512,256]{1,0:T(8,128)(2,1)S(1)}, u32[]{:S(2)}, u32[]{:S(2)}) %collective-permute-start.11) | collective-permute-done | bytes 262176 | tf_op jit(solution)/shard_map/ppermute | solution.py:42
  54.3 2.6 %collective-permute-start.17 = (bf16[512,256]{1,0:T(8,128)(2,1)S(1)}, bf16[512,256]{1,0:T(8,128)(2,1)S(1)}, u32[]{:S(2)}, u32[]{:S(2)}) collective-permute-start(bf16[512,256]{1,0:T(8,128)(2,1)S(1)} %shard_map.108.refs_8_), channel_id=1, source_target_pairs={{0,96},{8,104},{16,112},{24,120},{1,97},{9,105},{17,113},{25,121},... | collective-permute-start | bytes 786440 | tf_op jit(solution)/shard_map/ppermute | solution.py:42
  56.9 1.9 %collective-permute-start.18 = (bf16[512,256]{1,0:T(8,128)(2,1)S(1)}, bf16[512,256]{1,0:T(8,128)(2,1)S(1)}, u32[]{:S(2)}, u32[]{:S(2)}) collective-permute-start(bf16[512,256]{1,0:T(8,128)(2,1)S(1)} %shard_map.108.refs_8_), channel_id=1, source_target_pairs={{0,64},{8,72},{16,80},{24,88},{1,65},{9,73},{17,81},{25,89},{32,96... | collective-permute-start | bytes 786440 | tf_op jit(solution)/shard_map/ppermute | solution.py:42
  60.8 2.4 %collective-permute-start.15 = (bf16[256,1024]{1,0:T(8,128)(2,1)S(1)}, bf16[256,1024]{1,0:T(8,128)(2,1)S(1)}, u32[]{:S(2)}, u32[]{:S(2)}) collective-permute-start(bf16[256,1024]{1,0:T(8,128)(2,1)S(1)} %collective-permute-done.8.refs_2_), channel_id=1, source_target_pairs={{0,6},{8,14},{16,22},{24,30},{1,7},{9,15},{17,23},{25,31},{32,38},... | collective-permute-start | bytes 1572872 | tf_op jit(solution)/shard_map/ppermute | solution.py:42
  63.2 1.9 %collective-permute-done.18.refs_1_.refs_10_ = bf16[512,256]{1,0:T(8,128)(2,1)S(1)} collective-permute-done((bf16[512,256]{1,0:T(8,128)(2,1)S(1)}, bf16[512,256]{1,0:T(8,128)(2,1)S(1)}, u32[]{:S(2)}, u32[]{:S(2)}) %collective-permute-start.18) | collective-permute-done | bytes 262176 | tf_op jit(solution)/shard_map/ppermute | solution.py:42
  65.1 7.2 %collective-permute-done.19.refs_2_.refs_11_ = bf16[512,256]{1,0:T(8,128)(2,1)S(1)} collective-permute-done((bf16[512,256]{1,0:T(8,128)(2,1)S(1)}, bf16[512,256]{1,0:T(8,128)(2,1)S(1)}, u32[]{:S(2)}, u32[]{:S(2)}) %collective-permute-start.19) | collective-permute-done | bytes 262176 | tf_op jit(solution)/shard_map/ppermute | solution.py:42
  73.0 3.1 %collective-permute-done.16.refs_5_ = bf16[256,1024]{1,0:T(8,128)(2,1)S(1)} collective-permute-done((bf16[256,1024]{1,0:T(8,128)(2,1)S(1)}, bf16[256,1024]{1,0:T(8,128)(2,1)S(1)}, u32[]{:S(2)}, u32[]{:S(2)}) %collective-permute-start.16) | collective-permute-done | bytes 524320 | tf_op jit(solution)/shard_map/ppermute | solution.py:42
  77.4 2.7 %collective-permute-start.20 = (f32[256,512]{1,0:T(8,128)S(1)}, f32[256,512]{1,0:T(8,128)S(1)}, u32[]{:S(2)}, u32[]{:S(2)}) collective-permute-start(f32[256,512]{1,0:T(8,128)S(1)} %get-tuple-element.88), channel_id=1, source_target_pairs={{0,8},{8,0},{16,24},{24,16},{1,9},{9,1},{17,25},{25,17},{32,40},{4... | collective-permute-start | bytes 1572872 | tf_op jit(solution)/shard_map/ppermute | solution.py:42
  80.1 1.5 %collective-permute-done.20.got_ref = f32[256,512]{1,0:T(8,128)S(1)} collective-permute-done((f32[256,512]{1,0:T(8,128)S(1)}, f32[256,512]{1,0:T(8,128)S(1)}, u32[]{:S(2)}, u32[]{:S(2)}) %collective-permute-start.20) | collective-permute-done | bytes 524320 | tf_op jit(solution)/shard_map/ppermute | solution.py:42
  (38 shorter events, 10.8 us)
Async XLA Ops:
  0.6 19.0 %copy-start.1 = (bf16[256,1024]{1,0:T(8,128)(2,1)S(1)}, bf16[256,1024]{1,0:T(8,128)(2,1)}, u32[]{:S(2)}) copy-start(bf16[256,1024]{1,0:T(8,128)(2,1)} %refs_3_.3) | copy-start | bytes 1572868
  0.6 19.0 %copy-start = (bf16[256,1024]{1,0:T(8,128)(2,1)S(1)}, bf16[256,1024]{1,0:T(8,128)(2,1)}, u32[]{:S(2)}) copy-start(bf16[256,1024]{1,0:T(8,128)(2,1)} %refs_5_.3) | copy-start | bytes 1572868
  0.7 6.3 %collective-permute-start.1 = (bf16[256,1024]{1,0:T(8,128)(2,1)}, bf16[256,1024]{1,0:T(8,128)(2,1)S(1)}, u32[]{:S(2)}, u32[]{:S(2)}) collective-permute-start(bf16[256,1024]{1,0:T(8,128)(2,1)} %refs_3_.3), channel_id=1, source_target_pairs={{0,8},{8,0},{16,24},{24,16},{1,9},{9,1},{17,25},{25,17},{32,40},{4... | collective-permute-start | bytes 1572872 | tf_op jit(solution)/shard_map/ppermute | solution.py:42
  2.2 4.8 %collective-permute-start.2 = (bf16[256,1024]{1,0:T(8,128)(2,1)}, bf16[256,1024]{1,0:T(8,128)(2,1)S(1)}, u32[]{:S(2)}, u32[]{:S(2)}) collective-permute-start(bf16[256,1024]{1,0:T(8,128)(2,1)} %refs_5_.3), channel_id=1, source_target_pairs={{0,8},{8,0},{16,24},{24,16},{1,9},{9,1},{17,25},{25,17},{32,40},{4... | collective-permute-start | bytes 1572872 | tf_op jit(solution)/shard_map/ppermute | solution.py:42
  2.2 22.1 %collective-permute-start = (bf16[256,1024]{1,0:T(8,128)(2,1)}, bf16[256,1024]{1,0:T(8,128)(2,1)S(1)}, u32[]{:S(2)}, u32[]{:S(2)}) collective-permute-start(bf16[256,1024]{1,0:T(8,128)(2,1)} %param.14), channel_id=1, source_target_pairs={{0,0},{8,8},{16,1},{24,9},{1,16},{9,24},{17,17},{25,25},{32,2},{40... | collective-permute-start | bytes 1572872 | tf_op jit(solution)/shard_map/ppermute | solution.py:42
  6.9 1.6 %collective-permute-start.3 = (f32[24,256]{1,0:T(8,128)}, f32[24,256]{1,0:T(8,128)S(1)}, u32[]{:S(2)}, u32[]{:S(2)}) collective-permute-start(f32[24,256]{1,0:T(8,128)} %get-tuple-element.50.refs_1_.refs_2_), channel_id=1, source_target_pairs={{0,8},{8,0},{16,24},{24,16},{1,9},{9,1},{17,25},{25,17},{32,40},{4... | collective-permute-start | bytes 73736 | tf_op jit(solution)/shard_map/ppermute | solution.py:42
  8.5 15.8 %collective-permute-start.4 = (bf16[256,256]{1,0:T(8,128)(2,1)}, bf16[256,256]{1,0:T(8,128)(2,1)S(1)}, u32[]{:S(2)}, u32[]{:S(2)}) collective-permute-start(bf16[256,256]{1,0:T(8,128)(2,1)} %get-tuple-element.51.refs_0_), channel_id=1, source_target_pairs={{0,32},{8,40},{16,48},{24,56},{1,33},{9,41},{17,49},{25,57},{64,96... | collective-permute-start | bytes 393224 | tf_op jit(solution)/shard_map/ppermute | solution.py:42
  13.4 10.9 %collective-permute-start.5 = (bf16[256,256]{1,0:T(8,128)(2,1)}, bf16[256,256]{1,0:T(8,128)(2,1)S(1)}, u32[]{:S(2)}, u32[]{:S(2)}) collective-permute-start(bf16[256,256]{1,0:T(8,128)(2,1)} %get-tuple-element.51.refs_0_), channel_id=1, source_target_pairs={{0,48},{8,56},{16,32},{24,40},{1,49},{9,57},{17,33},{25,41},{64,11... | collective-permute-start | bytes 393224 | tf_op jit(solution)/shard_map/ppermute | solution.py:42
  17.4 6.9 %collective-permute-start.6 = (bf16[256,256]{1,0:T(8,128)(2,1)}, bf16[256,256]{1,0:T(8,128)(2,1)S(1)}, u32[]{:S(2)}, u32[]{:S(2)}) collective-permute-start(bf16[256,256]{1,0:T(8,128)(2,1)} %get-tuple-element.51.refs_0_), channel_id=1, source_target_pairs={{0,16},{8,24},{1,17},{9,25},{32,48},{40,56},{33,49},{41,57},{64,80... | collective-permute-start | bytes 393224 | tf_op jit(solution)/shard_map/ppermute | solution.py:42
  21.3 8.4 %copy-start.4 = (f32[24,256]{1,0:T(8,128)S(1)}, f32[24,256]{1,0:T(8,128)}, u32[]{:S(2)}) copy-start(f32[24,256]{1,0:T(8,128)} %get-tuple-element.50.refs_1_.refs_2_) | copy-start | bytes 73732
  24.3 19.4 %collective-permute-start.7 = (bf16[256,1024]{1,0:T(8,128)(2,1)S(1)}, bf16[256,1024]{1,0:T(8,128)(2,1)S(1)}, u32[]{:S(2)}, u32[]{:S(2)}) collective-permute-start(bf16[256,1024]{1,0:T(8,128)(2,1)S(1)} %collective-permute-done.refs_0_), channel_id=1, source_target_pairs={{0,1},{8,9},{16,17},{24,25},{1,0},{9,8},{17,16},{25,24},{32,33},{4... | collective-permute-start | bytes 1572872 | tf_op jit(solution)/shard_map/ppermute | solution.py:42
  26.4 17.4 %collective-permute-start.8 = (bf16[256,1024]{1,0:T(8,128)(2,1)S(1)}, bf16[256,1024]{1,0:T(8,128)(2,1)S(1)}, u32[]{:S(2)}, u32[]{:S(2)}) collective-permute-start(bf16[256,1024]{1,0:T(8,128)(2,1)S(1)} %collective-permute-done.refs_0_), channel_id=1, source_target_pairs={{0,6},{8,14},{16,22},{24,30},{1,7},{9,15},{17,23},{25,31},{32,38},... | collective-permute-start | bytes 1572872 | tf_op jit(solution)/shard_map/ppermute | solution.py:42
  29.7 14.1 %collective-permute-start.9 = (bf16[256,1024]{1,0:T(8,128)(2,1)S(1)}, bf16[256,1024]{1,0:T(8,128)(2,1)S(1)}, u32[]{:S(2)}, u32[]{:S(2)}) collective-permute-start(bf16[256,1024]{1,0:T(8,128)(2,1)S(1)} %collective-permute-done.refs_0_), channel_id=1, source_target_pairs={{0,2},{8,10},{16,18},{24,26},{1,3},{9,11},{17,19},{25,27},{32,34},... | collective-permute-start | bytes 1572872 | tf_op jit(solution)/shard_map/ppermute | solution.py:42
  35.5 8.2 %collective-permute-start.10 = (bf16[512,256]{1,0:T(8,128)(2,1)S(1)}, bf16[512,256]{1,0:T(8,128)(2,1)S(1)}, u32[]{:S(2)}, u32[]{:S(2)}) collective-permute-start(bf16[512,256]{1,0:T(8,128)(2,1)S(1)} %get-tuple-element.64), channel_id=1, source_target_pairs={{32,0},{40,8},{48,16},{56,24},{33,1},{41,9},{49,17},{57,25},{96,64... | collective-permute-start | bytes 786440 | tf_op jit(solution)/shard_map/ppermute | solution.py:42
  43.8 5.2 %collective-permute-start.12 = (bf16[256,1024]{1,0:T(8,128)(2,1)S(1)}, bf16[256,1024]{1,0:T(8,128)(2,1)S(1)}, u32[]{:S(2)}, u32[]{:S(2)}) collective-permute-start(bf16[256,1024]{1,0:T(8,128)(2,1)S(1)} %get-tuple-element.76), channel_id=1, source_target_pairs={{0,8},{8,0},{16,24},{24,16},{1,9},{9,1},{17,25},{25,17},{32,40},{4... | collective-permute-start | bytes 1572872 | tf_op jit(solution)/shard_map/ppermute | solution.py:42
  46.3 7.9 %collective-permute-start.11 = (bf16[512,256]{1,0:T(8,128)(2,1)S(1)}, bf16[512,256]{1,0:T(8,128)(2,1)S(1)}, u32[]{:S(2)}, u32[]{:S(2)}) collective-permute-start(bf16[512,256]{1,0:T(8,128)(2,1)S(1)} %get-tuple-element.73), channel_id=1, source_target_pairs={{0,16},{8,24},{16,0},{24,8},{1,17},{9,25},{17,1},{25,9},{32,48},{4... | collective-permute-start | bytes 786440 | tf_op jit(solution)/shard_map/ppermute | solution.py:42
  46.3 14.5 %collective-permute-start.13 = (bf16[256,1024]{1,0:T(8,128)(2,1)S(1)}, bf16[256,1024]{1,0:T(8,128)(2,1)S(1)}, u32[]{:S(2)}, u32[]{:S(2)}) collective-permute-start(bf16[256,1024]{1,0:T(8,128)(2,1)S(1)} %collective-permute-done.7.refs_1_), channel_id=1, source_target_pairs={{0,2},{8,10},{16,18},{24,26},{1,3},{9,11},{17,19},{25,27},{32,34},... | collective-permute-start | bytes 1572872 | tf_op jit(solution)/shard_map/ppermute | solution.py:42
  47.7 13.1 %collective-permute-start.14 = (bf16[256,1024]{1,0:T(8,128)(2,1)S(1)}, bf16[256,1024]{1,0:T(8,128)(2,1)S(1)}, u32[]{:S(2)}, u32[]{:S(2)}) collective-permute-start(bf16[256,1024]{1,0:T(8,128)(2,1)S(1)} %collective-permute-done.7.refs_1_), channel_id=1, source_target_pairs={{0,6},{8,14},{16,22},{24,30},{1,7},{9,15},{17,23},{25,31},{32,38},... | collective-permute-start | bytes 1572872 | tf_op jit(solution)/shard_map/ppermute | solution.py:42
  54.3 8.8 %collective-permute-start.17 = (bf16[512,256]{1,0:T(8,128)(2,1)S(1)}, bf16[512,256]{1,0:T(8,128)(2,1)S(1)}, u32[]{:S(2)}, u32[]{:S(2)}) collective-permute-start(bf16[512,256]{1,0:T(8,128)(2,1)S(1)} %shard_map.108.refs_8_), channel_id=1, source_target_pairs={{0,96},{8,104},{16,112},{24,120},{1,97},{9,105},{17,113},{25,121},... | collective-permute-start | bytes 786440 | tf_op jit(solution)/shard_map/ppermute | solution.py:42
  56.9 8.2 %collective-permute-start.18 = (bf16[512,256]{1,0:T(8,128)(2,1)S(1)}, bf16[512,256]{1,0:T(8,128)(2,1)S(1)}, u32[]{:S(2)}, u32[]{:S(2)}) collective-permute-start(bf16[512,256]{1,0:T(8,128)(2,1)S(1)} %shard_map.108.refs_8_), channel_id=1, source_target_pairs={{0,64},{8,72},{16,80},{24,88},{1,65},{9,73},{17,81},{25,89},{32,96... | collective-permute-start | bytes 786440 | tf_op jit(solution)/shard_map/ppermute | solution.py:42
  58.8 13.4 %collective-permute-start.19 = (bf16[512,256]{1,0:T(8,128)(2,1)S(1)}, bf16[512,256]{1,0:T(8,128)(2,1)S(1)}, u32[]{:S(2)}, u32[]{:S(2)}) collective-permute-start(bf16[512,256]{1,0:T(8,128)(2,1)S(1)} %shard_map.108.refs_8_), channel_id=1, source_target_pairs={{0,32},{8,40},{16,48},{24,56},{1,33},{9,41},{17,49},{25,57},{32,64... | collective-permute-start | bytes 786440 | tf_op jit(solution)/shard_map/ppermute | solution.py:42
  60.8 12.2 %collective-permute-start.15 = (bf16[256,1024]{1,0:T(8,128)(2,1)S(1)}, bf16[256,1024]{1,0:T(8,128)(2,1)S(1)}, u32[]{:S(2)}, u32[]{:S(2)}) collective-permute-start(bf16[256,1024]{1,0:T(8,128)(2,1)S(1)} %collective-permute-done.8.refs_2_), channel_id=1, source_target_pairs={{0,6},{8,14},{16,22},{24,30},{1,7},{9,15},{17,23},{25,31},{32,38},... | collective-permute-start | bytes 1572872 | tf_op jit(solution)/shard_map/ppermute | solution.py:42
  63.1 12.9 %collective-permute-start.16 = (bf16[256,1024]{1,0:T(8,128)(2,1)S(1)}, bf16[256,1024]{1,0:T(8,128)(2,1)S(1)}, u32[]{:S(2)}, u32[]{:S(2)}) collective-permute-start(bf16[256,1024]{1,0:T(8,128)(2,1)S(1)} %collective-permute-done.13.refs_7_), channel_id=1, source_target_pairs={{0,2},{8,10},{16,18},{24,26},{1,3},{9,11},{17,19},{25,27},{32,34},... | collective-permute-start | bytes 1572872 | tf_op jit(solution)/shard_map/ppermute | solution.py:42
  77.4 4.2 %collective-permute-start.20 = (f32[256,512]{1,0:T(8,128)S(1)}, f32[256,512]{1,0:T(8,128)S(1)}, u32[]{:S(2)}, u32[]{:S(2)}) collective-permute-start(f32[256,512]{1,0:T(8,128)S(1)} %get-tuple-element.88), channel_id=1, source_target_pairs={{0,8},{8,0},{16,24},{24,16},{1,9},{9,1},{17,25},{25,17},{32,40},{4... | collective-permute-start | bytes 1572872 | tf_op jit(solution)/shard_map/ppermute | solution.py:42
  (2 other events, 1.7 us)

commit v9 on v8

--- a/solution.py
+++ b/solution.py
@@ -57,6 +57,11 @@
 def spread(x, y, z, core):
     zh, zl = divmod(z, 2)
     return ((x + y) % 4, x, zl * 2 + zh, core)
+
+
+def spread_across(x, y, z, core):
+    x, y, z, core = spread(x, y, z, core)
+    return (x, y, (z + 2) % 4, core)
 
 
 def within_half(flip, later):
@@ -235,7 +240,7 @@
         low_ref[rows, :] = total.astype(bf16)
 
 
-def close_kernel(sum_ref, got_ref, d_ref):
+def close_kernel(sum_ref, got_ref, _, d_ref):
     for half in range(2):
         mine = slice(half * ROWS, (half + 1) * ROWS)
         its = slice((1 - half) * ROWS, (2 - half) * ROWS)
@@ -287,33 +292,37 @@
     l_own = send(layer_input, spread)
     kv, aux_own = prepare(doc_lengths, key_states, value_states, output_grad, attn_output, log_norms)
     kv, aux_own, q_par, do_par = together(kv, aux_own, q_par, do_par)
+    layer_late, kv = together(layer_input, kv)
+    other_0 = send(layer_late, spread_across)
     aux_par = send(aux_own, other_core)
     kv, aux_par = together(kv, aux_par)
     aux, q, do = (aux_own, aux_par), (queries, q_par), (output_grad, do_par)
 
     kv_far, kv_y, kv_zl = (send(kv, within_half(flip, True)) for flip in (3, 2, 1))
 
-    behind, ahead, across = shifted(dx=-1), shifted(dx=1), shifted(dz=2)
+    behind, ahead = shifted(dx=-1), shifted(dx=1)
     *dqs, dkv_own = attention((0,), (kv,), aux, q, do, None, (f32, f32), f32, 0.3)
     l_own, dkv_own, kv_y, kv_far, kv_zl, *dqs = together(l_own, dkv_own, kv_y, kv_far, kv_zl, *dqs)
-    other_0, own_1, own_3 = (send(l_own, t) for t in (across, behind, ahead))
+    own_1, own_3 = send(l_own, behind), send(l_own, ahead)
 
     *dqs, dkv_far = attention((4, 6), (kv_y, kv_far), aux, q, do, dqs, (f32, f32), bf16, 0.3)
     got_far = send(dkv_far, within_half(2, False))
+    other_0, *dqs = together(other_0, *dqs)
+    other_3, other_1 = send(other_0, ahead), send(other_0, behind)
     dq_own, dq_par, dkv_zl = attention((2,), (kv_zl,), aux, q, do, dqs, (f32, bf16), f32, 1.5)
-    other_0, own_1, own_3, l_own, got_far, dkv_zl, dq_own, dq_par = together(
-        other_0, own_1, own_3, l_own, got_far, dkv_zl, dq_own, dq_par
+    own_1, own_3, l_own, got_far, dkv_zl, dq_own, dq_par = together(
+        own_1, own_3, l_own, got_far, dkv_zl, dq_own, dq_par
     )
 
     pair = (2 * ROWS, 2 * HD)
     dkv, dkv_low = call(add_kernel, (struct(pair, f32), struct(pair, bf16)), (dkv_own, dkv_zl, got_far))
     got_zl = send(dkv_low, other_zl)
     dq_par, _ = together(dq_par, dkv_low)
-    other_3, other_1 = send(other_0, ahead), send(other_0, behind)
     dq_got = send(dq_par, other_core)
     query_grad = ((dq_own + dq_got.astype(f32)) * SCALE).astype(bf16)
+    early = arrived((other_1, other_3), 8)
     got_zl, query_grad = together(got_zl, query_grad)
-    d_own = call(close_kernel, struct((4 * HD, ROWS), bf16), (dkv, got_zl))
+    d_own = call(close_kernel, struct((4 * HD, ROWS), bf16), (dkv, got_zl, early))
     d_2, d_1, d_3 = (send(d_own, shifted(dy=-dy)) for dy in (2, 1, 3))
     ready = arrived((d_1, d_2, d_3), 8)
 

time: 83.6 us -> 90.7 us (1.085)
  starting transfers between devices: 37.1 us -> 47.4 us
  waiting for transfers between devices: 24.7 us -> 22.1 us
    ppermute x21, starting transfers between devices: 37.1 us -> 47.4 us  [send(): return lax.ppermute(value, AXES, route(target))]
    ppermute x21, waiting for transfers between devices: 24.7 us -> 22.1 us  [send(): return lax.ppermute(value, AXES, route(target))]
    pallas_call x9 -> x10, Pallas kernels: 17.3 us -> 17.3 us  [call(): pl.pallas_call(kernel, out_shape=out_shape, compiler_params=pltpu.Compile...]
  transfers between devices with their start and end apart: 21 -> 21, of which waited for: 9 -> 6; matrix products, arithmetic and copies ran while one was open for 1% -> 1% of each run, Pallas kernels for 18% -> 17%
where the time goes in v9:
time: 90.7 us; the launch traced here: 90.3 us
  starting transfers between devices  47.4 us (52%)
  waiting for transfers between devices  22.1 us (24%)
  Pallas kernels  17.3 us (19%)
  local copies, waits for them, and re-layouts  1.67 us (2%)
  other arithmetic  0.95 us (1%)
    ppermute x21, starting transfers between devices, send(): return lax.ppermute(value, AXES, route(target))  47.4 us
    ppermute x21, waiting for transfers between devices, send(): return lax.ppermute(value, AXES, route(target))  22.1 us
    pallas_call x10, Pallas kernels, call(): pl.pallas_call(kernel, out_shape=out_shape, compiler_params=pltpu.Compile...  17.3 us
  transfers between devices with their start and end apart: 21, of which 6 were waited for; matrix products, arithmetic and copies ran while one was open for 1% of the time, Pallas kernels for 17%

profile of v9, /device:TPU:1, one launch (start us, length us, event | category | flops | bytes accessed | tf_op | source)
XLA Modules:
  0.0 90.3 jit_solution(11975491208522716984)
XLA Ops:
  0.7 1.5 %collective-permute-start.1 = (bf16[256,1024]{1,0:T(8,128)(2,1)}, bf16[256,1024]{1,0:T(8,128)(2,1)S(1)}, u32[]{:S(2)}, u32[]{:S(2)}) collective-permute-start(bf16[256,1024]{1,0:T(8,128)(2,1)} %refs_3_.3), channel_id=1, source_target_pairs={{0,8},{8,0},{16,24},{24,16},{1,9},{9,1},{17,25},{25,17},{32,40},{4... | collective-permute-start | bytes 1572872 | tf_op jit(solution)/shard_map/ppermute | solution.py:42
  2.2 1.7 %collective-permute-start = (bf16[256,1024]{1,0:T(8,128)(2,1)}, bf16[256,1024]{1,0:T(8,128)(2,1)S(1)}, u32[]{:S(2)}, u32[]{:S(2)}) collective-permute-start(bf16[256,1024]{1,0:T(8,128)(2,1)} %param.14), channel_id=1, source_target_pairs={{0,0},{8,8},{16,1},{24,9},{1,16},{9,24},{17,17},{25,25},{32,2},{40... | collective-permute-start | bytes 1572872 | tf_op jit(solution)/shard_map/ppermute | solution.py:42
  3.9 3.0 %shard_map.103 = (bf16[256,256]{1,0:T(8,128)(2,1)}, f32[24,256]{1,0:T(8,128)}) custom-call(s32[16]{0:T(128)} %lengths_ref.1, bf16[256,128]{1,0:T(8,128)(2,1)} %k_any.1, bf16[256,128]{1,0:T(8,128)(2,1)} %v_any.1, bf16[256,1024]{1,0:T(8,128)(2,1)} %refs_5_.3, bf16[256,1024]{1,0:T(8,128)(2,1)} %out_any.1, f32[8,256]{1,0:T(8,128)} %ln_any.1), custom_call_target="tpu_custom_call" | custom-call | flops 345000000 | bytes 65536 | tf_op jit(solution)/shard_map/pallas_call | solution.py:95
  6.9 4.0 %collective-permute-start.10 = (bf16[256,1024]{1,0:T(8,128)(2,1)}, bf16[256,1024]{1,0:T(8,128)(2,1)S(1)}, u32[]{:S(2)}, u32[]{:S(2)}) collective-permute-start(bf16[256,1024]{1,0:T(8,128)(2,1)} %param.14), channel_id=1, source_target_pairs={{0,1},{8,9},{16,0},{24,8},{1,17},{9,25},{17,16},{25,24},{32,3},{40... | collective-permute-start | bytes 1572872 | tf_op jit(solution)/shard_map/ppermute | solution.py:42
  12.8 5.0 %collective-permute-start.4 = (bf16[256,256]{1,0:T(8,128)(2,1)}, bf16[256,256]{1,0:T(8,128)(2,1)S(1)}, u32[]{:S(2)}, u32[]{:S(2)}) collective-permute-start(bf16[256,256]{1,0:T(8,128)(2,1)} %get-tuple-element.56.refs_0_), channel_id=1, source_target_pairs={{0,32},{8,40},{16,48},{24,56},{1,33},{9,41},{17,49},{25,57},{64,96... | collective-permute-start | bytes 393224 | tf_op jit(solution)/shard_map/ppermute | solution.py:42
  17.8 1.3 %collective-permute-start.5 = (bf16[256,256]{1,0:T(8,128)(2,1)}, bf16[256,256]{1,0:T(8,128)(2,1)S(1)}, u32[]{:S(2)}, u32[]{:S(2)}) collective-permute-start(bf16[256,256]{1,0:T(8,128)(2,1)} %get-tuple-element.56.refs_0_), channel_id=1, source_target_pairs={{0,48},{8,56},{16,32},{24,40},{1,49},{9,57},{17,33},{25,41},{64,11... | collective-permute-start | bytes 393224 | tf_op jit(solution)/shard_map/ppermute | solution.py:42
  19.1 3.1 %collective-permute-start.6 = (bf16[256,256]{1,0:T(8,128)(2,1)}, bf16[256,256]{1,0:T(8,128)(2,1)S(1)}, u32[]{:S(2)}, u32[]{:S(2)}) collective-permute-start(bf16[256,256]{1,0:T(8,128)(2,1)} %get-tuple-element.56.refs_0_), channel_id=1, source_target_pairs={{0,16},{8,24},{1,17},{9,25},{32,48},{40,56},{33,49},{41,57},{64,80... | collective-permute-start | bytes 393224 | tf_op jit(solution)/shard_map/ppermute | solution.py:42
  23.9 3.0 %shard_map.104 = (f32[256,1024]{1,0:T(8,128)S(1)}, f32[256,1024]{1,0:T(8,128)S(1)}, f32[256,256]{1,0:T(8,128)S(1)}) custom-call(bf16[256,256]{1,0:T(8,128)(2,1)S(1)} %copy-done.2, f32[24,256]{1,0:T(8,128)S(1)} %copy-done.3, f32[24,256]{1,0:T(8,128)S(1)} %collective-permute-done.3.refs_2_.refs_3_, bf16[256,1024]{1,0:T(8,128)(2,1)S(1)} %copy-done.1, ...), custom_call_target="tpu_custom_call" | custom-call | flops 345000000 | bytes 65536 | tf_op jit(solution)/shard_map/pallas_call | solution.py:95
  27.0 11.2 %collective-permute-start.7 = (bf16[256,1024]{1,0:T(8,128)(2,1)S(1)}, bf16[256,1024]{1,0:T(8,128)(2,1)S(1)}, u32[]{:S(2)}, u32[]{:S(2)}) collective-permute-start(bf16[256,1024]{1,0:T(8,128)(2,1)S(1)} %collective-permute-done.refs_0_), channel_id=1, source_target_pairs={{0,6},{8,14},{16,22},{24,30},{1,7},{9,15},{17,23},{25,31},{32,38},... | collective-permute-start | bytes 1572872 | tf_op jit(solution)/shard_map/ppermute | solution.py:42
  38.2 5.8 %shard_map.105 = (f32[256,1024]{1,0:T(8,128)S(1)}, f32[256,1024]{1,0:T(8,128)S(1)}, bf16[512,256]{1,0:T(8,128)(2,1)S(1)}) custom-call(bf16[256,256]{1,0:T(8,128)(2,1)S(1)} %collective-permute-done.4.refs_0_, bf16[256,256]{1,0:T(8,128)(2,1)S(1)} %collective-permute-done.5.refs_1_, f32[24,256]{1,0:T(8,128)S(1)} %copy-done.3, ...), custom_call_target="tpu_custom_call" | custom-call | flops 345000000 | bytes 65536 | tf_op jit(solution)/shard_map/pallas_call | solution.py:95
  44.0 1.2 %collective-permute-start.13 = (bf16[256,1024]{1,0:T(8,128)(2,1)S(1)}, bf16[256,1024]{1,0:T(8,128)(2,1)S(1)}, u32[]{:S(2)}, u32[]{:S(2)}) collective-permute-start(bf16[256,1024]{1,0:T(8,128)(2,1)S(1)} %collective-permute-done.10.refs_1_), channel_id=1, source_target_pairs={{0,2},{8,10},{16,18},{24,26},{1,3},{9,11},{17,19},{25,27},{32,34},... | collective-permute-start | bytes 1572872 | tf_op jit(solution)/shard_map/ppermute | solution.py:42
  45.2 1.8 %collective-permute-start.14 = (bf16[256,1024]{1,0:T(8,128)(2,1)S(1)}, bf16[256,1024]{1,0:T(8,128)(2,1)S(1)}, u32[]{:S(2)}, u32[]{:S(2)}) collective-permute-start(bf16[256,1024]{1,0:T(8,128)(2,1)S(1)} %collective-permute-done.10.refs_1_), channel_id=1, source_target_pairs={{0,6},{8,14},{16,22},{24,30},{1,7},{9,15},{17,23},{25,31},{32,38},... | collective-permute-start | bytes 1572872 | tf_op jit(solution)/shard_map/ppermute | solution.py:42
  47.1 1.3 %collective-permute-start.9 = (bf16[512,256]{1,0:T(8,128)(2,1)S(1)}, bf16[512,256]{1,0:T(8,128)(2,1)S(1)}, u32[]{:S(2)}, u32[]{:S(2)}) collective-permute-start(bf16[512,256]{1,0:T(8,128)(2,1)S(1)} %get-tuple-element.69), channel_id=1, source_target_pairs={{32,0},{40,8},{48,16},{56,24},{33,1},{41,9},{49,17},{57,25},{96,64... | collective-permute-start | bytes 786440 | tf_op jit(solution)/shard_map/ppermute | solution.py:42
  48.4 3.1 %shard_map.106 = (f32[256,1024]{1,0:T(8,128)S(1)}, bf16[256,1024]{1,0:T(8,128)(2,1)S(1)}, f32[256,256]{1,0:T(8,128)S(1)}) custom-call(bf16[256,256]{1,0:T(8,128)(2,1)S(1)} %collective-permute-done.6.refs_0_, f32[24,256]{1,0:T(8,128)S(1)} %copy-done.4, f32[24,256]{1,0:T(8,128)S(1)} %collective-permute-done.3.refs_2_.refs_3_, bf16[256,1024]{1,0:T(8,128)(2,1)S(1)} %copy-done.1, ...), custom_call_target="tpu_custom_call" | custom-call | flops 1724999936 | bytes 65536 | tf_op jit(solution)/shard_map/pallas_call | solution.py:95
  51.4 4.2 %collective-permute-done.9.got_ref = bf16[512,256]{1,0:T(8,128)(2,1)S(1)} collective-permute-done((bf16[512,256]{1,0:T(8,128)(2,1)S(1)}, bf16[512,256]{1,0:T(8,128)(2,1)S(1)}, u32[]{:S(2)}, u32[]{:S(2)}) %collective-permute-start.9) | collective-permute-done | bytes 262176 | tf_op jit(solution)/shard_map/ppermute | solution.py:42
  55.7 1.8 %collective-permute-start.11 = (bf16[512,256]{1,0:T(8,128)(2,1)S(1)}, bf16[512,256]{1,0:T(8,128)(2,1)S(1)}, u32[]{:S(2)}, u32[]{:S(2)}) collective-permute-start(bf16[512,256]{1,0:T(8,128)(2,1)S(1)} %get-tuple-element.81), channel_id=1, source_target_pairs={{0,16},{8,24},{16,0},{24,8},{1,17},{9,25},{17,1},{25,9},{32,48},{4... | collective-permute-start | bytes 786440 | tf_op jit(solution)/shard_map/ppermute | solution.py:42
  57.5 2.8 %collective-permute-start.12 = (bf16[256,1024]{1,0:T(8,128)(2,1)S(1)}, bf16[256,1024]{1,0:T(8,128)(2,1)S(1)}, u32[]{:S(2)}, u32[]{:S(2)}) collective-permute-start(bf16[256,1024]{1,0:T(8,128)(2,1)S(1)} %get-tuple-element.84), channel_id=1, source_target_pairs={{0,8},{8,0},{16,24},{24,16},{1,9},{9,1},{17,25},{25,17},{32,40},{4... | collective-permute-start | bytes 1572872 | tf_op jit(solution)/shard_map/ppermute | solution.py:42
  60.3 2.7 %collective-permute-done.13.refs_1_.refs_7_ = bf16[256,1024]{1,0:T(8,128)(2,1)S(1)} collective-permute-done((bf16[256,1024]{1,0:T(8,128)(2,1)S(1)}, bf16[256,1024]{1,0:T(8,128)(2,1)S(1)}, u32[]{:S(2)}, u32[]{:S(2)}) %collective-permute-start.13) | collective-permute-done | bytes 524320 | tf_op jit(solution)/shard_map/ppermute | solution.py:42
  64.1 5.0 %collective-permute-start.17 = (bf16[512,256]{1,0:T(8,128)(2,1)S(1)}, bf16[512,256]{1,0:T(8,128)(2,1)S(1)}, u32[]{:S(2)}, u32[]{:S(2)}) collective-permute-start(bf16[512,256]{1,0:T(8,128)(2,1)S(1)} %shard_map.109.refs_8_), channel_id=1, source_target_pairs={{0,96},{8,104},{16,112},{24,120},{1,97},{9,105},{17,113},{25,121},... | collective-permute-start | bytes 786440 | tf_op jit(solution)/shard_map/ppermute | solution.py:42
  71.2 8.5 %collective-permute-done.17.refs_0_.refs_9_ = bf16[512,256]{1,0:T(8,128)(2,1)S(1)} collective-permute-done((bf16[512,256]{1,0:T(8,128)(2,1)S(1)}, bf16[512,256]{1,0:T(8,128)(2,1)S(1)}, u32[]{:S(2)}, u32[]{:S(2)}) %collective-permute-start.17) | collective-permute-done | bytes 262176 | tf_op jit(solution)/shard_map/ppermute | solution.py:42
  79.7 4.1 %collective-permute-done.19.refs_2_.refs_11_ = bf16[512,256]{1,0:T(8,128)(2,1)S(1)} collective-permute-done((bf16[512,256]{1,0:T(8,128)(2,1)S(1)}, bf16[512,256]{1,0:T(8,128)(2,1)S(1)}, u32[]{:S(2)}, u32[]{:S(2)}) %collective-permute-start.19) | collective-permute-done | bytes 262176 | tf_op jit(solution)/shard_map/ppermute | solution.py:42
  83.8 1.3 %shard_map.111 = (f32[256,512]{1,0:T(8,128)S(1)}, f32[256,512]{1,0:T(8,128)S(1)}) custom-call(bf16[256,1024]{1,0:T(8,128)(2,1)S(1)} %collective-permute-done.refs_0_, bf16[256,1024]{1,0:T(8,128)(2,1)S(1)} %collective-permute-done.10.refs_1_, bf16[256,1024]{1,0:T(8,128)(2,1)S(1)} %collective-permute-done.7.refs_2_, ...), custom_call_target="tpu_custom_call" | custom-call | flops 11500000 | bytes 65536 | tf_op jit(solution)/shard_map/pallas_call | solution.py:95
  85.1 2.7 %collective-permute-start.20 = (f32[256,512]{1,0:T(8,128)S(1)}, f32[256,512]{1,0:T(8,128)S(1)}, u32[]{:S(2)}, u32[]{:S(2)}) collective-permute-start(f32[256,512]{1,0:T(8,128)S(1)} %get-tuple-element.96), channel_id=1, source_target_pairs={{0,8},{8,0},{16,24},{24,16},{1,9},{9,1},{17,25},{25,17},{32,40},{4... | collective-permute-start | bytes 1572872 | tf_op jit(solution)/shard_map/ppermute | solution.py:42
  87.8 1.5 %collective-permute-done.20.got_ref = f32[256,512]{1,0:T(8,128)S(1)} collective-permute-done((f32[256,512]{1,0:T(8,128)S(1)}, f32[256,512]{1,0:T(8,128)S(1)}, u32[]{:S(2)}, u32[]{:S(2)}) %collective-permute-start.20) | collective-permute-done | bytes 524320 | tf_op jit(solution)/shard_map/ppermute | solution.py:42
  (39 shorter events, 7.9 us)
Async XLA Ops:
  0.6 21.6 %copy-start.1 = (bf16[256,1024]{1,0:T(8,128)(2,1)S(1)}, bf16[256,1024]{1,0:T(8,128)(2,1)}, u32[]{:S(2)}) copy-start(bf16[256,1024]{1,0:T(8,128)(2,1)} %refs_3_.3) | copy-start | bytes 1572868
  0.6 21.6 %copy-start = (bf16[256,1024]{1,0:T(8,128)(2,1)S(1)}, bf16[256,1024]{1,0:T(8,128)(2,1)}, u32[]{:S(2)}) copy-start(bf16[256,1024]{1,0:T(8,128)(2,1)} %refs_5_.3) | copy-start | bytes 1572868
  0.7 6.3 %collective-permute-start.1 = (bf16[256,1024]{1,0:T(8,128)(2,1)}, bf16[256,1024]{1,0:T(8,128)(2,1)S(1)}, u32[]{:S(2)}, u32[]{:S(2)}) collective-permute-start(bf16[256,1024]{1,0:T(8,128)(2,1)} %refs_3_.3), channel_id=1, source_target_pairs={{0,8},{8,0},{16,24},{24,16},{1,9},{9,1},{17,25},{25,17},{32,40},{4... | collective-permute-start | bytes 1572872 | tf_op jit(solution)/shard_map/ppermute | solution.py:42
  2.2 4.8 %collective-permute-start.2 = (bf16[256,1024]{1,0:T(8,128)(2,1)}, bf16[256,1024]{1,0:T(8,128)(2,1)S(1)}, u32[]{:S(2)}, u32[]{:S(2)}) collective-permute-start(bf16[256,1024]{1,0:T(8,128)(2,1)} %refs_5_.3), channel_id=1, source_target_pairs={{0,8},{8,0},{16,24},{24,16},{1,9},{9,1},{17,25},{25,17},{32,40},{4... | collective-permute-start | bytes 1572872 | tf_op jit(solution)/shard_map/ppermute | solution.py:42
  2.2 24.7 %collective-permute-start = (bf16[256,1024]{1,0:T(8,128)(2,1)}, bf16[256,1024]{1,0:T(8,128)(2,1)S(1)}, u32[]{:S(2)}, u32[]{:S(2)}) collective-permute-start(bf16[256,1024]{1,0:T(8,128)(2,1)} %param.14), channel_id=1, source_target_pairs={{0,0},{8,8},{16,1},{24,9},{1,16},{9,24},{17,17},{25,25},{32,2},{40... | collective-permute-start | bytes 1572872 | tf_op jit(solution)/shard_map/ppermute | solution.py:42
  6.9 37.1 %collective-permute-start.10 = (bf16[256,1024]{1,0:T(8,128)(2,1)}, bf16[256,1024]{1,0:T(8,128)(2,1)S(1)}, u32[]{:S(2)}, u32[]{:S(2)}) collective-permute-start(bf16[256,1024]{1,0:T(8,128)(2,1)} %param.14), channel_id=1, source_target_pairs={{0,1},{8,9},{16,0},{24,8},{1,17},{9,25},{17,16},{25,24},{32,3},{40... | collective-permute-start | bytes 1572872 | tf_op jit(solution)/shard_map/ppermute | solution.py:42
  10.9 1.9 %collective-permute-start.3 = (f32[24,256]{1,0:T(8,128)}, f32[24,256]{1,0:T(8,128)S(1)}, u32[]{:S(2)}, u32[]{:S(2)}) collective-permute-start(f32[24,256]{1,0:T(8,128)} %get-tuple-element.55.refs_1_.refs_2_), channel_id=1, source_target_pairs={{0,8},{8,0},{16,24},{24,16},{1,9},{9,1},{17,25},{25,17},{32,40},{4... | collective-permute-start | bytes 73736 | tf_op jit(solution)/shard_map/ppermute | solution.py:42
  12.8 14.1 %collective-permute-start.4 = (bf16[256,256]{1,0:T(8,128)(2,1)}, bf16[256,256]{1,0:T(8,128)(2,1)S(1)}, u32[]{:S(2)}, u32[]{:S(2)}) collective-permute-start(bf16[256,256]{1,0:T(8,128)(2,1)} %get-tuple-element.56.refs_0_), channel_id=1, source_target_pairs={{0,32},{8,40},{16,48},{24,56},{1,33},{9,41},{17,49},{25,57},{64,96... | collective-permute-start | bytes 393224 | tf_op jit(solution)/shard_map/ppermute | solution.py:42
  17.8 9.1 %collective-permute-start.5 = (bf16[256,256]{1,0:T(8,128)(2,1)}, bf16[256,256]{1,0:T(8,128)(2,1)S(1)}, u32[]{:S(2)}, u32[]{:S(2)}) collective-permute-start(bf16[256,256]{1,0:T(8,128)(2,1)} %get-tuple-element.56.refs_0_), channel_id=1, source_target_pairs={{0,48},{8,56},{16,32},{24,40},{1,49},{9,57},{17,33},{25,41},{64,11... | collective-permute-start | bytes 393224 | tf_op jit(solution)/shard_map/ppermute | solution.py:42
  19.1 7.8 %collective-permute-start.6 = (bf16[256,256]{1,0:T(8,128)(2,1)}, bf16[256,256]{1,0:T(8,128)(2,1)S(1)}, u32[]{:S(2)}, u32[]{:S(2)}) collective-permute-start(bf16[256,256]{1,0:T(8,128)(2,1)} %get-tuple-element.56.refs_0_), channel_id=1, source_target_pairs={{0,16},{8,24},{1,17},{9,25},{32,48},{40,56},{33,49},{41,57},{64,80... | collective-permute-start | bytes 393224 | tf_op jit(solution)/shard_map/ppermute | solution.py:42
  26.9 21.4 %copy-start.4 = (f32[24,256]{1,0:T(8,128)S(1)}, f32[24,256]{1,0:T(8,128)}, u32[]{:S(2)}) copy-start(f32[24,256]{1,0:T(8,128)} %get-tuple-element.55.refs_1_.refs_2_) | copy-start | bytes 73732
  27.0 28.6 %collective-permute-start.7 = (bf16[256,1024]{1,0:T(8,128)(2,1)S(1)}, bf16[256,1024]{1,0:T(8,128)(2,1)S(1)}, u32[]{:S(2)}, u32[]{:S(2)}) collective-permute-start(bf16[256,1024]{1,0:T(8,128)(2,1)S(1)} %collective-permute-done.refs_0_), channel_id=1, source_target_pairs={{0,6},{8,14},{16,22},{24,30},{1,7},{9,15},{17,23},{25,31},{32,38},... | collective-permute-start | bytes 1572872 | tf_op jit(solution)/shard_map/ppermute | solution.py:42
  38.2 17.4 %collective-permute-start.8 = (bf16[256,1024]{1,0:T(8,128)(2,1)S(1)}, bf16[256,1024]{1,0:T(8,128)(2,1)S(1)}, u32[]{:S(2)}, u32[]{:S(2)}) collective-permute-start(bf16[256,1024]{1,0:T(8,128)(2,1)S(1)} %collective-permute-done.refs_0_), channel_id=1, source_target_pairs={{0,2},{8,10},{16,18},{24,26},{1,3},{9,11},{17,19},{25,27},{32,34},... | collective-permute-start | bytes 1572872 | tf_op jit(solution)/shard_map/ppermute | solution.py:42
  44.0 18.9 %collective-permute-start.13 = (bf16[256,1024]{1,0:T(8,128)(2,1)S(1)}, bf16[256,1024]{1,0:T(8,128)(2,1)S(1)}, u32[]{:S(2)}, u32[]{:S(2)}) collective-permute-start(bf16[256,1024]{1,0:T(8,128)(2,1)S(1)} %collective-permute-done.10.refs_1_), channel_id=1, source_target_pairs={{0,2},{8,10},{16,18},{24,26},{1,3},{9,11},{17,19},{25,27},{32,34},... | collective-permute-start | bytes 1572872 | tf_op jit(solution)/shard_map/ppermute | solution.py:42
  45.2 17.7 %collective-permute-start.14 = (bf16[256,1024]{1,0:T(8,128)(2,1)S(1)}, bf16[256,1024]{1,0:T(8,128)(2,1)S(1)}, u32[]{:S(2)}, u32[]{:S(2)}) collective-permute-start(bf16[256,1024]{1,0:T(8,128)(2,1)S(1)} %collective-permute-done.10.refs_1_), channel_id=1, source_target_pairs={{0,6},{8,14},{16,22},{24,30},{1,7},{9,15},{17,23},{25,31},{32,38},... | collective-permute-start | bytes 1572872 | tf_op jit(solution)/shard_map/ppermute | solution.py:42
  47.1 8.5 %collective-permute-start.9 = (bf16[512,256]{1,0:T(8,128)(2,1)S(1)}, bf16[512,256]{1,0:T(8,128)(2,1)S(1)}, u32[]{:S(2)}, u32[]{:S(2)}) collective-permute-start(bf16[512,256]{1,0:T(8,128)(2,1)S(1)} %get-tuple-element.69), channel_id=1, source_target_pairs={{32,0},{40,8},{48,16},{56,24},{33,1},{41,9},{49,17},{57,25},{96,64... | collective-permute-start | bytes 786440 | tf_op jit(solution)/shard_map/ppermute | solution.py:42
  55.7 8.2 %collective-permute-start.11 = (bf16[512,256]{1,0:T(8,128)(2,1)S(1)}, bf16[512,256]{1,0:T(8,128)(2,1)S(1)}, u32[]{:S(2)}, u32[]{:S(2)}) collective-permute-start(bf16[512,256]{1,0:T(8,128)(2,1)S(1)} %get-tuple-element.81), channel_id=1, source_target_pairs={{0,16},{8,24},{16,0},{24,8},{1,17},{9,25},{17,1},{25,9},{32,48},{4... | collective-permute-start | bytes 786440 | tf_op jit(solution)/shard_map/ppermute | solution.py:42
  57.5 5.5 %collective-permute-start.12 = (bf16[256,1024]{1,0:T(8,128)(2,1)S(1)}, bf16[256,1024]{1,0:T(8,128)(2,1)S(1)}, u32[]{:S(2)}, u32[]{:S(2)}) collective-permute-start(bf16[256,1024]{1,0:T(8,128)(2,1)S(1)} %get-tuple-element.84), channel_id=1, source_target_pairs={{0,8},{8,0},{16,24},{24,16},{1,9},{9,1},{17,25},{25,17},{32,40},{4... | collective-permute-start | bytes 1572872 | tf_op jit(solution)/shard_map/ppermute | solution.py:42
  64.1 15.6 %collective-permute-start.17 = (bf16[512,256]{1,0:T(8,128)(2,1)S(1)}, bf16[512,256]{1,0:T(8,128)(2,1)S(1)}, u32[]{:S(2)}, u32[]{:S(2)}) collective-permute-start(bf16[512,256]{1,0:T(8,128)(2,1)S(1)} %shard_map.109.refs_8_), channel_id=1, source_target_pairs={{0,96},{8,104},{16,112},{24,120},{1,97},{9,105},{17,113},{25,121},... | collective-permute-start | bytes 786440 | tf_op jit(solution)/shard_map/ppermute | solution.py:42
  69.1 10.6 %collective-permute-start.18 = (bf16[512,256]{1,0:T(8,128)(2,1)S(1)}, bf16[512,256]{1,0:T(8,128)(2,1)S(1)}, u32[]{:S(2)}, u32[]{:S(2)}) collective-permute-start(bf16[512,256]{1,0:T(8,128)(2,1)S(1)} %shard_map.109.refs_8_), channel_id=1, source_target_pairs={{0,64},{8,72},{16,80},{24,88},{1,65},{9,73},{17,81},{25,89},{32,96... | collective-permute-start | bytes 786440 | tf_op jit(solution)/shard_map/ppermute | solution.py:42
  69.1 14.7 %collective-permute-start.19 = (bf16[512,256]{1,0:T(8,128)(2,1)S(1)}, bf16[512,256]{1,0:T(8,128)(2,1)S(1)}, u32[]{:S(2)}, u32[]{:S(2)}) collective-permute-start(bf16[512,256]{1,0:T(8,128)(2,1)S(1)} %shard_map.109.refs_8_), channel_id=1, source_target_pairs={{0,32},{8,40},{16,48},{24,56},{1,33},{9,41},{17,49},{25,57},{32,64... | collective-permute-start | bytes 786440 | tf_op jit(solution)/shard_map/ppermute | solution.py:42
  69.7 14.0 %collective-permute-start.15 = (bf16[256,1024]{1,0:T(8,128)(2,1)S(1)}, bf16[256,1024]{1,0:T(8,128)(2,1)S(1)}, u32[]{:S(2)}, u32[]{:S(2)}) collective-permute-start(bf16[256,1024]{1,0:T(8,128)(2,1)S(1)} %collective-permute-done.7.refs_2_), channel_id=1, source_target_pairs={{0,6},{8,14},{16,22},{24,30},{1,7},{9,15},{17,23},{25,31},{32,38},... | collective-permute-start | bytes 1572872 | tf_op jit(solution)/shard_map/ppermute | solution.py:42
  70.9 12.9 %collective-permute-start.16 = (bf16[256,1024]{1,0:T(8,128)(2,1)S(1)}, bf16[256,1024]{1,0:T(8,128)(2,1)S(1)}, u32[]{:S(2)}, u32[]{:S(2)}) collective-permute-start(bf16[256,1024]{1,0:T(8,128)(2,1)S(1)} %collective-permute-done.13.refs_1_.refs_7_), channel_id=1, source_target_pairs={{0,2},{8,10},{16,18},{24,26},{1,3},{9,11},{17,19},{25,27},{32,34},... | collective-permute-start | bytes 1572872 | tf_op jit(solution)/shard_map/ppermute | solution.py:42
  85.1 4.3 %collective-permute-start.20 = (f32[256,512]{1,0:T(8,128)S(1)}, f32[256,512]{1,0:T(8,128)S(1)}, u32[]{:S(2)}, u32[]{:S(2)}) collective-permute-start(f32[256,512]{1,0:T(8,128)S(1)} %get-tuple-element.96), channel_id=1, source_target_pairs={{0,8},{8,0},{16,24},{24,16},{1,9},{9,1},{17,25},{25,17},{32,40},{4... | collective-permute-start | bytes 1572872 | tf_op jit(solution)/shard_map/ppermute | solution.py:42
  (2 other events, 1.7 us)

commit v10 on v8

--- a/solution.py
+++ b/solution.py
@@ -227,7 +227,7 @@
     )
 
 
-def add_kernel(own_ref, zl_ref, got_ref, sum_ref, low_ref):
+def add_kernel(own_ref, zl_ref, got_ref, _, sum_ref, low_ref):
     for half, near_ref in enumerate((own_ref, zl_ref)):
         rows = slice(half * ROWS, (half + 1) * ROWS)
         total = near_ref[...] + got_ref[rows, :].astype(f32)
@@ -235,7 +235,7 @@
         low_ref[rows, :] = total.astype(bf16)
 
 
-def close_kernel(sum_ref, got_ref, d_ref):
+def close_kernel(sum_ref, got_ref, _, d_ref):
     for half in range(2):
         mine = slice(half * ROWS, (half + 1) * ROWS)
         its = slice((1 - half) * ROWS, (2 - half) * ROWS)
@@ -301,19 +301,20 @@
     *dqs, dkv_far = attention((4, 6), (kv_y, kv_far), aux, q, do, dqs, (f32, f32), bf16, 0.3)
     got_far = send(dkv_far, within_half(2, False))
     dq_own, dq_par, dkv_zl = attention((2,), (kv_zl,), aux, q, do, dqs, (f32, bf16), f32, 1.5)
-    other_0, own_1, own_3, l_own, got_far, dkv_zl, dq_own, dq_par = together(
-        other_0, own_1, own_3, l_own, got_far, dkv_zl, dq_own, dq_par
-    )
+    other_0, own_1, own_3, l_own, dkv_zl = together(other_0, own_1, own_3, l_own, dkv_zl)
+
+    other_3, other_1 = send(other_0, ahead), send(other_0, behind)
+    early = arrived((other_1, other_3), 8)
 
     pair = (2 * ROWS, 2 * HD)
-    dkv, dkv_low = call(add_kernel, (struct(pair, f32), struct(pair, bf16)), (dkv_own, dkv_zl, got_far))
+    there = arrived((got_far,), 4)
+    dkv, dkv_low = call(add_kernel, (struct(pair, f32), struct(pair, bf16)), (dkv_own, dkv_zl, got_far, there))
     got_zl = send(dkv_low, other_zl)
     dq_par, _ = together(dq_par, dkv_low)
-    other_3, other_1 = send(other_0, ahead), send(other_0, behind)
     dq_got = send(dq_par, other_core)
     query_grad = ((dq_own + dq_got.astype(f32)) * SCALE).astype(bf16)
-    got_zl, query_grad = together(got_zl, query_grad)
-    d_own = call(close_kernel, struct((4 * HD, ROWS), bf16), (dkv, got_zl))
+    got_zl, query_grad, early = together(got_zl, query_grad, early)
+    d_own = call(close_kernel, struct((4 * HD, ROWS), bf16), (dkv, got_zl, early))
     d_2, d_1, d_3 = (send(d_own, shifted(dy=-dy)) for dy in (2, 1, 3))
     ready = arrived((d_1, d_2, d_3), 8)
 

time: 83.6 us -> 82.5 us (0.987)
  starting transfers between devices: 37.1 us -> 36.2 us
    ppermute x21, starting transfers between devices: 37.1 us -> 36.2 us  [send(): return lax.ppermute(value, AXES, route(target))]
    pallas_call x9 -> x11, Pallas kernels: 17.3 us -> 17.3 us  [call(): pl.pallas_call(kernel, out_shape=out_shape, compiler_params=pltpu.Compile...]
  transfers between devices with their start and end apart: 21 -> 21, of which waited for: 9 -> 7; matrix products, arithmetic and copies ran while one was open for 1% -> 1% of each run, Pallas kernels for 18% -> 18%
where the time goes in v10:
time: 82.5 us; the launch traced here: 82.1 us
  starting transfers between devices  36.2 us (44%)
  waiting for transfers between devices  25.1 us (30%)
  Pallas kernels  17.3 us (21%)
  local copies, waits for them, and re-layouts  1.67 us (2%)
  other arithmetic  0.95 us (1%)
  between operations  0.84 us (1%)
    ppermute x21, starting transfers between devices, send(): return lax.ppermute(value, AXES, route(target))  36.2 us
    ppermute x21, waiting for transfers between devices, send(): return lax.ppermute(value, AXES, route(target))  25.1 us
    pallas_call x11, Pallas kernels, call(): pl.pallas_call(kernel, out_shape=out_shape, compiler_params=pltpu.Compile...  17.3 us
    unnamed x10, local copies, waits for them, and re-layouts  1.67 us
  transfers between devices with their start and end apart: 21, of which 7 were waited for; matrix products, arithmetic and copies ran while one was open for 1% of the time, Pallas kernels for 18%

profile of v10, /device:TPU:1, one launch (start us, length us, event | category | flops | bytes accessed | tf_op | source)
XLA Modules:
  0.0 82.1 jit_solution(12070756855066436541)
XLA Ops:
  0.7 1.5 %collective-permute-start.1 = (bf16[256,1024]{1,0:T(8,128)(2,1)}, bf16[256,1024]{1,0:T(8,128)(2,1)S(1)}, u32[]{:S(2)}, u32[]{:S(2)}) collective-permute-start(bf16[256,1024]{1,0:T(8,128)(2,1)} %refs_3_.3), channel_id=1, source_target_pairs={{0,8},{8,0},{16,24},{24,16},{1,9},{9,1},{17,25},{25,17},{32,40},{4... | collective-permute-start | bytes 1572872 | tf_op jit(solution)/shard_map/ppermute | solution.py:42
  2.2 1.7 %collective-permute-start = (bf16[256,1024]{1,0:T(8,128)(2,1)}, bf16[256,1024]{1,0:T(8,128)(2,1)S(1)}, u32[]{:S(2)}, u32[]{:S(2)}) collective-permute-start(bf16[256,1024]{1,0:T(8,128)(2,1)} %param.14), channel_id=1, source_target_pairs={{0,0},{8,8},{16,1},{24,9},{1,16},{9,24},{17,17},{25,25},{32,2},{40... | collective-permute-start | bytes 1572872 | tf_op jit(solution)/shard_map/ppermute | solution.py:42
  3.9 3.0 %shard_map.103 = (bf16[256,256]{1,0:T(8,128)(2,1)}, f32[24,256]{1,0:T(8,128)}) custom-call(s32[16]{0:T(128)} %lengths_ref.1, bf16[256,128]{1,0:T(8,128)(2,1)} %k_any.1, bf16[256,128]{1,0:T(8,128)(2,1)} %v_any.1, bf16[256,1024]{1,0:T(8,128)(2,1)} %refs_5_.3, bf16[256,1024]{1,0:T(8,128)(2,1)} %out_any.1, f32[8,256]{1,0:T(8,128)} %ln_any.1), custom_call_target="tpu_custom_call" | custom-call | flops 345000000 | bytes 65536 | tf_op jit(solution)/shard_map/pallas_call | solution.py:90
  8.5 4.9 %collective-permute-start.4 = (bf16[256,256]{1,0:T(8,128)(2,1)}, bf16[256,256]{1,0:T(8,128)(2,1)S(1)}, u32[]{:S(2)}, u32[]{:S(2)}) collective-permute-start(bf16[256,256]{1,0:T(8,128)(2,1)} %get-tuple-element.49.refs_0_), channel_id=1, source_target_pairs={{0,32},{8,40},{16,48},{24,56},{1,33},{9,41},{17,49},{25,57},{64,96... | collective-permute-start | bytes 393224 | tf_op jit(solution)/shard_map/ppermute | solution.py:42
  13.4 4.0 %collective-permute-start.5 = (bf16[256,256]{1,0:T(8,128)(2,1)}, bf16[256,256]{1,0:T(8,128)(2,1)S(1)}, u32[]{:S(2)}, u32[]{:S(2)}) collective-permute-start(bf16[256,256]{1,0:T(8,128)(2,1)} %get-tuple-element.49.refs_0_), channel_id=1, source_target_pairs={{0,48},{8,56},{16,32},{24,40},{1,49},{9,57},{17,33},{25,41},{64,11... | collective-permute-start | bytes 393224 | tf_op jit(solution)/shard_map/ppermute | solution.py:42
  17.4 2.2 %collective-permute-start.6 = (bf16[256,256]{1,0:T(8,128)(2,1)}, bf16[256,256]{1,0:T(8,128)(2,1)S(1)}, u32[]{:S(2)}, u32[]{:S(2)}) collective-permute-start(bf16[256,256]{1,0:T(8,128)(2,1)} %get-tuple-element.49.refs_0_), channel_id=1, source_target_pairs={{0,16},{8,24},{1,17},{9,25},{32,48},{40,56},{33,49},{41,57},{64,80... | collective-permute-start | bytes 393224 | tf_op jit(solution)/shard_map/ppermute | solution.py:42
  21.3 3.0 %shard_map.104 = (f32[256,1024]{1,0:T(8,128)S(1)}, f32[256,1024]{1,0:T(8,128)S(1)}, f32[256,256]{1,0:T(8,128)S(1)}) custom-call(bf16[256,256]{1,0:T(8,128)(2,1)S(1)} %copy-done.2, f32[24,256]{1,0:T(8,128)S(1)} %copy-done.3, f32[24,256]{1,0:T(8,128)S(1)} %collective-permute-done.3.refs_2_.refs_3_, bf16[256,1024]{1,0:T(8,128)(2,1)S(1)} %copy-done.1, ...), custom_call_target="tpu_custom_call" | custom-call | flops 345000000 | bytes 65536 | tf_op jit(solution)/shard_map/pallas_call | solution.py:90
  24.3 2.0 %collective-permute-start.7 = (bf16[256,1024]{1,0:T(8,128)(2,1)S(1)}, bf16[256,1024]{1,0:T(8,128)(2,1)S(1)}, u32[]{:S(2)}, u32[]{:S(2)}) collective-permute-start(bf16[256,1024]{1,0:T(8,128)(2,1)S(1)} %collective-permute-done.refs_0_), channel_id=1, source_target_pairs={{0,1},{8,9},{16,17},{24,25},{1,0},{9,8},{17,16},{25,24},{32,33},{4... | collective-permute-start | bytes 1572872 | tf_op jit(solution)/shard_map/ppermute | solution.py:42
  26.4 3.3 %collective-permute-start.8 = (bf16[256,1024]{1,0:T(8,128)(2,1)S(1)}, bf16[256,1024]{1,0:T(8,128)(2,1)S(1)}, u32[]{:S(2)}, u32[]{:S(2)}) collective-permute-start(bf16[256,1024]{1,0:T(8,128)(2,1)S(1)} %collective-permute-done.refs_0_), channel_id=1, source_target_pairs={{0,6},{8,14},{16,22},{24,30},{1,7},{9,15},{17,23},{25,31},{32,38},... | collective-permute-start | bytes 1572872 | tf_op jit(solution)/shard_map/ppermute | solution.py:42
  29.7 5.8 %shard_map.105 = (f32[256,1024]{1,0:T(8,128)S(1)}, f32[256,1024]{1,0:T(8,128)S(1)}, bf16[512,256]{1,0:T(8,128)(2,1)S(1)}) custom-call(bf16[256,256]{1,0:T(8,128)(2,1)S(1)} %collective-permute-done.4.refs_0_, bf16[256,256]{1,0:T(8,128)(2,1)S(1)} %collective-permute-done.5.refs_1_, f32[24,256]{1,0:T(8,128)S(1)} %copy-done.4, ...), custom_call_target="tpu_custom_call" | custom-call | flops 345000000 | bytes 65536 | tf_op jit(solution)/shard_map/pallas_call | solution.py:90
  35.5 1.5 %collective-permute-start.10 = (bf16[512,256]{1,0:T(8,128)(2,1)S(1)}, bf16[512,256]{1,0:T(8,128)(2,1)S(1)}, u32[]{:S(2)}, u32[]{:S(2)}) collective-permute-start(bf16[512,256]{1,0:T(8,128)(2,1)S(1)} %get-tuple-element.67), channel_id=1, source_target_pairs={{32,0},{40,8},{48,16},{56,24},{33,1},{41,9},{49,17},{57,25},{96,64... | collective-permute-start | bytes 786440 | tf_op jit(solution)/shard_map/ppermute | solution.py:42
  37.0 3.0 %shard_map.106 = (f32[256,1024]{1,0:T(8,128)S(1)}, bf16[256,1024]{1,0:T(8,128)(2,1)S(1)}, f32[256,256]{1,0:T(8,128)S(1)}) custom-call(bf16[256,256]{1,0:T(8,128)(2,1)S(1)} %collective-permute-done.6.refs_0_, f32[24,256]{1,0:T(8,128)S(1)} %copy-done.4, f32[24,256]{1,0:T(8,128)S(1)} %collective-permute-done.3.refs_2_.refs_3_, bf16[256,1024]{1,0:T(8,128)(2,1)S(1)} %copy-done.1, ...), custom_call_target="tpu_custom_call" | custom-call | flops 1724999936 | bytes 65536 | tf_op jit(solution)/shard_map/pallas_call | solution.py:90
  40.1 2.8 %collective-permute-done.9.refs_6_ = bf16[256,1024]{1,0:T(8,128)(2,1)S(1)} collective-permute-done((bf16[256,1024]{1,0:T(8,128)(2,1)S(1)}, bf16[256,1024]{1,0:T(8,128)(2,1)S(1)}, u32[]{:S(2)}, u32[]{:S(2)}) %collective-permute-start.9) | collective-permute-done | bytes 524320 | tf_op jit(solution)/shard_map/ppermute | solution.py:42
  43.1 1.2 %collective-permute-start.14 = (bf16[256,1024]{1,0:T(8,128)(2,1)S(1)}, bf16[256,1024]{1,0:T(8,128)(2,1)S(1)}, u32[]{:S(2)}, u32[]{:S(2)}) collective-permute-start(bf16[256,1024]{1,0:T(8,128)(2,1)S(1)} %collective-permute-done.7.refs_1_), channel_id=1, source_target_pairs={{0,2},{8,10},{16,18},{24,26},{1,3},{9,11},{17,19},{25,27},{32,34},... | collective-permute-start | bytes 1572872 | tf_op jit(solution)/shard_map/ppermute | solution.py:42
  44.5 3.0 %collective-permute-start.12 = (bf16[256,1024]{1,0:T(8,128)(2,1)S(1)}, bf16[256,1024]{1,0:T(8,128)(2,1)S(1)}, u32[]{:S(2)}, u32[]{:S(2)}) collective-permute-start(bf16[256,1024]{1,0:T(8,128)(2,1)S(1)} %get-tuple-element.71), channel_id=1, source_target_pairs={{0,8},{8,0},{16,24},{24,16},{1,9},{9,1},{17,25},{25,17},{32,40},{4... | collective-permute-start | bytes 1572872 | tf_op jit(solution)/shard_map/ppermute | solution.py:42
  47.5 6.4 %collective-permute-done.13.refs_0_.refs_3_ = bf16[256,1024]{1,0:T(8,128)(2,1)S(1)} collective-permute-done((bf16[256,1024]{1,0:T(8,128)(2,1)S(1)}, bf16[256,1024]{1,0:T(8,128)(2,1)S(1)}, u32[]{:S(2)}, u32[]{:S(2)}) %collective-permute-start.13) | collective-permute-done | bytes 524320 | tf_op jit(solution)/shard_map/ppermute | solution.py:42
  53.9 1.5 %collective-permute-done.14.refs_1_.refs_7_ = bf16[256,1024]{1,0:T(8,128)(2,1)S(1)} collective-permute-done((bf16[256,1024]{1,0:T(8,128)(2,1)S(1)}, bf16[256,1024]{1,0:T(8,128)(2,1)S(1)}, u32[]{:S(2)}, u32[]{:S(2)}) %collective-permute-start.14) | collective-permute-done | bytes 524320 | tf_op jit(solution)/shard_map/ppermute | solution.py:42
  56.5 5.3 %collective-permute-start.17 = (bf16[512,256]{1,0:T(8,128)(2,1)S(1)}, bf16[512,256]{1,0:T(8,128)(2,1)S(1)}, u32[]{:S(2)}, u32[]{:S(2)}) collective-permute-start(bf16[512,256]{1,0:T(8,128)(2,1)S(1)} %shard_map.110.refs_8_), channel_id=1, source_target_pairs={{0,96},{8,104},{16,112},{24,120},{1,97},{9,105},{17,113},{25,121},... | collective-permute-start | bytes 786440 | tf_op jit(solution)/shard_map/ppermute | solution.py:42
  62.7 1.2 %collective-permute-start.16 = (bf16[256,1024]{1,0:T(8,128)(2,1)S(1)}, bf16[256,1024]{1,0:T(8,128)(2,1)S(1)}, u32[]{:S(2)}, u32[]{:S(2)}) collective-permute-start(bf16[256,1024]{1,0:T(8,128)(2,1)S(1)} %collective-permute-done.14.refs_1_.refs_7_), channel_id=1, source_target_pairs={{0,2},{8,10},{16,18},{24,26},{1,3},{9,11},{17,19},{25,27},{32,34},... | collective-permute-start | bytes 1572872 | tf_op jit(solution)/shard_map/ppermute | solution.py:42
  63.9 7.4 %collective-permute-done.17.refs_0_.refs_9_ = bf16[512,256]{1,0:T(8,128)(2,1)S(1)} collective-permute-done((bf16[512,256]{1,0:T(8,128)(2,1)S(1)}, bf16[512,256]{1,0:T(8,128)(2,1)S(1)}, u32[]{:S(2)}, u32[]{:S(2)}) %collective-permute-start.17) | collective-permute-done | bytes 262176 | tf_op jit(solution)/shard_map/ppermute | solution.py:42
  71.3 4.5 %collective-permute-done.19.refs_2_.refs_11_ = bf16[512,256]{1,0:T(8,128)(2,1)S(1)} collective-permute-done((bf16[512,256]{1,0:T(8,128)(2,1)S(1)}, bf16[512,256]{1,0:T(8,128)(2,1)S(1)}, u32[]{:S(2)}, u32[]{:S(2)}) %collective-permute-start.19) | collective-permute-done | bytes 262176 | tf_op jit(solution)/shard_map/ppermute | solution.py:42
  75.8 1.3 %shard_map.112 = (f32[256,512]{1,0:T(8,128)S(1)}, f32[256,512]{1,0:T(8,128)S(1)}) custom-call(bf16[256,1024]{1,0:T(8,128)(2,1)S(1)} %collective-permute-done.refs_0_, bf16[256,1024]{1,0:T(8,128)(2,1)S(1)} %collective-permute-done.7.refs_1_, bf16[256,1024]{1,0:T(8,128)(2,1)S(1)} %collective-permute-done.8.refs_2_, ...), custom_call_target="tpu_custom_call" | custom-call | flops 11500000 | bytes 65536 | tf_op jit(solution)/shard_map/pallas_call | solution.py:90
  77.1 2.6 %collective-permute-start.20 = (f32[256,512]{1,0:T(8,128)S(1)}, f32[256,512]{1,0:T(8,128)S(1)}, u32[]{:S(2)}, u32[]{:S(2)}) collective-permute-start(f32[256,512]{1,0:T(8,128)S(1)} %get-tuple-element.84), channel_id=1, source_target_pairs={{0,8},{8,0},{16,24},{24,16},{1,9},{9,1},{17,25},{25,17},{32,40},{4... | collective-permute-start | bytes 1572872 | tf_op jit(solution)/shard_map/ppermute | solution.py:42
  79.7 1.5 %collective-permute-done.20.got_ref = f32[256,512]{1,0:T(8,128)S(1)} collective-permute-done((f32[256,512]{1,0:T(8,128)S(1)}, f32[256,512]{1,0:T(8,128)S(1)}, u32[]{:S(2)}, u32[]{:S(2)}) %collective-permute-start.20) | collective-permute-done | bytes 524320 | tf_op jit(solution)/shard_map/ppermute | solution.py:42
  (40 shorter events, 6.8 us)
Async XLA Ops:
  0.6 19.0 %copy-start.1 = (bf16[256,1024]{1,0:T(8,128)(2,1)S(1)}, bf16[256,1024]{1,0:T(8,128)(2,1)}, u32[]{:S(2)}) copy-start(bf16[256,1024]{1,0:T(8,128)(2,1)} %refs_3_.3) | copy-start | bytes 1572868
  0.6 19.0 %copy-start = (bf16[256,1024]{1,0:T(8,128)(2,1)S(1)}, bf16[256,1024]{1,0:T(8,128)(2,1)}, u32[]{:S(2)}) copy-start(bf16[256,1024]{1,0:T(8,128)(2,1)} %refs_5_.3) | copy-start | bytes 1572868
  0.7 6.3 %collective-permute-start.1 = (bf16[256,1024]{1,0:T(8,128)(2,1)}, bf16[256,1024]{1,0:T(8,128)(2,1)S(1)}, u32[]{:S(2)}, u32[]{:S(2)}) collective-permute-start(bf16[256,1024]{1,0:T(8,128)(2,1)} %refs_3_.3), channel_id=1, source_target_pairs={{0,8},{8,0},{16,24},{24,16},{1,9},{9,1},{17,25},{25,17},{32,40},{4... | collective-permute-start | bytes 1572872 | tf_op jit(solution)/shard_map/ppermute | solution.py:42
  2.2 4.8 %collective-permute-start.2 = (bf16[256,1024]{1,0:T(8,128)(2,1)}, bf16[256,1024]{1,0:T(8,128)(2,1)S(1)}, u32[]{:S(2)}, u32[]{:S(2)}) collective-permute-start(bf16[256,1024]{1,0:T(8,128)(2,1)} %refs_5_.3), channel_id=1, source_target_pairs={{0,8},{8,0},{16,24},{24,16},{1,9},{9,1},{17,25},{25,17},{32,40},{4... | collective-permute-start | bytes 1572872 | tf_op jit(solution)/shard_map/ppermute | solution.py:42
  2.2 22.1 %collective-permute-start = (bf16[256,1024]{1,0:T(8,128)(2,1)}, bf16[256,1024]{1,0:T(8,128)(2,1)S(1)}, u32[]{:S(2)}, u32[]{:S(2)}) collective-permute-start(bf16[256,1024]{1,0:T(8,128)(2,1)} %param.14), channel_id=1, source_target_pairs={{0,0},{8,8},{16,1},{24,9},{1,16},{9,24},{17,17},{25,25},{32,2},{40... | collective-permute-start | bytes 1572872 | tf_op jit(solution)/shard_map/ppermute | solution.py:42
  6.9 1.6 %collective-permute-start.3 = (f32[24,256]{1,0:T(8,128)}, f32[24,256]{1,0:T(8,128)S(1)}, u32[]{:S(2)}, u32[]{:S(2)}) collective-permute-start(f32[24,256]{1,0:T(8,128)} %get-tuple-element.48.refs_1_.refs_2_), channel_id=1, source_target_pairs={{0,8},{8,0},{16,24},{24,16},{1,9},{9,1},{17,25},{25,17},{32,40},{4... | collective-permute-start | bytes 73736 | tf_op jit(solution)/shard_map/ppermute | solution.py:42
  8.5 15.8 %collective-permute-start.4 = (bf16[256,256]{1,0:T(8,128)(2,1)}, bf16[256,256]{1,0:T(8,128)(2,1)S(1)}, u32[]{:S(2)}, u32[]{:S(2)}) collective-permute-start(bf16[256,256]{1,0:T(8,128)(2,1)} %get-tuple-element.49.refs_0_), channel_id=1, source_target_pairs={{0,32},{8,40},{16,48},{24,56},{1,33},{9,41},{17,49},{25,57},{64,96... | collective-permute-start | bytes 393224 | tf_op jit(solution)/shard_map/ppermute | solution.py:42
  13.4 10.9 %collective-permute-start.5 = (bf16[256,256]{1,0:T(8,128)(2,1)}, bf16[256,256]{1,0:T(8,128)(2,1)S(1)}, u32[]{:S(2)}, u32[]{:S(2)}) collective-permute-start(bf16[256,256]{1,0:T(8,128)(2,1)} %get-tuple-element.49.refs_0_), channel_id=1, source_target_pairs={{0,48},{8,56},{16,32},{24,40},{1,49},{9,57},{17,33},{25,41},{64,11... | collective-permute-start | bytes 393224 | tf_op jit(solution)/shard_map/ppermute | solution.py:42
  17.4 6.9 %collective-permute-start.6 = (bf16[256,256]{1,0:T(8,128)(2,1)}, bf16[256,256]{1,0:T(8,128)(2,1)S(1)}, u32[]{:S(2)}, u32[]{:S(2)}) collective-permute-start(bf16[256,256]{1,0:T(8,128)(2,1)} %get-tuple-element.49.refs_0_), channel_id=1, source_target_pairs={{0,16},{8,24},{1,17},{9,25},{32,48},{40,56},{33,49},{41,57},{64,80... | collective-permute-start | bytes 393224 | tf_op jit(solution)/shard_map/ppermute | solution.py:42
  21.3 8.4 %copy-start.4 = (f32[24,256]{1,0:T(8,128)S(1)}, f32[24,256]{1,0:T(8,128)}, u32[]{:S(2)}) copy-start(f32[24,256]{1,0:T(8,128)} %get-tuple-element.48.refs_1_.refs_2_) | copy-start | bytes 73732
  24.3 15.7 %collective-permute-start.7 = (bf16[256,1024]{1,0:T(8,128)(2,1)S(1)}, bf16[256,1024]{1,0:T(8,128)(2,1)S(1)}, u32[]{:S(2)}, u32[]{:S(2)}) collective-permute-start(bf16[256,1024]{1,0:T(8,128)(2,1)S(1)} %collective-permute-done.refs_0_), channel_id=1, source_target_pairs={{0,1},{8,9},{16,17},{24,25},{1,0},{9,8},{17,16},{25,24},{32,33},{4... | collective-permute-start | bytes 1572872 | tf_op jit(solution)/shard_map/ppermute | solution.py:42
  26.4 13.7 %collective-permute-start.8 = (bf16[256,1024]{1,0:T(8,128)(2,1)S(1)}, bf16[256,1024]{1,0:T(8,128)(2,1)S(1)}, u32[]{:S(2)}, u32[]{:S(2)}) collective-permute-start(bf16[256,1024]{1,0:T(8,128)(2,1)S(1)} %collective-permute-done.refs_0_), channel_id=1, source_target_pairs={{0,6},{8,14},{16,22},{24,30},{1,7},{9,15},{17,23},{25,31},{32,38},... | collective-permute-start | bytes 1572872 | tf_op jit(solution)/shard_map/ppermute | solution.py:42
  29.7 13.2 %collective-permute-start.9 = (bf16[256,1024]{1,0:T(8,128)(2,1)S(1)}, bf16[256,1024]{1,0:T(8,128)(2,1)S(1)}, u32[]{:S(2)}, u32[]{:S(2)}) collective-permute-start(bf16[256,1024]{1,0:T(8,128)(2,1)S(1)} %collective-permute-done.refs_0_), channel_id=1, source_target_pairs={{0,2},{8,10},{16,18},{24,26},{1,3},{9,11},{17,19},{25,27},{32,34},... | collective-permute-start | bytes 1572872 | tf_op jit(solution)/shard_map/ppermute | solution.py:42
  35.5 8.8 %collective-permute-start.10 = (bf16[512,256]{1,0:T(8,128)(2,1)S(1)}, bf16[512,256]{1,0:T(8,128)(2,1)S(1)}, u32[]{:S(2)}, u32[]{:S(2)}) collective-permute-start(bf16[512,256]{1,0:T(8,128)(2,1)S(1)} %get-tuple-element.67), channel_id=1, source_target_pairs={{32,0},{40,8},{48,16},{56,24},{33,1},{41,9},{49,17},{57,25},{96,64... | collective-permute-start | bytes 786440 | tf_op jit(solution)/shard_map/ppermute | solution.py:42
  42.8 11.0 %collective-permute-start.13 = (bf16[256,1024]{1,0:T(8,128)(2,1)S(1)}, bf16[256,1024]{1,0:T(8,128)(2,1)S(1)}, u32[]{:S(2)}, u32[]{:S(2)}) collective-permute-start(bf16[256,1024]{1,0:T(8,128)(2,1)S(1)} %collective-permute-done.7.refs_1_), channel_id=1, source_target_pairs={{0,6},{8,14},{16,22},{24,30},{1,7},{9,15},{17,23},{25,31},{32,38},... | collective-permute-start | bytes 1572872 | tf_op jit(solution)/shard_map/ppermute | solution.py:42
  43.1 12.2 %collective-permute-start.14 = (bf16[256,1024]{1,0:T(8,128)(2,1)S(1)}, bf16[256,1024]{1,0:T(8,128)(2,1)S(1)}, u32[]{:S(2)}, u32[]{:S(2)}) collective-permute-start(bf16[256,1024]{1,0:T(8,128)(2,1)S(1)} %collective-permute-done.7.refs_1_), channel_id=1, source_target_pairs={{0,2},{8,10},{16,18},{24,26},{1,3},{9,11},{17,19},{25,27},{32,34},... | collective-permute-start | bytes 1572872 | tf_op jit(solution)/shard_map/ppermute | solution.py:42
  44.4 11.9 %collective-permute-start.11 = (bf16[512,256]{1,0:T(8,128)(2,1)S(1)}, bf16[512,256]{1,0:T(8,128)(2,1)S(1)}, u32[]{:S(2)}, u32[]{:S(2)}) collective-permute-start(bf16[512,256]{1,0:T(8,128)(2,1)S(1)} %get-tuple-element.68), channel_id=1, source_target_pairs={{0,16},{8,24},{16,0},{24,8},{1,17},{9,25},{17,1},{25,9},{32,48},{4... | collective-permute-start | bytes 786440 | tf_op jit(solution)/shard_map/ppermute | solution.py:42
  44.5 10.9 %collective-permute-start.12 = (bf16[256,1024]{1,0:T(8,128)(2,1)S(1)}, bf16[256,1024]{1,0:T(8,128)(2,1)S(1)}, u32[]{:S(2)}, u32[]{:S(2)}) collective-permute-start(bf16[256,1024]{1,0:T(8,128)(2,1)S(1)} %get-tuple-element.71), channel_id=1, source_target_pairs={{0,8},{8,0},{16,24},{24,16},{1,9},{9,1},{17,25},{25,17},{32,40},{4... | collective-permute-start | bytes 1572872 | tf_op jit(solution)/shard_map/ppermute | solution.py:42
  56.5 14.8 %collective-permute-start.17 = (bf16[512,256]{1,0:T(8,128)(2,1)S(1)}, bf16[512,256]{1,0:T(8,128)(2,1)S(1)}, u32[]{:S(2)}, u32[]{:S(2)}) collective-permute-start(bf16[512,256]{1,0:T(8,128)(2,1)S(1)} %shard_map.110.refs_8_), channel_id=1, source_target_pairs={{0,96},{8,104},{16,112},{24,120},{1,97},{9,105},{17,113},{25,121},... | collective-permute-start | bytes 786440 | tf_op jit(solution)/shard_map/ppermute | solution.py:42
  61.7 9.5 %collective-permute-start.18 = (bf16[512,256]{1,0:T(8,128)(2,1)S(1)}, bf16[512,256]{1,0:T(8,128)(2,1)S(1)}, u32[]{:S(2)}, u32[]{:S(2)}) collective-permute-start(bf16[512,256]{1,0:T(8,128)(2,1)S(1)} %shard_map.110.refs_8_), channel_id=1, source_target_pairs={{0,64},{8,72},{16,80},{24,88},{1,65},{9,73},{17,81},{25,89},{32,96... | collective-permute-start | bytes 786440 | tf_op jit(solution)/shard_map/ppermute | solution.py:42
  61.7 14.0 %collective-permute-start.19 = (bf16[512,256]{1,0:T(8,128)(2,1)S(1)}, bf16[512,256]{1,0:T(8,128)(2,1)S(1)}, u32[]{:S(2)}, u32[]{:S(2)}) collective-permute-start(bf16[512,256]{1,0:T(8,128)(2,1)S(1)} %shard_map.110.refs_8_), channel_id=1, source_target_pairs={{0,32},{8,40},{16,48},{24,56},{1,33},{9,41},{17,49},{25,57},{32,64... | collective-permute-start | bytes 786440 | tf_op jit(solution)/shard_map/ppermute | solution.py:42
  62.4 13.3 %collective-permute-start.15 = (bf16[256,1024]{1,0:T(8,128)(2,1)S(1)}, bf16[256,1024]{1,0:T(8,128)(2,1)S(1)}, u32[]{:S(2)}, u32[]{:S(2)}) collective-permute-start(bf16[256,1024]{1,0:T(8,128)(2,1)S(1)} %collective-permute-done.8.refs_2_), channel_id=1, source_target_pairs={{0,6},{8,14},{16,22},{24,30},{1,7},{9,15},{17,23},{25,31},{32,38},... | collective-permute-start | bytes 1572872 | tf_op jit(solution)/shard_map/ppermute | solution.py:42
  62.7 13.1 %collective-permute-start.16 = (bf16[256,1024]{1,0:T(8,128)(2,1)S(1)}, bf16[256,1024]{1,0:T(8,128)(2,1)S(1)}, u32[]{:S(2)}, u32[]{:S(2)}) collective-permute-start(bf16[256,1024]{1,0:T(8,128)(2,1)S(1)} %collective-permute-done.14.refs_1_.refs_7_), channel_id=1, source_target_pairs={{0,2},{8,10},{16,18},{24,26},{1,3},{9,11},{17,19},{25,27},{32,34},... | collective-permute-start | bytes 1572872 | tf_op jit(solution)/shard_map/ppermute | solution.py:42
  77.1 4.1 %collective-permute-start.20 = (f32[256,512]{1,0:T(8,128)S(1)}, f32[256,512]{1,0:T(8,128)S(1)}, u32[]{:S(2)}, u32[]{:S(2)}) collective-permute-start(f32[256,512]{1,0:T(8,128)S(1)} %get-tuple-element.84), channel_id=1, source_target_pairs={{0,8},{8,0},{16,24},{24,16},{1,9},{9,1},{17,25},{25,17},{32,40},{4... | collective-permute-start | bytes 1572872 | tf_op jit(solution)/shard_map/ppermute | solution.py:42
  (2 other events, 1.7 us)

commit v11 on v10

--- a/solution.py
+++ b/solution.py
@@ -246,31 +246,31 @@
         d_ref[half * 2 * HD + HD : (half + 1) * 2 * HD, :] = v_grad
 
 
-def weights_kernel(*refs):
-    l_refs, d_refs, (_, sent_ref, kept_ref, d_all) = refs[:8], refs[8:12], refs[12:]
+def weights_kernel(own_half, *refs):
+    l_refs, d_refs, (_, out_ref, d_all) = refs[:8], refs[8:12], refs[12:]
     me, tp = lax.axis_index("ctx"), lax.axis_index("tp")
     core, zl, y = me % 2, (me // 2) % 2, me // 4
     x, zh = tp // 2, tp % 2
     for r in range(4):
         d_all[r] = d_refs[r][...]
     half_width = WIDTH // 2
-    for out_ref, whose in ((sent_ref, 1 - core), (kept_ref, core)):
-        for t in range(2):
-            tile = half_width // 2
-            cols = pl.ds(pl.multiple_of(whose * half_width + t * tile, tile), tile)
-            total = None
-            for s in range(4):
-                for j in range(2):
-                    rows = pl.ds(pl.multiple_of(((zh ^ j) ^ zl) * 2 * HD, 2 * HD), 2 * HD)
-                    term = nn(d_all[(x + s + 2 * y) % 4, rows, :], l_refs[s * 2 + j][:, cols])
-                    total = term if total is None else total + term
-            out_ref[:, t * tile : (t + 1) * tile] = total
-
-
-def weights(l_blocks, d_blocks, ready):
+    whose = core if own_half else 1 - core
+    for t in range(2):
+        tile = half_width // 2
+        cols = pl.ds(pl.multiple_of(whose * half_width + t * tile, tile), tile)
+        total = None
+        for s in range(4):
+            for j in range(2):
+                rows = pl.ds(pl.multiple_of(((zh ^ j) ^ zl) * 2 * HD, 2 * HD), 2 * HD)
+                term = nn(d_all[(x + s + 2 * y) % 4, rows, :], l_refs[s * 2 + j][:, cols])
+                total = term if total is None else total + term
+        out_ref[:, t * tile : (t + 1) * tile] = total
+
+
+def weights(own_half, l_blocks, d_blocks, ready):
     return call(
-        weights_kernel,
-        (struct((2 * HD, WIDTH // 2), f32),) * 2,
+        functools.partial(weights_kernel, own_half),
+        struct((2 * HD, WIDTH // 2), f32),
         (*l_blocks, *d_blocks, ready),
         scratch_shapes=[pltpu.VMEM((4, 4 * HD, ROWS), bf16)],
     )
@@ -312,18 +312,20 @@
     got_zl = send(dkv_low, other_zl)
     dq_par, _ = together(dq_par, dkv_low)
     dq_got = send(dq_par, other_core)
-    query_grad = ((dq_own + dq_got.astype(f32)) * SCALE).astype(bf16)
-    got_zl, query_grad, early = together(got_zl, query_grad, early)
+    got_zl, dq_got, early = together(got_zl, dq_got, early)
     d_own = call(close_kernel, struct((4 * HD, ROWS), bf16), (dkv, got_zl, early))
     d_2, d_1, d_3 = (send(d_own, shifted(dy=-dy)) for dy in (2, 1, 3))
     ready = arrived((d_1, d_2, d_3), 8)
 
     other_3, other_1, own_1, _ = together(other_3, other_1, own_1, d_own)
     own_2, other_2 = send(own_1, behind), send(other_3, ahead)
+    dq_got, d_own = together(dq_got, d_own)
+    query_grad = ((dq_own + dq_got.astype(f32)) * SCALE).astype(bf16)
     l_blocks = (l_own, other_0, own_1, other_1, own_2, other_2, own_3, other_3)
     d_blocks = (d_own, d_1, d_2, d_3)
-    sent, kept = weights(l_blocks, d_blocks, ready)
+    sent = weights(False, l_blocks, d_blocks, ready)
     got = send(sent, other_core)
+    kept = weights(True, l_blocks, d_blocks, ready)
     key_weight, value_weight = call(
         finish_kernel, (struct((WIDTH // 2, HD), f32),) * 2, (kept, got)
     )

time: 82.5 us -> 81.2 us (0.984)
  waiting for transfers between devices: 25.1 us -> 23.6 us
    ppermute x21, waiting for transfers between devices: 25.1 us -> 23.6 us  [send(): return lax.ppermute(value, AXES, route(target))]
    pallas_call x11 -> x12, Pallas kernels: 17.3 us -> 17.6 us  [call(): pl.pallas_call(kernel, out_shape=out_shape, compiler_params=pltpu.Compile...]
  transfers between devices with their start and end apart: 21 -> 21, of which waited for: 7 -> 6; matrix products, arithmetic and copies ran while one was open for 1% -> 1% of each run, Pallas kernels for 18% -> 19%
where the time goes in v11:
time: 81.2 us; the launch traced here: 80.9 us
  starting transfers between devices  36.3 us (45%)
  waiting for transfers between devices  23.6 us (29%)
  Pallas kernels  17.6 us (22%)
  local copies, waits for them, and re-layouts  1.67 us (2%)
  other arithmetic  0.95 us (1%)
  between operations  0.86 us (1%)
    ppermute x21, starting transfers between devices, send(): return lax.ppermute(value, AXES, route(target))  36.3 us
    ppermute x21, waiting for transfers between devices, send(): return lax.ppermute(value, AXES, route(target))  23.6 us
    pallas_call x12, Pallas kernels, call(): pl.pallas_call(kernel, out_shape=out_shape, compiler_params=pltpu.Compile...  17.6 us
    unnamed x10, local copies, waits for them, and re-layouts  1.67 us
  transfers between devices with their start and end apart: 21, of which 6 were waited for; matrix products, arithmetic and copies ran while one was open for 1% of the time, Pallas kernels for 19%

profile of v11, /device:TPU:1, one launch (start us, length us, event | category | flops | bytes accessed | tf_op | source)
XLA Modules:
  0.0 80.9 jit_solution(2169111259328383262)
XLA Ops:
  0.7 1.5 %collective-permute-start.1 = (bf16[256,1024]{1,0:T(8,128)(2,1)}, bf16[256,1024]{1,0:T(8,128)(2,1)S(1)}, u32[]{:S(2)}, u32[]{:S(2)}) collective-permute-start(bf16[256,1024]{1,0:T(8,128)(2,1)} %refs_3_.3), channel_id=1, source_target_pairs={{0,8},{8,0},{16,24},{24,16},{1,9},{9,1},{17,25},{25,17},{32,40},{4... | collective-permute-start | bytes 1572872 | tf_op jit(solution)/shard_map/ppermute | solution.py:42
  2.2 1.7 %collective-permute-start = (bf16[256,1024]{1,0:T(8,128)(2,1)}, bf16[256,1024]{1,0:T(8,128)(2,1)S(1)}, u32[]{:S(2)}, u32[]{:S(2)}) collective-permute-start(bf16[256,1024]{1,0:T(8,128)(2,1)} %param.14), channel_id=1, source_target_pairs={{0,0},{8,8},{16,1},{24,9},{1,16},{9,24},{17,17},{25,25},{32,2},{40... | collective-permute-start | bytes 1572872 | tf_op jit(solution)/shard_map/ppermute | solution.py:42
  3.9 3.0 %shard_map.103 = (bf16[256,256]{1,0:T(8,128)(2,1)}, f32[24,256]{1,0:T(8,128)}) custom-call(s32[16]{0:T(128)} %lengths_ref.1, bf16[256,128]{1,0:T(8,128)(2,1)} %k_any.1, bf16[256,128]{1,0:T(8,128)(2,1)} %v_any.1, bf16[256,1024]{1,0:T(8,128)(2,1)} %refs_5_.3, bf16[256,1024]{1,0:T(8,128)(2,1)} %out_any.1, f32[8,256]{1,0:T(8,128)} %ln_any.1), custom_call_target="tpu_custom_call" | custom-call | flops 345000000 | bytes 65536 | tf_op jit(solution)/shard_map/pallas_call | solution.py:90
  7.4 1.1 %collective-permute-done.3.refs_2_.refs_3_ = f32[24,256]{1,0:T(8,128)S(1)} collective-permute-done((f32[24,256]{1,0:T(8,128)}, f32[24,256]{1,0:T(8,128)S(1)}, u32[]{:S(2)}, u32[]{:S(2)}) %collective-permute-start.3) | collective-permute-done | bytes 24608 | tf_op jit(solution)/shard_map/ppermute | solution.py:42
  8.5 4.9 %collective-permute-start.4 = (bf16[256,256]{1,0:T(8,128)(2,1)}, bf16[256,256]{1,0:T(8,128)(2,1)S(1)}, u32[]{:S(2)}, u32[]{:S(2)}) collective-permute-start(bf16[256,256]{1,0:T(8,128)(2,1)} %get-tuple-element.49.refs_0_), channel_id=1, source_target_pairs={{0,32},{8,40},{16,48},{24,56},{1,33},{9,41},{17,49},{25,57},{64,96... | collective-permute-start | bytes 393224 | tf_op jit(solution)/shard_map/ppermute | solution.py:42
  13.4 4.0 %collective-permute-start.5 = (bf16[256,256]{1,0:T(8,128)(2,1)}, bf16[256,256]{1,0:T(8,128)(2,1)S(1)}, u32[]{:S(2)}, u32[]{:S(2)}) collective-permute-start(bf16[256,256]{1,0:T(8,128)(2,1)} %get-tuple-element.49.refs_0_), channel_id=1, source_target_pairs={{0,48},{8,56},{16,32},{24,40},{1,49},{9,57},{17,33},{25,41},{64,11... | collective-permute-start | bytes 393224 | tf_op jit(solution)/shard_map/ppermute | solution.py:42
  17.4 2.2 %collective-permute-start.6 = (bf16[256,256]{1,0:T(8,128)(2,1)}, bf16[256,256]{1,0:T(8,128)(2,1)S(1)}, u32[]{:S(2)}, u32[]{:S(2)}) collective-permute-start(bf16[256,256]{1,0:T(8,128)(2,1)} %get-tuple-element.49.refs_0_), channel_id=1, source_target_pairs={{0,16},{8,24},{1,17},{9,25},{32,48},{40,56},{33,49},{41,57},{64,80... | collective-permute-start | bytes 393224 | tf_op jit(solution)/shard_map/ppermute | solution.py:42
  21.3 3.0 %shard_map.104 = (f32[256,1024]{1,0:T(8,128)S(1)}, f32[256,1024]{1,0:T(8,128)S(1)}, f32[256,256]{1,0:T(8,128)S(1)}) custom-call(bf16[256,256]{1,0:T(8,128)(2,1)S(1)} %copy-done.2, f32[24,256]{1,0:T(8,128)S(1)} %copy-done.3, f32[24,256]{1,0:T(8,128)S(1)} %collective-permute-done.3.refs_2_.refs_3_, bf16[256,1024]{1,0:T(8,128)(2,1)S(1)} %copy-done.1, ...), custom_call_target="tpu_custom_call" | custom-call | flops 345000000 | bytes 65536 | tf_op jit(solution)/shard_map/pallas_call | solution.py:90
  24.3 2.0 %collective-permute-start.7 = (bf16[256,1024]{1,0:T(8,128)(2,1)S(1)}, bf16[256,1024]{1,0:T(8,128)(2,1)S(1)}, u32[]{:S(2)}, u32[]{:S(2)}) collective-permute-start(bf16[256,1024]{1,0:T(8,128)(2,1)S(1)} %collective-permute-done.refs_0_), channel_id=1, source_target_pairs={{0,1},{8,9},{16,17},{24,25},{1,0},{9,8},{17,16},{25,24},{32,33},{4... | collective-permute-start | bytes 1572872 | tf_op jit(solution)/shard_map/ppermute | solution.py:42
  26.4 3.3 %collective-permute-start.8 = (bf16[256,1024]{1,0:T(8,128)(2,1)S(1)}, bf16[256,1024]{1,0:T(8,128)(2,1)S(1)}, u32[]{:S(2)}, u32[]{:S(2)}) collective-permute-start(bf16[256,1024]{1,0:T(8,128)(2,1)S(1)} %collective-permute-done.refs_0_), channel_id=1, source_target_pairs={{0,6},{8,14},{16,22},{24,30},{1,7},{9,15},{17,23},{25,31},{32,38},... | collective-permute-start | bytes 1572872 | tf_op jit(solution)/shard_map/ppermute | solution.py:42
  29.7 5.8 %shard_map.105 = (f32[256,1024]{1,0:T(8,128)S(1)}, f32[256,1024]{1,0:T(8,128)S(1)}, bf16[512,256]{1,0:T(8,128)(2,1)S(1)}) custom-call(bf16[256,256]{1,0:T(8,128)(2,1)S(1)} %collective-permute-done.4.refs_0_, bf16[256,256]{1,0:T(8,128)(2,1)S(1)} %collective-permute-done.5.refs_1_, f32[24,256]{1,0:T(8,128)S(1)} %copy-done.4, ...), custom_call_target="tpu_custom_call" | custom-call | flops 345000000 | bytes 65536 | tf_op jit(solution)/shard_map/pallas_call | solution.py:90
  35.5 1.5 %collective-permute-start.10 = (bf16[512,256]{1,0:T(8,128)(2,1)S(1)}, bf16[512,256]{1,0:T(8,128)(2,1)S(1)}, u32[]{:S(2)}, u32[]{:S(2)}) collective-permute-start(bf16[512,256]{1,0:T(8,128)(2,1)S(1)} %get-tuple-element.68), channel_id=1, source_target_pairs={{32,0},{40,8},{48,16},{56,24},{33,1},{41,9},{49,17},{57,25},{96,64... | collective-permute-start | bytes 786440 | tf_op jit(solution)/shard_map/ppermute | solution.py:42
  37.0 3.1 %shard_map.106 = (f32[256,1024]{1,0:T(8,128)S(1)}, bf16[256,1024]{1,0:T(8,128)(2,1)S(1)}, f32[256,256]{1,0:T(8,128)S(1)}) custom-call(bf16[256,256]{1,0:T(8,128)(2,1)S(1)} %collective-permute-done.6.refs_0_, f32[24,256]{1,0:T(8,128)S(1)} %copy-done.4, f32[24,256]{1,0:T(8,128)S(1)} %collective-permute-done.3.refs_2_.refs_3_, bf16[256,1024]{1,0:T(8,128)(2,1)S(1)} %copy-done.1, ...), custom_call_target="tpu_custom_call" | custom-call | flops 1724999936 | bytes 65536 | tf_op jit(solution)/shard_map/pallas_call | solution.py:90
  40.1 2.7 %collective-permute-done.9.refs_6_ = bf16[256,1024]{1,0:T(8,128)(2,1)S(1)} collective-permute-done((bf16[256,1024]{1,0:T(8,128)(2,1)S(1)}, bf16[256,1024]{1,0:T(8,128)(2,1)S(1)}, u32[]{:S(2)}, u32[]{:S(2)}) %collective-permute-start.9) | collective-permute-done | bytes 524320 | tf_op jit(solution)/shard_map/ppermute | solution.py:42
  43.1 1.2 %collective-permute-start.14 = (bf16[256,1024]{1,0:T(8,128)(2,1)S(1)}, bf16[256,1024]{1,0:T(8,128)(2,1)S(1)}, u32[]{:S(2)}, u32[]{:S(2)}) collective-permute-start(bf16[256,1024]{1,0:T(8,128)(2,1)S(1)} %collective-permute-done.7.refs_1_), channel_id=1, source_target_pairs={{0,2},{8,10},{16,18},{24,26},{1,3},{9,11},{17,19},{25,27},{32,34},... | collective-permute-start | bytes 1572872 | tf_op jit(solution)/shard_map/ppermute | solution.py:42
  44.5 3.0 %collective-permute-start.12 = (bf16[256,1024]{1,0:T(8,128)(2,1)S(1)}, bf16[256,1024]{1,0:T(8,128)(2,1)S(1)}, u32[]{:S(2)}, u32[]{:S(2)}) collective-permute-start(bf16[256,1024]{1,0:T(8,128)(2,1)S(1)} %get-tuple-element.71), channel_id=1, source_target_pairs={{0,8},{8,0},{16,24},{24,16},{1,9},{9,1},{17,25},{25,17},{32,40},{4... | collective-permute-start | bytes 1572872 | tf_op jit(solution)/shard_map/ppermute | solution.py:42
  47.5 6.4 %collective-permute-done.13.refs_0_.refs_3_ = bf16[256,1024]{1,0:T(8,128)(2,1)S(1)} collective-permute-done((bf16[256,1024]{1,0:T(8,128)(2,1)S(1)}, bf16[256,1024]{1,0:T(8,128)(2,1)S(1)}, u32[]{:S(2)}, u32[]{:S(2)}) %collective-permute-start.13) | collective-permute-done | bytes 524320 | tf_op jit(solution)/shard_map/ppermute | solution.py:42
  53.9 1.5 %collective-permute-done.14.refs_1_.refs_7_ = bf16[256,1024]{1,0:T(8,128)(2,1)S(1)} collective-permute-done((bf16[256,1024]{1,0:T(8,128)(2,1)S(1)}, bf16[256,1024]{1,0:T(8,128)(2,1)S(1)}, u32[]{:S(2)}, u32[]{:S(2)}) %collective-permute-start.14) | collective-permute-done | bytes 524320 | tf_op jit(solution)/shard_map/ppermute | solution.py:42
  55.5 5.3 %collective-permute-start.17 = (bf16[512,256]{1,0:T(8,128)(2,1)S(1)}, bf16[512,256]{1,0:T(8,128)(2,1)S(1)}, u32[]{:S(2)}, u32[]{:S(2)}) collective-permute-start(bf16[512,256]{1,0:T(8,128)(2,1)S(1)} %shard_map.110.refs_8_), channel_id=1, source_target_pairs={{0,96},{8,104},{16,112},{24,120},{1,97},{9,105},{17,113},{25,121},... | collective-permute-start | bytes 786440 | tf_op jit(solution)/shard_map/ppermute | solution.py:42
  61.8 1.2 %collective-permute-start.16 = (bf16[256,1024]{1,0:T(8,128)(2,1)S(1)}, bf16[256,1024]{1,0:T(8,128)(2,1)S(1)}, u32[]{:S(2)}, u32[]{:S(2)}) collective-permute-start(bf16[256,1024]{1,0:T(8,128)(2,1)S(1)} %collective-permute-done.14.refs_1_.refs_7_), channel_id=1, source_target_pairs={{0,2},{8,10},{16,18},{24,26},{1,3},{9,11},{17,19},{25,27},{32,34},... | collective-permute-start | bytes 1572872 | tf_op jit(solution)/shard_map/ppermute | solution.py:42
  62.9 7.4 %collective-permute-done.17.refs_0_.refs_9_ = bf16[512,256]{1,0:T(8,128)(2,1)S(1)} collective-permute-done((bf16[512,256]{1,0:T(8,128)(2,1)S(1)}, bf16[512,256]{1,0:T(8,128)(2,1)S(1)}, u32[]{:S(2)}, u32[]{:S(2)}) %collective-permute-start.17) | collective-permute-done | bytes 262176 | tf_op jit(solution)/shard_map/ppermute | solution.py:42
  70.3 4.5 %collective-permute-done.19.refs_2_.refs_11_ = bf16[512,256]{1,0:T(8,128)(2,1)S(1)} collective-permute-done((bf16[512,256]{1,0:T(8,128)(2,1)S(1)}, bf16[512,256]{1,0:T(8,128)(2,1)S(1)}, u32[]{:S(2)}, u32[]{:S(2)}) %collective-permute-start.19) | collective-permute-done | bytes 262176 | tf_op jit(solution)/shard_map/ppermute | solution.py:42
  75.6 2.6 %collective-permute-start.20 = (f32[256,512]{1,0:T(8,128)S(1)}, f32[256,512]{1,0:T(8,128)S(1)}, u32[]{:S(2)}, u32[]{:S(2)}) collective-permute-start(f32[256,512]{1,0:T(8,128)S(1)} %shard_map.113), channel_id=1, source_target_pairs={{0,8},{8,0},{16,24},{24,16},{1,9},{9,1},{17,25},{25,17},{32,40},{4... | collective-permute-start | bytes 1572872 | tf_op jit(solution)/shard_map/ppermute | solution.py:42
  78.2 0.9 %multiply_convert_fusion = bf16[256,1024]{1,0:T(8,128)(2,1)} fusion(f32[256,1024]{1,0:T(8,128)S(1)} %get-tuple-element.63, bf16[256,1024]{1,0:T(8,128)(2,1)S(1)} %collective-permute-done.12), kind=kLoop, calls=%fused_computation | loop fusion | flops 1048576 | bytes 2097152 | tf_op jit(solution)/shard_map/convert_element_type | solution.py:323
  (41 shorter events, 6.3 us)
Async XLA Ops:
  0.6 19.0 %copy-start.1 = (bf16[256,1024]{1,0:T(8,128)(2,1)S(1)}, bf16[256,1024]{1,0:T(8,128)(2,1)}, u32[]{:S(2)}) copy-start(bf16[256,1024]{1,0:T(8,128)(2,1)} %refs_3_.3) | copy-start | bytes 1572868
  0.6 19.0 %copy-start = (bf16[256,1024]{1,0:T(8,128)(2,1)S(1)}, bf16[256,1024]{1,0:T(8,128)(2,1)}, u32[]{:S(2)}) copy-start(bf16[256,1024]{1,0:T(8,128)(2,1)} %refs_5_.3) | copy-start | bytes 1572868
  0.7 6.3 %collective-permute-start.1 = (bf16[256,1024]{1,0:T(8,128)(2,1)}, bf16[256,1024]{1,0:T(8,128)(2,1)S(1)}, u32[]{:S(2)}, u32[]{:S(2)}) collective-permute-start(bf16[256,1024]{1,0:T(8,128)(2,1)} %refs_3_.3), channel_id=1, source_target_pairs={{0,8},{8,0},{16,24},{24,16},{1,9},{9,1},{17,25},{25,17},{32,40},{4... | collective-permute-start | bytes 1572872 | tf_op jit(solution)/shard_map/ppermute | solution.py:42
  2.2 4.8 %collective-permute-start.2 = (bf16[256,1024]{1,0:T(8,128)(2,1)}, bf16[256,1024]{1,0:T(8,128)(2,1)S(1)}, u32[]{:S(2)}, u32[]{:S(2)}) collective-permute-start(bf16[256,1024]{1,0:T(8,128)(2,1)} %refs_5_.3), channel_id=1, source_target_pairs={{0,8},{8,0},{16,24},{24,16},{1,9},{9,1},{17,25},{25,17},{32,40},{4... | collective-permute-start | bytes 1572872 | tf_op jit(solution)/shard_map/ppermute | solution.py:42
  2.2 22.1 %collective-permute-start = (bf16[256,1024]{1,0:T(8,128)(2,1)}, bf16[256,1024]{1,0:T(8,128)(2,1)S(1)}, u32[]{:S(2)}, u32[]{:S(2)}) collective-permute-start(bf16[256,1024]{1,0:T(8,128)(2,1)} %param.14), channel_id=1, source_target_pairs={{0,0},{8,8},{16,1},{24,9},{1,16},{9,24},{17,17},{25,25},{32,2},{40... | collective-permute-start | bytes 1572872 | tf_op jit(solution)/shard_map/ppermute | solution.py:42
  6.9 1.6 %collective-permute-start.3 = (f32[24,256]{1,0:T(8,128)}, f32[24,256]{1,0:T(8,128)S(1)}, u32[]{:S(2)}, u32[]{:S(2)}) collective-permute-start(f32[24,256]{1,0:T(8,128)} %get-tuple-element.48.refs_1_.refs_2_), channel_id=1, source_target_pairs={{0,8},{8,0},{16,24},{24,16},{1,9},{9,1},{17,25},{25,17},{32,40},{4... | collective-permute-start | bytes 73736 | tf_op jit(solution)/shard_map/ppermute | solution.py:42
  8.5 15.8 %collective-permute-start.4 = (bf16[256,256]{1,0:T(8,128)(2,1)}, bf16[256,256]{1,0:T(8,128)(2,1)S(1)}, u32[]{:S(2)}, u32[]{:S(2)}) collective-permute-start(bf16[256,256]{1,0:T(8,128)(2,1)} %get-tuple-element.49.refs_0_), channel_id=1, source_target_pairs={{0,32},{8,40},{16,48},{24,56},{1,33},{9,41},{17,49},{25,57},{64,96... | collective-permute-start | bytes 393224 | tf_op jit(solution)/shard_map/ppermute | solution.py:42
  13.4 10.9 %collective-permute-start.5 = (bf16[256,256]{1,0:T(8,128)(2,1)}, bf16[256,256]{1,0:T(8,128)(2,1)S(1)}, u32[]{:S(2)}, u32[]{:S(2)}) collective-permute-start(bf16[256,256]{1,0:T(8,128)(2,1)} %get-tuple-element.49.refs_0_), channel_id=1, source_target_pairs={{0,48},{8,56},{16,32},{24,40},{1,49},{9,57},{17,33},{25,41},{64,11... | collective-permute-start | bytes 393224 | tf_op jit(solution)/shard_map/ppermute | solution.py:42
  17.4 6.9 %collective-permute-start.6 = (bf16[256,256]{1,0:T(8,128)(2,1)}, bf16[256,256]{1,0:T(8,128)(2,1)S(1)}, u32[]{:S(2)}, u32[]{:S(2)}) collective-permute-start(bf16[256,256]{1,0:T(8,128)(2,1)} %get-tuple-element.49.refs_0_), channel_id=1, source_target_pairs={{0,16},{8,24},{1,17},{9,25},{32,48},{40,56},{33,49},{41,57},{64,80... | collective-permute-start | bytes 393224 | tf_op jit(solution)/shard_map/ppermute | solution.py:42
  21.3 8.4 %copy-start.4 = (f32[24,256]{1,0:T(8,128)S(1)}, f32[24,256]{1,0:T(8,128)}, u32[]{:S(2)}) copy-start(f32[24,256]{1,0:T(8,128)} %get-tuple-element.48.refs_1_.refs_2_) | copy-start | bytes 73732
  24.3 15.8 %collective-permute-start.7 = (bf16[256,1024]{1,0:T(8,128)(2,1)S(1)}, bf16[256,1024]{1,0:T(8,128)(2,1)S(1)}, u32[]{:S(2)}, u32[]{:S(2)}) collective-permute-start(bf16[256,1024]{1,0:T(8,128)(2,1)S(1)} %collective-permute-done.refs_0_), channel_id=1, source_target_pairs={{0,1},{8,9},{16,17},{24,25},{1,0},{9,8},{17,16},{25,24},{32,33},{4... | collective-permute-start | bytes 1572872 | tf_op jit(solution)/shard_map/ppermute | solution.py:42
  26.4 13.7 %collective-permute-start.8 = (bf16[256,1024]{1,0:T(8,128)(2,1)S(1)}, bf16[256,1024]{1,0:T(8,128)(2,1)S(1)}, u32[]{:S(2)}, u32[]{:S(2)}) collective-permute-start(bf16[256,1024]{1,0:T(8,128)(2,1)S(1)} %collective-permute-done.refs_0_), channel_id=1, source_target_pairs={{0,6},{8,14},{16,22},{24,30},{1,7},{9,15},{17,23},{25,31},{32,38},... | collective-permute-start | bytes 1572872 | tf_op jit(solution)/shard_map/ppermute | solution.py:42
  29.7 13.2 %collective-permute-start.9 = (bf16[256,1024]{1,0:T(8,128)(2,1)S(1)}, bf16[256,1024]{1,0:T(8,128)(2,1)S(1)}, u32[]{:S(2)}, u32[]{:S(2)}) collective-permute-start(bf16[256,1024]{1,0:T(8,128)(2,1)S(1)} %collective-permute-done.refs_0_), channel_id=1, source_target_pairs={{0,2},{8,10},{16,18},{24,26},{1,3},{9,11},{17,19},{25,27},{32,34},... | collective-permute-start | bytes 1572872 | tf_op jit(solution)/shard_map/ppermute | solution.py:42
  35.5 8.8 %collective-permute-start.10 = (bf16[512,256]{1,0:T(8,128)(2,1)S(1)}, bf16[512,256]{1,0:T(8,128)(2,1)S(1)}, u32[]{:S(2)}, u32[]{:S(2)}) collective-permute-start(bf16[512,256]{1,0:T(8,128)(2,1)S(1)} %get-tuple-element.68), channel_id=1, source_target_pairs={{32,0},{40,8},{48,16},{56,24},{33,1},{41,9},{49,17},{57,25},{96,64... | collective-permute-start | bytes 786440 | tf_op jit(solution)/shard_map/ppermute | solution.py:42
  42.8 11.0 %collective-permute-start.13 = (bf16[256,1024]{1,0:T(8,128)(2,1)S(1)}, bf16[256,1024]{1,0:T(8,128)(2,1)S(1)}, u32[]{:S(2)}, u32[]{:S(2)}) collective-permute-start(bf16[256,1024]{1,0:T(8,128)(2,1)S(1)} %collective-permute-done.7.refs_1_), channel_id=1, source_target_pairs={{0,6},{8,14},{16,22},{24,30},{1,7},{9,15},{17,23},{25,31},{32,38},... | collective-permute-start | bytes 1572872 | tf_op jit(solution)/shard_map/ppermute | solution.py:42
  43.1 12.2 %collective-permute-start.14 = (bf16[256,1024]{1,0:T(8,128)(2,1)S(1)}, bf16[256,1024]{1,0:T(8,128)(2,1)S(1)}, u32[]{:S(2)}, u32[]{:S(2)}) collective-permute-start(bf16[256,1024]{1,0:T(8,128)(2,1)S(1)} %collective-permute-done.7.refs_1_), channel_id=1, source_target_pairs={{0,2},{8,10},{16,18},{24,26},{1,3},{9,11},{17,19},{25,27},{32,34},... | collective-permute-start | bytes 1572872 | tf_op jit(solution)/shard_map/ppermute | solution.py:42
  44.4 11.0 %collective-permute-start.11 = (bf16[512,256]{1,0:T(8,128)(2,1)S(1)}, bf16[512,256]{1,0:T(8,128)(2,1)S(1)}, u32[]{:S(2)}, u32[]{:S(2)}) collective-permute-start(bf16[512,256]{1,0:T(8,128)(2,1)S(1)} %get-tuple-element.69), channel_id=1, source_target_pairs={{0,16},{8,24},{16,0},{24,8},{1,17},{9,25},{17,1},{25,9},{32,48},{4... | collective-permute-start | bytes 786440 | tf_op jit(solution)/shard_map/ppermute | solution.py:42
  44.5 10.9 %collective-permute-start.12 = (bf16[256,1024]{1,0:T(8,128)(2,1)S(1)}, bf16[256,1024]{1,0:T(8,128)(2,1)S(1)}, u32[]{:S(2)}, u32[]{:S(2)}) collective-permute-start(bf16[256,1024]{1,0:T(8,128)(2,1)S(1)} %get-tuple-element.71), channel_id=1, source_target_pairs={{0,8},{8,0},{16,24},{24,16},{1,9},{9,1},{17,25},{25,17},{32,40},{4... | collective-permute-start | bytes 1572872 | tf_op jit(solution)/shard_map/ppermute | solution.py:42
  55.5 14.8 %collective-permute-start.17 = (bf16[512,256]{1,0:T(8,128)(2,1)S(1)}, bf16[512,256]{1,0:T(8,128)(2,1)S(1)}, u32[]{:S(2)}, u32[]{:S(2)}) collective-permute-start(bf16[512,256]{1,0:T(8,128)(2,1)S(1)} %shard_map.110.refs_8_), channel_id=1, source_target_pairs={{0,96},{8,104},{16,112},{24,120},{1,97},{9,105},{17,113},{25,121},... | collective-permute-start | bytes 786440 | tf_op jit(solution)/shard_map/ppermute | solution.py:42
  60.8 9.5 %collective-permute-start.18 = (bf16[512,256]{1,0:T(8,128)(2,1)S(1)}, bf16[512,256]{1,0:T(8,128)(2,1)S(1)}, u32[]{:S(2)}, u32[]{:S(2)}) collective-permute-start(bf16[512,256]{1,0:T(8,128)(2,1)S(1)} %shard_map.110.refs_8_), channel_id=1, source_target_pairs={{0,64},{8,72},{16,80},{24,88},{1,65},{9,73},{17,81},{25,89},{32,96... | collective-permute-start | bytes 786440 | tf_op jit(solution)/shard_map/ppermute | solution.py:42
  60.8 14.0 %collective-permute-start.19 = (bf16[512,256]{1,0:T(8,128)(2,1)S(1)}, bf16[512,256]{1,0:T(8,128)(2,1)S(1)}, u32[]{:S(2)}, u32[]{:S(2)}) collective-permute-start(bf16[512,256]{1,0:T(8,128)(2,1)S(1)} %shard_map.110.refs_8_), channel_id=1, source_target_pairs={{0,32},{8,40},{16,48},{24,56},{1,33},{9,41},{17,49},{25,57},{32,64... | collective-permute-start | bytes 786440 | tf_op jit(solution)/shard_map/ppermute | solution.py:42
  61.5 13.3 %collective-permute-start.15 = (bf16[256,1024]{1,0:T(8,128)(2,1)S(1)}, bf16[256,1024]{1,0:T(8,128)(2,1)S(1)}, u32[]{:S(2)}, u32[]{:S(2)}) collective-permute-start(bf16[256,1024]{1,0:T(8,128)(2,1)S(1)} %collective-permute-done.8.refs_2_), channel_id=1, source_target_pairs={{0,6},{8,14},{16,22},{24,30},{1,7},{9,15},{17,23},{25,31},{32,38},... | collective-permute-start | bytes 1572872 | tf_op jit(solution)/shard_map/ppermute | solution.py:42
  61.8 13.1 %collective-permute-start.16 = (bf16[256,1024]{1,0:T(8,128)(2,1)S(1)}, bf16[256,1024]{1,0:T(8,128)(2,1)S(1)}, u32[]{:S(2)}, u32[]{:S(2)}) collective-permute-start(bf16[256,1024]{1,0:T(8,128)(2,1)S(1)} %collective-permute-done.14.refs_1_.refs_7_), channel_id=1, source_target_pairs={{0,2},{8,10},{16,18},{24,26},{1,3},{9,11},{17,19},{25,27},{32,34},... | collective-permute-start | bytes 1572872 | tf_op jit(solution)/shard_map/ppermute | solution.py:42
  75.6 4.3 %collective-permute-start.20 = (f32[256,512]{1,0:T(8,128)S(1)}, f32[256,512]{1,0:T(8,128)S(1)}, u32[]{:S(2)}, u32[]{:S(2)}) collective-permute-start(f32[256,512]{1,0:T(8,128)S(1)} %shard_map.113), channel_id=1, source_target_pairs={{0,8},{8,0},{16,24},{24,16},{1,9},{9,1},{17,25},{25,17},{32,40},{4... | collective-permute-start | bytes 1572872 | tf_op jit(solution)/shard_map/ppermute | solution.py:42
  (2 other events, 1.7 us)

commit v12 on v11

--- a/solution.py
+++ b/solution.py
@@ -304,7 +304,7 @@
     other_0, own_1, own_3, l_own, dkv_zl = together(other_0, own_1, own_3, l_own, dkv_zl)
 
     other_3, other_1 = send(other_0, ahead), send(other_0, behind)
-    early = arrived((other_1, other_3), 8)
+    early = arrived((other_3,), 8)
 
     pair = (2 * ROWS, 2 * HD)
     there = arrived((got_far,), 4)

time: 81.2 us -> 80.4 us (level)
  transfers between devices with their start and end apart: 21 -> 21, of which waited for: 6 -> 6; matrix products, arithmetic and copies ran while one was open for 1% -> 1% of each run, Pallas kernels for 19% -> 20%
where the time goes in v12:
time: 80.4 us; the launch traced here: 80 us
  starting transfers between devices  36.1 us (45%)
  waiting for transfers between devices  22.9 us (28%)
  Pallas kernels  17.6 us (22%)
  local copies, waits for them, and re-layouts  1.67 us (2%)
  other arithmetic  0.95 us (1%)
  between operations  0.85 us (1%)
    ppermute x21, starting transfers between devices, send(): return lax.ppermute(value, AXES, route(target))  36.1 us
    ppermute x21, waiting for transfers between devices, send(): return lax.ppermute(value, AXES, route(target))  22.9 us
    pallas_call x12, Pallas kernels, call(): pl.pallas_call(kernel, out_shape=out_shape, compiler_params=pltpu.Compile...  17.6 us
    unnamed x10, local copies, waits for them, and re-layouts  1.67 us
  transfers between devices with their start and end apart: 21, of which 6 were waited for; matrix products, arithmetic and copies ran while one was open for 1% of the time, Pallas kernels for 20%

profile of v12, /device:TPU:1, one launch (start us, length us, event | category | flops | bytes accessed | tf_op | source)
XLA Modules:
  0.0 80.0 jit_solution(3562302219557324073)
XLA Ops:
  0.7 1.5 %collective-permute-start.1 = (bf16[256,1024]{1,0:T(8,128)(2,1)}, bf16[256,1024]{1,0:T(8,128)(2,1)S(1)}, u32[]{:S(2)}, u32[]{:S(2)}) collective-permute-start(bf16[256,1024]{1,0:T(8,128)(2,1)} %refs_3_.3), channel_id=1, source_target_pairs={{0,8},{8,0},{16,24},{24,16},{1,9},{9,1},{17,25},{25,17},{32,40},{4... | collective-permute-start | bytes 1572872 | tf_op jit(solution)/shard_map/ppermute | solution.py:42
  2.2 1.7 %collective-permute-start = (bf16[256,1024]{1,0:T(8,128)(2,1)}, bf16[256,1024]{1,0:T(8,128)(2,1)S(1)}, u32[]{:S(2)}, u32[]{:S(2)}) collective-permute-start(bf16[256,1024]{1,0:T(8,128)(2,1)} %param.14), channel_id=1, source_target_pairs={{0,0},{8,8},{16,1},{24,9},{1,16},{9,24},{17,17},{25,25},{32,2},{40... | collective-permute-start | bytes 1572872 | tf_op jit(solution)/shard_map/ppermute | solution.py:42
  3.9 3.0 %shard_map.103 = (bf16[256,256]{1,0:T(8,128)(2,1)}, f32[24,256]{1,0:T(8,128)}) custom-call(s32[16]{0:T(128)} %lengths_ref.1, bf16[256,128]{1,0:T(8,128)(2,1)} %k_any.1, bf16[256,128]{1,0:T(8,128)(2,1)} %v_any.1, bf16[256,1024]{1,0:T(8,128)(2,1)} %refs_5_.3, bf16[256,1024]{1,0:T(8,128)(2,1)} %out_any.1, f32[8,256]{1,0:T(8,128)} %ln_any.1), custom_call_target="tpu_custom_call" | custom-call | flops 345000000 | bytes 65536 | tf_op jit(solution)/shard_map/pallas_call | solution.py:90
  7.4 1.1 %collective-permute-done.3.refs_2_.refs_3_ = f32[24,256]{1,0:T(8,128)S(1)} collective-permute-done((f32[24,256]{1,0:T(8,128)}, f32[24,256]{1,0:T(8,128)S(1)}, u32[]{:S(2)}, u32[]{:S(2)}) %collective-permute-start.3) | collective-permute-done | bytes 24608 | tf_op jit(solution)/shard_map/ppermute | solution.py:42
  8.5 4.9 %collective-permute-start.4 = (bf16[256,256]{1,0:T(8,128)(2,1)}, bf16[256,256]{1,0:T(8,128)(2,1)S(1)}, u32[]{:S(2)}, u32[]{:S(2)}) collective-permute-start(bf16[256,256]{1,0:T(8,128)(2,1)} %get-tuple-element.49.refs_0_), channel_id=1, source_target_pairs={{0,32},{8,40},{16,48},{24,56},{1,33},{9,41},{17,49},{25,57},{64,96... | collective-permute-start | bytes 393224 | tf_op jit(solution)/shard_map/ppermute | solution.py:42
  13.4 4.0 %collective-permute-start.5 = (bf16[256,256]{1,0:T(8,128)(2,1)}, bf16[256,256]{1,0:T(8,128)(2,1)S(1)}, u32[]{:S(2)}, u32[]{:S(2)}) collective-permute-start(bf16[256,256]{1,0:T(8,128)(2,1)} %get-tuple-element.49.refs_0_), channel_id=1, source_target_pairs={{0,48},{8,56},{16,32},{24,40},{1,49},{9,57},{17,33},{25,41},{64,11... | collective-permute-start | bytes 393224 | tf_op jit(solution)/shard_map/ppermute | solution.py:42
  17.4 2.2 %collective-permute-start.6 = (bf16[256,256]{1,0:T(8,128)(2,1)}, bf16[256,256]{1,0:T(8,128)(2,1)S(1)}, u32[]{:S(2)}, u32[]{:S(2)}) collective-permute-start(bf16[256,256]{1,0:T(8,128)(2,1)} %get-tuple-element.49.refs_0_), channel_id=1, source_target_pairs={{0,16},{8,24},{1,17},{9,25},{32,48},{40,56},{33,49},{41,57},{64,80... | collective-permute-start | bytes 393224 | tf_op jit(solution)/shard_map/ppermute | solution.py:42
  21.3 3.0 %shard_map.104 = (f32[256,1024]{1,0:T(8,128)S(1)}, f32[256,1024]{1,0:T(8,128)S(1)}, f32[256,256]{1,0:T(8,128)S(1)}) custom-call(bf16[256,256]{1,0:T(8,128)(2,1)S(1)} %copy-done.2, f32[24,256]{1,0:T(8,128)S(1)} %copy-done.3, f32[24,256]{1,0:T(8,128)S(1)} %collective-permute-done.3.refs_2_.refs_3_, bf16[256,1024]{1,0:T(8,128)(2,1)S(1)} %copy-done.1, ...), custom_call_target="tpu_custom_call" | custom-call | flops 345000000 | bytes 65536 | tf_op jit(solution)/shard_map/pallas_call | solution.py:90
  24.3 2.0 %collective-permute-start.7 = (bf16[256,1024]{1,0:T(8,128)(2,1)S(1)}, bf16[256,1024]{1,0:T(8,128)(2,1)S(1)}, u32[]{:S(2)}, u32[]{:S(2)}) collective-permute-start(bf16[256,1024]{1,0:T(8,128)(2,1)S(1)} %collective-permute-done.refs_0_), channel_id=1, source_target_pairs={{0,1},{8,9},{16,17},{24,25},{1,0},{9,8},{17,16},{25,24},{32,33},{4... | collective-permute-start | bytes 1572872 | tf_op jit(solution)/shard_map/ppermute | solution.py:42
  26.4 3.3 %collective-permute-start.8 = (bf16[256,1024]{1,0:T(8,128)(2,1)S(1)}, bf16[256,1024]{1,0:T(8,128)(2,1)S(1)}, u32[]{:S(2)}, u32[]{:S(2)}) collective-permute-start(bf16[256,1024]{1,0:T(8,128)(2,1)S(1)} %collective-permute-done.refs_0_), channel_id=1, source_target_pairs={{0,6},{8,14},{16,22},{24,30},{1,7},{9,15},{17,23},{25,31},{32,38},... | collective-permute-start | bytes 1572872 | tf_op jit(solution)/shard_map/ppermute | solution.py:42
  29.7 5.8 %shard_map.105 = (f32[256,1024]{1,0:T(8,128)S(1)}, f32[256,1024]{1,0:T(8,128)S(1)}, bf16[512,256]{1,0:T(8,128)(2,1)S(1)}) custom-call(bf16[256,256]{1,0:T(8,128)(2,1)S(1)} %collective-permute-done.4.refs_0_, bf16[256,256]{1,0:T(8,128)(2,1)S(1)} %collective-permute-done.5.refs_1_, f32[24,256]{1,0:T(8,128)S(1)} %copy-done.4, ...), custom_call_target="tpu_custom_call" | custom-call | flops 345000000 | bytes 65536 | tf_op jit(solution)/shard_map/pallas_call | solution.py:90
  35.5 1.5 %collective-permute-start.10 = (bf16[512,256]{1,0:T(8,128)(2,1)S(1)}, bf16[512,256]{1,0:T(8,128)(2,1)S(1)}, u32[]{:S(2)}, u32[]{:S(2)}) collective-permute-start(bf16[512,256]{1,0:T(8,128)(2,1)S(1)} %get-tuple-element.68), channel_id=1, source_target_pairs={{32,0},{40,8},{48,16},{56,24},{33,1},{41,9},{49,17},{57,25},{96,64... | collective-permute-start | bytes 786440 | tf_op jit(solution)/shard_map/ppermute | solution.py:42
  37.0 3.1 %shard_map.106 = (f32[256,1024]{1,0:T(8,128)S(1)}, bf16[256,1024]{1,0:T(8,128)(2,1)S(1)}, f32[256,256]{1,0:T(8,128)S(1)}) custom-call(bf16[256,256]{1,0:T(8,128)(2,1)S(1)} %collective-permute-done.6.refs_0_, f32[24,256]{1,0:T(8,128)S(1)} %copy-done.4, f32[24,256]{1,0:T(8,128)S(1)} %collective-permute-done.3.refs_2_.refs_3_, bf16[256,1024]{1,0:T(8,128)(2,1)S(1)} %copy-done.1, ...), custom_call_target="tpu_custom_call" | custom-call | flops 1724999936 | bytes 65536 | tf_op jit(solution)/shard_map/pallas_call | solution.py:90
  40.1 2.7 %collective-permute-done.9.refs_6_ = bf16[256,1024]{1,0:T(8,128)(2,1)S(1)} collective-permute-done((bf16[256,1024]{1,0:T(8,128)(2,1)S(1)}, bf16[256,1024]{1,0:T(8,128)(2,1)S(1)}, u32[]{:S(2)}, u32[]{:S(2)}) %collective-permute-start.9) | collective-permute-done | bytes 524320 | tf_op jit(solution)/shard_map/ppermute | solution.py:42
  43.8 2.4 %collective-permute-start.14 = (bf16[256,1024]{1,0:T(8,128)(2,1)S(1)}, bf16[256,1024]{1,0:T(8,128)(2,1)S(1)}, u32[]{:S(2)}, u32[]{:S(2)}) collective-permute-start(bf16[256,1024]{1,0:T(8,128)(2,1)S(1)} %collective-permute-done.7.refs_1_), channel_id=1, source_target_pairs={{0,6},{8,14},{16,22},{24,30},{1,7},{9,15},{17,23},{25,31},{32,38},... | collective-permute-start | bytes 1572872 | tf_op jit(solution)/shard_map/ppermute | solution.py:42
  46.3 3.1 %collective-permute-start.12 = (bf16[256,1024]{1,0:T(8,128)(2,1)S(1)}, bf16[256,1024]{1,0:T(8,128)(2,1)S(1)}, u32[]{:S(2)}, u32[]{:S(2)}) collective-permute-start(bf16[256,1024]{1,0:T(8,128)(2,1)S(1)} %get-tuple-element.71), channel_id=1, source_target_pairs={{0,8},{8,0},{16,24},{24,16},{1,9},{9,1},{17,25},{25,17},{32,40},{4... | collective-permute-start | bytes 1572872 | tf_op jit(solution)/shard_map/ppermute | solution.py:42
  49.4 5.7 %collective-permute-done.13.refs_0_.refs_7_ = bf16[256,1024]{1,0:T(8,128)(2,1)S(1)} collective-permute-done((bf16[256,1024]{1,0:T(8,128)(2,1)S(1)}, bf16[256,1024]{1,0:T(8,128)(2,1)S(1)}, u32[]{:S(2)}, u32[]{:S(2)}) %collective-permute-start.13) | collective-permute-done | bytes 524320 | tf_op jit(solution)/shard_map/ppermute | solution.py:42
  55.2 5.0 %collective-permute-start.17 = (bf16[512,256]{1,0:T(8,128)(2,1)S(1)}, bf16[512,256]{1,0:T(8,128)(2,1)S(1)}, u32[]{:S(2)}, u32[]{:S(2)}) collective-permute-start(bf16[512,256]{1,0:T(8,128)(2,1)S(1)} %shard_map.110.refs_8_), channel_id=1, source_target_pairs={{0,96},{8,104},{16,112},{24,120},{1,97},{9,105},{17,113},{25,121},... | collective-permute-start | bytes 786440 | tf_op jit(solution)/shard_map/ppermute | solution.py:42
  60.9 1.5 %collective-permute-start.16 = (bf16[256,1024]{1,0:T(8,128)(2,1)S(1)}, bf16[256,1024]{1,0:T(8,128)(2,1)S(1)}, u32[]{:S(2)}, u32[]{:S(2)}) collective-permute-start(bf16[256,1024]{1,0:T(8,128)(2,1)S(1)} %collective-permute-done.13.refs_0_.refs_7_), channel_id=1, source_target_pairs={{0,2},{8,10},{16,18},{24,26},{1,3},{9,11},{17,19},{25,27},{32,34},... | collective-permute-start | bytes 1572872 | tf_op jit(solution)/shard_map/ppermute | solution.py:42
  62.4 7.7 %collective-permute-done.17.refs_0_.refs_9_ = bf16[512,256]{1,0:T(8,128)(2,1)S(1)} collective-permute-done((bf16[512,256]{1,0:T(8,128)(2,1)S(1)}, bf16[512,256]{1,0:T(8,128)(2,1)S(1)}, u32[]{:S(2)}, u32[]{:S(2)}) %collective-permute-start.17) | collective-permute-done | bytes 262176 | tf_op jit(solution)/shard_map/ppermute | solution.py:42
  70.1 4.7 %collective-permute-done.19.refs_2_.refs_11_ = bf16[512,256]{1,0:T(8,128)(2,1)S(1)} collective-permute-done((bf16[512,256]{1,0:T(8,128)(2,1)S(1)}, bf16[512,256]{1,0:T(8,128)(2,1)S(1)}, u32[]{:S(2)}, u32[]{:S(2)}) %collective-permute-start.19) | collective-permute-done | bytes 262176 | tf_op jit(solution)/shard_map/ppermute | solution.py:42
  75.6 1.7 %collective-permute-start.20 = (f32[256,512]{1,0:T(8,128)S(1)}, f32[256,512]{1,0:T(8,128)S(1)}, u32[]{:S(2)}, u32[]{:S(2)}) collective-permute-start(f32[256,512]{1,0:T(8,128)S(1)} %shard_map.113), channel_id=1, source_target_pairs={{0,8},{8,0},{16,24},{24,16},{1,9},{9,1},{17,25},{25,17},{32,40},{4... | collective-permute-start | bytes 1572872 | tf_op jit(solution)/shard_map/ppermute | solution.py:42
  77.4 0.9 %multiply_convert_fusion = bf16[256,1024]{1,0:T(8,128)(2,1)} fusion(f32[256,1024]{1,0:T(8,128)S(1)} %get-tuple-element.63, bf16[256,1024]{1,0:T(8,128)(2,1)S(1)} %collective-permute-done.12), kind=kLoop, calls=%fused_computation | loop fusion | flops 1048576 | bytes 2097152 | tf_op jit(solution)/shard_map/convert_element_type | solution.py:323
  79.1 0.9 %shard_map.114 = (f32[512,128]{1,0:T(8,128)}, f32[512,128]{1,0:T(8,128)}) custom-call(f32[256,512]{1,0:T(8,128)S(1)} %shard_map.112.mine_ref, f32[256,512]{1,0:T(8,128)S(1)} %collective-permute-done.20.got_ref), custom_call_target="tpu_custom_call" | custom-call | flops 11500000 | bytes 65536 | tf_op jit(solution)/shard_map/pallas_call | solution.py:90
  (41 shorter events, 5.8 us)
Async XLA Ops:
  0.6 19.0 %copy-start.1 = (bf16[256,1024]{1,0:T(8,128)(2,1)S(1)}, bf16[256,1024]{1,0:T(8,128)(2,1)}, u32[]{:S(2)}) copy-start(bf16[256,1024]{1,0:T(8,128)(2,1)} %refs_3_.3) | copy-start | bytes 1572868
  0.6 19.0 %copy-start = (bf16[256,1024]{1,0:T(8,128)(2,1)S(1)}, bf16[256,1024]{1,0:T(8,128)(2,1)}, u32[]{:S(2)}) copy-start(bf16[256,1024]{1,0:T(8,128)(2,1)} %refs_5_.3) | copy-start | bytes 1572868
  0.7 6.3 %collective-permute-start.1 = (bf16[256,1024]{1,0:T(8,128)(2,1)}, bf16[256,1024]{1,0:T(8,128)(2,1)S(1)}, u32[]{:S(2)}, u32[]{:S(2)}) collective-permute-start(bf16[256,1024]{1,0:T(8,128)(2,1)} %refs_3_.3), channel_id=1, source_target_pairs={{0,8},{8,0},{16,24},{24,16},{1,9},{9,1},{17,25},{25,17},{32,40},{4... | collective-permute-start | bytes 1572872 | tf_op jit(solution)/shard_map/ppermute | solution.py:42
  2.2 4.8 %collective-permute-start.2 = (bf16[256,1024]{1,0:T(8,128)(2,1)}, bf16[256,1024]{1,0:T(8,128)(2,1)S(1)}, u32[]{:S(2)}, u32[]{:S(2)}) collective-permute-start(bf16[256,1024]{1,0:T(8,128)(2,1)} %refs_5_.3), channel_id=1, source_target_pairs={{0,8},{8,0},{16,24},{24,16},{1,9},{9,1},{17,25},{25,17},{32,40},{4... | collective-permute-start | bytes 1572872 | tf_op jit(solution)/shard_map/ppermute | solution.py:42
  2.2 22.1 %collective-permute-start = (bf16[256,1024]{1,0:T(8,128)(2,1)}, bf16[256,1024]{1,0:T(8,128)(2,1)S(1)}, u32[]{:S(2)}, u32[]{:S(2)}) collective-permute-start(bf16[256,1024]{1,0:T(8,128)(2,1)} %param.14), channel_id=1, source_target_pairs={{0,0},{8,8},{16,1},{24,9},{1,16},{9,24},{17,17},{25,25},{32,2},{40... | collective-permute-start | bytes 1572872 | tf_op jit(solution)/shard_map/ppermute | solution.py:42
  6.9 1.6 %collective-permute-start.3 = (f32[24,256]{1,0:T(8,128)}, f32[24,256]{1,0:T(8,128)S(1)}, u32[]{:S(2)}, u32[]{:S(2)}) collective-permute-start(f32[24,256]{1,0:T(8,128)} %get-tuple-element.48.refs_1_.refs_2_), channel_id=1, source_target_pairs={{0,8},{8,0},{16,24},{24,16},{1,9},{9,1},{17,25},{25,17},{32,40},{4... | collective-permute-start | bytes 73736 | tf_op jit(solution)/shard_map/ppermute | solution.py:42
  8.5 15.8 %collective-permute-start.4 = (bf16[256,256]{1,0:T(8,128)(2,1)}, bf16[256,256]{1,0:T(8,128)(2,1)S(1)}, u32[]{:S(2)}, u32[]{:S(2)}) collective-permute-start(bf16[256,256]{1,0:T(8,128)(2,1)} %get-tuple-element.49.refs_0_), channel_id=1, source_target_pairs={{0,32},{8,40},{16,48},{24,56},{1,33},{9,41},{17,49},{25,57},{64,96... | collective-permute-start | bytes 393224 | tf_op jit(solution)/shard_map/ppermute | solution.py:42
  13.4 10.9 %collective-permute-start.5 = (bf16[256,256]{1,0:T(8,128)(2,1)}, bf16[256,256]{1,0:T(8,128)(2,1)S(1)}, u32[]{:S(2)}, u32[]{:S(2)}) collective-permute-start(bf16[256,256]{1,0:T(8,128)(2,1)} %get-tuple-element.49.refs_0_), channel_id=1, source_target_pairs={{0,48},{8,56},{16,32},{24,40},{1,49},{9,57},{17,33},{25,41},{64,11... | collective-permute-start | bytes 393224 | tf_op jit(solution)/shard_map/ppermute | solution.py:42
  17.4 6.9 %collective-permute-start.6 = (bf16[256,256]{1,0:T(8,128)(2,1)}, bf16[256,256]{1,0:T(8,128)(2,1)S(1)}, u32[]{:S(2)}, u32[]{:S(2)}) collective-permute-start(bf16[256,256]{1,0:T(8,128)(2,1)} %get-tuple-element.49.refs_0_), channel_id=1, source_target_pairs={{0,16},{8,24},{1,17},{9,25},{32,48},{40,56},{33,49},{41,57},{64,80... | collective-permute-start | bytes 393224 | tf_op jit(solution)/shard_map/ppermute | solution.py:42
  21.3 8.4 %copy-start.4 = (f32[24,256]{1,0:T(8,128)S(1)}, f32[24,256]{1,0:T(8,128)}, u32[]{:S(2)}) copy-start(f32[24,256]{1,0:T(8,128)} %get-tuple-element.48.refs_1_.refs_2_) | copy-start | bytes 73732
  24.3 15.8 %collective-permute-start.7 = (bf16[256,1024]{1,0:T(8,128)(2,1)S(1)}, bf16[256,1024]{1,0:T(8,128)(2,1)S(1)}, u32[]{:S(2)}, u32[]{:S(2)}) collective-permute-start(bf16[256,1024]{1,0:T(8,128)(2,1)S(1)} %collective-permute-done.refs_0_), channel_id=1, source_target_pairs={{0,1},{8,9},{16,17},{24,25},{1,0},{9,8},{17,16},{25,24},{32,33},{4... | collective-permute-start | bytes 1572872 | tf_op jit(solution)/shard_map/ppermute | solution.py:42
  26.4 13.7 %collective-permute-start.8 = (bf16[256,1024]{1,0:T(8,128)(2,1)S(1)}, bf16[256,1024]{1,0:T(8,128)(2,1)S(1)}, u32[]{:S(2)}, u32[]{:S(2)}) collective-permute-start(bf16[256,1024]{1,0:T(8,128)(2,1)S(1)} %collective-permute-done.refs_0_), channel_id=1, source_target_pairs={{0,6},{8,14},{16,22},{24,30},{1,7},{9,15},{17,23},{25,31},{32,38},... | collective-permute-start | bytes 1572872 | tf_op jit(solution)/shard_map/ppermute | solution.py:42
  29.7 13.2 %collective-permute-start.9 = (bf16[256,1024]{1,0:T(8,128)(2,1)S(1)}, bf16[256,1024]{1,0:T(8,128)(2,1)S(1)}, u32[]{:S(2)}, u32[]{:S(2)}) collective-permute-start(bf16[256,1024]{1,0:T(8,128)(2,1)S(1)} %collective-permute-done.refs_0_), channel_id=1, source_target_pairs={{0,2},{8,10},{16,18},{24,26},{1,3},{9,11},{17,19},{25,27},{32,34},... | collective-permute-start | bytes 1572872 | tf_op jit(solution)/shard_map/ppermute | solution.py:42
  35.5 8.2 %collective-permute-start.10 = (bf16[512,256]{1,0:T(8,128)(2,1)S(1)}, bf16[512,256]{1,0:T(8,128)(2,1)S(1)}, u32[]{:S(2)}, u32[]{:S(2)}) collective-permute-start(bf16[512,256]{1,0:T(8,128)(2,1)S(1)} %get-tuple-element.68), channel_id=1, source_target_pairs={{32,0},{40,8},{48,16},{56,24},{33,1},{41,9},{49,17},{57,25},{96,64... | collective-permute-start | bytes 786440 | tf_op jit(solution)/shard_map/ppermute | solution.py:42
  42.8 12.2 %collective-permute-start.13 = (bf16[256,1024]{1,0:T(8,128)(2,1)S(1)}, bf16[256,1024]{1,0:T(8,128)(2,1)S(1)}, u32[]{:S(2)}, u32[]{:S(2)}) collective-permute-start(bf16[256,1024]{1,0:T(8,128)(2,1)S(1)} %collective-permute-done.7.refs_1_), channel_id=1, source_target_pairs={{0,2},{8,10},{16,18},{24,26},{1,3},{9,11},{17,19},{25,27},{32,34},... | collective-permute-start | bytes 1572872 | tf_op jit(solution)/shard_map/ppermute | solution.py:42
  43.8 17.2 %collective-permute-start.14 = (bf16[256,1024]{1,0:T(8,128)(2,1)S(1)}, bf16[256,1024]{1,0:T(8,128)(2,1)S(1)}, u32[]{:S(2)}, u32[]{:S(2)}) collective-permute-start(bf16[256,1024]{1,0:T(8,128)(2,1)S(1)} %collective-permute-done.7.refs_1_), channel_id=1, source_target_pairs={{0,6},{8,14},{16,22},{24,30},{1,7},{9,15},{17,23},{25,31},{32,38},... | collective-permute-start | bytes 1572872 | tf_op jit(solution)/shard_map/ppermute | solution.py:42
  46.2 8.9 %collective-permute-start.11 = (bf16[512,256]{1,0:T(8,128)(2,1)S(1)}, bf16[512,256]{1,0:T(8,128)(2,1)S(1)}, u32[]{:S(2)}, u32[]{:S(2)}) collective-permute-start(bf16[512,256]{1,0:T(8,128)(2,1)S(1)} %get-tuple-element.69), channel_id=1, source_target_pairs={{0,16},{8,24},{16,0},{24,8},{1,17},{9,25},{17,1},{25,9},{32,48},{4... | collective-permute-start | bytes 786440 | tf_op jit(solution)/shard_map/ppermute | solution.py:42
  46.3 8.8 %collective-permute-start.12 = (bf16[256,1024]{1,0:T(8,128)(2,1)S(1)}, bf16[256,1024]{1,0:T(8,128)(2,1)S(1)}, u32[]{:S(2)}, u32[]{:S(2)}) collective-permute-start(bf16[256,1024]{1,0:T(8,128)(2,1)S(1)} %get-tuple-element.71), channel_id=1, source_target_pairs={{0,8},{8,0},{16,24},{24,16},{1,9},{9,1},{17,25},{25,17},{32,40},{4... | collective-permute-start | bytes 1572872 | tf_op jit(solution)/shard_map/ppermute | solution.py:42
  55.2 14.9 %collective-permute-start.17 = (bf16[512,256]{1,0:T(8,128)(2,1)S(1)}, bf16[512,256]{1,0:T(8,128)(2,1)S(1)}, u32[]{:S(2)}, u32[]{:S(2)}) collective-permute-start(bf16[512,256]{1,0:T(8,128)(2,1)S(1)} %shard_map.110.refs_8_), channel_id=1, source_target_pairs={{0,96},{8,104},{16,112},{24,120},{1,97},{9,105},{17,113},{25,121},... | collective-permute-start | bytes 786440 | tf_op jit(solution)/shard_map/ppermute | solution.py:42
  60.3 9.9 %collective-permute-start.18 = (bf16[512,256]{1,0:T(8,128)(2,1)S(1)}, bf16[512,256]{1,0:T(8,128)(2,1)S(1)}, u32[]{:S(2)}, u32[]{:S(2)}) collective-permute-start(bf16[512,256]{1,0:T(8,128)(2,1)S(1)} %shard_map.110.refs_8_), channel_id=1, source_target_pairs={{0,64},{8,72},{16,80},{24,88},{1,65},{9,73},{17,81},{25,89},{32,96... | collective-permute-start | bytes 786440 | tf_op jit(solution)/shard_map/ppermute | solution.py:42
  60.3 14.6 %collective-permute-start.19 = (bf16[512,256]{1,0:T(8,128)(2,1)S(1)}, bf16[512,256]{1,0:T(8,128)(2,1)S(1)}, u32[]{:S(2)}, u32[]{:S(2)}) collective-permute-start(bf16[512,256]{1,0:T(8,128)(2,1)S(1)} %shard_map.110.refs_8_), channel_id=1, source_target_pairs={{0,32},{8,40},{16,48},{24,56},{1,33},{9,41},{17,49},{25,57},{32,64... | collective-permute-start | bytes 786440 | tf_op jit(solution)/shard_map/ppermute | solution.py:42
  60.9 13.9 %collective-permute-start.15 = (bf16[256,1024]{1,0:T(8,128)(2,1)S(1)}, bf16[256,1024]{1,0:T(8,128)(2,1)S(1)}, u32[]{:S(2)}, u32[]{:S(2)}) collective-permute-start(bf16[256,1024]{1,0:T(8,128)(2,1)S(1)} %collective-permute-done.8.refs_2_), channel_id=1, source_target_pairs={{0,6},{8,14},{16,22},{24,30},{1,7},{9,15},{17,23},{25,31},{32,38},... | collective-permute-start | bytes 1572872 | tf_op jit(solution)/shard_map/ppermute | solution.py:42
  60.9 13.9 %collective-permute-start.16 = (bf16[256,1024]{1,0:T(8,128)(2,1)S(1)}, bf16[256,1024]{1,0:T(8,128)(2,1)S(1)}, u32[]{:S(2)}, u32[]{:S(2)}) collective-permute-start(bf16[256,1024]{1,0:T(8,128)(2,1)S(1)} %collective-permute-done.13.refs_0_.refs_7_), channel_id=1, source_target_pairs={{0,2},{8,10},{16,18},{24,26},{1,3},{9,11},{17,19},{25,27},{32,34},... | collective-permute-start | bytes 1572872 | tf_op jit(solution)/shard_map/ppermute | solution.py:42
  75.6 3.5 %collective-permute-start.20 = (f32[256,512]{1,0:T(8,128)S(1)}, f32[256,512]{1,0:T(8,128)S(1)}, u32[]{:S(2)}, u32[]{:S(2)}) collective-permute-start(f32[256,512]{1,0:T(8,128)S(1)} %shard_map.113), channel_id=1, source_target_pairs={{0,8},{8,0},{16,24},{24,16},{1,9},{9,1},{17,25},{25,17},{32,40},{4... | collective-permute-start | bytes 1572872 | tf_op jit(solution)/shard_map/ppermute | solution.py:42
  (2 other events, 1.7 us)
